TPU v7x, 32 devices: a whole 2x2x4 slice. The times are simulated.
32 devices in a mesh: dp: 16 (over z, y, core), mp: 2 (over x).
Axes of the slice: x: 2, y: 2, z: 4, core: 2. Of those that a mesh axis runs over, the one named last changes fastest.
Arguments:
- layer_input: bfloat16 [32, 64, 1024], P('dp', None, 'mp'), may hold values from -6 to 6
- labels: int32 [32], P('dp'), may hold values from 0 to 999
- text_ids: int32 [32, 64], P('dp'), may hold values from 0 to 999
- noise_seeds: int32 [32], P('dp'), may hold values from 0 to 999999
- penalty_mask: int32 [32], P('dp'), may hold values from 0 to 1, as said below
- class_table: bfloat16 [1000, 512], replicated, may hold values from -6 to 6
- token_table: bfloat16 [1000, 768], replicated, may hold values from -6 to 6
- sel_weight: bfloat16 [512, 8], replicated, may hold values from -0.25 to 0.25
- mod_weight: bfloat16 [512, 1024], replicated, may hold values from -0.09375 to 0.09375
- rgb_mod: bfloat16 [512, 1024], replicated, may hold values from -0.09375 to 0.09375
- rgb_weight: bfloat16 [3, 1024], replicated, may hold values from -0.1875 to 0.1875
- conv_bias: bfloat16 [1024], replicated, may hold values from -3 to 3
- noise_strength: bfloat16 [1024], replicated, may hold values from -4 to 4
- kernel_bank: bfloat16 [8, 9, 1024, 1024], P(None, None, 'dp', 'mp'), may hold values from -0.0625 to 0.0625
- qk_weight: bfloat16 [1024, 1024], P('dp', 'mp'), may hold values from -0.0625 to 0.0625
- value_weight: bfloat16 [1024, 1024], P('dp', 'mp'), may hold values from -0.1875 to 0.1875
- attn_out: bfloat16 [1024, 1024], P('mp', 'dp'), may hold values from -1.5 to 1.5
- cross_query: bfloat16 [1024, 1024], P('dp', 'mp'), may hold values from -0.1875 to 0.1875
- cross_key: bfloat16 [768, 1024], P('dp', 'mp'), may hold values from -0.21875 to 0.21875
- cross_value: bfloat16 [768, 1024], P('dp', 'mp'), may hold values from -0.21875 to 0.21875
- cross_out: bfloat16 [1024, 1024], P('mp', 'dp'), may hold values from -1 to 1
- mlp_in: bfloat16 [1024, 4096], P('dp', 'mp'), may hold values from -0.1875 to 0.1875
- mlp_out: bfloat16 [4096, 1024], P('mp', 'dp'), may hold values from -0.09375 to 0.09375
- cot_feat: bfloat16 [32, 256, 1024], P('dp', None, 'mp'), may hold values from -6 to 6
- cot_rgb: bfloat16 [32, 3, 256], P('dp'), may hold values from -6 to 6
- penalty_dir: bfloat16 [32, 3, 256], P('dp'), may hold values from -6 to 6
Outputs:
- layer_output: float32 [32, 256, 1024], P('dp', None, 'mp')
- rgb_output: float32 [32, 3, 256], P('dp')
- input_grad: float32 [32, 64, 1024], P('dp', None, 'mp')
- class_table_grad: float32 [1000, 512], replicated
- token_table_grad: float32 [1000, 768], replicated
- sel_weight_grad: float32 [512, 8], replicated
- mod_weight_grad: float32 [512, 1024], replicated
- rgb_mod_grad: float32 [512, 1024], replicated
- rgb_weight_grad: float32 [3, 1024], replicated
- conv_bias_grad: float32 [1024], replicated
- noise_strength_grad: float32 [1024], replicated
- kernel_bank_grad: float32 [8, 9, 1024, 1024], P(None, None, 'dp', 'mp')
- qk_weight_grad: float32 [1024, 1024], P('dp', 'mp')
- value_weight_grad: float32 [1024, 1024], P('dp', 'mp')
- attn_out_grad: float32 [1024, 1024], P('mp', 'dp')
- cross_query_grad: float32 [1024, 1024], P('dp', 'mp')
- cross_key_grad: float32 [768, 1024], P('dp', 'mp')
- cross_value_grad: float32 [768, 1024], P('dp', 'mp')
- cross_out_grad: float32 [1024, 1024], P('mp', 'dp')
- mlp_in_grad: float32 [1024, 4096], P('dp', 'mp')
- mlp_out_grad: float32 [4096, 1024], P('mp', 'dp')
Inputs may be any that keep to these rules, and one draw needn't show every extreme that they name: `penalty_mask`: 1 marks a sample whose input-gradient penalty counts, 0 one whose does not.
All inputs are finite; a program needn't handle non-finite values.
Results may differ from a plain program's by a relative error of at most 0.025.
Values may be sent and summed in bfloat16 or wider, within the bound.
A program may use at most 512 MiB of HBM per device.

v0:
```python
import jax
import jax.numpy as jnp
from jax import lax
from jax.sharding import PartitionSpec as P

HEAD = 64
SIDE = 16


penalty_weight = 1.0


def rounded(values):
    return lax.optimization_barrier(values.astype(jnp.bfloat16)).astype(jnp.float32)


def matmul_high(left, right):
    return jnp.matmul(left, right, precision=lax.Precision.HIGHEST)


def einsum_high(form, *operands):
    return jnp.einsum(form, *operands, precision=lax.Precision.HIGHEST)


def einsum_low(form, left, right):
    return jnp.einsum(
        form,
        left.astype(jnp.bfloat16),
        right.astype(jnp.bfloat16),
        preferred_element_type=jnp.float32,
    )


def noise_field(seed_ids, pixel_count):
    pixel_ids = jnp.arange(pixel_count, dtype=jnp.int32)
    mixed = seed_ids[:, None] * 1103515245 + pixel_ids[None, :] * 40503
    mixed = jnp.bitwise_xor(mixed, jnp.right_shift(mixed, 13)) * 1664525 + 1013904223
    levels = jnp.bitwise_and(jnp.right_shift(mixed, 8), 65535)
    return levels.astype(jnp.float32) / 65536.0 - 0.5


def patches_of(flat_rows, side_len):
    samples_here, pixels, width_here = flat_rows.shape
    half_side = side_len // 2
    picture = flat_rows.reshape(samples_here, half_side, half_side, width_here)
    picture = jnp.repeat(jnp.repeat(picture, 2, axis=1), 2, axis=2)
    padded = jnp.pad(picture, ((0, 0), (1, 1), (1, 1), (0, 0)))
    pieces = [
        padded[:, shift_row : shift_row + side_len, shift_col : shift_col + side_len, :]
        for shift_row in range(3)
        for shift_col in range(3)
    ]
    return jnp.concatenate(pieces, axis=-1).reshape(
        samples_here, side_len * side_len, 9 * width_here
    )


def rms_norm(values):
    return values * lax.rsqrt(jnp.mean(values * values, axis=-1, keepdims=True) + 1e-06)


def conv_part(gathered, kernel, scales, bias_local, strength_local, noise_map):
    samples_here = gathered.shape[0]
    width_out = kernel.shape[2]
    columns = patches_of(gathered, SIDE)
    conv_out = einsum_low("bpr,bro->bpo", columns, kernel)
    squares = jnp.sum((kernel * kernel).reshape(samples_here, 9, -1, width_out), axis=1)
    demodulate = lax.rsqrt(einsum_high("bi,bio->bo", scales * scales, squares) + 1e-08)
    before = conv_out * demodulate[:, None, :] + bias_local + noise_map[:, :, None] * strength_local
    return jax.nn.silu(before)


def self_attention(active, qk_w, value_w, out_w):
    normed = rounded(rms_norm(active))
    queries = rounded(matmul_high(normed, qk_w))
    values = rounded(matmul_high(normed, value_w))
    samples_here, pixels, width_here = queries.shape
    heads_here = width_here // HEAD
    q_heads = queries.reshape(samples_here, pixels, heads_here, HEAD)
    v_heads = values.reshape(samples_here, pixels, heads_here, HEAD)
    lengths = jnp.transpose(jnp.sum(q_heads * q_heads, axis=-1), (0, 2, 1))
    scores = (
        2.0 * einsum_low("bphd,bqhd->bhpq", q_heads, q_heads) - lengths[:, :, None, :]
    ) * HEAD ** (-0.5)
    soft_weights = rounded(jax.nn.softmax(scores, axis=-1))
    mixture = rounded(
        einsum_low("bhpq,bqhd->bphd", soft_weights, v_heads).reshape(
            samples_here, pixels, width_here
        )
    )
    return matmul_high(mixture, out_w)


def cross_attention(active, text_rows, query_w, key_w, value_w, out_w):
    normed = rounded(rms_norm(active))
    queries = rounded(matmul_high(normed, query_w))
    key_rows = rounded(matmul_high(text_rows, key_w))
    values = rounded(matmul_high(text_rows, value_w))
    samples_here, pixels, width_here = queries.shape
    tokens = key_rows.shape[1]
    heads_here = width_here // HEAD
    q_heads = queries.reshape(samples_here, pixels, heads_here, HEAD)
    k_heads = key_rows.reshape(samples_here, tokens, heads_here, HEAD)
    v_heads = values.reshape(samples_here, tokens, heads_here, HEAD)
    scores = einsum_low("bphd,bthd->bhpt", q_heads, k_heads) * HEAD ** (-0.5)
    soft_weights = rounded(jax.nn.softmax(scores, axis=-1))
    mixture = rounded(
        einsum_low("bhpt,bthd->bphd", soft_weights, v_heads).reshape(
            samples_here, pixels, width_here
        )
    )
    return matmul_high(mixture, out_w)


def feed_forward(active, weight_in, weight_out):
    normed = rounded(rms_norm(active))
    inner = rounded(jax.nn.gelu(matmul_high(normed, weight_in)))
    return matmul_high(inner, weight_out)


def tree_add(first, second):
    return jax.tree.map(jnp.add, first, second)


def per_device(
    layer_input,
    labels,
    text_ids,
    noise_seeds,
    penalty_mask,
    class_table,
    token_table,
    sel_weight,
    mod_weight,
    rgb_mod,
    rgb_weight,
    conv_bias,
    noise_strength,
    kernel_bank,
    qk_weight,
    value_weight,
    attn_out,
    cross_query,
    cross_key,
    cross_value,
    cross_out,
    mlp_in,
    mlp_out,
    cot_feat,
    cot_rgb,
    penalty_dir,
):
    width_local = layer_input.shape[2]
    offset = lax.axis_index("mp") * width_local
    small_params = tuple(
        (
            entry.astype(jnp.float32)
            for entry in (
                class_table,
                token_table,
                sel_weight,
                mod_weight,
                rgb_mod,
                rgb_weight,
                conv_bias,
                noise_strength,
            )
        )
    )

    def fetch_proj():
        fetched = (
            lax.all_gather(qk_weight, "dp", axis=0, tiled=True),
            lax.all_gather(value_weight, "dp", axis=0, tiled=True),
            lax.all_gather(attn_out, "dp", axis=1, tiled=True),
            lax.all_gather(cross_query, "dp", axis=0, tiled=True),
            lax.all_gather(cross_key, "dp", axis=0, tiled=True),
            lax.all_gather(cross_value, "dp", axis=0, tiled=True),
            lax.all_gather(cross_out, "dp", axis=1, tiled=True),
            lax.all_gather(mlp_in, "dp", axis=0, tiled=True),
            lax.all_gather(mlp_out, "dp", axis=1, tiled=True),
        )
        return tuple((entry.astype(jnp.float32) for entry in fetched))

    def style_part(param_set):
        table_class, table_word, select_w, modul_w, rgbmod_w, rgbout_w, bias_w, strength_w = (
            param_set
        )
        onehot_class = (
            labels[:, None] == jnp.arange(table_class.shape[0], dtype=jnp.int32)[None, :]
        ).astype(jnp.float32)
        latent = matmul_high(onehot_class, table_class)
        onehot_word = (
            text_ids[:, :, None] == jnp.arange(table_word.shape[0], dtype=jnp.int32)
        ).astype(jnp.float32)
        text_rows = matmul_high(onehot_word, table_word)
        select = jax.nn.softmax(matmul_high(latent, select_w), axis=-1)
        scales = 1.0 + matmul_high(latent, modul_w)
        rgb_scales = 1.0 + matmul_high(
            latent, lax.dynamic_slice_in_dim(rgbmod_w, offset, width_local, 1)
        )
        bias_local = lax.dynamic_slice_in_dim(bias_w, offset, width_local, 0)
        strength_local = lax.dynamic_slice_in_dim(strength_w, offset, width_local, 0)
        colour_local = lax.dynamic_slice_in_dim(rgbout_w, offset, width_local, 1)
        return (select, scales, rgb_scales, text_rows, bias_local, strength_local, colour_local)

    styles, style_pull = jax.vjp(style_part, small_params)
    noise_map = noise_field(noise_seeds, SIDE * SIDE)

    def owned_sets():
        proj_set = fetch_proj()
        conv_set = (lax.all_gather(kernel_bank, "dp", axis=2, tiled=True).astype(jnp.float32),)
        return ((), conv_set, proj_set[0:3], proj_set[3:7], proj_set[7:9], ())

    def seg_in(active, styles_in, own_set):
        return active * lax.dynamic_slice_in_dim(styles_in[1], offset, width_local, 1)[:, None, :]

    def seg_conv(active, styles_in, own_set):
        bank_full = own_set[0]
        kernel = rounded(matmul_high(styles_in[0], bank_full.reshape(bank_full.shape[0], -1)))
        kernel = kernel.reshape(active.shape[0], -1, bank_full.shape[3])
        return conv_part(active, kernel, styles_in[1], styles_in[4], styles_in[5], noise_map)

    def seg_self(active, styles_in, own_set):
        return self_attention(active, own_set[0], own_set[1], own_set[2])

    def seg_cross(active, styles_in, own_set):
        return cross_attention(active, styles_in[3], own_set[0], own_set[1], own_set[2], own_set[3])

    def seg_mlp(active, styles_in, own_set):
        return feed_forward(active, own_set[0], own_set[1])

    def seg_rgb(active, styles_in, own_set):
        return einsum_high("bpc,bc,kc->bkp", active, styles_in[2], styles_in[6])

    def spread(stacked):
        return lax.all_gather(stacked, "mp", axis=3, tiled=True)

    def collect(stacked):
        return lax.psum_scatter(
            stacked.astype(jnp.bfloat16), "mp", scatter_dimension=3, tiled=True
        ).astype(jnp.float32)

    def spread_one(values):
        return spread(values.astype(jnp.bfloat16)[None])[0].astype(jnp.float32)

    def collect_one(values):
        return collect(values[None])[0]

    own_first = owned_sets()
    input_full = layer_input.astype(jnp.float32)
    gathered_x = spread_one(seg_in(input_full, styles, own_first[0]))
    hidden_one = seg_conv(gathered_x, styles, own_first[1])
    gathered_one = spread_one(hidden_one)
    hidden_two = hidden_one + collect_one(seg_self(gathered_one, styles, own_first[2]))
    gathered_two = spread_one(hidden_two)
    hidden_three = hidden_two + collect_one(seg_cross(gathered_two, styles, own_first[3]))
    gathered_three = spread_one(hidden_three)
    hidden_four = hidden_three + collect_one(seg_mlp(gathered_three, styles, own_first[4]))
    picture = lax.psum(seg_rgb(hidden_four, styles, own_first[5]), "mp")
    own_second = owned_sets()

    def pull_act(segment, active, own_set, cotan):
        return jax.vjp(lambda inner_x: segment(inner_x, styles, own_set), active)[1](cotan)[0]

    grad_four = pull_act(seg_rgb, hidden_four, own_second[5], penalty_dir.astype(jnp.float32))
    back_three = pull_act(seg_mlp, gathered_three, own_second[4], spread_one(grad_four))
    grad_three = grad_four + rounded(collect_one(back_three))
    back_two = pull_act(seg_cross, gathered_two, own_second[3], spread_one(grad_three))
    grad_two = grad_three + rounded(collect_one(back_two))
    back_one = pull_act(seg_self, gathered_one, own_second[2], spread_one(grad_two))
    grad_one = grad_two + rounded(collect_one(back_one))
    grad_moduled = rounded(collect_one(pull_act(seg_conv, gathered_x, own_second[1], grad_one)))
    penalty_grad = pull_act(seg_in, input_full, own_second[0], grad_moduled)
    tangent = penalty_weight * penalty_mask.astype(jnp.float32)[:, None, None] * penalty_grad
    own_third = owned_sets()

    def push(segment, active, own_set, tangent_in):
        return jax.jvp(lambda inner_x: segment(inner_x, styles, own_set), (active,), (tangent_in,))[
            1
        ]

    tan_x = spread_one(push(seg_in, input_full, own_third[0], tangent))
    tan_one = push(seg_conv, gathered_x, own_third[1], tan_x)
    tan_g1 = spread_one(tan_one)
    tan_two = tan_one + collect_one(push(seg_self, gathered_one, own_third[2], tan_g1))
    tan_g2 = spread_one(tan_two)
    tan_three = tan_two + collect_one(push(seg_cross, gathered_two, own_third[3], tan_g2))
    tan_g3 = spread_one(tan_three)
    tan_four = tan_three + collect_one(push(seg_mlp, gathered_three, own_third[4], tan_g3))
    own_fourth = owned_sets()

    def pull_both(segment, active, tangent_in, own_set, cotan, cotan_tangent):

        def joint(inner_x, inner_tangent, styles_in, own_in):
            return jax.jvp(
                lambda value_x: segment(value_x, styles_in, own_in), (inner_x,), (inner_tangent,)
            )

        return jax.vjp(joint, active, tangent_in, styles, own_set)[1]((cotan, cotan_tangent))

    grad_act, grad_tan, style_acc, ignored = pull_both(
        seg_rgb,
        hidden_four,
        tan_four,
        own_fourth[5],
        cot_rgb.astype(jnp.float32),
        penalty_dir.astype(jnp.float32),
    )
    main_now = cot_feat.astype(jnp.float32) + grad_act
    side_now = grad_tan
    layer_grads = []
    for segment, active, tangent_in, own_set in (
        (seg_mlp, gathered_three, tan_g3, own_fourth[4]),
        (seg_cross, gathered_two, tan_g2, own_fourth[3]),
        (seg_self, gathered_one, tan_g1, own_fourth[2]),
    ):
        both_wide = spread(jnp.stack([main_now, side_now]).astype(jnp.bfloat16)).astype(jnp.float32)
        grad_act, grad_tan, grad_sty, grad_own = pull_both(
            segment, active, tangent_in, own_set, both_wide[0], both_wide[1]
        )
        style_acc = tree_add(style_acc, grad_sty)
        layer_grads.append(grad_own)
        both_sums = collect(jnp.stack([grad_act, grad_tan]))
        main_now = main_now + rounded(both_sums[0])
        side_now = side_now + rounded(both_sums[1])
    grad_act, grad_tan, grad_sty, grads_conv = pull_both(
        seg_conv, gathered_x, tan_x, own_fourth[1], main_now, side_now
    )
    style_acc = tree_add(style_acc, grad_sty)
    both_sums = collect(jnp.stack([grad_act, grad_tan]))
    grad_act, grad_tan, grad_sty, ignored = pull_both(
        seg_in, input_full, tangent, own_fourth[0], rounded(both_sums[0]), rounded(both_sums[1])
    )
    style_acc = tree_add(style_acc, grad_sty)
    proj_terms = layer_grads[2] + layer_grads[1] + layer_grads[0]
    big_terms = grads_conv + proj_terms
    big_sums = (
        lax.psum_scatter(
            big_terms[0].astype(jnp.bfloat16), "dp", scatter_dimension=2, tiled=True
        ).astype(jnp.float32),
        lax.psum_scatter(
            big_terms[1].astype(jnp.bfloat16), "dp", scatter_dimension=0, tiled=True
        ).astype(jnp.float32),
        lax.psum_scatter(
            big_terms[2].astype(jnp.bfloat16), "dp", scatter_dimension=0, tiled=True
        ).astype(jnp.float32),
        lax.psum_scatter(
            big_terms[3].astype(jnp.bfloat16), "dp", scatter_dimension=1, tiled=True
        ).astype(jnp.float32),
        lax.psum_scatter(
            big_terms[4].astype(jnp.bfloat16), "dp", scatter_dimension=0, tiled=True
        ).astype(jnp.float32),
        lax.psum_scatter(
            big_terms[5].astype(jnp.bfloat16), "dp", scatter_dimension=0, tiled=True
        ).astype(jnp.float32),
        lax.psum_scatter(
            big_terms[6].astype(jnp.bfloat16), "dp", scatter_dimension=0, tiled=True
        ).astype(jnp.float32),
        lax.psum_scatter(
            big_terms[7].astype(jnp.bfloat16), "dp", scatter_dimension=1, tiled=True
        ).astype(jnp.float32),
        lax.psum_scatter(
            big_terms[8].astype(jnp.bfloat16), "dp", scatter_dimension=0, tiled=True
        ).astype(jnp.float32),
        lax.psum_scatter(
            big_terms[9].astype(jnp.bfloat16), "dp", scatter_dimension=1, tiled=True
        ).astype(jnp.float32),
    )
    small_terms = style_pull(style_acc)[0]
    small_sums = lax.psum(
        (
            small_terms[0],
            small_terms[1],
            small_terms[2],
            small_terms[3],
            small_terms[4],
            small_terms[5],
            small_terms[6],
            small_terms[7],
        ),
        ("dp", "mp"),
    )
    return (hidden_four, picture, grad_act) + tuple(small_sums) + tuple(big_sums)


def solution(mesh):
    in_specs = (
        P("dp", None, "mp"),
        P("dp"),
        P("dp", None),
        P("dp"),
        P("dp"),
        P(),
        P(),
        P(),
        P(),
        P(),
        P(),
        P(),
        P(),
        P(None, None, "dp", "mp"),
        P("dp", "mp"),
        P("dp", "mp"),
        P("mp", "dp"),
        P("dp", "mp"),
        P("dp", "mp"),
        P("dp", "mp"),
        P("mp", "dp"),
        P("dp", "mp"),
        P("mp", "dp"),
        P("dp", None, "mp"),
        P("dp", None, None),
        P("dp", None, None),
    )
    out_specs = (
        P("dp", None, "mp"),
        P("dp", None, None),
        P("dp", None, "mp"),
        P(),
        P(),
        P(),
        P(),
        P(),
        P(),
        P(),
        P(),
        P(None, None, "dp", "mp"),
        P("dp", "mp"),
        P("dp", "mp"),
        P("mp", "dp"),
        P("dp", "mp"),
        P("dp", "mp"),
        P("dp", "mp"),
        P("mp", "dp"),
        P("dp", "mp"),
        P("mp", "dp"),
    )
    return jax.shard_map(
        per_device, mesh=mesh, in_specs=in_specs, out_specs=out_specs, check_vma=False
    )
```

profile of v0, /device:TPU:9, one launch (start us, length us, event | category | flops | bytes accessed | tf_op | source)
XLA Modules:
  0.0 3327.9 jit_solution(4373378103160404493)
XLA Ops:
  35.1 341.8 %all-gather.32.cloned.1.call-done = bf16[8,9,1024,512]{3,2,1,0:T(8,128)(2,1)} async-done(((bf16[8,9,64,512]{3,2,1,0:T(8,128)(2,1)}), bf16[8,9,1024,512]{3,2,1,0:T(8,128)(2,1)}) %all-gather.32.cloned.1.call-update) | async-done | bytes 75497488 | tf_op jit(solution)/shard_map/all_gather | solution.py:212
  376.9 66.6 %copy.408 = bf16[1,8,9216,512]{3,1,2,0:T(8,128)(2,1)} copy(bf16[1,8,9216,512]{3,2,1,0:T(8,128)(2,1)} %bitcast.198) | data formatting | bytes 150994944
  443.5 66.9 %convolution_convert_fusion.1 = bf16[2,4718592]{1,0:T(2,128)(2,1)} fusion(bf16[8,4718592]{1,0:T(8,128)(2,1)} %bitcast.199, f32[2,8]{1,0:T(2,128)S(1)} %get-tuple-element.132, f32[2]{0:T(128)S(1)} %get-tuple-element.131), kind=kOutput, calls=%fused_computation.3 | convolution fusion | flops 915406848 | bytes 94371912 | tf_op jit(solution)/shard_map/dot_general | solution.py:18
  510.3 30.4 convert_add_fusion
  540.8 32.9 reduce.4
  578.4 12.9 fusion.495
  593.3 19.1 all-gather.54.cloned.1.call-done
  615.4 36.6 %all-gather.34.cloned.1.call-done = bf16[1024,512]{1,0:T(8,128)(2,1)} async-done(((bf16[64,512]{1,0:T(8,128)(2,1)}), bf16[1024,512]{1,0:T(8,128)(2,1)}) %all-gather.34.cloned.1.call-update) | async-done | bytes 1048592 | tf_op jit(solution)/shard_map/all_gather | solution.py:174
  656.0 34.9 %all-gather.36.cloned.1.call-done = bf16[1024,512]{1,0:T(8,128)(2,1)} async-done(((bf16[64,512]{1,0:T(8,128)(2,1)}), bf16[1024,512]{1,0:T(8,128)(2,1)}) %all-gather.36.cloned.1.call-update) | async-done | bytes 1048592 | tf_op jit(solution)/shard_map/all_gather | solution.py:173
  703.3 26.5 all-gather.38.cloned.1.call-done
  732.8 19.9 reduce-scatter.25.cloned.1.call-done
  756.9 21.3 all_gather.111
  779.8 20.0 all_gather.108
  804.8 12.7 all-gather.40.cloned.1.call-done
  824.5 32.3 all-gather.42.cloned.1.call-done
  864.0 15.8 reduce-scatter.27.cloned.1.call-done
  883.1 20.1 all-gather.60.cloned.1.call-done
  903.3 53.0 %all-gather.46.cloned.1.call-done = bf16[2048,1024]{0,1:T(8,128)(2,1)} async-done(((bf16[2048,64]{0,1:T(8,128)(2,1)}), bf16[2048,1024]{0,1:T(8,128)(2,1)}) %all-gather.46.cloned.1.call-update) | async-done | bytes 4194320 | tf_op jit(solution)/shard_map/all_gather | solution.py:181
  962.5 15.3 all-gather.58.cloned.1.call-done
  980.8 50.2 %all-gather.44.cloned.1.call-done = bf16[1024,2048]{1,0:T(8,128)(2,1)} async-done(((bf16[64,2048]{1,0:T(8,128)(2,1)}), bf16[1024,2048]{1,0:T(8,128)(2,1)}) %all-gather.44.cloned.1.call-update) | async-done | bytes 4194320 | tf_op jit(solution)/shard_map/all_gather | solution.py:180
  1035.7 9.6 fusion.188
  1047.4 18.5 reduce-scatter.31.cloned.1.call-done
  1069.9 19.5 all-gather.62.cloned.1.call-done
  1096.6 20.4 reduce-scatter.33.cloned.1.call-done
  1119.3 21.4 all-gather.64.cloned.1.call-done
  1156.4 20.0 reduce-scatter.35.cloned.1.call-done
  1176.4 17.0 fusion.14
  1193.4 6.8 fusion.510
  1218.6 11.8 reduce-scatter.37.cloned.1.call-done
  1263.7 13.2 fusion.506
  1277.2 22.1 all-gather.66.cloned.1.call-done
  1328.2 20.4 reduce-scatter.39.cloned.1.call-done
  1356.0 16.5 all-gather.68.cloned.1.call-done
  1388.3 19.4 all-gather.48.cloned.1.call-done
  1417.6 12.7 reduce-scatter.41.cloned.1.call-done
  1432.9 13.7 fusion.182
  1446.6 7.7 all-gather.70.cloned.1.call-done
  1458.4 12.4 add_convert_fusion
  1470.9 6.7 fusion.185
  1482.1 31.9 reduce-scatter.43.cloned.1.call-done
  1519.6 32.8 all-gather.50.cloned.1.call-done
  1576.9 31.9 reduce-scatter.45.cloned.1.call-done
  1614.4 33.2 all-gather.52.cloned.1.call-done
  1696.2 6.7 fusion.203
  1703.3 18.5 reduce-scatter.47.cloned.1.call-done
  1724.1 20.5 reduce-scatter.29.cloned.1.call-done
  1750.1 16.4 fusion.20
  1766.5 15.7 fusion.17
  1818.9 12.7 fusion.496
  1831.6 8.5 fusion.29
  1882.9 11.5 fusion.372
  1903.3 43.3 %fusion.3 = bf16[2,9216,512]{2,1,0:T(8,128)(2,1)} fusion(f32[1,2,9216,512]{3,1,2,0:T(2,128)} %bitcast.661, bf16[2,9216,512]{2,1,0:T(8,128)(2,1)} %fusion.372, f32[2,1024,512]{2,1,0:T(8,128)} %broadcast_multiply_fusion, bf16[2,256,9216]{2,1,0:T(8,128)(2,1)} %constant_dynamic-update-slice_fusion, f32[2,256,512]{2,1,0:T(8,128)S(1)} %copy-done.84, ...), kind=kOutput, calls=%fused_computation.8 | convolution fusion | flops 4888723456 | bytes 90181632 | tf_op jit(solution)/shard_map/transpose(jvp(jvp(bpr,bro->bpo)))/dot_general | solution.py:26
  1946.6 34.6 %copy.412 = bf16[1,2,9216,512]{3,1,2,0:T(2,128)(2,1)} copy(bf16[1,2,9216,512]{3,2,1,0:T(8,128)(2,1)} %bitcast.670) | data formatting | bytes 37748736
  1981.3 81.2 %convolution_convert_fusion = bf16[8,4718592]{1,0:T(8,128)(2,1)} fusion(bf16[2,4718592]{1,0:T(2,128)(2,1)} %bitcast.668, f32[2,8]{1,0:T(2,128)S(1)} %copy-done.160, f32[2]{0:T(128)S(1)} %copy-done.164), kind=kOutput, calls=%fused_computation.2 | convolution fusion | flops 943718400 | bytes 94371912 | tf_op jit(solution)/shard_map/transpose(jvp(jvp()))/dot_general | solution.py:18
  2062.4 49.7 %copy.301 = bf16[8,9,1024,512]{3,2,1,0:T(8,128)(2,1)} copy(bf16[8,9,1024,512]{3,0,2,1:T(8,128)(2,1)} %bitcast.160) | data formatting | bytes 150994944 | tf_op jit(solution)/shard_map/convert_element_type | solution.py:340
  2119.4 49.1 %multiply_reduce_fusion.7 = (f32[2]{0:T(128)S(1)}, f32[2,8]{1,0:T(2,128)S(1)}) fusion(f32[2,8]{1,0:T(2,128)S(1)} %copy-done.160, f32[2]{0:T(128)S(1)} %multiply_divide_fusion.2, bf16[2,4718592]{1,0:T(2,128)(2,1)} %bitcast.669, bf16[8,4718592]{1,0:T(8,128)(2,1)} %bitcast.199), kind=kOutput, calls=%fused_computation.707 | convolution fusion | flops 150994992 | bytes 94371984 | tf_op jit(solution)/shard_map/transpose(jvp(jvp()))/dot_general | solution.py:18
  2189.8 35.7 %reduce-scatter.67.cloned.1.call-done = bf16[512,64]{0,1:T(8,128)(2,1)} async-done(((bf16[512,1024]{0,1:T(8,128)(2,1)}), bf16[512,64]{0,1:T(8,128)(2,1)}) %reduce-scatter.67.cloned.1.call-update) | async-done | bytes 65552 | tf_op jit(solution)/shard_map/reduce_scatter | solution.py:360
  2227.0 58.5 %reduce-scatter.55.cloned.1.call-done = bf16[64,512]{1,0:T(8,128)(2,1)} async-done(((bf16[1024,512]{1,0:T(8,128)(2,1)}), bf16[64,512]{1,0:T(8,128)(2,1)}) %reduce-scatter.55.cloned.1.call-update) | async-done | bytes 65552 | tf_op jit(solution)/shard_map/reduce_scatter | solution.py:342
  2287.1 59.1 %reduce-scatter.57.cloned.1.call-done = bf16[64,512]{1,0:T(8,128)(2,1)} async-done(((bf16[1024,512]{1,0:T(8,128)(2,1)}), bf16[64,512]{1,0:T(8,128)(2,1)}) %reduce-scatter.57.cloned.1.call-update) | async-done | bytes 65552 | tf_op jit(solution)/shard_map/reduce_scatter | solution.py:345
  2347.6 58.4 %reduce-scatter.59.cloned.1.call-done = bf16[512,64]{0,1:T(8,128)(2,1)} async-done(((bf16[512,1024]{0,1:T(8,128)(2,1)}), bf16[512,64]{0,1:T(8,128)(2,1)}) %reduce-scatter.59.cloned.1.call-update) | async-done | bytes 65552 | tf_op jit(solution)/shard_map/reduce_scatter | solution.py:348
  2413.7 42.4 %all-reduce.29 = (f32[512,8]{0,1:T(8,128)}, f32[3,1024]{1,0:T(4,128)}, f32[1024]{0:T(1024)}, f32[1024]{0:T(1024)}) all-reduce(f32[512,8]{0,1:T(8,128)S(1)} %fusion.494, f32[3,1024]{1,0:T(4,128)S(1)} %bitcast_dynamic-update-slice_fusion, f32[1024]{0:T(1024)S(1)} %dynamic_update_slice.18, ...), channel_id=1, replica_groups=mesh['dp'=16,'mp'=2] {'dp','mp'}, use_global_device_ids=true, to_apply=%region_70.71 | all-reduce | flops 9216 | bytes 73728 | tf_op jit(solution)/shard_map/psum | solution.py:371
  2456.1 658.7 %reduce-scatter.53.cloned.1.call-done = bf16[8,9,64,512]{3,2,1,0:T(8,128)(2,1)} async-done(((bf16[8,9,1024,512]{3,2,1,0:T(8,128)(2,1)}), bf16[8,9,64,512]{3,2,1,0:T(8,128)(2,1)}) %reduce-scatter.53.cloned.1.call-update) | async-done | bytes 4718608 | tf_op jit(solution)/shard_map/reduce_scatter | solution.py:339
  3114.8 7.5 convert_element_type.1260
  3122.2 191.1 %all-reduce.33.cloned.1.call-done = (f32[1000,512]{1,0:T(8,128)}, f32[1000,768]{1,0:T(8,128)}, f32[512,1024]{1,0:T(8,128)}, f32[512,1024]{1,0:T(8,128)}) async-done(((f32[1000,512]{1,0:T(8,128)}, f32[1000,768]{1,0:T(8,128)}, f32[512,1024]{1,0:T(8,128)}, f32[512,1024]{1,0:T(8,128)}), (f32[1000,512]{1,0:T(8,128)}, f32[1000,768]{1,0:T(8,128)}, f32[512,1024]{1,0:T(8,128)}, ...) | async-done | bytes 9314320 | tf_op jit(solution)/shard_map/psum | solution.py:371
  (782 shorter events, 481.5 us)
Async XLA Ops:
  7.2 771.0 %copy-start = (bf16[1000,768]{1,0:T(8,128)(2,1)S(1)}, bf16[1000,768]{1,0:T(8,128)(2,1)}, u32[]{:S(2)}) copy-start(bf16[1000,768]{1,0:T(8,128)(2,1)} %param.32) | copy-start | bytes 4608004
  7.3 369.6 %all-gather.32.cloned.1.call-start = ((), (), s32[]{:S(2)}) async-start(), calls=%async_computation.24 | async-start | bytes 80216064 | tf_op jit(solution)/shard_map/all_gather | solution.py:212
  8.0 604.4 %all-gather.54.cloned.1.call-start = ((), (), s32[]{:S(2)}) async-start(), calls=%async_computation.59 | async-start | bytes 1572864 | tf_op jit(solution)/shard_map/all_gather | solution.py:237
  9.7 850.8 %copy-start.132 = (f32[2,512]{1,0:T(2,128)}, f32[2,512]{1,0:T(2,128)S(1)}, u32[]{:S(2)}) copy-start(f32[2,512]{1,0:T(2,128)S(1)} %fusion.446) | copy-start | bytes 12292
  35.0 408.5 %copy-start.159 = (f32[2,8]{1,0:T(2,128)}, f32[2,8]{1,0:T(2,128)S(1)}, u32[]{:S(2)}) copy-start(f32[2,8]{1,0:T(2,128)S(1)} %get-tuple-element.132) | copy-start | bytes 196
  35.0 408.5 %copy-start.163 = (f32[2]{0:T(128)}, f32[2]{0:T(128)S(1)}, u32[]{:S(2)}) copy-start(f32[2]{0:T(128)S(1)} %get-tuple-element.131) | copy-start | bytes 28
  591.4 60.6 %all-gather.34.cloned.1.call-start = ((), (), s32[]{:S(2)}) async-start(), calls=%async_computation.25 | async-start | bytes 1114112 | tf_op jit(solution)/shard_map/all_gather | solution.py:174
  592.1 98.8 %all-gather.36.cloned.1.call-start = ((), (), s32[]{:S(2)}) async-start(), calls=%async_computation.26 | async-start | bytes 1114112 | tf_op jit(solution)/shard_map/all_gather | solution.py:173
  592.7 137.1 %all-gather.38.cloned.1.call-start = ((), (), s32[]{:S(2)}) async-start(), calls=%async_computation.27 | async-start | bytes 1114112 | tf_op jit(solution)/shard_map/all_gather | solution.py:175
  593.3 159.4 %reduce-scatter.25.cloned.1.call-start = ((), (), s32[]{:S(2)}) async-start(), calls=%async_computation.28 | async-start | bytes 1572864 | tf_op jit(solution)/shard_map/reduce_scatter | solution.py:240
  613.9 540.5 %copy-start.149 = (f32[2,256]{1,0:T(2,128)}, f32[2,256]{1,0:T(2,128)S(1)}, u32[]{:S(2)}) copy-start(f32[2,256]{1,0:T(2,128)S(1)} %fusion.140) | copy-start | bytes 6148
  615.4 75.5 %copy-start.47 = (bf16[2,256,1024]{2,1,0:T(8,128)(2,1)}, bf16[2,256,1024]{2,1,0:T(8,128)(2,1)S(1)}, u32[]{:S(2)}) copy-start(bf16[2,256,1024]{2,1,0:T(8,128)(2,1)S(1)} %fusion.141) | copy-start | bytes 3145732
  703.3 75.4 %copy-start.114 = (bf16[2,8,64,256]{3,2,1,0:T(8,128)(2,1)}, bf16[2,8,64,256]{3,2,1,0:T(8,128)(2,1)S(1)}, u32[]{:S(2)}) copy-start(bf16[2,8,64,256]{3,2,1,0:T(8,128)(2,1)S(1)} %convolution_convert_fusion.23) | copy-start | bytes 1572868
  703.3 75.0 %copy-start.165 = (s32[2,64]{1,0:T(2,128)S(1)}, s32[2,64]{1,0:T(2,128)}, u32[]{:S(2)}) copy-start(s32[2,64]{1,0:T(2,128)} %param.28) | copy-start | bytes 1540
  732.8 68.0 %all-gather.56.cloned.1.call-start = ((), (), s32[]{:S(2)}) async-start(), calls=%async_computation.60 | async-start | bytes 1572864 | tf_op jit(solution)/shard_map/all_gather | solution.py:237
  755.4 62.1 %all-gather.40.cloned.1.call-start = ((), (), s32[]{:S(2)}) async-start(), calls=%async_computation.29 | async-start | bytes 1114112 | tf_op jit(solution)/shard_map/all_gather | solution.py:176
  756.1 100.6 %all-gather.42.cloned.1.call-start = ((), (), s32[]{:S(2)}) async-start(), calls=%async_computation.30 | async-start | bytes 1114112 | tf_op jit(solution)/shard_map/all_gather | solution.py:179
  756.8 122.9 %reduce-scatter.27.cloned.1.call-start = ((), (), s32[]{:S(2)}) async-start(), calls=%async_computation.31 | async-start | bytes 1572864 | tf_op jit(solution)/shard_map/reduce_scatter | solution.py:240
  800.5 291.4 %copy-start.61 = (bf16[2,64,8,64]{3,2,1,0:T(8,128)(2,1)}, bf16[2,64,8,64]{3,2,1,0:T(8,128)(2,1)S(1)}, u32[]{:S(2)}) copy-start(bf16[2,64,8,64]{3,2,1,0:T(8,128)(2,1)S(1)} %convert_element_type.1070) | copy-start | bytes 393220
  802.3 292.8 %copy-start.151 = (f32[2,256]{1,0:T(2,128)}, f32[2,256]{1,0:T(2,128)S(1)}, u32[]{:S(2)}) copy-start(f32[2,256]{1,0:T(2,128)S(1)} %fusion.146) | copy-start | bytes 6148
  822.2 747.1 %copy-start.128 = (f32[2,8,256]{2,1,0:T(8,128)}, f32[2,8,256]{2,1,0:T(8,128)S(1)}, u32[]{:S(2)}) copy-start(f32[2,8,256]{2,1,0:T(8,128)S(1)} %get-tuple-element.219) | copy-start | bytes 49156
  859.9 43.4 %all-gather.60.cloned.1.call-start = ((), (), s32[]{:S(2)}) async-start(), calls=%async_computation.62 | async-start | bytes 1572864 | tf_op jit(solution)/shard_map/all_gather | solution.py:237
  860.5 490.5 %copy-start.130 = (f32[512,3]{0,1:T(4,128)}, f32[512,3]{0,1:T(4,128)S(1)}, u32[]{:S(2)}) copy-start(f32[512,3]{0,1:T(4,128)S(1)} %get-tuple-element.205) | copy-start | bytes 18436
  861.9 489.1 %copy-start.134 = (f32[512,2]{0,1:T(2,128)}, f32[512,2]{0,1:T(2,128)S(1)}, u32[]{:S(2)}) copy-start(f32[512,2]{0,1:T(2,128)S(1)} %fusion.303) | copy-start | bytes 12292
  863.3 202.5 %copy-start.13 = (f32[2,256,512]{2,1,0:T(8,128)}, f32[2,256,512]{2,1,0:T(8,128)S(1)}, u32[]{:S(2)}) copy-start(f32[2,256,512]{2,1,0:T(8,128)S(1)} %get-tuple-element.222) | copy-start | bytes 3145732
  863.4 92.9 %all-gather.46.cloned.1.call-start = ((), (), s32[]{:S(2)}) async-start(), calls=%async_computation.33 | async-start | bytes 4456448 | tf_op jit(solution)/shard_map/all_gather | solution.py:181
  864.0 113.9 %all-gather.58.cloned.1.call-start = ((), (), s32[]{:S(2)}) async-start(), calls=%async_computation.61 | async-start | bytes 1572864 | tf_op jit(solution)/shard_map/all_gather | solution.py:237
  882.3 148.7 %all-gather.44.cloned.1.call-start = ((), (), s32[]{:S(2)}) async-start(), calls=%async_computation.32 | async-start | bytes 4456448 | tf_op jit(solution)/shard_map/all_gather | solution.py:180
  882.9 182.9 %reduce-scatter.31.cloned.1.call-start = ((), (), s32[]{:S(2)}) async-start(), calls=%async_computation.36 | async-start | bytes 1572864 | tf_op jit(solution)/shard_map/reduce_scatter | solution.py:240
  979.3 66.5 %copy-start.153 = (f32[2,256]{1,0:T(2,128)}, f32[2,256]{1,0:T(2,128)S(1)}, u32[]{:S(2)}) copy-start(f32[2,256]{1,0:T(2,128)S(1)} %fusion.152) | copy-start | bytes 6148
  1047.3 42.1 %all-gather.62.cloned.1.call-start = ((), (), s32[]{:S(2)}) async-start(), calls=%async_computation.63 | async-start | bytes 1572864 | tf_op jit(solution)/shard_map/all_gather | solution.py:237
  1068.0 49.1 %reduce-scatter.33.cloned.1.call-start = ((), (), s32[]{:S(2)}) async-start(), calls=%async_computation.37 | async-start | bytes 1572864 | tf_op jit(solution)/shard_map/reduce_scatter | solution.py:240
  1096.6 44.1 %all-gather.64.cloned.1.call-start = ((), (), s32[]{:S(2)}) async-start(), calls=%async_computation.64 | async-start | bytes 1572864 | tf_op jit(solution)/shard_map/all_gather | solution.py:237
  1119.3 57.1 %reduce-scatter.35.cloned.1.call-start = ((), (), s32[]{:S(2)}) async-start(), calls=%async_computation.38 | async-start | bytes 1572864 | tf_op jit(solution)/shard_map/reduce_scatter | solution.py:240
  1155.9 74.5 %reduce-scatter.37.cloned.1.call-start = ((), (), s32[]{:S(2)}) async-start(), calls=%async_computation.39 | async-start | bytes 393216 | tf_op jit(solution)/shard_map/reduce_scatter | solution.py:240
  1218.6 80.7 %all-gather.66.cloned.1.call-start = ((), (), s32[]{:S(2)}) async-start(), calls=%async_computation.65 | async-start | bytes 1572864 | tf_op jit(solution)/shard_map/all_gather | solution.py:237
  1276.9 71.7 %reduce-scatter.39.cloned.1.call-start = ((), (), s32[]{:S(2)}) async-start(), calls=%async_computation.40 | async-start | bytes 1572864 | tf_op jit(solution)/shard_map/reduce_scatter | solution.py:240
  1328.2 44.3 %all-gather.68.cloned.1.call-start = ((), (), s32[]{:S(2)}) async-start(), calls=%async_computation.66 | async-start | bytes 1572864 | tf_op jit(solution)/shard_map/all_gather | solution.py:237
  1351.0 56.7 %all-gather.48.cloned.1.call-start = ((), (), s32[]{:S(2)}) async-start(), calls=%async_computation.35 | async-start | bytes 3145728 | tf_op jit(solution)/shard_map/all_gather | solution.py:237
  1355.9 74.4 %reduce-scatter.41.cloned.1.call-start = ((), (), s32[]{:S(2)}) async-start(), calls=%async_computation.41 | async-start | bytes 1572864 | tf_op jit(solution)/shard_map/reduce_scatter | solution.py:240
  1387.8 66.5 %all-gather.70.cloned.1.call-start = ((), (), s32[]{:S(2)}) async-start(), calls=%async_computation.67 | async-start | bytes 1572864 | tf_op jit(solution)/shard_map/all_gather | solution.py:237
  1432.9 81.2 %reduce-scatter.43.cloned.1.call-start = ((), (), s32[]{:S(2)}) async-start(), calls=%async_computation.42 | async-start | bytes 3145728 | tf_op jit(solution)/shard_map/reduce_scatter | solution.py:240
  1482.1 70.3 %all-gather.50.cloned.1.call-start = ((), (), s32[]{:S(2)}) async-start(), calls=%async_computation.43 | async-start | bytes 3145728 | tf_op jit(solution)/shard_map/all_gather | solution.py:237
  1519.1 89.8 %reduce-scatter.45.cloned.1.call-start = ((), (), s32[]{:S(2)}) async-start(), calls=%async_computation.44 | async-start | bytes 3145728 | tf_op jit(solution)/shard_map/reduce_scatter | solution.py:240
  1576.9 70.8 %all-gather.52.cloned.1.call-start = ((), (), s32[]{:S(2)}) async-start(), calls=%async_computation.45 | async-start | bytes 3145728 | tf_op jit(solution)/shard_map/all_gather | solution.py:237
  1614.4 107.4 %reduce-scatter.47.cloned.1.call-start = ((), (), s32[]{:S(2)}) async-start(), calls=%async_computation.46 | async-start | bytes 3145728 | tf_op jit(solution)/shard_map/reduce_scatter | solution.py:240
  1689.8 54.7 %reduce-scatter.29.cloned.1.call-start = ((), (), s32[]{:S(2)}) async-start(), calls=%async_computation.34 | async-start | bytes 1572864 | tf_op jit(solution)/shard_map/reduce_scatter | solution.py:240
  1696.1 416.2 %reduce-scatter.51.cloned.1.call-start = ((), (), s32[]{:S(2)}) async-start(), calls=%async_computation.48 | async-start | bytes 1572864 | tf_op jit(solution)/shard_map/reduce_scatter | solution.py:240
  1702.9 470.3 %reduce-scatter.49.cloned.1.call-start = ((), (), s32[]{:S(2)}) async-start(), calls=%async_computation.47 | async-start | bytes 786432 | tf_op jit(solution)/shard_map/reduce_scatter | solution.py:240
  1818.8 363.0 %reduce-scatter.69.cloned.1.call-start = ((), (), s32[]{:S(2)}) async-start(), calls=%async_computation.57 | async-start | bytes 4456448 | tf_op jit(solution)/shard_map/reduce_scatter | solution.py:363
  1840.1 343.5 %reduce-scatter.71.cloned.1.call-start = ((), (), s32[]{:S(2)}) async-start(), calls=%async_computation.58 | async-start | bytes 4456448 | tf_op jit(solution)/shard_map/reduce_scatter | solution.py:366
  1849.4 335.9 %reduce-scatter.63.cloned.1.call-start = ((), (), s32[]{:S(2)}) async-start(), calls=%async_computation.54 | async-start | bytes 835584 | tf_op jit(solution)/shard_map/reduce_scatter | solution.py:354
  1854.9 331.9 %reduce-scatter.65.cloned.1.call-start = ((), (), s32[]{:S(2)}) async-start(), calls=%async_computation.55 | async-start | bytes 835584 | tf_op jit(solution)/shard_map/reduce_scatter | solution.py:357
  1859.7 328.5 %reduce-scatter.61.cloned.1.call-start = ((), (), s32[]{:S(2)}) async-start(), calls=%async_computation.53 | async-start | bytes 1114112 | tf_op jit(solution)/shard_map/reduce_scatter | solution.py:351
  1864.5 361.0 %reduce-scatter.67.cloned.1.call-start = ((), (), s32[]{:S(2)}) async-start(), calls=%async_computation.56 | async-start | bytes 1114112 | tf_op jit(solution)/shard_map/reduce_scatter | solution.py:360
  1869.7 415.8 %reduce-scatter.55.cloned.1.call-start = ((), (), s32[]{:S(2)}) async-start(), calls=%async_computation.50 | async-start | bytes 1114112 | tf_op jit(solution)/shard_map/reduce_scatter | solution.py:342
  1873.7 472.4 %reduce-scatter.57.cloned.1.call-start = ((), (), s32[]{:S(2)}) async-start(), calls=%async_computation.51 | async-start | bytes 1114112 | tf_op jit(solution)/shard_map/reduce_scatter | solution.py:345
  1877.5 528.6 %reduce-scatter.59.cloned.1.call-start = ((), (), s32[]{:S(2)}) async-start(), calls=%async_computation.52 | async-start | bytes 1114112 | tf_op jit(solution)/shard_map/reduce_scatter | solution.py:348
  1882.8 1232.0 %reduce-scatter.53.cloned.1.call-start = ((), (), s32[]{:S(2)}) async-start(), calls=%async_computation.49 | async-start | bytes 80216064 | tf_op jit(solution)/shard_map/reduce_scatter | solution.py:339
  2112.2 1201.2 %all-reduce.33.cloned.1.call-start = ((), (), s32[]{:S(2)}) async-start(), calls=%async_computation.68 | async-start | bytes 18628608 | tf_op jit(solution)/shard_map/psum | solution.py:371
  2181.7 225.8 %copy-start.131 = (f32[512,3]{0,1:T(4,128)S(1)}, f32[512,3]{0,1:T(4,128)}, u32[]{:S(2)}) copy-start(f32[512,3]{0,1:T(4,128)} %copy-done.130) | copy-start | bytes 18436
  2181.7 225.8 %copy-start.135 = (f32[512,2]{0,1:T(2,128)S(1)}, f32[512,2]{0,1:T(2,128)}, u32[]{:S(2)}) copy-start(f32[512,2]{0,1:T(2,128)} %copy-done.134) | copy-start | bytes 12292
  2181.7 231.2 %copy-start.162 = (f32[512]{0:T(512)S(1)}, f32[512]{0:T(512)}, u32[]{:S(2)}) copy-start(f32[512]{0:T(512)} %get-tuple-element.92) | copy-start | bytes 6148
  2181.7 231.4 %copy-start.161 = (f32[512]{0:T(512)S(1)}, f32[512]{0:T(512)}, u32[]{:S(2)}) copy-start(f32[512]{0:T(512)} %get-tuple-element.91) | copy-start | bytes 6148
  (173 other events, 1734.3 us)
Sparse Core Ops, SparseCore 0:
  9.6 367.1 all-gather.31
  591.5 20.8 all-gather.53
  614.5 37.3 all-gather.33
  654.0 36.8 all-gather.35
  692.9 36.8 all-gather.37
  732.9 19.7 reduce-scatter.24
  755.5 21.2 all-gather.55
  779.2 38.1 all-gather.39
  819.8 36.8 all-gather.41
  860.0 19.7 reduce-scatter.26
  881.9 21.2 all-gather.59
  905.3 50.9 all-gather.45
  958.4 19.3 all-gather.57
  979.8 51.1 all-gather.43
  1047.4 18.3 reduce-scatter.30
  1068.1 21.2 all-gather.61
  1096.7 20.2 reduce-scatter.32
  1119.4 21.3 all-gather.63
  1156.1 20.2 reduce-scatter.34
  1218.7 11.6 reduce-scatter.36
  1277.0 22.1 all-gather.65
  1328.3 20.3 reduce-scatter.38
  1351.1 21.3 all-gather.67
  1374.5 33.1 all-gather.47
  1410.0 20.3 reduce-scatter.40
  1433.0 21.2 all-gather.69
  1482.2 31.8 reduce-scatter.42
  1519.3 33.1 all-gather.49
  1577.0 31.8 reduce-scatter.44
  1614.5 33.1 all-gather.51
  1690.0 31.8 reduce-scatter.46
  1724.2 20.3 reduce-scatter.28
  1746.6 20.3 reduce-scatter.50
  1818.9 14.5 reduce-scatter.48
  1840.2 70.3 reduce-scatter.68
  1914.8 71.4 reduce-scatter.70
  1989.8 55.6 reduce-scatter.62
  2049.4 55.5 reduce-scatter.64
  2108.5 56.4 reduce-scatter.60
  2169.0 56.4 reduce-scatter.66
  2229.1 56.3 reduce-scatter.54
  2289.6 56.4 reduce-scatter.56
  2349.6 56.4 reduce-scatter.58
  2410.8 703.9 reduce-scatter.52
  3121.5 191.8 all-reduce.32
where the time goes:
time: 3340 us; the launch traced here: 3330 us
  waiting for transfers between devices  2120 us (63%)
  matrix products  593 us (18%)
  local copies, waits for them, and re-layouts  280 us (8%)
  other arithmetic  211 us (6%)
  blocking collectives  97.9 us (3%)
    reduce_scatter x1, waiting for transfers between devices, per_device(): lax.psum_scatter(big_terms[0].astype(jnp.bfloat16), 'dp', scatter_dimensi...  659 us
    dot_general x71, matrix products, matmul_high(): return jnp.matmul(left, right, precision=lax.Precision.HIGHEST)  394 us
    all_gather x1, waiting for transfers between devices, owned_sets(): lax.all_gather(kernel_bank, 'dp', axis=2, tiled=True).astype(jnp.float32)  342 us
    reduce_scatter x14, waiting for transfers between devices, collect(): lax.psum_scatter(stacked.astype(jnp.bfloat16), 'mp', scatter_dimension=3,...  242 us
    all_gather x12, waiting for transfers between devices, spread(): return lax.all_gather(stacked, 'mp', axis=3, tiled=True)  227 us
    psum x1, waiting for transfers between devices, per_device(): lax.psum((small_terms[0], small_terms[1], small_terms[2], small_terms[3],...  191 us
    dot_general x41, matrix products, einsum_low(): jnp.einsum(form, left.astype(jnp.bfloat16), right.astype(jnp.bfloat16), p...  176 us
    unnamed x407, local copies, waits for them, and re-layouts  147 us
  transfers between devices with their start and end apart: 45, of which 37 were waited for; matrix products, arithmetic and copies ran while one was open for 17% of the time, Pallas kernels for 0%

commit v1 on v0

--- a/solution.py
+++ b/solution.py
@@ -122,7 +122,7 @@
     return jax.tree.map(jnp.add, first, second)
 
 
-def per_device(
+def tensor_parallel(
     layer_input,
     labels,
     text_ids,
@@ -384,6 +384,561 @@
     return (hidden_four, picture, grad_act) + tuple(small_sums) + tuple(big_sums)
 
 
+def fits_samples(mesh):
+    return mesh.shape["dp"] == 16 and mesh.shape["mp"] == 2
+
+
+def dot_wide(left, right, left_dim, right_dim):
+    return lax.dot_general(
+        left.astype(jnp.bfloat16),
+        right.astype(jnp.bfloat16),
+        (((left_dim,), (right_dim,)), ((), ())),
+        preferred_element_type=jnp.float32,
+    )
+
+
+def make_products(flip):
+    depth = 1 if flip else 0
+
+    def weight_grad(rows, cotan):
+        if flip:
+            return dot_wide(cotan, rows, 0, 0).astype(jnp.bfloat16)
+        return dot_wide(rows, cotan, 0, 0).astype(jnp.bfloat16)
+
+    @jax.custom_vjp
+    def single(rows, weight):
+        return dot_wide(rows, weight, 1, depth)
+
+    def single_fwd(rows, weight):
+        return single(rows, weight), (rows, weight)
+
+    def single_bwd(kept, cotan):
+        rows, weight = kept
+        return dot_wide(cotan, weight, 1, 1 - depth), weight_grad(rows, cotan)
+
+    single.defvjp(single_fwd, single_bwd)
+
+    @jax.custom_vjp
+    def pair(rows, tangents, weight):
+        return dot_wide(rows, weight, 1, depth), dot_wide(tangents, weight, 1, depth)
+
+    def pair_fwd(rows, tangents, weight):
+        return pair(rows, tangents, weight), (rows, tangents, weight)
+
+    def pair_bwd(kept, cotans):
+        rows, tangents, weight = kept
+        count = rows.shape[0]
+        both = jnp.concatenate([entry.astype(jnp.bfloat16) for entry in cotans], axis=0)
+        inputs = jnp.concatenate(
+            [rows.astype(jnp.bfloat16), tangents.astype(jnp.bfloat16)], axis=0
+        )
+        back = dot_wide(both, weight, 1, 1 - depth)
+        return back[:count], back[count:], weight_grad(inputs, both)
+
+    pair.defvjp(pair_fwd, pair_bwd)
+    return single, pair
+
+
+product, product_pair = make_products(False)
+product_flip, product_flip_pair = make_products(True)
+
+
+def make_bilinear(left_ids, right_ids, out_ids):
+    @jax.custom_vjp
+    def form(left, right):
+        return einsum_low(f"{left_ids},{right_ids}->{out_ids}", left, right)
+
+    def form_fwd(left, right):
+        return form(left, right), (left, right)
+
+    def form_bwd(kept, cotan):
+        left, right = kept
+        return (
+            einsum_low(f"{out_ids},{right_ids}->{left_ids}", cotan, right),
+            einsum_low(f"{left_ids},{out_ids}->{right_ids}", left, cotan),
+        )
+
+    form.defvjp(form_fwd, form_bwd)
+    return form
+
+
+head_scores = make_bilinear("phd", "qhd", "hpq")
+head_mix = make_bilinear("hpq", "qhd", "phd")
+
+
+def heads_of(rows):
+    return rows.reshape(rows.shape[0], -1, HEAD)
+
+
+def with_tangent(fun, value, tangent):
+    return jax.jvp(fun, (value,), (tangent,))
+
+
+def self_scores(q_heads):
+    short = q_heads.astype(jnp.bfloat16).astype(jnp.float32)
+    return jnp.transpose(jnp.sum(short * short, axis=-1))
+
+
+def last_softmax(scores):
+    return jax.nn.softmax(scores, axis=-1)
+
+
+def post_conv(conv_out, sums, bias, strength, noise):
+    demodulate = lax.rsqrt(sums + 1e-08)
+    return jax.nn.silu(conv_out * demodulate[None] + bias[None] + noise[:, None] * strength[None])
+
+
+def picture_of(hidden, rgb_scales, rgb_weight):
+    return einsum_high("pc,kc->kp", hidden, rgb_scales[None] * rgb_weight)
+
+
+def layer_forward(conv_out, sums, text_rows, small, weights, noise):
+    bias, strength, rgb_scales, rgb_weight = small
+    qk_w, value_w, attn_w, query_w, key_w, cval_w, cout_w, mlp_w, mout_w = weights
+    hidden_one = post_conv(conv_out, sums, bias, strength, noise)
+    normed = rms_norm(hidden_one)
+    queries = heads_of(product(normed, qk_w))
+    values = heads_of(product(normed, value_w))
+    scores = (2.0 * head_scores(queries, queries) - self_scores(queries)[:, None, :]) * HEAD ** (
+        -0.5
+    )
+    mixture = head_mix(last_softmax(scores), values).reshape(normed.shape)
+    hidden_two = hidden_one + product_flip(mixture, attn_w)
+    normed = rms_norm(hidden_two)
+    queries = heads_of(product(normed, query_w))
+    key_rows = heads_of(product(text_rows, key_w))
+    values = heads_of(product(text_rows, cval_w))
+    scores = head_scores(queries, key_rows) * HEAD ** (-0.5)
+    mixture = head_mix(last_softmax(scores), values).reshape(normed.shape)
+    hidden_three = hidden_two + product_flip(mixture, cout_w)
+    normed = rms_norm(hidden_three)
+    inner = jax.nn.gelu(product(normed, mlp_w))
+    hidden_four = hidden_three + product_flip(inner, mout_w)
+    return hidden_four, picture_of(hidden_four, rgb_scales, rgb_weight)
+
+
+def layer_joint(conv_out, conv_tan, sums, text_rows, small, weights, noise):
+    bias, strength, rgb_scales, rgb_weight = small
+    qk_w, value_w, attn_w, query_w, key_w, cval_w, cout_w, mlp_w, mout_w = weights
+    hidden_one, tan_one = with_tangent(
+        lambda value: post_conv(value, sums, bias, strength, noise), conv_out, conv_tan
+    )
+    normed, tan_normed = with_tangent(rms_norm, hidden_one, tan_one)
+    queries, tan_queries = product_pair(normed, tan_normed, qk_w)
+    queries, tan_queries = heads_of(queries), heads_of(tan_queries)
+    values, tan_values = product_pair(normed, tan_normed, value_w)
+    values, tan_values = heads_of(values), heads_of(tan_values)
+    lengths, tan_lengths = with_tangent(self_scores, queries, tan_queries)
+    scores = (2.0 * head_scores(queries, queries) - lengths[:, None, :]) * HEAD ** (-0.5)
+    half = head_scores(tan_queries, queries)
+    tan_scores = (2.0 * (half + jnp.swapaxes(half, 1, 2)) - tan_lengths[:, None, :]) * HEAD ** (
+        -0.5
+    )
+    soft, tan_soft = with_tangent(last_softmax, scores, tan_scores)
+    mixture = head_mix(soft, values).reshape(normed.shape)
+    tan_mixture = (head_mix(tan_soft, values) + head_mix(soft, tan_values)).reshape(normed.shape)
+    added, tan_added = product_flip_pair(mixture, tan_mixture, attn_w)
+    hidden_two, tan_two = hidden_one + added, tan_one + tan_added
+    normed, tan_normed = with_tangent(rms_norm, hidden_two, tan_two)
+    queries, tan_queries = product_pair(normed, tan_normed, query_w)
+    queries, tan_queries = heads_of(queries), heads_of(tan_queries)
+    key_rows = heads_of(product(text_rows, key_w))
+    values = heads_of(product(text_rows, cval_w))
+    scores = head_scores(queries, key_rows) * HEAD ** (-0.5)
+    tan_scores = head_scores(tan_queries, key_rows) * HEAD ** (-0.5)
+    soft, tan_soft = with_tangent(last_softmax, scores, tan_scores)
+    mixture = head_mix(soft, values).reshape(normed.shape)
+    tan_mixture = head_mix(tan_soft, values).reshape(normed.shape)
+    added, tan_added = product_flip_pair(mixture, tan_mixture, cout_w)
+    hidden_three, tan_three = hidden_two + added, tan_two + tan_added
+    normed, tan_normed = with_tangent(rms_norm, hidden_three, tan_three)
+    before, tan_before = product_pair(normed, tan_normed, mlp_w)
+    inner, tan_inner = with_tangent(jax.nn.gelu, before, tan_before)
+    added, tan_added = product_flip_pair(inner, tan_inner, mout_w)
+    hidden_four, tan_four = hidden_three + added, tan_three + tan_added
+    return (
+        hidden_four,
+        picture_of(hidden_four, rgb_scales, rgb_weight),
+        picture_of(tan_four, rgb_scales, rgb_weight),
+    )
+
+
+SWAP = ((0, 1), (1, 0))
+
+
+def swap_mp(values):
+    return lax.ppermute(values, "mp", SWAP)
+
+
+def pick(values, index):
+    return lax.dynamic_index_in_dim(values, index, 0, keepdims=False)
+
+
+def own_whole(values, mp):
+    mine, other = pick(values, mp), swap_mp(pick(values, 1 - mp))
+    first = jnp.where(mp == 0, mine, other)
+    second = jnp.where(mp == 0, other, mine)
+    return jnp.concatenate([first, second], axis=-1)
+
+
+def both_half(whole, mp):
+    half = whole.shape[-1] // 2
+    mine = lax.dynamic_slice_in_dim(whole, mp * half, half, whole.ndim - 1)
+    other = swap_mp(lax.dynamic_slice_in_dim(whole, (1 - mp) * half, half, whole.ndim - 1))
+    first = jnp.where(mp == 0, mine, other)
+    second = jnp.where(mp == 0, other, mine)
+    return jnp.stack([first, second])
+
+
+def to_slabs(both):
+    devices = lax.axis_size("dp")
+    parts = both.reshape(2, both.shape[1], devices, -1).transpose(2, 0, 1, 3)
+    parts = lax.all_to_all(parts, "dp", 0, 0, tiled=True)
+    return parts.reshape(2 * devices, both.shape[1], -1)
+
+
+def from_slabs(slabs, mp):
+    devices = lax.axis_size("dp")
+    rows = slabs.shape[1]
+    parts = slabs.astype(jnp.bfloat16).reshape((devices, 2) + slabs.shape[1:])
+    parts = lax.all_to_all(parts, "dp", 0, 0, tiled=True)
+    parts = parts.transpose(1, 2, 0, 3).reshape(2, rows, -1)
+    other = swap_mp(pick(parts, 1 - mp))
+    return pick(parts, mp).astype(jnp.float32) + other.astype(jnp.float32)
+
+
+def halve(values, axis_name, bit, dim):
+    size = lax.axis_size(axis_name)
+    side = (lax.axis_index(axis_name) // bit) % 2
+    pairs = [(index, index ^ bit) for index in range(size)]
+    sent = lax.dynamic_index_in_dim(values, 1 - side, dim, keepdims=False)
+    kept = lax.dynamic_index_in_dim(values, side, dim, keepdims=False)
+    return kept + lax.ppermute(sent, axis_name, pairs)
+
+
+def line_sum(values, dim):
+    place = lax.axis_index("dp") // 4
+    up = down = None
+    for step in range(1, 4):
+        send_up = lax.dynamic_index_in_dim(
+            values, jnp.clip(4 - step + place, 0, 3), dim, keepdims=False
+        )
+        send_down = lax.dynamic_index_in_dim(
+            values, jnp.clip(place - 4 + step, 0, 3), dim, keepdims=False
+        )
+        if up is not None:
+            send_up = send_up + up
+            send_down = send_down + down
+        up_pairs = [
+            (z * 4 + rest, z * 4 + 4 + rest) for z in range(3) if z < step for rest in range(4)
+        ]
+        down_pairs = [
+            (z * 4 + rest, z * 4 - 4 + rest) for z in range(1, 4) if 3 - z < step for rest in range(4)
+        ]
+        up = lax.ppermute(send_up, "dp", up_pairs)
+        down = lax.ppermute(send_down, "dp", down_pairs)
+    own = lax.dynamic_index_in_dim(values, place, dim, keepdims=False)
+    return own + up + down
+
+
+def sum_dp(partial):
+    parts = partial.reshape((4, 2, 2, 2) + partial.shape[1:])
+    parts = halve(parts, "dp", 1, 2)
+    parts = halve(parts, "dp", 2, 1)
+    return line_sum(parts, 0)
+
+
+def sum_all(partial):
+    parts = partial.reshape((4, 2, 2, 2) + partial.shape[2:])
+    parts = halve(parts, "dp", 1, 2)
+    rows = parts.shape[3]
+    first, second = parts[:, :, :, : rows // 2], parts[:, :, :, rows // 2 :]
+    first = halve(halve(first, "mp", 1, 2), "dp", 2, 1)
+    second = halve(halve(second, "dp", 2, 1), "mp", 1, 1)
+    return jnp.concatenate([line_sum(first, 0), line_sum(second, 0)], axis=0)
+
+
+def gather_dp(values):
+    return lax.all_gather(values, "dp", axis=0, tiled=True)
+
+
+def pack_rows(entry, flip):
+    if flip:
+        entry = entry.T
+    rows = entry.shape[0]
+    return entry.reshape(rows, -1, 512).transpose(1, 0, 2).reshape(-1, 512)
+
+
+def unpack_shard(entry, rows, flip):
+    entry = entry.reshape(-1, rows, 512).transpose(1, 0, 2).reshape(rows, -1)
+    return entry.T if flip else entry
+
+
+def whole_weight(gathered, start, rows, count):
+    piece = gathered[:, start : start + rows * count]
+    piece = piece.reshape(16, 2, count, rows, 512).transpose(0, 3, 1, 2, 4)
+    return piece.reshape(16 * rows, 2 * count * 512)
+
+
+def spread_weight(grad, rows, count):
+    piece = grad.reshape(16, rows, 2, count, 512).transpose(0, 2, 3, 1, 4)
+    return piece.reshape(16, 2, count * rows, 512)
+
+
+def sample_parallel(
+    layer_input,
+    labels,
+    text_ids,
+    noise_seeds,
+    penalty_mask,
+    class_table,
+    token_table,
+    sel_weight,
+    mod_weight,
+    rgb_mod,
+    rgb_weight,
+    conv_bias,
+    noise_strength,
+    kernel_bank,
+    qk_weight,
+    value_weight,
+    attn_out,
+    cross_query,
+    cross_key,
+    cross_value,
+    cross_out,
+    mlp_in,
+    mlp_out,
+    cot_feat,
+    cot_rgb,
+    penalty_dir,
+):
+    mp = lax.axis_index("mp")
+    dp = lax.axis_index("dp")
+    half_px = layer_input.shape[1]
+    slab = kernel_bank.shape[2]
+    width_out = kernel_bank.shape[3]
+    float32, bfloat16 = jnp.float32, jnp.bfloat16
+
+    flips = (False, False, True, False, False, False, True, False, True)
+    shards = (
+        qk_weight,
+        value_weight,
+        attn_out,
+        cross_query,
+        cross_key,
+        cross_value,
+        cross_out,
+        mlp_in,
+        mlp_out,
+    )
+    rows_of = [entry.shape[1] if flip else entry.shape[0] for entry, flip in zip(shards, flips)]
+    packed = [pack_rows(entry, flip) for entry, flip in zip(shards, flips)]
+    counts = [entry.shape[0] // rows for entry, rows in zip(packed, rows_of)]
+    stacked = jnp.concatenate(packed, axis=0)
+    gathered = lax.all_gather(stacked, ("dp", "mp"), axis=0, tiled=False)
+    weights = []
+    start = 0
+    for rows, count in zip(rows_of, counts):
+        weights.append(whole_weight(gathered, start, rows, count))
+        start += rows * count
+    weights = tuple(weights)
+
+    labels_all = lax.all_gather(labels, "dp", axis=0, tiled=True)
+    sample_count = labels_all.shape[0]
+    classes = jnp.arange(class_table.shape[0], dtype=jnp.int32)
+    onehot_class = (labels_all[:, None] == classes[None, :]).astype(bfloat16)
+    latent = dot_wide(onehot_class, class_table, 1, 0)
+    select_all, select_pull = jax.vjp(last_softmax, dot_wide(latent, sel_weight, 1, 0))
+    scales_all = 1.0 + dot_wide(latent, mod_weight, 1, 0)
+    rgb_scales_all = 1.0 + dot_wide(latent, rgb_mod, 1, 0)
+    me = 2 * dp + mp
+    scales = pick(scales_all, me)
+    rgb_scales = pick(rgb_scales_all, me)
+    scales_slab = lax.dynamic_slice_in_dim(scales_all, dp * slab, slab, 1)
+    words = jnp.arange(token_table.shape[0], dtype=jnp.int32)
+    text_own = pick(text_ids, mp)
+    text_rows = dot_wide((text_own[:, None] == words[None, :]).astype(bfloat16), token_table, 1, 0)
+    noise = noise_field(pick(noise_seeds, mp)[None], SIDE * SIDE)[0]
+    small = (
+        conv_bias.astype(float32),
+        noise_strength.astype(float32),
+        rgb_scales,
+        rgb_weight.astype(float32),
+    )
+
+    bank_rows = kernel_bank.reshape(kernel_bank.shape[0], 9 * slab, width_out)
+    kernel = jnp.einsum(
+        "bk,kro->bro",
+        select_all,
+        bank_rows.astype(float32),
+        precision=lax.Precision.HIGHEST,
+    ).astype(bfloat16)
+    kernel_wide = kernel.astype(float32)
+    squares = jnp.sum(
+        (kernel_wide * kernel_wide).reshape(sample_count, 9, slab, width_out), axis=1
+    )
+    scales_two = scales_slab * scales_slab
+    sums_part = jnp.sum(scales_two[:, :, None] * squares, axis=1)
+
+    def convolve(slabs):
+        columns = patches_of(slabs, SIDE)
+        return columns, einsum_low("bpr,bro->bpo", columns, kernel)
+
+    input_own = own_whole(layer_input, mp).astype(float32)
+    scales_pair = lax.dynamic_slice_in_dim(scales_all, 2 * dp, 2, 0)
+    input_pair = lax.all_gather(layer_input, "mp", axis=2, tiled=True).astype(float32)
+    slabs_x = to_slabs((input_pair * scales_pair[:, None, :]).astype(bfloat16))
+    columns_x, conv_part_x = convolve(slabs_x)
+    partial = jnp.concatenate([conv_part_x, sums_part[:, None, :]], axis=1).astype(bfloat16)
+    summed = own_whole(sum_dp(partial), mp).astype(float32)
+    conv_out, sums = summed[:-1], summed[-1]
+
+    (hidden_four, picture), pull = jax.vjp(
+        lambda value: layer_forward(value, sums, text_rows, small, weights, noise), conv_out
+    )
+
+    dir_own = pick(penalty_dir, mp).astype(float32)
+    grad_conv = pull((jnp.zeros_like(hidden_four), dir_own))[0]
+    grads_all = gather_dp(both_half(grad_conv.astype(bfloat16), mp))
+
+    def pull_columns(cotans):
+        return einsum_low("bpo,bro->bpr", cotans, kernel)
+
+    fold = jax.linear_transpose(
+        lambda slabs: patches_of(slabs, SIDE),
+        jax.ShapeDtypeStruct((sample_count, half_px, slab), float32),
+    )
+    grad_moduled = from_slabs(fold(pull_columns(grads_all))[0], mp)
+    mask_own = pick(penalty_mask, mp).astype(float32)
+    tangent = penalty_weight * mask_own * grad_moduled.astype(bfloat16).astype(float32) * scales
+
+    tan_moduled = (tangent * scales).astype(bfloat16)
+    tan_other = swap_mp(tan_moduled)
+    tan_pair = jnp.stack(
+        [jnp.where(mp == 0, tan_moduled, tan_other), jnp.where(mp == 0, tan_other, tan_moduled)]
+    )
+    slabs_t = to_slabs(tan_pair)
+    columns_t, conv_part_t = convolve(slabs_t)
+    conv_tan = own_whole(sum_dp(conv_part_t.astype(bfloat16)), mp).astype(float32)
+
+    (ignored_out, ignored_pic, ignored_tan), pull_joint = jax.vjp(
+        lambda *given: layer_joint(*given, noise),
+        conv_out,
+        conv_tan,
+        sums,
+        text_rows,
+        small,
+        weights,
+    )
+    cot_own = own_whole(cot_feat, mp).astype(float32)
+    grad_main, grad_side, grad_sums, grad_text, grad_small, grad_weights = pull_joint(
+        (cot_own, pick(cot_rgb, mp).astype(float32), dir_own)
+    )
+
+    spreads = [
+        spread_weight(grad, rows, count)
+        for grad, rows, count in zip(grad_weights, rows_of, counts)
+    ]
+    mlp_sum = sum_all(jnp.concatenate(spreads[7:], axis=2))
+    rest_sum = sum_all(jnp.concatenate(spreads[:7], axis=2))
+    weight_sums = jnp.concatenate([rest_sum, mlp_sum], axis=0).astype(float32)
+    big_sums = []
+    start = 0
+    for rows, count, flip in zip(rows_of, counts, flips):
+        big_sums.append(unpack_shard(weight_sums[start : start + rows * count], rows, flip))
+        start += rows * count
+
+    wide = jnp.concatenate([grad_main, grad_side, grad_sums[None]], axis=0).astype(bfloat16)
+    wide_all = gather_dp(both_half(wide, mp))
+    pixels = SIDE * SIDE
+    both_cot = wide_all[:, : 2 * pixels]
+    sums_cot = wide_all[:, 2 * pixels].astype(float32)
+    both_columns = jnp.concatenate([columns_x, columns_t], axis=1)
+    grad_kernel = einsum_low("bpr,bpo->bro", both_columns, both_cot)
+    scales_rows = jnp.tile(scales_two, (1, 9))
+    grad_kernel = grad_kernel + 2.0 * kernel_wide * scales_rows[:, :, None] * sums_cot[:, None, :]
+    grad_kernel = grad_kernel.astype(bfloat16)
+    grad_scales_slab = (
+        2.0 * scales_slab * jnp.sum(squares * sums_cot[:, None, :], axis=2)
+    )
+    bank_grad = jnp.einsum(
+        "bk,bro->kro",
+        select_all,
+        grad_kernel.astype(float32),
+        precision=lax.Precision.HIGHEST,
+    ).reshape(kernel_bank.shape)
+    grad_select = jnp.einsum(
+        "bro,kro->bk", grad_kernel, bank_rows, preferred_element_type=float32
+    )
+    back_columns = pull_columns(both_cot)
+    both_back = jnp.concatenate(
+        [
+            fold(back_columns[:, :pixels])[0],
+            fold(back_columns[:, pixels:])[0],
+        ],
+        axis=1,
+    )
+    both_back = from_slabs(both_back, mp).astype(bfloat16).astype(float32)
+    back_main, back_side = both_back[:half_px], both_back[half_px:]
+    input_grad = back_main * scales
+    grad_scales = jnp.sum(back_main * input_own + back_side * tangent, axis=0)
+
+    grad_bias, grad_strength, grad_rgb_scales, grad_rgb_weight = grad_small
+    row = jnp.concatenate(
+        [
+            grad_scales,
+            grad_rgb_scales,
+            grad_rgb_weight.reshape(-1),
+            grad_bias,
+            grad_strength,
+            grad_scales_slab.reshape(-1),
+            grad_select.reshape(-1),
+        ]
+    ).reshape(-1, 128)
+    rows_all = lax.all_gather(row, ("dp", "mp"), axis=0, tiled=False).reshape(sample_count, -1)
+    channels = scales.shape[0]
+    scale_terms = rows_all[:, :channels]
+    rgb_terms = rows_all[:, channels : 2 * channels]
+    sums_all = jnp.sum(rows_all[:, 2 * channels : 7 * channels], axis=0)
+    slab_terms = rows_all[:, 7 * channels : 7 * channels + sample_count * slab]
+    slab_terms = slab_terms.reshape(-1, 2, sample_count, slab).sum(axis=1)
+    scale_terms = scale_terms + slab_terms.transpose(1, 0, 2).reshape(sample_count, channels)
+    select_terms = jnp.sum(rows_all[:, 7 * channels + sample_count * slab :], axis=0)
+    logit_terms = select_pull(select_terms.reshape(sample_count, -1))[0]
+    latent_terms = (
+        matmul_high(scale_terms, mod_weight.astype(float32).T)
+        + matmul_high(rgb_terms, rgb_mod.astype(float32).T)
+        + matmul_high(logit_terms, sel_weight.astype(float32).T)
+    )
+    class_grad = matmul_high(onehot_class.astype(float32).T, latent_terms)
+    sel_grad = matmul_high(latent.T, logit_terms)
+    mod_grad = matmul_high(latent.T, scale_terms)
+    rgb_mod_grad = matmul_high(latent.T, rgb_terms)
+    text_all = lax.all_gather(grad_text.astype(bfloat16), ("dp", "mp"), axis=0, tiled=True)
+    ids_all = lax.all_gather(text_ids, "dp", axis=0, tiled=True).reshape(-1)
+    token_grad = dot_wide((ids_all[:, None] == words[None, :]).astype(bfloat16), text_all, 0, 0)
+
+    picture_other = swap_mp(picture)
+    pictures = jnp.stack(
+        [jnp.where(mp == 0, picture, picture_other), jnp.where(mp == 0, picture_other, picture)]
+    )
+    return (
+        both_half(hidden_four, mp),
+        pictures,
+        both_half(input_grad, mp),
+        class_grad,
+        token_grad,
+        sel_grad,
+        mod_grad,
+        rgb_mod_grad,
+        sums_all[: 3 * channels].reshape(3, channels),
+        sums_all[3 * channels : 4 * channels],
+        sums_all[4 * channels :],
+        bank_grad,
+    ) + tuple(big_sums)
+
+
 def solution(mesh):
     in_specs = (
         P("dp", None, "mp"),
@@ -437,5 +992,6 @@
         P("mp", "dp"),
     )
     return jax.shard_map(
-        per_device, mesh=mesh, in_specs=in_specs, out_specs=out_specs, check_vma=False
-    )
+        sample_parallel if fits_samples(mesh) else tensor_parallel,
+        mesh=mesh, in_specs=in_specs, out_specs=out_specs, check_vma=False
+    )

time: 3340 us -> 2050 us (0.61)
  waiting for transfers between devices: 2120 us -> 401 us
  local copies, waits for them, and re-layouts: 280 us -> 717 us
  matrix products: 593 us -> 446 us
  starting transfers between devices: 4.43 us -> 122 us
  other arithmetic: 211 us -> 265 us
  blocking collectives: 97.9 us -> 62.1 us
    reduce_scatter x24 -> x0, waiting for transfers between devices: 1110 us -> none  [the longest x1 659 us: per_device(): lax.psum_scatter(big_terms[0].astype(jnp.bfloat16), 'dp', scatter_dimensi...]
    all_gather x20 -> x5, waiting for transfers between devices: 815 us -> 105 us  [the longest x2 79.6 us: gather_dp(): return lax.all_gather(values, 'dp', axis=0, tiled=True)]
    dot_general x71 -> x7, matrix products: 394 us -> 14.2 us  [matmul_high(): return jnp.matmul(left, right, precision=lax.Precision.HIGHEST)]
    ppermute x0 -> x62, waiting for transfers between devices: none -> 296 us  [the longest x14 190 us: halve(): return kept + lax.ppermute(sent, axis_name, pairs)]
    dot_general x0 -> x72, matrix products: none -> 237 us  [the longest x22 62.4 us: dot_wide(): lax.dot_general(left.astype(jnp.bfloat16), right.astype(jnp.bfloat16), ((...]
    psum x1 -> x0, waiting for transfers between devices: 191 us -> none  [per_device(): lax.psum((small_terms[0], small_terms[1], small_terms[2], small_terms[3],...]
    reshape x5 -> x29, local copies, waits for them, and re-layouts: 13.8 us -> 142 us  [the longest x11 80 us: spread_weight(): piece = grad.reshape(16, rows, 2, count, 512).transpose(0, 2, 3, 1, 4)]
    slice x0 -> x18, local copies, waits for them, and re-layouts: none -> 108 us  [the longest x2 47.2 us: sample_parallel(): back_columns[:, :pixels]]
  transfers between devices with their start and end apart: 45 -> 69, of which waited for: 37 -> 32; matrix products, arithmetic and copies ran while one was open for 17% -> 38% of each run, Pallas kernels for 0% -> 0%
where the time goes in v1:
time: 2050 us; the launch traced here: 2030 us
  local copies, waits for them, and re-layouts  717 us (35%)
  matrix products  446 us (22%)
  waiting for transfers between devices  401 us (20%)
  other arithmetic  265 us (13%)
  starting transfers between devices  122 us (6%)
  blocking collectives  62.1 us (3%)
  between operations  20.6 us (1%)
    ppermute x14, waiting for transfers between devices, halve(): return kept + lax.ppermute(sent, axis_name, pairs)  190 us
    dot_general x14, matrix products, einsum_low(): jnp.einsum(form, left.astype(jnp.bfloat16), right.astype(jnp.bfloat16), p...  186 us
    unnamed x576, local copies, waits for them, and re-layouts  103 us
    split x3, local copies, waits for them, and re-layouts, patches_of(): jnp.concatenate(pieces, axis=-1)  83.7 us
    reshape x11, local copies, waits for them, and re-layouts, spread_weight(): piece = grad.reshape(16, rows, 2, count, 512).transpose(0, 2, 3, 1, 4)  80 us
    all_gather x2, waiting for transfers between devices, gather_dp(): return lax.all_gather(values, 'dp', axis=0, tiled=True)  79.6 us
    slice x18, local copies, waits for them, and re-layouts, patches_of(): padded[:, shift_row:shift_row + side_len, shift_col:shift_col + side_len, :]  68 us
    dot_general x22, matrix products, dot_wide(): lax.dot_general(left.astype(jnp.bfloat16), right.astype(jnp.bfloat16), ((...  62.4 us
  transfers between devices with their start and end apart: 69, of which 32 were waited for; matrix products, arithmetic and copies ran while one was open for 38% of the time, Pallas kernels for 0%

profile of v1, /device:TPU:9, one launch (start us, length us, event | category | flops | bytes accessed | tf_op | source)
XLA Modules:
  0.0 2034.5 jit_solution(15690644359352876678)
XLA Ops:
  23.1 8.7 all-reduce.29
  31.9 7.6 all_gather.27
  43.0 8.7 all-to-all-start
  52.1 26.9 %convert_multiply_fusion.1 = (f32[32,576,512]{2,0,1:T(8,128)}, bf16[32,576,512]{2,0,1:T(8,128)(2,1)}) fusion(bf16[8,576,512]{2,1,0:T(8,128)(2,1)} %bitcast.801, f32[32]{0:T(128)S(1)} %fusion.171, f32[32,8]{0,1:T(8,128)S(1)} %get-tuple-element.404, f32[32]{0:T(128)S(1)} %get-tuple-element.403), kind=kOutput, calls=%fused_computation.2 | convolution fusion | flops 934281728 | bytes 61342976 | tf_op jit(solution)/shard_map/bk,kro->bro/dot_general | solution.py:771
  79.8 16.2 reduce_sum.510
  102.1 7.5 pad_slice_fusion.8
  171.8 24.5 %fusion.24 = bf16[32,256,512]{2,1,0:T(8,128)(2,1)S(1)} fusion(bf16[32,256,576]{1,2,0:T(8,128)(2,1)} %copy-done.196, bf16[32,576,512]{2,0,1:T(8,128)(2,1)} %get-tuple-element.406), kind=kOutput, calls=%fused_computation.43 | convolution fusion | flops 4836032512 | bytes 36700160 | tf_op jit(solution)/shard_map/bpr,bro->bpo/dot_general | solution.py:26
  212.2 7.4 bitcast_add_fusion.1
  224.2 46.2 %collective-permute-done.1 = bf16[4,2,257,512]{3,0,2,1:T(4,128)(2,1)} collective-permute-done((bf16[4,2,257,512]{3,0,2,1:T(4,128)(2,1)}, bf16[4,2,257,512]{3,0,2,1:T(4,128)(2,1)}, u32[]{:S(2)}, u32[]{:S(2)}) %collective-permute-start.1) | collective-permute-done | bytes 2105376 | tf_op jit(solution)/shard_map/ppermute | solution.py:616
  281.9 9.0 collective-permute-done.2
  298.2 7.8 collective-permute-done.3
  332.6 7.5 fusion.248
  343.9 11.5 fusion.247
  436.8 11.0 copy.1072
  447.8 14.4 reshape.744
  462.2 11.0 copy.1071
  473.2 14.8 reshape.746
  489.4 7.9 fusion.265
  497.3 12.5 multiply_reduce_fusion.31
  553.5 79.6 %all-gather.8.cloned.1.call-done = bf16[32,256,512]{2,1,0:T(8,128)(2,1)} async-done(((bf16[2,256,512]{2,1,0:T(8,128)(2,1)}), bf16[32,256,512]{2,1,0:T(8,128)(2,1)}) %all-gather.8.cloned.1.call-update) | async-done | bytes 8388624 | tf_op jit(solution)/shard_map/all_gather | solution.py:662
  633.2 64.9 %fusion.14 = f32[32,256,576]{2,1,0:T(8,128)} fusion(bf16[32,256,512]{2,1,0:T(8,128)(2,1)} %all-gather.8.cloned.1.call-done, bf16[32,576,512]{2,0,1:T(8,128)(2,1)} %get-tuple-element.406), kind=kOutput, calls=%fused_computation.20 | convolution fusion | flops 4831838208 | bytes 46137344 | tf_op jit(solution)/shard_map/bpo,bro->bpr/dot_general | solution.py:26
  698.1 27.9 %fusion.252 = (f32[32,16,16,64]{3,2,1,0:T(8,128)}, f32[32,16,16,64]{3,2,1,0:T(8,128)}, f32[32,16,16,64]{3,2,1,0:T(8,128)}, f32[32,16,16,64]{3,2,1,0:T(8,128)}, f...) fusion(f32[32,16,16,576]{3,2,1,0:T(8,128)} %bitcast.705), kind=kLoop, calls=%fused_computation.687 | loop fusion | bytes 37748736 | tf_op jit(solution)/shard_map/transpose()/split | solution.py:53
  731.8 10.4 pad_add_fusion.15
  761.0 12.4 all_to_all.20
  794.2 14.1 all_to_all.21
  814.5 7.6 pad_slice_fusion
  890.6 23.7 %fusion.27 = bf16[32,256,512]{2,1,0:T(8,128)(2,1)S(1)} fusion(bf16[32,256,576]{1,2,0:T(8,128)(2,1)} %constant_dynamic-update-slice_fusion.18, bf16[32,576,512]{2,0,1:T(8,128)(2,1)} %get-tuple-element.406), kind=kOutput, calls=%fused_computation.44 | convolution fusion | flops 4836032512 | bytes 36700160 | tf_op jit(solution)/shard_map/bpr,bro->bpo/dot_general | solution.py:26
  914.8 7.3 collective-permute-done.15
  925.7 46.6 %collective-permute-done.16 = bf16[4,2,256,512]{3,2,1,0:T(8,128)(2,1)S(1)} collective-permute-done((bf16[4,2,256,512]{3,2,1,0:T(8,128)(2,1)S(1)}, bf16[4,2,256,512]{3,2,1,0:T(8,128)(2,1)S(1)}, u32[]{:S(2)}, u32[]{:S(2)}) %collective-permute-start.16) | collective-permute-done | bytes 2097184 | tf_op jit(solution)/shard_map/ppermute | solution.py:616
  974.9 12.4 collective-permute-done.17
  989.6 11.5 collective-permute-done.18
  1017.6 7.9 collective-permute-done.22
  1067.1 13.1 add_convert_fusion.2
  1080.3 8.2 fusion.50
  1152.1 8.4 multiply_reduce_fusion.1
  1203.2 8.3 collective-permute-done.24
  1285.5 8.7 collective-permute-start.28
  1301.5 14.7 reshape.777
  1316.2 10.5 copy.980
  1333.6 14.7 reshape.776
  1348.3 10.1 copy.979
  1358.4 7.5 fusion.19
  1367.6 19.3 all-gather.1
  1411.2 8.8 bitcast_add_fusion
  1426.1 13.8 constant_dynamic-slice_fusion.3
  1460.9 19.1 collective-permute-done.29
  1485.2 7.6 fusion.23
  1492.8 54.8 %collective-permute-done.30 = bf16[4,208,512]{2,1,0:T(8,128)(2,1)} collective-permute-done((bf16[4,208,512]{2,1,0:T(8,128)(2,1)}, bf16[4,208,512]{2,1,0:T(8,128)(2,1)}, u32[]{:S(2)}, u32[]{:S(2)}) %collective-permute-start.30) | collective-permute-done | bytes 852000 | tf_op jit(solution)/shard_map/ppermute | solution.py:616
  1582.2 8.1 collective-permute-done.47
  1634.7 31.5 %fusion.9 = f32[32,512,576]{1,2,0:T(8,128)} fusion(bf16[32,513,512]{2,1,0:T(8,128)(2,1)} %all-gather.10.cloned.1.call-done, bf16[32,576,512]{2,0,1:T(8,128)(2,1)} %get-tuple-element.406), kind=kOutput, calls=%fused_computation.15 | convolution fusion | flops 9663676416 | bytes 73400320 | tf_op jit(solution)/shard_map/bpo,bro->bpr/dot_general | solution.py:26
  1666.2 26.7 %fusion.246 = (f32[32,256,576]{1,2,0:T(8,128)}, f32[32,256,576]{1,2,0:T(8,128)}) fusion(f32[32,512,576]{1,2,0:T(8,128)} %fusion.9), kind=kLoop, calls=%fused_computation.681 | loop fusion | bytes 75497472 | tf_op jit(solution)/shard_map/slice | solution.py:877
  1692.9 20.6 %copy.956 = f32[32,256,576]{2,1,0:T(8,128)} copy(f32[32,256,576]{1,2,0:T(8,128)} %get-tuple-element.250) | data formatting | bytes 37748736 | tf_op jit(solution)/shard_map/slice | solution.py:877
  1713.4 27.9 %fusion.250 = (f32[32,16,16,64]{3,2,1,0:T(8,128)}, f32[32,16,16,64]{3,2,1,0:T(8,128)}, f32[32,16,16,64]{3,2,1,0:T(8,128)}, f32[32,16,16,64]{3,2,1,0:T(8,128)}, f...) fusion(f32[32,16,16,576]{3,2,1,0:T(8,128)} %bitcast.706), kind=kLoop, calls=%fused_computation.685 | loop fusion | bytes 37748736 | tf_op jit(solution)/shard_map/transpose()/split | solution.py:53
  1748.5 9.0 pad_add_fusion.9
  1772.2 20.6 %copy.959 = f32[32,256,576]{2,1,0:T(8,128)} copy(f32[32,256,576]{1,2,0:T(8,128)} %get-tuple-element.251) | data formatting | bytes 37748736 | tf_op jit(solution)/shard_map/slice | solution.py:878
  1792.8 27.9 %fusion.251 = (f32[32,16,16,64]{3,2,1,0:T(8,128)}, f32[32,16,16,64]{3,2,1,0:T(8,128)}, f32[32,16,16,64]{3,2,1,0:T(8,128)}, f32[32,16,16,64]{3,2,1,0:T(8,128)}, f...) fusion(f32[32,16,16,576]{3,2,1,0:T(8,128)} %bitcast.707), kind=kLoop, calls=%fused_computation.686 | loop fusion | bytes 37748736 | tf_op jit(solution)/shard_map/transpose()/split | solution.py:53
  1827.8 9.3 pad_add_fusion.3
  1853.2 12.5 all-to-all-start.3
  1865.8 28.1 %fusion.4 = f32[32,576,512]{2,1,0:T(8,128)} fusion(bf16[32,256,576]{1,2,0:T(8,128)(2,1)} %constant_dynamic-update-slice_fusion.18, bf16[32,256,576]{1,2,0:T(8,128)(2,1)} %copy-done.196, bf16[32,513,512]{2,1,0:T(8,128)(2,1)} %all-gather.10.cloned.1.call-done), kind=kOutput, calls=%fused_computation.10 | convolution fusion | flops 9701425152 | bytes 73400320 | tf_op jit(solution)/shard_map/bpr,bpo->bro/dot_general | solution.py:26
  1893.9 38.4 %fusion.3 = bf16[32,576,512]{2,0,1:T(8,128)(2,1)} fusion(bf16[32,576,512]{2,0,1:T(8,128)(2,1)} %get-tuple-element.406, f32[32,576,512]{2,1,0:T(8,128)} %fusion.4, f32[32,512]{1,0:T(8,128)S(1)} %bitcast.861, f32[32,576]{0,1:T(8,128)S(1)} %bitcast.853), kind=kLoop, calls=%fused_computation.5 | loop fusion | flops 47185920 | bytes 75636736 | tf_op jit(solution)/shard_map/convert_element_type | solution.py:861
  1932.2 13.7 fusion.76
  1962.8 11.7 fusion.167
  1974.5 9.2 copy.984
  1984.4 25.2 %all-gather.12.cloned.1.call-done = f32[32,74,128]{2,1,0:T(8,128)} async-done(((f32[1,74,128]{2,1,0:T(8,128)}), f32[32,74,128]{2,1,0:T(8,128)}) %all-gather.12.cloned.1.call-update) | async-done | bytes 1212432 | tf_op jit(solution)/shard_map/all_gather | solution.py:899
  (1101 shorter events, 878.7 us)
Async XLA Ops:
  7.2 325.4 %all-gather.16.cloned.1.call-start = ((), (), s32[]{:S(2)}) async-start(), calls=%async_computation.8 | async-start | bytes 31358976 | tf_op jit(solution)/shard_map/all_gather | solution.py:739
  43.0 55.6 %all-to-all-start = ((bf16[16,2,4096]{2,1,0:T(2,128)(2,1)}), bf16[16,2,4096]{2,1,0:T(2,128)(2,1)S(1)}, u32[]{:S(2)}, u32[]{:S(2)}) async-start(bf16[16,2,4096]{2,1,0:T(2,128)(2,1)} %reshape.803), calls=%async_computation | async-start | bytes 524288 | tf_op jit(solution)/shard_map/all_to_all | solution.py:596
  51.7 581.4 %all-gather.8.cloned.1.call-start = ((), (), s32[]{:S(2)}) async-start(), calls=%async_computation.4 | async-start | bytes 8912896 | tf_op jit(solution)/shard_map/all_gather | solution.py:662
  204.5 7.7 collective-permute-start
  223.0 47.3 %collective-permute-start.1 = (bf16[4,2,257,512]{3,0,2,1:T(4,128)(2,1)}, bf16[4,2,257,512]{3,0,2,1:T(4,128)(2,1)}, u32[]{:S(2)}, u32[]{:S(2)}) collective-permute-start(bf16[4,2,257,512]{3,0,2,1:T(4,128)(2,1)} %get-tuple-element.302), channel_id=1, source_target_pairs={{0,4},{2,6},{4,0},{6,2},{8,12},{10,14},{12,8},{14,10},{16,20},{18,... | collective-permute-start | bytes 6316040 | tf_op jit(solution)/shard_map/ppermute | solution.py:616
  276.5 14.5 collective-permute-start.2
  279.2 15.5 collective-permute-start.5
  292.8 13.2 collective-permute-start.3
  296.6 13.2 collective-permute-start.6
  307.4 12.5 collective-permute-start.4
  311.2 12.5 collective-permute-start.7
  553.5 931.7 %all-gather.14.cloned.1.call-start = ((), (), s32[]{:S(2)}) async-start(), calls=%async_computation.7 | async-start | bytes 3244032 | tf_op jit(solution)/shard_map/all_gather | solution.py:918
  914.7 7.4 collective-permute-start.15
  925.2 47.2 %collective-permute-start.16 = (bf16[4,2,256,512]{3,2,1,0:T(8,128)(2,1)S(1)}, bf16[4,2,256,512]{3,2,1,0:T(8,128)(2,1)S(1)}, u32[]{:S(2)}, u32[]{:S(2)}) collective-permute-start(bf16[4,2,256,512]{3,2,1,0:T(8,128)(2,1)S(1)} %dynamic-slice_bitcast_fusion.5), channel_id=1, source_target_pairs={{0,4},{2,6},{4,0},{6,2},{8,12},{10,14},{12,8},{14,10},{16,20},{18,... | collective-permute-start | bytes 6291464 | tf_op jit(solution)/shard_map/ppermute | solution.py:616
  972.7 14.6 collective-permute-start.17
  974.2 15.3 collective-permute-start.20
  987.4 13.7 collective-permute-start.18
  1001.2 12.7 collective-permute-start.21
  1002.7 13.2 collective-permute-start.11
  1003.9 13.8 collective-permute-start.19
  1013.9 11.6 collective-permute-start.22
  1025.6 8.4 collective-permute-start.23
  1185.4 447.7 %all-gather.10.cloned.1.call-start = ((), (), s32[]{:S(2)}) async-start(), calls=%async_computation.5 | async-start | bytes 18104320 | tf_op jit(solution)/shard_map/all_gather | solution.py:662
  1202.8 8.7 collective-permute-start.24
  1285.5 125.7 %collective-permute-start.28 = (bf16[4,2,2,416,512]{4,2,3,1,0:T(2,128)(2,1)}, bf16[4,2,2,416,512]{4,2,3,1,0:T(2,128)(2,1)}, u32[]{:S(2)}, u32[]{:S(2)}) collective-permute-start(bf16[4,2,2,416,512]{4,2,3,1,0:T(2,128)(2,1)} %dynamic-slice_bitcast_fusion), channel_id=1, source_target_pairs={{0,2},{2,0},{4,6},{6,4},{8,10},{10,8},{12,14},{14,12},{16,18},{18,... | collective-permute-start | bytes 20447240 | tf_op jit(solution)/shard_map/ppermute | solution.py:616
  1365.9 82.5 %collective-permute-start.45 = (bf16[4,2,2,512,512]{4,3,2,1,0:T(8,128)(2,1)}, bf16[4,2,2,512,512]{4,3,2,1,0:T(8,128)(2,1)}, u32[]{:S(2)}, u32[]{:S(2)}) collective-permute-start(bf16[4,2,2,512,512]{4,3,2,1,0:T(8,128)(2,1)} %fusion.19), channel_id=1, source_target_pairs={{0,2},{2,0},{4,6},{6,4},{8,10},{10,8},{12,14},{14,12},{16,18},{18,... | collective-permute-start | bytes 25165832 | tf_op jit(solution)/shard_map/ppermute | solution.py:616
  1366.0 20.9 %collective-permute-start.27 = (bf16[64,512]{1,0:T(8,128)(2,1)S(1)}, bf16[64,512]{1,0:T(8,128)(2,1)S(1)}, u32[]{:S(2)}, u32[]{:S(2)}) collective-permute-start(bf16[64,512]{1,0:T(8,128)(2,1)S(1)} %dynamic-slice_bitcast_fusion.30), channel_id=1, source_target_pairs={{0,1},{1,0},{2,3},{3,2},{4,5},{5,4},{6,7},{7,6},{8,9},{9,8},{10,11... | collective-permute-start | bytes 196616 | tf_op jit(solution)/shard_map/ppermute | solution.py:570
  1395.1 9.5 collective-permute-start.10
  1395.7 13.3 collective-permute-start.9
  1442.5 37.5 %collective-permute-start.29 = (bf16[4,2,208,512]{3,2,0,1:T(8,128)(2,1)S(1)}, bf16[4,2,208,512]{3,2,0,1:T(8,128)(2,1)S(1)}, u32[]{:S(2)}, u32[]{:S(2)}) collective-permute-start(bf16[4,2,208,512]{3,2,0,1:T(8,128)(2,1)S(1)} %bitcast.850), channel_id=1, source_target_pairs={{0,1},{1,0},{2,3},{3,2},{4,5},{5,4},{6,7},{7,6},{8,9},{9,8},{10,11... | collective-permute-start | bytes 5111816 | tf_op jit(solution)/shard_map/ppermute | solution.py:616
  1446.1 38.3 %collective-permute-start.37 = (bf16[4,2,208,512]{3,2,0,1:T(8,128)(2,1)S(1)}, bf16[4,2,208,512]{3,2,0,1:T(8,128)(2,1)S(1)}, u32[]{:S(2)}, u32[]{:S(2)}) collective-permute-start(bf16[4,2,208,512]{3,2,0,1:T(8,128)(2,1)S(1)} %bitcast.851), channel_id=1, source_target_pairs={{0,4},{2,6},{4,0},{6,2},{8,12},{10,14},{12,8},{14,10},{16,20},{18,... | collective-permute-start | bytes 5111816 | tf_op jit(solution)/shard_map/ppermute | solution.py:616
  1457.2 106.2 %collective-permute-start.46 = (bf16[4,2,256,512]{3,2,1,0:T(8,128)(2,1)}, bf16[4,2,256,512]{3,2,1,0:T(8,128)(2,1)}, u32[]{:S(2)}, u32[]{:S(2)}) collective-permute-start(bf16[4,2,256,512]{3,2,1,0:T(8,128)(2,1)} %dynamic-slice_bitcast_fusion.4), channel_id=1, source_target_pairs={{0,1},{1,0},{2,3},{3,2},{4,5},{5,4},{6,7},{7,6},{8,9},{9,8},{10,11... | collective-permute-start | bytes 6291464 | tf_op jit(solution)/shard_map/ppermute | solution.py:616
  1460.9 106.8 %collective-permute-start.54 = (bf16[4,2,256,512]{3,2,1,0:T(8,128)(2,1)}, bf16[4,2,256,512]{3,2,1,0:T(8,128)(2,1)}, u32[]{:S(2)}, u32[]{:S(2)}) collective-permute-start(bf16[4,2,256,512]{3,2,1,0:T(8,128)(2,1)} %dynamic-slice_bitcast_fusion.3), channel_id=1, source_target_pairs={{0,4},{2,6},{4,0},{6,2},{8,12},{10,14},{12,8},{14,10},{16,20},{18,... | collective-permute-start | bytes 6291464 | tf_op jit(solution)/shard_map/ppermute | solution.py:616
  1481.3 66.3 %collective-permute-start.30 = (bf16[4,208,512]{2,1,0:T(8,128)(2,1)}, bf16[4,208,512]{2,1,0:T(8,128)(2,1)}, u32[]{:S(2)}, u32[]{:S(2)}) collective-permute-start(bf16[4,208,512]{2,1,0:T(8,128)(2,1)} %dynamic-slice_bitcast_fusion.9), channel_id=1, source_target_pairs={{0,4},{2,6},{4,0},{6,2},{8,12},{10,14},{12,8},{14,10},{16,20},{18,... | collective-permute-start | bytes 2555912 | tf_op jit(solution)/shard_map/ppermute | solution.py:616
  1484.8 66.2 %collective-permute-start.38 = (bf16[4,208,512]{2,1,0:T(8,128)(2,1)S(1)}, bf16[4,208,512]{2,1,0:T(8,128)(2,1)}, u32[]{:S(2)}, u32[]{:S(2)}) collective-permute-start(bf16[4,208,512]{2,1,0:T(8,128)(2,1)S(1)} %dynamic-slice_bitcast_fusion.8), channel_id=1, source_target_pairs={{0,1},{1,0},{2,3},{3,2},{4,5},{5,4},{6,7},{7,6},{8,9},{9,8},{10,11... | collective-permute-start | bytes 2555912 | tf_op jit(solution)/shard_map/ppermute | solution.py:616
  1550.3 20.7 %collective-permute-start.34 = (bf16[208,512]{1,0:T(8,128)(2,1)S(1)}, bf16[208,512]{1,0:T(8,128)(2,1)S(1)}, u32[]{:S(2)}, u32[]{:S(2)}) collective-permute-start(bf16[208,512]{1,0:T(8,128)(2,1)S(1)} %get-tuple-element.369), channel_id=1, source_target_pairs={{24,16},{26,18},{28,20},{30,22},{25,17},{27,19},{29,21},{31,23}} | collective-permute-start | bytes 638984 | tf_op jit(solution)/shard_map/ppermute | solution.py:639
  1552.3 9.1 collective-permute-start.39
  1555.6 17.2 collective-permute-start.42
  1561.5 9.9 collective-permute-start.32
  1563.4 13.3 collective-permute-start.40
  1567.7 22.6 %collective-permute-start.47 = (bf16[4,256,512]{2,1,0:T(8,128)(2,1)S(1)}, bf16[4,256,512]{2,1,0:T(8,128)(2,1)S(1)}, u32[]{:S(2)}, u32[]{:S(2)}) collective-permute-start(bf16[4,256,512]{2,1,0:T(8,128)(2,1)S(1)} %dynamic-slice_bitcast_fusion.7), channel_id=1, source_target_pairs={{0,4},{2,6},{4,0},{6,2},{8,12},{10,14},{12,8},{14,10},{16,20},{18,... | collective-permute-start | bytes 3145736 | tf_op jit(solution)/shard_map/ppermute | solution.py:616
  1570.9 22.7 %collective-permute-start.55 = (bf16[4,256,512]{2,1,0:T(8,128)(2,1)S(1)}, bf16[4,256,512]{2,1,0:T(8,128)(2,1)S(1)}, u32[]{:S(2)}, u32[]{:S(2)}) collective-permute-start(bf16[4,256,512]{2,1,0:T(8,128)(2,1)S(1)} %dynamic-slice_bitcast_fusion.6), channel_id=1, source_target_pairs={{0,1},{1,0},{2,3},{3,2},{4,5},{5,4},{6,7},{7,6},{8,9},{9,8},{10,11... | collective-permute-start | bytes 3145736 | tf_op jit(solution)/shard_map/ppermute | solution.py:616
  1571.5 6.9 collective-permute-start.35
  1572.8 34.6 %collective-permute-start.33 = (bf16[208,512]{1,0:T(8,128)(2,1)S(1)}, bf16[208,512]{1,0:T(8,128)(2,1)S(1)}, u32[]{:S(2)}, u32[]{:S(2)}) collective-permute-start(bf16[208,512]{1,0:T(8,128)(2,1)S(1)} %get-tuple-element.366), channel_id=1, source_target_pairs={{0,8},{2,10},{4,12},{6,14},{8,16},{10,18},{12,20},{14,22},{16,24},... | collective-permute-start | bytes 638984 | tf_op jit(solution)/shard_map/ppermute | solution.py:638
  1576.9 18.2 collective-permute-start.43
  1578.4 39.9 %collective-permute-start.41 = (bf16[208,512]{1,0:T(8,128)(2,1)S(1)}, bf16[208,512]{1,0:T(8,128)(2,1)S(1)}, u32[]{:S(2)}, u32[]{:S(2)}) collective-permute-start(bf16[208,512]{1,0:T(8,128)(2,1)S(1)} %get-tuple-element.370), channel_id=1, source_target_pairs={{0,8},{2,10},{4,12},{6,14},{8,16},{10,18},{12,20},{14,22},{16,24},... | collective-permute-start | bytes 638984 | tf_op jit(solution)/shard_map/ppermute | solution.py:638
  1590.3 17.7 collective-permute-start.36
  1593.6 7.1 collective-permute-start.48
  1595.1 10.3 collective-permute-start.56
  1600.7 10.0 collective-permute-start.51
  1605.4 8.7 collective-permute-start.49
  1607.3 8.8 collective-permute-start.59
  1608.0 8.2 collective-permute-start.57
  1610.7 7.6 collective-permute-start.44
  1614.8 12.2 collective-permute-start.52
  1617.0 13.4 collective-permute-start.60
  1619.0 335.9 %collective-permute-start.50 = (bf16[256,512]{1,0:T(8,128)(2,1)}, bf16[256,512]{1,0:T(8,128)(2,1)}, u32[]{:S(2)}, u32[]{:S(2)}) collective-permute-start(bf16[256,512]{1,0:T(8,128)(2,1)} %get-tuple-element.346), channel_id=1, source_target_pairs={{0,8},{2,10},{4,12},{6,14},{8,16},{10,18},{12,20},{14,22},{16,24},... | collective-permute-start | bytes 786440 | tf_op jit(solution)/shard_map/ppermute | solution.py:638
  1623.6 332.5 %collective-permute-start.58 = (bf16[256,512]{1,0:T(8,128)(2,1)}, bf16[256,512]{1,0:T(8,128)(2,1)}, u32[]{:S(2)}, u32[]{:S(2)}) collective-permute-start(bf16[256,512]{1,0:T(8,128)(2,1)} %get-tuple-element.350), channel_id=1, source_target_pairs={{0,8},{2,10},{4,12},{6,14},{8,16},{10,18},{12,20},{14,22},{16,24},... | collective-permute-start | bytes 786440 | tf_op jit(solution)/shard_map/ppermute | solution.py:638
  1627.7 327.2 %collective-permute-start.53 = (bf16[256,512]{1,0:T(8,128)(2,1)}, bf16[256,512]{1,0:T(8,128)(2,1)}, u32[]{:S(2)}, u32[]{:S(2)}) collective-permute-start(bf16[256,512]{1,0:T(8,128)(2,1)} %bitcast_add_fusion.27), channel_id=1, source_target_pairs={{8,0},{10,2},{12,4},{14,6},{16,8},{18,10},{20,12},{22,14},{24,16},... | collective-permute-start | bytes 786440 | tf_op jit(solution)/shard_map/ppermute | solution.py:639
  1631.1 325.0 %collective-permute-start.61 = (bf16[256,512]{1,0:T(8,128)(2,1)}, bf16[256,512]{1,0:T(8,128)(2,1)}, u32[]{:S(2)}, u32[]{:S(2)}) collective-permute-start(bf16[256,512]{1,0:T(8,128)(2,1)} %bitcast_add_fusion.22), channel_id=1, source_target_pairs={{8,0},{10,2},{12,4},{14,6},{16,8},{18,10},{20,12},{22,14},{24,16},... | collective-permute-start | bytes 786440 | tf_op jit(solution)/shard_map/ppermute | solution.py:639
  1853.2 92.8 %all-to-all-start.3 = ((bf16[16,2,128,64]{2,3,1,0:T(8,128)(2,1)}), bf16[16,2,128,64]{2,3,1,0:T(8,128)(2,1)S(1)}, u32[]{:S(2)}, u32[]{:S(2)}) async-start(bf16[16,2,128,64]{2,3,1,0:T(8,128)(2,1)} %copy.962), calls=%async_computation.3 | async-start | bytes 1048576 | tf_op jit(solution)/shard_map/all_to_all | solution.py:604
  1865.7 143.9 %all-gather.12.cloned.1.call-start = ((), (), s32[]{:S(2)}) async-start(), calls=%async_computation.6 | async-start | bytes 1351680 | tf_op jit(solution)/shard_map/all_gather | solution.py:899
  1946.3 7.6 collective-permute-start.25
  1962.2 21.4 %collective-permute-start.26 = (f32[64,512]{1,0:T(8,128)S(1)}, f32[64,512]{1,0:T(8,128)S(1)}, u32[]{:S(2)}, u32[]{:S(2)}) collective-permute-start(f32[64,512]{1,0:T(8,128)S(1)} %constant_dynamic-slice_fusion.4), channel_id=1, source_target_pairs={{0,1},{1,0},{2,3},{3,2},{4,5},{5,4},{6,7},{7,6},{8,9},{9,8},{10,11... | collective-permute-start | bytes 393224 | tf_op jit(solution)/shard_map/ppermute | solution.py:570
  (263 other events, 4134.4 us)
Sparse Core Ops, SparseCore 0:
  21.7 183.5 all-gather.15
  553.6 79.5 all-gather.7
  1185.5 60.3 all-gather.13
  1247.4 90.0 all-gather.9
  1955.1 54.5 all-gather.11

commit v2 on v1

--- a/solution.py
+++ b/solution.py
@@ -1,6 +1,9 @@
 import jax
 import jax.numpy as jnp
+import numpy as np
 from jax import lax
+from jax.experimental import pallas as pl
+from jax.experimental.pallas import tpu as pltpu
 from jax.sharding import PartitionSpec as P
 
 HEAD = 64
@@ -563,6 +566,307 @@
     )
 
 
+CHUNK = 16
+PAD_ROWS = (SIDE + 2) * SIDE
+PIXELS = SIDE * SIDE
+
+
+def placing(half_side):
+    side = 2 * half_side
+    table = np.zeros((side + 2, side, 3, half_side * half_side), np.float32)
+    for row in range(1, side + 1):
+        for col in range(side):
+            for shift in range(3):
+                at = col + shift - 1
+                if 0 <= at < side:
+                    table[row, col, shift, (row - 1) // 2 * half_side + at // 2] = 1.0
+    return jnp.asarray(table.reshape((side + 2) * side, -1), jnp.bfloat16)
+
+
+def dot_f32(left, right, left_dim, right_dim):
+    return lax.dot_general(
+        left, right, (((left_dim,), (right_dim,)), ((), ())), preferred_element_type=jnp.float32
+    )
+
+
+def mix_matrix(select):
+    high = select.astype(jnp.bfloat16)
+    low = (select - high.astype(jnp.float32)).astype(jnp.bfloat16)
+    eye = jnp.eye(CHUNK, dtype=jnp.bfloat16)
+    parts = jnp.stack([high, low], axis=1)
+    wide = parts[:, None, :, :, None] * eye[None, :, None, None, :]
+    return wide.reshape(select.shape[0] * CHUNK, -1)
+
+
+def lanes_wide(column, width):
+    return jnp.concatenate([column] * (width // column.shape[-1]), axis=-1)
+
+
+def mix_body(pieces, mix_ref, bank_ref, squares_ref, kernel_ref, sums_ref):
+    step = pl.program_id(0)
+
+    @pl.when(step == 0)
+    def _():
+        sums_ref[...] = jnp.zeros_like(sums_ref)
+
+    kernels, rows, width = bank_ref.shape
+    samples = kernel_ref.shape[0]
+    per_tap = squares_ref.shape[1]
+    for piece in range(pieces):
+        part = bank_ref[:, piece * CHUNK : (piece + 1) * CHUNK, :].reshape(kernels * CHUNK, width)
+        mixed = dot_f32(mix_ref[...], jnp.concatenate([part, part], axis=0), 1, 0)
+        mixed = mixed.astype(jnp.bfloat16).reshape(samples, CHUNK, width)
+        kernel_ref[:, piece * CHUNK : (piece + 1) * CHUNK, :] = mixed
+        first = lax.rem(step * rows + piece * CHUNK, per_tap)
+        factor = squares_ref[:, pl.ds(pl.multiple_of(first, CHUNK), CHUNK), :]
+        wide = mixed.astype(jnp.float32)
+        sums_ref[...] += jnp.sum(wide * wide * lanes_wide(factor, width), axis=1)
+
+
+def mix_kernels(mix, bank_rows, squares):
+    kernels, depth, width = bank_rows.shape
+    samples = squares.shape[0]
+    pieces = 4
+    rows = pieces * CHUNK
+    return pl.pallas_call(
+        lambda *refs: mix_body(pieces, *refs),
+        grid=(depth // rows,),
+        in_specs=[
+            pl.BlockSpec(mix.shape, lambda step: (0, 0)),
+            pl.BlockSpec((kernels, rows, width), lambda step: (0, step, 0)),
+            pl.BlockSpec(squares.shape, lambda step: (0, 0, 0)),
+        ],
+        out_specs=[
+            pl.BlockSpec((samples, rows, width), lambda step: (0, step, 0)),
+            pl.BlockSpec((samples, width), lambda step: (0, 0)),
+        ],
+        out_shape=[
+            jax.ShapeDtypeStruct((samples, depth, width), jnp.bfloat16),
+            jax.ShapeDtypeStruct((samples, width), jnp.float32),
+        ],
+        compiler_params=pltpu.CompilerParams(vmem_limit_bytes=48 * 2**20),
+        name="mix_kernels",
+    )(mix, bank_rows, squares)
+
+
+def place_rows(slab, place_ref, spot_ref):
+    pixels, width = slab.shape
+    for shift in range(3):
+        spot_ref[
+            shift * pixels : (shift + 1) * pixels, shift * width : (shift + 1) * width
+        ] = slab
+    return dot_f32(place_ref[...], spot_ref[...], 1, 0).astype(jnp.bfloat16)
+
+
+def conv_body(extra, slab_ref, place_ref, kernel_ref, sums_ref, out_ref, spot_ref):
+    sample = pl.program_id(0)
+
+    @pl.when(sample == 0)
+    def _():
+        spot_ref[...] = jnp.zeros_like(spot_ref)
+
+    rows = place_rows(slab_ref[0], place_ref, spot_ref)
+    depth = rows.shape[1]
+    total = None
+    for shift in range(3):
+        term = dot_f32(
+            rows[shift * SIDE : shift * SIDE + PIXELS],
+            kernel_ref[0, shift * depth : (shift + 1) * depth, :],
+            1,
+            0,
+        )
+        total = term if total is None else total + term
+    out_ref[0, :PIXELS, :] = total.astype(jnp.bfloat16)
+    if extra:
+        line = sums_ref[pl.ds(sample, 1), :]
+        out_ref[0, PIXELS:, :] = jnp.broadcast_to(line, (CHUNK, line.shape[1])).astype(jnp.bfloat16)
+
+
+def convolve(slabs, place, kernel, sums, extra):
+    samples, pixels, width = slabs.shape
+    depth, width_out = kernel.shape[1:]
+    rows = PIXELS + (CHUNK if extra else 0)
+    return pl.pallas_call(
+        lambda *refs: conv_body(extra, *refs),
+        grid=(samples,),
+        in_specs=[
+            pl.BlockSpec((1, pixels, width), lambda step: (step, 0, 0)),
+            pl.BlockSpec(place.shape, lambda step: (0, 0)),
+            pl.BlockSpec((1, depth, width_out), lambda step: (step, 0, 0)),
+            pl.BlockSpec(sums.shape, lambda step: (0, 0)),
+        ],
+        out_specs=pl.BlockSpec((1, rows, width_out), lambda step: (step, 0, 0)),
+        out_shape=jax.ShapeDtypeStruct((samples, rows, width_out), jnp.bfloat16),
+        scratch_shapes=[pltpu.VMEM((3 * pixels, 3 * width), jnp.bfloat16)],
+        compiler_params=pltpu.CompilerParams(vmem_limit_bytes=32 * 2**20),
+        name="conv_forward",
+    )(slabs, place, kernel, sums)
+
+
+def fold_back(cotan, place_ref, kernel_ref, wide_ref, pixels, width):
+    depth = 3 * width
+    wide_ref[...] = jnp.zeros_like(wide_ref)
+    for shift in range(3):
+        wide_ref[shift * SIDE : shift * SIDE + PIXELS, :] += dot_f32(
+            cotan, kernel_ref[0, shift * depth : (shift + 1) * depth, :], 1, 1
+        )
+    back = dot_f32(place_ref[...], wide_ref[...].astype(jnp.bfloat16), 0, 0)
+    total = None
+    for shift in range(3):
+        term = back[shift * pixels : (shift + 1) * pixels, shift * width : (shift + 1) * width]
+        total = term if total is None else total + term
+    return total.astype(jnp.bfloat16)
+
+
+def back_body(cotan_ref, place_ref, kernel_ref, out_ref, wide_ref):
+    pixels, width = out_ref.shape[1:]
+    out_ref[0] = fold_back(cotan_ref[0], place_ref, kernel_ref, wide_ref, pixels, width)
+
+
+def conv_back(cotans, place, kernel, pixels, width):
+    samples, rows, width_out = cotans.shape
+    depth = kernel.shape[1]
+    return pl.pallas_call(
+        back_body,
+        grid=(samples,),
+        in_specs=[
+            pl.BlockSpec((1, rows, width_out), lambda step: (step, 0, 0)),
+            pl.BlockSpec(place.shape, lambda step: (0, 0)),
+            pl.BlockSpec((1, depth, width_out), lambda step: (step, 0, 0)),
+        ],
+        out_specs=pl.BlockSpec((1, pixels, width), lambda step: (step, 0, 0)),
+        out_shape=jax.ShapeDtypeStruct((samples, pixels, width), jnp.bfloat16),
+        scratch_shapes=[pltpu.VMEM((PAD_ROWS, 3 * width), jnp.float32)],
+        compiler_params=pltpu.CompilerParams(vmem_limit_bytes=32 * 2**20),
+        name="conv_back",
+    )(cotans, place, kernel)
+
+
+def second_body(
+    slab_ref,
+    tan_ref,
+    place_ref,
+    kernel_ref,
+    cotan_ref,
+    squares_ref,
+    grad_ref,
+    back_ref,
+    scale_ref,
+    spot_ref,
+    wide_ref,
+):
+    @pl.when(pl.program_id(0) == 0)
+    def _():
+        spot_ref[...] = jnp.zeros_like(spot_ref)
+
+    pixels, width = slab_ref.shape[1:]
+    depth = 3 * width
+    rows = place_rows(slab_ref[0], place_ref, spot_ref)
+    tan_rows = place_rows(tan_ref[0], place_ref, spot_ref)
+    line = cotan_ref[0, 2 * PIXELS : 2 * PIXELS + CHUNK, :][:1].astype(jnp.float32)
+    factor = 2.0 * lanes_wide(squares_ref[0], line.shape[1]) * line
+    totals = None
+    for shift in range(3):
+        span = slice(shift * SIDE, shift * SIDE + PIXELS)
+        grad = dot_f32(rows[span], cotan_ref[0, :PIXELS, :], 0, 0)
+        grad = grad + dot_f32(tan_rows[span], cotan_ref[0, PIXELS : 2 * PIXELS, :], 0, 0)
+        for tap in range(3):
+            at = shift * depth + tap * width
+            own = kernel_ref[0, at : at + width, :].astype(jnp.float32)
+            grad_ref[0, at : at + width, :] = (
+                grad[tap * width : (tap + 1) * width] + own * factor
+            ).astype(jnp.bfloat16)
+            term = own * own
+            totals = term if totals is None else totals + term
+    summed = jnp.sum(totals * line, axis=1, keepdims=True)
+    scale_ref[0] = jnp.broadcast_to(summed, scale_ref.shape[1:])
+    for part in range(2):
+        back_ref[0, part * pixels : (part + 1) * pixels, :] = fold_back(
+            cotan_ref[0, part * PIXELS : (part + 1) * PIXELS, :],
+            place_ref,
+            kernel_ref,
+            wide_ref,
+            pixels,
+            width,
+        )
+
+
+def conv_second(slabs, tans, place, kernel, cotans, squares):
+    samples, pixels, width = slabs.shape
+    depth, width_out = kernel.shape[1:]
+    return pl.pallas_call(
+        second_body,
+        grid=(samples,),
+        in_specs=[
+            pl.BlockSpec((1, pixels, width), lambda step: (step, 0, 0)),
+            pl.BlockSpec((1, pixels, width), lambda step: (step, 0, 0)),
+            pl.BlockSpec(place.shape, lambda step: (0, 0)),
+            pl.BlockSpec((1, depth, width_out), lambda step: (step, 0, 0)),
+            pl.BlockSpec((1,) + cotans.shape[1:], lambda step: (step, 0, 0)),
+            pl.BlockSpec((1,) + squares.shape[1:], lambda step: (step, 0, 0)),
+        ],
+        out_specs=[
+            pl.BlockSpec((1, depth, width_out), lambda step: (step, 0, 0)),
+            pl.BlockSpec((1, 2 * pixels, width), lambda step: (step, 0, 0)),
+            pl.BlockSpec((1,) + squares.shape[1:], lambda step: (step, 0, 0)),
+        ],
+        out_shape=[
+            jax.ShapeDtypeStruct((samples, depth, width_out), jnp.bfloat16),
+            jax.ShapeDtypeStruct((samples, 2 * pixels, width), jnp.bfloat16),
+            jax.ShapeDtypeStruct(squares.shape, jnp.float32),
+        ],
+        scratch_shapes=[
+            pltpu.VMEM((3 * pixels, 3 * width), jnp.bfloat16),
+            pltpu.VMEM((PAD_ROWS, 3 * width), jnp.float32),
+        ],
+        compiler_params=pltpu.CompilerParams(vmem_limit_bytes=32 * 2**20),
+        name="conv_second",
+    )(slabs, tans, place, kernel, cotans, squares)
+
+
+def unmix_body(pieces, mix_ref, bank_ref, grad_ref, out_ref, select_ref):
+    @pl.when(pl.program_id(0) == 0)
+    def _():
+        select_ref[...] = jnp.zeros_like(select_ref)
+
+    kernels, _, width = bank_ref.shape
+    samples = grad_ref.shape[0]
+    for piece in range(pieces):
+        span = slice(piece * CHUNK, (piece + 1) * CHUNK)
+        grad = grad_ref[:, span, :].reshape(samples * CHUNK, width)
+        mixed = dot_f32(mix_ref[...], grad, 0, 0)
+        count = kernels * CHUNK
+        out_ref[:, span, :] = (mixed[:count] + mixed[count:]).reshape(kernels, CHUNK, width)
+        part = bank_ref[:, span, :].reshape(count, width)
+        select_ref[...] += dot_f32(grad, part, 1, 1)
+
+
+def unmix_kernels(mix, bank_rows, grad):
+    kernels, depth, width = bank_rows.shape
+    samples = grad.shape[0]
+    pieces = 4
+    rows = pieces * CHUNK
+    return pl.pallas_call(
+        lambda *refs: unmix_body(pieces, *refs),
+        grid=(depth // rows,),
+        in_specs=[
+            pl.BlockSpec(mix.shape, lambda step: (0, 0)),
+            pl.BlockSpec((kernels, rows, width), lambda step: (0, step, 0)),
+            pl.BlockSpec((samples, rows, width), lambda step: (0, step, 0)),
+        ],
+        out_specs=[
+            pl.BlockSpec((kernels, rows, width), lambda step: (0, step, 0)),
+            pl.BlockSpec((samples * CHUNK, kernels * CHUNK), lambda step: (0, 0)),
+        ],
+        out_shape=[
+            jax.ShapeDtypeStruct((kernels, depth, width), jnp.float32),
+            jax.ShapeDtypeStruct((samples * CHUNK, kernels * CHUNK), jnp.float32),
+        ],
+        compiler_params=pltpu.CompilerParams(vmem_limit_bytes=48 * 2**20),
+        name="unmix_kernels",
+    )(mix, bank_rows, grad)
+
+
 SWAP = ((0, 1), (1, 0))
 
 
@@ -607,82 +911,638 @@
     return pick(parts, mp).astype(jnp.float32) + other.astype(jnp.float32)
 
 
-def halve(values, axis_name, bit, dim):
-    size = lax.axis_size(axis_name)
-    side = (lax.axis_index(axis_name) // bit) % 2
-    pairs = [(index, index ^ bit) for index in range(size)]
-    sent = lax.dynamic_index_in_dim(values, 1 - side, dim, keepdims=False)
-    kept = lax.dynamic_index_in_dim(values, side, dim, keepdims=False)
-    return kept + lax.ppermute(sent, axis_name, pairs)
-
-
-def line_sum(values, dim):
-    place = lax.axis_index("dp") // 4
-    up = down = None
-    for step in range(1, 4):
-        send_up = lax.dynamic_index_in_dim(
-            values, jnp.clip(4 - step + place, 0, 3), dim, keepdims=False
-        )
-        send_down = lax.dynamic_index_in_dim(
-            values, jnp.clip(place - 4 + step, 0, 3), dim, keepdims=False
-        )
-        if up is not None:
-            send_up = send_up + up
-            send_down = send_down + down
-        up_pairs = [
-            (z * 4 + rest, z * 4 + 4 + rest) for z in range(3) if z < step for rest in range(4)
-        ]
-        down_pairs = [
-            (z * 4 + rest, z * 4 - 4 + rest) for z in range(1, 4) if 3 - z < step for rest in range(4)
-        ]
-        up = lax.ppermute(send_up, "dp", up_pairs)
-        down = lax.ppermute(send_down, "dp", down_pairs)
-    own = lax.dynamic_index_in_dim(values, place, dim, keepdims=False)
-    return own + up + down
-
-
-def sum_dp(partial):
-    parts = partial.reshape((4, 2, 2, 2) + partial.shape[1:])
-    parts = halve(parts, "dp", 1, 2)
-    parts = halve(parts, "dp", 2, 1)
-    return line_sum(parts, 0)
-
-
-def sum_all(partial):
-    parts = partial.reshape((4, 2, 2, 2) + partial.shape[2:])
-    parts = halve(parts, "dp", 1, 2)
-    rows = parts.shape[3]
-    first, second = parts[:, :, :, : rows // 2], parts[:, :, :, rows // 2 :]
-    first = halve(halve(first, "mp", 1, 2), "dp", 2, 1)
-    second = halve(halve(second, "dp", 2, 1), "mp", 1, 1)
-    return jnp.concatenate([line_sum(first, 0), line_sum(second, 0)], axis=0)
-
-
-def gather_dp(values):
-    return lax.all_gather(values, "dp", axis=0, tiled=True)
-
-
-def pack_rows(entry, flip):
-    if flip:
-        entry = entry.T
-    rows = entry.shape[0]
-    return entry.reshape(rows, -1, 512).transpose(1, 0, 2).reshape(-1, 512)
-
-
-def unpack_shard(entry, rows, flip):
-    entry = entry.reshape(-1, rows, 512).transpose(1, 0, 2).reshape(rows, -1)
-    return entry.T if flip else entry
-
-
-def whole_weight(gathered, start, rows, count):
-    piece = gathered[:, start : start + rows * count]
-    piece = piece.reshape(16, 2, count, rows, 512).transpose(0, 3, 1, 2, 4)
-    return piece.reshape(16 * rows, 2 * count * 512)
-
-
-def spread_weight(grad, rows, count):
-    piece = grad.reshape(16, rows, 2, count, 512).transpose(0, 2, 3, 1, 4)
-    return piece.reshape(16, 2, count * rows, 512)
+PLANES = 4
+
+
+class Place:
+    def __init__(self):
+        dp = lax.axis_index("dp")
+        self.z, self.y, self.core = dp // 4, lax.rem(dp // 2, 2), lax.rem(dp, 2)
+        self.x = lax.axis_index("mp")
+
+
+def greet(place, axes):
+    barrier = pltpu.get_barrier_semaphore()
+
+    def tell(**there):
+        at = dict(z=place.z, y=place.y, core=place.core, x=place.x)
+        at.update(there)
+        pl.semaphore_signal(
+            barrier,
+            inc=1,
+            device_id=((at["z"] * 2 + at["y"]) * 2 + at["core"], at["x"]),
+            device_id_type=pl.DeviceIdType.MESH,
+        )
+
+    tell(core=1 - place.core)
+    count = 1
+    for name in ("y", "x"):
+        if name in axes:
+            tell(**{name: 1 - getattr(place, name)})
+            count += 1
+
+    @pl.when(place.z > 0)
+    def _():
+        tell(z=place.z - 1)
+
+    @pl.when(place.z < PLANES - 1)
+    def _():
+        tell(z=place.z + 1)
+
+    between = (place.z > 0) & (place.z < PLANES - 1)
+    pl.semaphore_wait(barrier, count + jnp.where(between, 2, 1))
+
+
+def gather_body(pieces, inputs, outputs, axes, send_sem, recv_sem, own_sem):
+    place = Place()
+    greet(place, axes)
+    sends = []
+
+    def spot(z, y, core, x):
+        return (z * 2 + y) * 2 + core, x
+
+    def chip(z, y, x):
+        return (z * 2 + y) * 2 + x
+
+    def send(number, piece, source, target, slot, parity, first, condition):
+        sz, sy, sx = source
+        dp, mp = spot(sz, sy, place.core, sx)
+        there = piece["to"](outputs, dp, mp)
+        copy = pltpu.make_async_remote_copy(
+            src_ref=piece["of"](inputs) if first else there,
+            dst_ref=there,
+            send_sem=send_sem.at[number, chip(sz, sy, sx), slot],
+            recv_sem=recv_sem.at[number, chip(sz, sy, sx), parity],
+            device_id=spot(*target),
+            device_id_type=pl.DeviceIdType.MESH,
+        )
+
+        if condition is None:
+            copy.start()
+        else:
+            pl.when(condition)(copy.start)
+        sends.append((condition, copy))
+
+    def onward(number, piece, source, came, first, condition):
+        def both(more):
+            if condition is None:
+                return more
+            return condition if more is None else condition & more
+
+        order = piece["order"]
+        later = order if came is None else order[order.index(came[0]) :]
+        for name in later:
+            here = dict(z=place.z, y=place.y, core=place.core, x=place.x)
+            if name == "z":
+                for way, slot in ((1, 0), (-1, 1)):
+                    if came is not None and came[0] == "z" and came[1] != way:
+                        continue
+                    fits = place.z < PLANES - 1 if way == 1 else place.z > 0
+                    target = (place.z + way, place.y, place.core, place.x)
+                    send(number, piece, source, target, slot, 0, first, both(fits))
+            elif came is None or came[0] != name:
+                here[name] = 1 - here[name]
+                target = (here["z"], here["y"], here["core"], here["x"])
+                slot = 2 if name == "y" else 3
+                send(number, piece, source, target, slot, 0, first, both(None))
+        target = (place.z, place.y, 1 - place.core, place.x)
+        send(number, piece, source, target, 4, 1, first, both(None))
+
+    def arrive(number, piece, source, parity, condition):
+        sz, sy, sx = source
+        core = place.core if parity == 0 else 1 - place.core
+        there = piece["to"](outputs, *spot(sz, sy, core, sx))
+
+        def wait():
+            pltpu.make_async_remote_copy(
+                src_ref=there,
+                dst_ref=there,
+                send_sem=send_sem.at[number, chip(sz, sy, sx), 0],
+                recv_sem=recv_sem.at[number, chip(sz, sy, sx), parity],
+                device_id=spot(place.z, place.y, 1 - place.core, place.x),
+                device_id_type=pl.DeviceIdType.MESH,
+            ).wait_recv()
+
+        if condition is None:
+            wait()
+        else:
+            pl.when(condition)(wait)
+
+    own = []
+    for number, piece in enumerate(pieces):
+        onward(number, piece, (place.z, place.y, place.x), None, True, None)
+        copy = pltpu.make_async_copy(
+            piece["of"](inputs),
+            piece["to"](outputs, *spot(place.z, place.y, place.core, place.x)),
+            own_sem.at[number],
+        )
+        copy.start()
+        own.append(copy)
+    flips = [(fy, fx) for fy in (0, 1) for fx in ((0, 1) if "x" in axes else (0,))]
+    blocks = [(dz, fy, fx) for dz in (0, 1, -1, 2, -2, 3, -3) for fy, fx in flips]
+    blocks = sorted(blocks, key=lambda block: abs(block[0]) + block[1] + block[2])
+    for dz, fy, fx in blocks:
+        if (dz, fy, fx) == (0, 0, 0):
+            continue
+        condition = None
+        if dz > 0:
+            condition = place.z >= dz
+        elif dz < 0:
+            condition = place.z < PLANES + dz
+        source = (
+            place.z - dz,
+            1 - place.y if fy else place.y,
+            1 - place.x if fx else place.x,
+        )
+        for number, piece in enumerate(pieces):
+            arrive(number, piece, source, 0, condition)
+            moved = dict(z=dz, y=fy, x=fx)
+            last = [name for name in piece["order"] if moved[name]][-1]
+            came = (last, (1 if dz > 0 else -1) if last == "z" else 0)
+            onward(number, piece, source, came, False, condition)
+    for number, piece in enumerate(pieces):
+        for sz in range(PLANES):
+            for sy in range(2):
+                for sx in (0, 1) if "x" in axes else (place.x,):
+                    arrive(number, piece, (sz, sy, sx), 1, None)
+    for condition, copy in sends:
+        if condition is None:
+            copy.wait_send()
+        else:
+            pl.when(condition)(copy.wait_send)
+    for copy in own:
+        copy.wait()
+
+
+def gather_call(pieces, axes, arrays, shapes, call_id, name):
+    count = len(arrays)
+
+    def body(*refs):
+        inputs, outputs = refs[:count], refs[count : count + len(shapes)]
+        gather_body(pieces, inputs, outputs, axes, *refs[count + len(shapes) :])
+
+    return pl.pallas_call(
+        body,
+        in_specs=[pl.BlockSpec(memory_space=pl.ANY)] * count,
+        out_specs=[pl.BlockSpec(memory_space=pl.ANY)] * len(shapes),
+        out_shape=[jax.ShapeDtypeStruct(shape, jnp.bfloat16) for shape in shapes],
+        scratch_shapes=[
+            pltpu.SemaphoreType.DMA((len(pieces), 16, 5)),
+            pltpu.SemaphoreType.DMA((len(pieces), 16, 2)),
+            pltpu.SemaphoreType.DMA((len(pieces),)),
+        ],
+        compiler_params=pltpu.CompilerParams(collective_id=call_id, has_side_effects=True),
+        name=name,
+    )(*arrays)
+
+
+def rows_at(index, rows):
+    return pl.ds(pl.multiple_of(index * rows, rows), rows)
+
+
+def lanes_at(index, lanes):
+    return pl.ds(pl.multiple_of(index * lanes, lanes), lanes)
+
+
+def gather_weights(stacks, call_id):
+    def piece(number, first, last, order):
+        rows, lanes = stacks[number].shape[1:]
+        return dict(
+            order=order,
+            of=lambda refs: refs[number].at[first:last],
+            to=lambda refs, dp, mp: refs[number].at[
+                first:last, rows_at(dp, rows), lanes_at(mp, lanes)
+            ],
+        )
+
+    pieces = [
+        piece(0, 0, 2, ("x", "y", "z")),
+        piece(0, 2, 5, ("z", "x", "y")),
+        piece(1, 0, 2, ("z", "y", "x")),
+        piece(2, 0, 1, ("z", "x", "y")),
+        piece(2, 1, 2, ("z", "y", "x")),
+    ]
+    shapes = [(a.shape[0], a.shape[1] * 16, a.shape[2] * 2) for a in stacks]
+    return gather_call(pieces, ("z", "y", "x"), stacks, shapes, call_id, "gather_weights")
+
+
+def gather_dp(values, call_id):
+    samples, rows, lanes = values.shape
+
+    def piece(sample, first, last, order):
+        return dict(
+            order=order,
+            of=lambda refs: refs[0].at[sample, :, first:last],
+            to=lambda refs, dp, mp: refs[0].at[dp * samples + sample, :, first:last],
+        )
+
+    cut = lanes * 3 // 4
+    pieces = [piece(sample, 0, cut, ("z", "y")) for sample in range(samples)]
+    pieces += [piece(sample, cut, lanes, ("y", "z")) for sample in range(samples)]
+    shapes = [(16 * samples, rows, lanes)]
+    return gather_call(pieces, ("z", "y"), [values], shapes, call_id, "gather_samples")[0]
+
+
+def add_rows(total, part):
+    shape = total.shape[:-2]
+    for number in range(int(np.prod(shape))):
+        spot = tuple(int(place) for place in np.unravel_index(number, shape))
+        total[spot] = (total[spot].astype(jnp.float32) + part[spot].astype(jnp.float32)).astype(
+            jnp.bfloat16
+        )
+
+
+def sum_body(
+    cut,
+    part_ref,
+    out_ref,
+    acc,
+    core_in,
+    y_in,
+    y_last,
+    z_first,
+    z_second,
+    x_in,
+    load_sem,
+    core_send,
+    core_recv,
+    y_send,
+    y_recv,
+    z_send,
+    z_recv,
+    x_send,
+    x_recv,
+):
+    place = Place()
+    greet(place, ("z", "y", "x"))
+    z, y, x = place.z, place.y, place.x
+    wide, narrow = slice(0, cut), slice(cut, acc.shape[-1])
+    finish = []
+
+    def spot(z, y, core, x):
+        return (z * 2 + y) * 2 + core, x
+
+    def remote(source, target, send, recv, device):
+        return pltpu.make_async_remote_copy(
+            src_ref=source,
+            dst_ref=target,
+            send_sem=send,
+            recv_sem=recv,
+            device_id=spot(*device),
+            device_id_type=pl.DeviceIdType.MESH,
+        )
+
+    other_core = (z, y, 1 - place.core, x)
+    other_y = (z, 1 - y, place.core, x)
+    other_x = (z, y, place.core, 1 - x)
+
+    chunks = [(dest, 1 - y) for dest in (3, 0, 2, 1)] + [(dest, y) for dest in (3, 0, 2, 1)]
+    first = []
+    for number, (dest, side) in enumerate(chunks):
+        sent = remote(
+            part_ref.at[dest, side, 1 - place.core],
+            core_in.at[dest, side],
+            core_send.at[number],
+            core_recv.at[number],
+            other_core,
+        )
+        sent.start()
+        mine = pltpu.make_async_copy(
+            part_ref.at[dest, side, place.core], acc.at[dest, side], load_sem.at[number]
+        )
+        mine.start()
+        first.append((sent, mine))
+
+    y_copies = []
+    for number, (dest, side) in enumerate(chunks):
+        sent, mine = first[number]
+        mine.wait()
+        sent.wait_recv()
+        add_rows(acc.at[dest, side], core_in.at[dest, side])
+        finish.append(sent)
+        if number < 4:
+            copy = remote(
+                acc.at[dest, side, :, :, wide],
+                y_in.at[dest],
+                y_send.at[dest],
+                y_recv.at[dest],
+                other_y,
+            )
+            copy.start()
+            y_copies.append(copy)
+
+    def along_z(slot, view, landing, dest):
+        for way in (0, 1):
+            near = dest > z if way == 0 else dest < z
+            has_before = z > 0 if way == 0 else z < PLANES - 1
+            copy = remote(
+                view,
+                landing.at[way, dest],
+                z_send.at[slot, way, dest],
+                z_recv.at[slot, way, dest],
+                (z + (1 if way == 0 else -1), y, place.core, x),
+            )
+
+            @pl.when(near & has_before)
+            def _():
+                copy.wait_recv()
+                add_rows(view, landing.at[way, dest])
+
+            pl.when(near)(copy.start)
+            finish.append((near, copy))
+
+    def end_z(slot, view, landing):
+        for way in (0, 1):
+            copy = remote(
+                view,
+                landing.at[way, z],
+                z_send.at[slot, way, z],
+                z_recv.at[slot, way, z],
+                other_core,
+            )
+
+            @pl.when(z > 0 if way == 0 else z < PLANES - 1)
+            def _():
+                copy.wait_recv()
+                add_rows(view, landing.at[way, z])
+
+    for number, dest in enumerate((3, 0, 2, 1)):
+        along_z(1, acc.at[dest, :, :, :, narrow], z_second, dest)
+        y_copies[number].wait_recv()
+        finish.append(y_copies[number])
+        view = acc.at[dest, y, :, :, wide]
+        add_rows(view, y_in.at[dest])
+        along_z(0, view, z_first, dest)
+    end_z(1, acc.at[z, :, :, :, narrow], z_second)
+    last = remote(
+        acc.at[z, 1 - y, :, :, narrow], y_last, y_send.at[PLANES], y_recv.at[PLANES], other_y
+    )
+    last.start()
+    finish.append(last)
+    end_z(0, acc.at[z, y, :, :, wide], z_first)
+    last.wait_recv()
+    add_rows(acc.at[z, y, :, :, narrow], y_last)
+    swap = remote(acc.at[z, y, 1 - x], x_in, x_send, x_recv, other_x)
+    swap.start()
+    lanes = acc.shape[-1]
+    out_ref[:, lanes_at(x, lanes)] = acc[z, y, x]
+    swap.wait_recv()
+    out_ref[:, lanes_at(1 - x, lanes)] = x_in[...]
+    finish.append(swap)
+    for item in finish:
+        if isinstance(item, tuple):
+            pl.when(item[0])(item[1].wait_send)
+        else:
+            item.wait_send()
+
+
+def sum_samples(partial, call_id):
+    samples, rows, lanes = partial.shape
+    cut = lanes * 3 // 4
+    bf16, dma = jnp.bfloat16, pltpu.SemaphoreType.DMA
+    return pl.pallas_call(
+        lambda *refs: sum_body(cut, *refs),
+        in_specs=[pl.BlockSpec(memory_space=pl.ANY)],
+        out_specs=pl.BlockSpec(memory_space=pltpu.VMEM),
+        out_shape=jax.ShapeDtypeStruct((rows, 2 * lanes), bf16),
+        scratch_shapes=[
+            pltpu.VMEM((PLANES, 2, 2, rows, lanes), bf16),
+            pltpu.VMEM((PLANES, 2, 2, rows, lanes), bf16),
+            pltpu.VMEM((PLANES, 2, rows, cut), bf16),
+            pltpu.VMEM((2, rows, lanes - cut), bf16),
+            pltpu.VMEM((2, PLANES, 2, rows, cut), bf16),
+            pltpu.VMEM((2, PLANES, 2, 2, rows, lanes - cut), bf16),
+            pltpu.VMEM((rows, lanes), bf16),
+            dma((8,)),
+            dma((8,)),
+            dma((8,)),
+            dma((PLANES + 1,)),
+            dma((PLANES + 1,)),
+            dma((2, 2, PLANES)),
+            dma((2, 2, PLANES)),
+            dma,
+            dma,
+        ],
+        compiler_params=pltpu.CompilerParams(
+            collective_id=call_id, has_side_effects=True, vmem_limit_bytes=40 * 2**20
+        ),
+        name="sum_samples",
+    )(partial.reshape(PLANES, 2, 2, 2, rows, lanes))
+
+
+def sum_weights_body(parts, count, refs):
+    inputs, outputs, rest = refs[:count], refs[count : 2 * count], refs[2 * count :]
+    acc, core_in, one_in, two_in, z_in = (rest[k * count : (k + 1) * count] for k in range(5))
+    (
+        load_sem,
+        core_send,
+        core_recv,
+        one_send,
+        one_recv,
+        two_send,
+        two_recv,
+        z_send,
+        z_recv,
+    ) = rest[5 * count :]
+    place = Place()
+    greet(place, ("z", "y", "x"))
+    z, y, x = place.z, place.y, place.x
+    order = (3, 0, 2, 1)
+    finish = []
+
+    def remote(source, target, send, recv, device):
+        dz, dy, core, dx = device
+        return pltpu.make_async_remote_copy(
+            src_ref=source,
+            dst_ref=target,
+            send_sem=send,
+            recv_sem=recv,
+            device_id=((dz * 2 + dy) * 2 + core, dx),
+            device_id_type=pl.DeviceIdType.MESH,
+        )
+
+    other_core = (z, y, 1 - place.core, x)
+    other_y = (z, 1 - y, place.core, x)
+    other_x = (z, y, place.core, 1 - x)
+    sides = (1 - y, y)
+
+    first = {}
+    for dest in order:
+        for w in range(count):
+            rows = acc[w].shape[2]
+            for turn, side in enumerate(sides):
+                at = ((dest * 2 + side) * 2 + (1 - place.core)) * rows
+                mine = ((dest * 2 + side) * 2 + place.core) * rows
+                sent = remote(
+                    inputs[w].at[pl.ds(pl.multiple_of(at, rows), rows)],
+                    core_in[w].at[dest, side],
+                    core_send.at[w, dest, turn],
+                    core_recv.at[w, dest, turn],
+                    other_core,
+                )
+                sent.start()
+                load = pltpu.make_async_copy(
+                    inputs[w].at[pl.ds(pl.multiple_of(mine, rows), rows)],
+                    acc[w].at[dest, side],
+                    load_sem.at[w, dest, turn],
+                )
+                load.start()
+                first[w, dest, turn] = (sent, load)
+
+    def half(w, index):
+        lanes = acc[w].shape[-1] // 2
+        return lanes_at(index, lanes)
+
+    ones, twos = {}, {}
+
+    def stage_one(dest):
+        for w in range(count):
+            for turn, side in enumerate(sides):
+                sent, load = first[w, dest, turn]
+                load.wait()
+                sent.wait_recv()
+                finish.append((None, sent))
+                add_rows(acc[w].at[dest, side], core_in[w].at[dest, side])
+                if parts[w] == "xy":
+                    copy = remote(
+                        acc[w].at[dest, side, :, half(w, 1 - x)],
+                        one_in[w].at[dest, side],
+                        one_send.at[w, dest, turn],
+                        one_recv.at[w, dest, turn],
+                        other_x,
+                    )
+                elif turn == 0:
+                    copy = remote(
+                        acc[w].at[dest, side],
+                        one_in[w].at[dest],
+                        one_send.at[w, dest, turn],
+                        one_recv.at[w, dest, turn],
+                        other_y,
+                    )
+                else:
+                    continue
+                copy.start()
+                ones[w, dest, turn] = copy
+
+    def stage_two(dest):
+        for w in range(count):
+            if parts[w] == "xy":
+                for turn, side in enumerate(sides):
+                    copy = ones[w, dest, turn]
+                    copy.wait_recv()
+                    finish.append((None, copy))
+                    view = acc[w].at[dest, side, :, half(w, x)]
+                    add_rows(view, one_in[w].at[dest, side])
+                    if turn == 0:
+                        twos[w, dest] = remote(
+                            view,
+                            two_in[w].at[dest],
+                            two_send.at[w, dest],
+                            two_recv.at[w, dest],
+                            other_y,
+                        )
+                        twos[w, dest].start()
+            else:
+                copy = ones[w, dest, 0]
+                copy.wait_recv()
+                finish.append((None, copy))
+                add_rows(acc[w].at[dest, y], one_in[w].at[dest])
+                twos[w, dest] = remote(
+                    acc[w].at[dest, y, :, half(w, 1 - x)],
+                    two_in[w].at[dest],
+                    two_send.at[w, dest],
+                    two_recv.at[w, dest],
+                    other_x,
+                )
+                twos[w, dest].start()
+
+    def z_copy(w, dest, way):
+        return remote(
+            acc[w].at[dest, y, :, half(w, x)],
+            z_in[w].at[way, dest],
+            z_send.at[w, way, dest],
+            z_recv.at[w, way, dest],
+            (z + (1 if way == 0 else -1), y, place.core, x),
+        )
+
+    def stage_z(dest):
+        for w in range(count):
+            copy = twos[w, dest]
+            copy.wait_recv()
+            finish.append((None, copy))
+            view = acc[w].at[dest, y, :, half(w, x)]
+            add_rows(view, two_in[w].at[dest])
+            for way in (0, 1):
+                near = dest > z if way == 0 else dest < z
+                has_before = z > 0 if way == 0 else z < PLANES - 1
+                copy = z_copy(w, dest, way)
+
+                @pl.when(near & has_before)
+                def _():
+                    copy.wait_recv()
+                    add_rows(view, z_in[w].at[way, dest])
+
+                pl.when(near)(copy.start)
+                finish.append((near, copy))
+
+    for turn in range(PLANES + 2):
+        if turn < PLANES:
+            stage_one(order[turn])
+        if 0 <= turn - 1 < PLANES:
+            stage_two(order[turn - 1])
+        if turn >= 2:
+            stage_z(order[turn - 2])
+    for w in range(count):
+        view = acc[w].at[z, y, :, half(w, x)]
+        for way in (0, 1):
+
+            @pl.when(z > 0 if way == 0 else z < PLANES - 1)
+            def _():
+                remote(
+                    view,
+                    z_in[w].at[way, z],
+                    z_send.at[w, way, z],
+                    z_recv.at[w, way, z],
+                    other_core,
+                ).wait_recv()
+                add_rows(view, z_in[w].at[way, z])
+
+        outputs[w][...] = acc[w][z, y, :, half(w, x)].astype(jnp.float32)
+    for condition, copy in finish:
+        if condition is None:
+            copy.wait_send()
+        else:
+            pl.when(condition)(copy.wait_send)
+
+
+def sum_weights(grads, parts, call_id):
+    count = len(grads)
+    bf16, dma = jnp.bfloat16, pltpu.SemaphoreType.DMA
+    blocks = [(grad.shape[0] // 16, grad.shape[1]) for grad in grads]
+    ones = [
+        (PLANES, 2, rows, lanes // 2) if part == "xy" else (PLANES, rows, lanes)
+        for (rows, lanes), part in zip(blocks, parts)
+    ]
+    return pl.pallas_call(
+        lambda *refs: sum_weights_body(parts, count, refs),
+        in_specs=[pl.BlockSpec(memory_space=pl.ANY)] * count,
+        out_specs=[pl.BlockSpec(memory_space=pltpu.VMEM)] * count,
+        out_shape=[
+            jax.ShapeDtypeStruct((rows, lanes // 2), jnp.float32) for rows, lanes in blocks
+        ],
+        scratch_shapes=[pltpu.VMEM((PLANES, 2, rows, lanes), bf16) for rows, lanes in blocks]
+        + [pltpu.VMEM((PLANES, 2, rows, lanes), bf16) for rows, lanes in blocks]
+        + [pltpu.VMEM(shape, bf16) for shape in ones]
+        + [pltpu.VMEM((PLANES, rows, lanes // 2), bf16) for rows, lanes in blocks]
+        + [pltpu.VMEM((2, PLANES, rows, lanes // 2), bf16) for rows, lanes in blocks]
+        + [dma((count, PLANES, 2))] * 5
+        + [dma((count, PLANES))] * 2
+        + [dma((count, 2, PLANES))] * 2,
+        compiler_params=pltpu.CompilerParams(
+            collective_id=call_id, has_side_effects=True, vmem_limit_bytes=60 * 2**20
+        ),
+        name="sum_weights",
+    )(*grads)
 
 
 def sample_parallel(
@@ -720,29 +1580,25 @@
     width_out = kernel_bank.shape[3]
     float32, bfloat16 = jnp.float32, jnp.bfloat16
 
-    flips = (False, False, True, False, False, False, True, False, True)
-    shards = (
-        qk_weight,
-        value_weight,
-        attn_out,
-        cross_query,
-        cross_key,
-        cross_value,
-        cross_out,
-        mlp_in,
-        mlp_out,
-    )
-    rows_of = [entry.shape[1] if flip else entry.shape[0] for entry, flip in zip(shards, flips)]
-    packed = [pack_rows(entry, flip) for entry, flip in zip(shards, flips)]
-    counts = [entry.shape[0] // rows for entry, rows in zip(packed, rows_of)]
-    stacked = jnp.concatenate(packed, axis=0)
-    gathered = lax.all_gather(stacked, ("dp", "mp"), axis=0, tiled=False)
-    weights = []
-    start = 0
-    for rows, count in zip(rows_of, counts):
-        weights.append(whole_weight(gathered, start, rows, count))
-        start += rows * count
-    weights = tuple(weights)
+    stack_attn, stack_text, stack_mlp = gather_weights(
+        [
+            jnp.stack([qk_weight, value_weight, attn_out.T, cross_query, cross_out.T]),
+            jnp.stack([cross_key, cross_value]),
+            jnp.stack([mlp_in, mlp_out.T]),
+        ],
+        1,
+    )
+    weights = (
+        stack_attn[0],
+        stack_attn[1],
+        stack_attn[2],
+        stack_attn[3],
+        stack_text[0],
+        stack_text[1],
+        stack_attn[4],
+        stack_mlp[0],
+        stack_mlp[1],
+    )
 
     labels_all = lax.all_gather(labels, "dp", axis=0, tiled=True)
     sample_count = labels_all.shape[0]
@@ -768,31 +1624,20 @@
     )
 
     bank_rows = kernel_bank.reshape(kernel_bank.shape[0], 9 * slab, width_out)
-    kernel = jnp.einsum(
-        "bk,kro->bro",
-        select_all,
-        bank_rows.astype(float32),
-        precision=lax.Precision.HIGHEST,
-    ).astype(bfloat16)
-    kernel_wide = kernel.astype(float32)
-    squares = jnp.sum(
-        (kernel_wide * kernel_wide).reshape(sample_count, 9, slab, width_out), axis=1
-    )
-    scales_two = scales_slab * scales_slab
-    sums_part = jnp.sum(scales_two[:, :, None] * squares, axis=1)
-
-    def convolve(slabs):
-        columns = patches_of(slabs, SIDE)
-        return columns, einsum_low("bpr,bro->bpo", columns, kernel)
+    mix = mix_matrix(select_all)
+    scales_two = jnp.broadcast_to(
+        (scales_slab * scales_slab)[:, :, None], (sample_count, slab, 128)
+    )
+    kernel, sums_part = mix_kernels(mix, bank_rows, scales_two)
+    place = placing(SIDE // 2)
 
     input_own = own_whole(layer_input, mp).astype(float32)
     scales_pair = lax.dynamic_slice_in_dim(scales_all, 2 * dp, 2, 0)
     input_pair = lax.all_gather(layer_input, "mp", axis=2, tiled=True).astype(float32)
     slabs_x = to_slabs((input_pair * scales_pair[:, None, :]).astype(bfloat16))
-    columns_x, conv_part_x = convolve(slabs_x)
-    partial = jnp.concatenate([conv_part_x, sums_part[:, None, :]], axis=1).astype(bfloat16)
-    summed = own_whole(sum_dp(partial), mp).astype(float32)
-    conv_out, sums = summed[:-1], summed[-1]
+    partial = convolve(slabs_x, place, kernel, sums_part, True)
+    summed = sum_samples(partial, 4).astype(float32)
+    conv_out, sums = summed[:PIXELS], summed[PIXELS]
 
     (hidden_four, picture), pull = jax.vjp(
         lambda value: layer_forward(value, sums, text_rows, small, weights, noise), conv_out
@@ -800,16 +1645,9 @@
 
     dir_own = pick(penalty_dir, mp).astype(float32)
     grad_conv = pull((jnp.zeros_like(hidden_four), dir_own))[0]
-    grads_all = gather_dp(both_half(grad_conv.astype(bfloat16), mp))
-
-    def pull_columns(cotans):
-        return einsum_low("bpo,bro->bpr", cotans, kernel)
-
-    fold = jax.linear_transpose(
-        lambda slabs: patches_of(slabs, SIDE),
-        jax.ShapeDtypeStruct((sample_count, half_px, slab), float32),
-    )
-    grad_moduled = from_slabs(fold(pull_columns(grads_all))[0], mp)
+    grads_all = gather_dp(both_half(grad_conv.astype(bfloat16), mp), 2)
+
+    grad_moduled = from_slabs(conv_back(grads_all, place, kernel, half_px, slab), mp)
     mask_own = pick(penalty_mask, mp).astype(float32)
     tangent = penalty_weight * mask_own * grad_moduled.astype(bfloat16).astype(float32) * scales
 
@@ -819,8 +1657,7 @@
         [jnp.where(mp == 0, tan_moduled, tan_other), jnp.where(mp == 0, tan_other, tan_moduled)]
     )
     slabs_t = to_slabs(tan_pair)
-    columns_t, conv_part_t = convolve(slabs_t)
-    conv_tan = own_whole(sum_dp(conv_part_t.astype(bfloat16)), mp).astype(float32)
+    conv_tan = sum_samples(convolve(slabs_t, place, kernel, sums_part, False), 5).astype(float32)
 
     (ignored_out, ignored_pic, ignored_tan), pull_joint = jax.vjp(
         lambda *given: layer_joint(*given, noise),
@@ -836,48 +1673,38 @@
         (cot_own, pick(cot_rgb, mp).astype(float32), dir_own)
     )
 
-    spreads = [
-        spread_weight(grad, rows, count)
-        for grad, rows, count in zip(grad_weights, rows_of, counts)
-    ]
-    mlp_sum = sum_all(jnp.concatenate(spreads[7:], axis=2))
-    rest_sum = sum_all(jnp.concatenate(spreads[:7], axis=2))
-    weight_sums = jnp.concatenate([rest_sum, mlp_sum], axis=0).astype(float32)
-    big_sums = []
-    start = 0
-    for rows, count, flip in zip(rows_of, counts, flips):
-        big_sums.append(unpack_shard(weight_sums[start : start + rows * count], rows, flip))
-        start += rows * count
-
-    wide = jnp.concatenate([grad_main, grad_side, grad_sums[None]], axis=0).astype(bfloat16)
-    wide_all = gather_dp(both_half(wide, mp))
-    pixels = SIDE * SIDE
-    both_cot = wide_all[:, : 2 * pixels]
-    sums_cot = wide_all[:, 2 * pixels].astype(float32)
-    both_columns = jnp.concatenate([columns_x, columns_t], axis=1)
-    grad_kernel = einsum_low("bpr,bpo->bro", both_columns, both_cot)
-    scales_rows = jnp.tile(scales_two, (1, 9))
-    grad_kernel = grad_kernel + 2.0 * kernel_wide * scales_rows[:, :, None] * sums_cot[:, None, :]
-    grad_kernel = grad_kernel.astype(bfloat16)
-    grad_scales_slab = (
-        2.0 * scales_slab * jnp.sum(squares * sums_cot[:, None, :], axis=2)
-    )
-    bank_grad = jnp.einsum(
-        "bk,bro->kro",
-        select_all,
-        grad_kernel.astype(float32),
-        precision=lax.Precision.HIGHEST,
-    ).reshape(kernel_bank.shape)
+    orders = ("xy", "yx", "xy", "yx", "xy", "yx", "yx", "xy", "xy")
+    d_qk, d_value, d_attn, d_query, d_key, d_cval, d_cout, d_mlp, d_mout = grad_weights
+    mlp_grad, mout_grad, qk_grad, value_grad, attn_grad, query_grad, cout_grad, key_grad, cval_grad = (
+        sum_weights(
+            [d_mlp, d_mout, d_qk, d_value, d_attn, d_query, d_cout, d_key, d_cval], orders, 6
+        )
+    )
+    big_sums = (
+        qk_grad,
+        value_grad,
+        attn_grad.T,
+        query_grad,
+        key_grad,
+        cval_grad,
+        cout_grad.T,
+        mlp_grad,
+        mout_grad.T,
+    )
+
+    lines = jnp.broadcast_to(grad_sums[None], (CHUNK,) + grad_sums.shape)
+    wide = jnp.concatenate(
+        [grad_main.astype(bfloat16), grad_side.astype(bfloat16), lines.astype(bfloat16)], axis=0
+    )
+    wide_all = gather_dp(both_half(wide, mp), 3)
+    grad_kernel, both_back, scale_sums = conv_second(
+        slabs_x, slabs_t, place, kernel, wide_all, scales_two
+    )
+    grad_scales_slab = 2.0 * scales_slab * scale_sums[:, :, 0]
+    bank_grad, select_products = unmix_kernels(mix, bank_rows, grad_kernel)
+    bank_grad = bank_grad.reshape(kernel_bank.shape)
     grad_select = jnp.einsum(
-        "bro,kro->bk", grad_kernel, bank_rows, preferred_element_type=float32
-    )
-    back_columns = pull_columns(both_cot)
-    both_back = jnp.concatenate(
-        [
-            fold(back_columns[:, :pixels])[0],
-            fold(back_columns[:, pixels:])[0],
-        ],
-        axis=1,
+        "brkr->bk", select_products.reshape(sample_count, CHUNK, -1, CHUNK)
     )
     both_back = from_slabs(both_back, mp).astype(bfloat16).astype(float32)
     back_main, back_side = both_back[:half_px], both_back[half_px:]
@@ -936,7 +1763,7 @@
         sums_all[3 * channels : 4 * channels],
         sums_all[4 * channels :],
         bank_grad,
-    ) + tuple(big_sums)
+    ) + big_sums
 
 
 def solution(mesh):

time: 2050 us -> 1410 us (0.69)
  Pallas kernels: 0 us -> 793 us
  local copies, waits for them, and re-layouts: 717 us -> 155 us
  waiting for transfers between devices: 401 us -> 29.4 us
  matrix products: 446 us -> 244 us
  other arithmetic: 265 us -> 80.6 us
  starting transfers between devices: 122 us -> 47.3 us
  blocking collectives: 62.1 us -> 32.6 us
    pallas_call x0 -> x12, Pallas kernels: none -> 793 us  [the longest x3 281 us: gather_call(): pl.pallas_call(body, in_specs=[pl.BlockSpec(memory_space=pl.ANY)] * count...]
    ppermute x50 -> x0, waiting for transfers between devices: 270 us -> none  [the longest x14 190 us: halve(): return kept + lax.ppermute(sent, axis_name, pairs)]
    dot_general x14 -> x9, matrix products: 186 us -> 11.9 us  [einsum_low(): jnp.einsum(form, left.astype(jnp.bfloat16), right.astype(jnp.bfloat16), p...]
    slice x26 -> x1, local copies, waits for them, and re-layouts: 166 us -> 0.34 us  [sample_parallel(): grad_scales_slab = 2.0 * scales_slab * scale_sums[:, :, 0]]
    reshape x21 -> x2, local copies, waits for them, and re-layouts: 141 us -> 3.09 us  [the longest x1 1.91 us: sample_parallel(): select_products.reshape(sample_count, CHUNK, -1, CHUNK)]
    ppermute x50 -> x0, starting transfers between devices: 89.4 us -> none  [the longest x18 42.1 us: line_sum(): up = lax.ppermute(send_up, 'dp', up_pairs)]
    split x3 -> x0, local copies, waits for them, and re-layouts: 83.7 us -> none  [patches_of(): jnp.concatenate(pieces, axis=-1)]
    all_gather x3 -> x0, waiting for transfers between devices: 79.7 us -> none  [the longest x2 79.6 us: gather_dp(): return lax.all_gather(values, 'dp', axis=0, tiled=True)]
  transfers between devices with their start and end apart: 69 -> 16, of which waited for: 32 -> 6; matrix products, arithmetic and copies ran while one was open for 38% -> 18% of each run, Pallas kernels for 0% -> 37%
where the time goes in v2:
time: 1410 us; the launch traced here: 1400 us
  Pallas kernels  793 us (56%)
  matrix products  244 us (17%)
  local copies, waits for them, and re-layouts  155 us (11%)
  other arithmetic  80.6 us (6%)
  starting transfers between devices  47.3 us (3%)
  blocking collectives  32.6 us (2%)
  waiting for transfers between devices  29.4 us (2%)
  between operations  20 us (1%)
    pallas_call x3, Pallas kernels, gather_call(): pl.pallas_call(body, in_specs=[pl.BlockSpec(memory_space=pl.ANY)] * count...  281 us
    pallas_call x1, Pallas kernels, sum_weights(): pl.pallas_call(lambda *refs: sum_weights_body(parts, count, refs), in_spe...  179 us
    pallas_call x2, Pallas kernels, sum_samples(): pl.pallas_call(lambda *refs: sum_body(cut, *refs), in_specs=[pl.BlockSpec...  152 us
    dot_general x22, matrix products, dot_wide(): lax.dot_general(left.astype(jnp.bfloat16), right.astype(jnp.bfloat16), ((...  67.6 us
    pallas_call x1, Pallas kernels, conv_second(): pl.pallas_call(second_body, grid=(samples,), in_specs=[pl.BlockSpec((1, p...  62.8 us
    pallas_call x2, Pallas kernels, convolve(): pl.pallas_call(lambda *refs: conv_body(extra, *refs), grid=(samples,), in...  57.2 us
    unnamed x568, local copies, waits for them, and re-layouts  55 us
    pallas_call x1, Pallas kernels, conv_back(): pl.pallas_call(back_body, grid=(samples,), in_specs=[pl.BlockSpec((1, row...  30.6 us
  transfers between devices with their start and end apart: 16, of which 6 were waited for; matrix products, arithmetic and copies ran while one was open for 18% of the time, Pallas kernels for 37%

profile of v2, /device:TPU:9, one launch (start us, length us, event | category | flops | bytes accessed | tf_op | source)
XLA Modules:
  0.0 1402.2 jit_solution(9561113231913441176)
XLA Ops:
  10.1 8.7 all-reduce
  18.9 4.7 all_gather.15
  28.9 9.4 all-to-all-start
  43.4 3.2 mul.1258.refs_0_
  59.2 126.8 %gather_weights.1 = (bf16[5,1024,1024]{2,1,0:T(8,128)(2,1)}, bf16[2,768,1024]{2,1,0:T(8,128)(2,1)}, bf16[2,1024,4096]{2,1,0:T(8,128)(2,1)}) custom-call(bf16[5,64,512]{2,1,0:T(8,128)(2,1)} %copy-done.153, bf16[2,48,512]{2,1,0:T(8,128)(2,1)} %pad_maximum_fusion.31.refs_1_, bf16[2,64,2048]{2,1,0:T(8,128)(2,1)} %pad_maximum_fusion.27.refs_2_), custom_call_target="tpu_custom_call" | custom-call | tf_op jit(solution)/shard_map/gather_weights/pallas_call | solution.py:1084
  185.9 7.7 slice_bitcast_fusion.6
  193.6 3.9 copy.195
  197.6 4.0 copy.194
  201.5 3.9 copy.199
  205.5 3.3 slice_bitcast_fusion.3
  214.5 3.9 copy.202
  218.5 3.9 copy.204
  228.3 13.5 mix_kernels.1
  245.9 28.7 %conv_forward.2 = bf16[32,272,512]{2,1,0:T(8,128)(2,1)S(1)} custom-call(bf16[32,64,64]{2,1,0:T(8,128)(2,1)S(1)} %bitcast.497, bf16[288,192]{1,0:T(8,128)(2,1)S(1)} %copy-done.10, bf16[32,576,512]{2,1,0:T(8,128)(2,1)} %get-tuple-element.40.refs_2_.kernel_ref, f32[32,512]{1,0:T(8,128)S(1)} %get-tuple-element.41.refs_3_), custom_call_target="tpu_custom_call" | custom-call | tf_op jit(solution)/shard_map/conv_forward/pallas_call | solution.py:689
  274.6 75.3 %sum_samples.2 = bf16[272,1024]{1,0:T(8,128)(2,1)S(1)} custom-call(bf16[4,2,2,2,272,512]{5,4,3,2,1,0:T(8,128)(2,1)S(1)} %bitcast.493), custom_call_target="tpu_custom_call" | custom-call | tf_op jit(solution)/shard_map/sum_samples/pallas_call | solution.py:1303
  357.1 5.4 copy.197
  384.3 8.0 fusion.15
  392.3 12.5 multiply_reduce_fusion.29
  408.4 4.2 multiply_reduce_fusion.28
  412.6 3.2 convolution_convert_fusion.12
  439.4 54.1 %gather_samples.2.cotan_ref = bf16[32,256,512]{2,1,0:T(8,128)(2,1)} custom-call(bf16[2,256,512]{2,1,0:T(8,128)(2,1)} %pad_maximum_fusion.28.refs_0_), custom_call_target="tpu_custom_call" | custom-call | tf_op jit(solution)/shard_map/gather_samples/pallas_call | solution.py:1084
  493.5 3.4 copy-done.3
  496.9 30.6 %conv_back.1 = bf16[32,64,64]{2,1,0:T(8,128)(2,1)S(1)} custom-call(bf16[32,256,512]{2,1,0:T(8,128)(2,1)S(1)} %copy-done.3, bf16[288,192]{1,0:T(8,128)(2,1)S(1)} %copy-done.10, bf16[32,576,512]{2,1,0:T(8,128)(2,1)} %get-tuple-element.40.refs_2_.kernel_ref), custom_call_target="tpu_custom_call" | custom-call | tf_op jit(solution)/shard_map/conv_back/pallas_call | solution.py:729
  528.6 11.3 all-to-all-start.1
  541.3 19.2 %all-gather = s32[16,2,64]{2,1,0:T(2,128)S(1)} all-gather(s32[1,2,64]{2,1,0:T(2,128)S(1)} %bitcast.587), channel_id=1, replica_groups=mesh['dp'=16,'mp'=2] {'dp'}, dimensions={0}, use_global_device_ids=true | all-gather | bytes 8704 | tf_op jit(solution)/shard_map/all_gather | solution.py:1746
  565.7 6.0 collective-permute-done.3
  574.6 4.3 collective-permute-done.4
  584.5 8.2 all-to-all-start.2
  592.7 11.6 fusion.3
  604.7 28.5 %conv_forward.3 = bf16[32,256,512]{2,1,0:T(8,128)(2,1)S(1)} custom-call(bf16[32,64,64]{2,1,0:T(8,128)(2,1)S(1)} %bitcast.499, bf16[288,192]{1,0:T(8,128)(2,1)S(1)} %copy-done.10, bf16[32,576,512]{2,1,0:T(8,128)(2,1)} %get-tuple-element.40.refs_2_.kernel_ref, f32[32,512]{1,0:T(8,128)S(1)} %get-tuple-element.41.refs_3_), custom_call_target="tpu_custom_call" | custom-call | tf_op jit(solution)/shard_map/conv_forward/pallas_call | solution.py:689
  633.2 76.9 %sum_samples.3 = bf16[256,1024]{1,0:T(8,128)(2,1)S(1)} custom-call(bf16[4,2,2,2,256,512]{5,4,3,2,1,0:T(8,128)(2,1)S(1)} %bitcast.494), custom_call_target="tpu_custom_call" | custom-call | tf_op jit(solution)/shard_map/sum_samples/pallas_call | solution.py:1303
  717.5 5.5 copy.211
  723.0 5.7 fusion.294
  745.5 14.7 %add_convert_fusion.2 = (bf16[256,4096]{1,0:T(8,128)(2,1)S(1)}, bf16[256,4096]{1,0:T(8,128)(2,1)S(1)}, bf16[256,4096]{1,0:T(8,128)(2,1)}, bf16[256,4096]{1,0:T(8,128)(2,1)}) fusion(f32[256,4096]{1,0:T(8,128)S(1)} %copy-done.260, f32[512,4096]{1,0:T(8,128)} %fusion.3, bf16[256,1024]{1,0:T(8,128)(2,1)S(1)} %add_convert_fusion.5, ...), kind=kOutput, calls=%fused_computation.58 | convolution fusion | flops 2205155328 | bytes 29884416 | tf_op jit(solution)/shard_map/jvp()/dot_general | solution.py:395
  761.6 7.2 fusion.9
  772.6 3.2 fusion.88
  788.0 3.2 fusion.53
  793.9 3.2 fusion.85
  809.1 3.4 fusion.134
  816.2 6.1 multiply_reduce_fusion.4
  822.3 6.3 multiply_add_fusion
  828.6 5.3 copy.225
  834.0 5.4 copy.229
  839.3 9.1 multiply_reduce_fusion
  848.5 5.3 copy.226
  853.8 4.2 fusion.34
  859.7 5.4 copy.230
  883.3 3.3 fusion.125
  886.6 7.4 collective-permute-done.6
  895.4 99.9 %gather_samples.3.cotan_ref = bf16[32,528,512]{2,1,0:T(8,128)(2,1)} custom-call(bf16[2,528,512]{2,1,0:T(8,128)(2,1)} %pad_maximum_fusion.4.refs_0_), custom_call_target="tpu_custom_call" | custom-call | tf_op jit(solution)/shard_map/gather_samples/pallas_call | solution.py:1084
  995.3 5.9 copy-done.2
  1001.2 62.8 %conv_second.1 = (bf16[32,576,512]{2,1,0:T(8,128)(2,1)}, bf16[32,128,64]{2,1,0:T(8,128)(2,1)S(1)}, f32[32,64,128]{2,1,0:T(8,128)S(1)}) custom-call(bf16[32,64,64]{2,1,0:T(8,128)(2,1)S(1)} %bitcast.498, bf16[32,64,64]{2,1,0:T(8,128)(2,1)S(1)} %bitcast.500, bf16[288,192]{1,0:T(8,128)(2,1)S(1)} %copy-done.10, ...), custom_call_target="tpu_custom_call" | custom-call | tf_op jit(solution)/shard_map/conv_second/pallas_call | solution.py:797
  1066.2 9.7 all-to-all-start.3
  1076.0 6.7 fusion.122
  1087.2 17.5 %unmix_kernels.1 = (f32[8,576,512]{2,1,0:T(8,128)}, f32[512,128]{1,0:T(8,128)S(1)}) custom-call(bf16[512,256]{1,0:T(8,128)(2,1)S(1)} %copy-done.12, bf16[8,576,512]{2,1,0:T(8,128)(2,1)S(1)} %bitcast.496, bf16[32,576,512]{2,1,0:T(8,128)(2,1)} %get-tuple-element.47.refs_2_), custom_call_target="tpu_custom_call" | custom-call | tf_op jit(solution)/shard_map/unmix_kernels/pallas_call | solution.py:849
  1111.6 5.6 collective-permute-done.7
  1124.7 4.0 convolution_convert_fusion.2.refs_6_
  1147.6 7.0 convolution_convert_fusion.refs_1_
  1154.7 6.8 convolution_convert_fusion.1.refs_0_
  1167.7 178.9 %sum_weights.1 = (f32[64,2048]{1,0:T(8,128)}, f32[64,2048]{1,0:T(8,128)}, f32[64,512]{1,0:T(8,128)}, f32[64,512]{1,0:T(8,128)}, f32[64,512]{1,0:T(8,128)}, /*ind...) custom-call(bf16[1024,4096]{1,0:T(8,128)(2,1)} %convolution_convert_fusion.1.refs_0_, ...), custom_call_target="tpu_custom_call" | custom-call | tf_op jit(solution)/shard_map/sum_weights/pallas_call | solution.py:1526
  1351.0 4.2 collective-permute-done.8
  1374.8 3.2 fusion.197
  1377.9 3.2 fusion.204
  1381.2 7.6 fusion.17
  (812 shorter events, 266.8 us)
Async XLA Ops:
  7.2 215.2 %copy-start = (bf16[1000,768]{1,0:T(8,128)(2,1)S(1)}, bf16[1000,768]{1,0:T(8,128)(2,1)}, u32[]{:S(2)}) copy-start(bf16[1000,768]{1,0:T(8,128)(2,1)} %param.33) | copy-start | bytes 4608004
  7.2 31.1 %copy-start.110 = (bf16[2,256,512]{2,1,0:T(8,128)(2,1)S(1)}, bf16[2,256,512]{2,1,0:T(8,128)(2,1)}, u32[]{:S(2)}) copy-start(bf16[2,256,512]{2,1,0:T(8,128)(2,1)} %param.50) | copy-start | bytes 1572868
  25.1 187.9 %copy-start.79 = (f32[32,512]{1,0:T(8,128)}, f32[32,512]{1,0:T(8,128)S(1)}, u32[]{:S(2)}) copy-start(f32[32,512]{1,0:T(8,128)S(1)} %fusion.196) | copy-start | bytes 196612
  27.3 23.2 %copy-start.252 = (bf16[1024]{0:T(1024)(128)(2,1)S(1)}, bf16[1024]{0:T(1024)(128)(2,1)}, u32[]{:S(2)}) copy-start(bf16[1024]{0:T(1024)(128)(2,1)} %param.38) | copy-start | bytes 6148
  27.3 25.1 %copy-start.197 = (bf16[64,512]{1,0:T(8,128)(2,1)S(1)}, bf16[64,512]{1,0:T(8,128)(2,1)}, u32[]{:S(2)}) copy-start(bf16[64,512]{1,0:T(8,128)(2,1)} %param.41) | copy-start | bytes 196612
  27.7 28.1 %copy-start.166 = (bf16[2048,64]{0,1:T(8,128)(2,1)S(1)}, bf16[2048,64]{0,1:T(8,128)(2,1)}, u32[]{:S(2)}) copy-start(bf16[2048,64]{0,1:T(8,128)(2,1)} %param.49) | copy-start | bytes 786436
  27.8 29.9 %copy-start.202 = (bf16[48,512]{1,0:T(8,128)(2,1)S(1)}, bf16[48,512]{1,0:T(8,128)(2,1)}, u32[]{:S(2)}) copy-start(bf16[48,512]{1,0:T(8,128)(2,1)} %param.46) | copy-start | bytes 147460
  28.9 215.5 %all-to-all-start = ((bf16[16,2,4096]{2,1,0:T(2,128)(2,1)}), bf16[16,2,4096]{2,1,0:T(2,128)(2,1)}, u32[]{:S(2)}, u32[]{:S(2)}) async-start(bf16[16,2,4096]{2,1,0:T(2,128)(2,1)} %reshape.565), calls=%async_computation | async-start | bytes 524288 | tf_op jit(solution)/shard_map/all_to_all | solution.py:900
  39.1 525.7 %collective-permute-start.5 = (bf16[256,512]{1,0:T(8,128)(2,1)}, bf16[256,512]{1,0:T(8,128)(2,1)}, u32[]{:S(2)}, u32[]{:S(2)}) collective-permute-start(bf16[256,512]{1,0:T(8,128)(2,1)} %dynamic-slice_bitcast_fusion.1), channel_id=1, source_target_pairs={{0,1},{1,0},{2,3},{3,2},{4,5},{5,4},{6,7},{7,6},{8,9},{9,8},{10,11... | collective-permute-start | bytes 786440 | tf_op jit(solution)/shard_map/ppermute | solution.py:874
  46.6 179.0 %copy-start.11 = (bf16[512,256]{1,0:T(8,128)(2,1)}, bf16[512,256]{1,0:T(8,128)(2,1)S(1)}, u32[]{:S(2)}) copy-start(bf16[512,256]{1,0:T(8,128)(2,1)S(1)} %mul.1258.refs_0_) | copy-start | bytes 786436
  214.5 27.2 %copy-start.219 = (bf16[1,3,256]{2,0,1:T(2,128)(2,1)}, bf16[1,3,256]{2,0,1:T(2,128)(2,1)S(1)}, u32[]{:S(2)}) copy-start(bf16[1,3,256]{2,0,1:T(2,128)(2,1)S(1)} %constant_dynamic-slice_fusion.7) | copy-start | bytes 4612
  222.8 20.7 %copy-start.81 = (bf16[64,768]{1,0:T(8,128)(2,1)}, bf16[64,768]{1,0:T(8,128)(2,1)S(1)}, u32[]{:S(2)}) copy-start(bf16[64,768]{1,0:T(8,128)(2,1)S(1)} %convolution_convert_fusion.27) | copy-start | bytes 294916
  244.4 163.9 %copy-start.59 = (bf16[64,16,64]{2,0,1:T(8,128)(2,1)}, bf16[64,16,64]{2,0,1:T(8,128)(2,1)S(1)}, u32[]{:S(2)}) copy-start(bf16[64,16,64]{2,0,1:T(8,128)(2,1)S(1)} %convolution_convert_fusion.26) | copy-start | bytes 393220
  245.9 28.7 %copy-start.8 = (bf16[16,2,64,64]{3,2,1,0:T(8,128)(2,1)}, bf16[16,2,64,64]{3,2,1,0:T(8,128)(2,1)S(1)}, u32[]{:S(2)}) copy-start(bf16[16,2,64,64]{3,2,1,0:T(8,128)(2,1)S(1)} %reshape.566) | copy-start | bytes 786436
  274.6 75.5 %copy-start.184 = (f32[1024]{0:T(1024)S(1)}, f32[1024]{0:T(1024)}, u32[]{:S(2)}) copy-start(f32[1024]{0:T(1024)} %convert_element_type.542) | copy-start | bytes 12292
  274.6 75.5 %copy-start.187 = (f32[1024]{0:T(1024)S(1)}, f32[1024]{0:T(1024)}, u32[]{:S(2)}) copy-start(f32[1024]{0:T(1024)} %convert_element_type.544) | copy-start | bytes 12292
  274.6 75.5 %copy-start.214 = (f32[256]{0:T(256)S(1)}, f32[256]{0:T(256)}, u32[]{:S(2)}) copy-start(f32[256]{0:T(256)} %fusion.248) | copy-start | bytes 3076
  350.1 82.1 %copy-start.190 = (f32[1,1024]{1,0:T(1,128)}, f32[1,1024]{1,0:T(1,128)S(1)}, u32[]{:S(2)}) copy-start(f32[1,1024]{1,0:T(1,128)S(1)} %fusion.251) | copy-start | bytes 12292
  350.7 80.9 %copy-start.223 = (f32[256]{0:T(256)}, f32[256]{0:T(256)S(1)}, u32[]{:S(2)}) copy-start(f32[256]{0:T(256)S(1)} %get-tuple-element.198) | copy-start | bytes 3076
  350.7 81.5 %copy-start.206 = (f32[256]{0:T(256)}, f32[256]{0:T(256)S(1)}, u32[]{:S(2)}) copy-start(f32[256]{0:T(256)S(1)} %fusion.252) | copy-start | bytes 3076
  352.9 72.9 %copy-start.34 = (bf16[256,16,64]{0,2,1:T(8,128)(2,1)}, bf16[256,16,64]{0,2,1:T(8,128)(2,1)S(1)}, u32[]{:S(2)}) copy-start(bf16[256,16,64]{0,2,1:T(8,128)(2,1)S(1)} %get-tuple-element.261) | copy-start | bytes 1572868
  357.1 66.7 %copy-start.107 = (f32[16,256]{1,0:T(8,128)}, f32[16,256]{1,0:T(8,128)S(1)}, u32[]{:S(2)}) copy-start(f32[16,256]{1,0:T(8,128)S(1)} %get-tuple-element.196) | copy-start | bytes 49156
  372.4 46.1 %copy-start.241 = (f32[256]{0:T(256)}, f32[256]{0:T(256)S(1)}, u32[]{:S(2)}) copy-start(f32[256]{0:T(256)S(1)} %get-tuple-element.264) | copy-start | bytes 3076
  372.4 46.7 %copy-start.22 = (f32[256,1024]{1,0:T(8,128)}, f32[256,1024]{1,0:T(8,128)S(1)}, u32[]{:S(2)}) copy-start(f32[256,1024]{1,0:T(8,128)S(1)} %get-tuple-element.265) | copy-start | bytes 3145732
  372.4 46.7 %copy-start.209 = (f32[256]{0:T(256)}, f32[256]{0:T(256)S(1)}, u32[]{:S(2)}) copy-start(f32[256]{0:T(256)S(1)} %fusion.253) | copy-start | bytes 3076
  378.0 34.6 %copy-start.162 = (f32[16,256]{1,0:T(8,128)}, f32[16,256]{1,0:T(8,128)S(1)}, u32[]{:S(2)}) copy-start(f32[16,256]{1,0:T(8,128)S(1)} %get-tuple-element.266) | copy-start | bytes 49156
  378.0 42.6 %copy-start.157 = (f32[16,256]{1,0:T(8,128)}, f32[16,256]{1,0:T(8,128)S(1)}, u32[]{:S(2)}) copy-start(f32[16,256]{1,0:T(8,128)S(1)} %multiply_divide_fusion) | copy-start | bytes 49156
  378.1 30.3 %copy-start.154 = (f32[16,256]{1,0:T(8,128)}, f32[16,256]{1,0:T(8,128)S(1)}, u32[]{:S(2)}) copy-start(f32[16,256]{1,0:T(8,128)S(1)} %multiply_divide_fusion.1) | copy-start | bytes 49156
  383.2 21.6 %copy-start.243 = (f32[256]{0:T(256)}, f32[256]{0:T(256)S(1)}, u32[]{:S(2)}) copy-start(f32[256]{0:T(256)S(1)} %get-tuple-element.268) | copy-start | bytes 3076
  383.2 22.1 %copy-start.212 = (f32[256]{0:T(256)}, f32[256]{0:T(256)S(1)}, u32[]{:S(2)}) copy-start(f32[256]{0:T(256)S(1)} %fusion.254) | copy-start | bytes 3076
  433.1 5.3 collective-permute-start.2
  434.6 128.0 %collective-permute-start.9 = (bf16[64,512]{0,1:T(8,128)(2,1)}, bf16[64,512]{0,1:T(8,128)(2,1)S(1)}, u32[]{:S(2)}, u32[]{:S(2)}) collective-permute-start(bf16[64,512]{0,1:T(8,128)(2,1)} %bitcast.125), channel_id=1, source_target_pairs={{0,1},{1,0},{2,3},{3,2},{4,5},{5,4},{6,7},{7,6},{8,9},{9,8},{10,11... | collective-permute-start | bytes 196616 | tf_op jit(solution)/shard_map/ppermute | solution.py:874
  496.9 43.0 %copy-start.250 = (bf16[2,3,256]{2,0,1:T(2,128)(2,1)S(1)}, bf16[2,3,256]{2,0,1:T(2,128)(2,1)}, u32[]{:S(2)}) copy-start(bf16[2,3,256]{2,0,1:T(2,128)(2,1)} %param.51) | copy-start | bytes 9220
  496.9 43.0 %copy-start.256 = (s32[2]{0:T(128)S(1)}, s32[2]{0:T(128)}, u32[]{:S(2)}) copy-start(s32[2]{0:T(128)} %param.31) | copy-start | bytes 28
  496.9 44.4 %copy-start.254 = (s32[2,64]{1,0:T(2,128)S(1)}, s32[2,64]{1,0:T(2,128)}, u32[]{:S(2)}) copy-start(s32[2,64]{1,0:T(2,128)} %param.29) | copy-start | bytes 1540
  527.5 37.2 %copy-start.111 = (bf16[2,256,512]{2,1,0:T(8,128)(2,1)S(1)}, bf16[2,256,512]{2,1,0:T(8,128)(2,1)}, u32[]{:S(2)}) copy-start(bf16[2,256,512]{2,1,0:T(8,128)(2,1)} %param.50) | copy-start | bytes 1572868
  527.5 45.2 %copy-start.174 = (bf16[3,1024]{1,0:T(4,128)(2,1)S(1)}, bf16[3,1024]{1,0:T(4,128)(2,1)}, u32[]{:S(2)}) copy-start(bf16[3,1024]{1,0:T(4,128)(2,1)} %param.37) | copy-start | bytes 18436
  527.5 45.2 %copy-start.182 = (f32[1,1024]{1,0:T(1,128)S(1)}, f32[1,1024]{1,0:T(1,128)}, u32[]{:S(2)}) copy-start(f32[1,1024]{1,0:T(1,128)} %copy-done.181) | copy-start | bytes 12292
  528.6 34.7 %all-to-all-start.1 = ((bf16[16,2,4096]{2,1,0:T(2,128)(2,1)}), bf16[16,2,4096]{2,1,0:T(2,128)(2,1)S(1)}, u32[]{:S(2)}, u32[]{:S(2)}) async-start(bf16[16,2,4096]{2,1,0:T(2,128)(2,1)} %reshape.567), calls=%async_computation.1 | async-start | bytes 524288 | tf_op jit(solution)/shard_map/all_to_all | solution.py:908
  540.0 41.4 %copy-start.221 = (bf16[1,3,256]{2,0,1:T(2,128)(2,1)}, bf16[1,3,256]{2,0,1:T(2,128)(2,1)S(1)}, u32[]{:S(2)}) copy-start(bf16[1,3,256]{2,0,1:T(2,128)(2,1)S(1)} %constant_dynamic-slice_fusion.4) | copy-start | bytes 4612
  564.0 7.8 collective-permute-start.3
  565.7 38.6 %copy-start.83 = (bf16[256,512]{1,0:T(8,128)(2,1)}, bf16[256,512]{1,0:T(8,128)(2,1)S(1)}, u32[]{:S(2)}) copy-start(bf16[256,512]{1,0:T(8,128)(2,1)S(1)} %get-tuple-element.233) | copy-start | bytes 786436
  565.7 38.6 %copy-start.85 = (bf16[256,512]{1,0:T(8,128)(2,1)}, bf16[256,512]{1,0:T(8,128)(2,1)S(1)}, u32[]{:S(2)}) copy-start(bf16[256,512]{1,0:T(8,128)(2,1)S(1)} %get-tuple-element.234) | copy-start | bytes 786436
  572.0 6.9 collective-permute-start.4
  584.5 19.8 %all-to-all-start.2 = ((bf16[16,2,4096]{2,1,0:T(2,128)(2,1)}), bf16[16,2,4096]{2,1,0:T(2,128)(2,1)S(1)}, u32[]{:S(2)}, u32[]{:S(2)}) async-start(bf16[16,2,4096]{2,1,0:T(2,128)(2,1)} %reshape.569), calls=%async_computation.2 | async-start | bytes 524288 | tf_op jit(solution)/shard_map/all_to_all | solution.py:900
  633.2 77.0 %copy-start.32 = (f32[272,1024]{1,0:T(8,128)S(1)}, f32[272,1024]{1,0:T(8,128)}, u32[]{:S(2)}) copy-start(f32[272,1024]{1,0:T(8,128)} %copy-done.30) | copy-start | bytes 3342340
  633.2 77.0 %copy-start.185 = (f32[1024]{0:T(1024)S(1)}, f32[1024]{0:T(1024)}, u32[]{:S(2)}) copy-start(f32[1024]{0:T(1024)} %convert_element_type.542) | copy-start | bytes 12292
  633.2 77.0 %copy-start.188 = (f32[1024]{0:T(1024)S(1)}, f32[1024]{0:T(1024)}, u32[]{:S(2)}) copy-start(f32[1024]{0:T(1024)} %convert_element_type.544) | copy-start | bytes 12292
  633.2 77.0 %copy-start.191 = (f32[1,1024]{1,0:T(1,128)S(1)}, f32[1,1024]{1,0:T(1,128)}, u32[]{:S(2)}) copy-start(f32[1,1024]{1,0:T(1,128)} %copy-done.190) | copy-start | bytes 12292
  633.2 77.0 %copy-start.215 = (f32[256]{0:T(256)S(1)}, f32[256]{0:T(256)}, u32[]{:S(2)}) copy-start(f32[256]{0:T(256)} %fusion.248) | copy-start | bytes 3076
  633.2 77.8 %copy-start.236 = (f32[256]{0:T(256)S(1)}, f32[256]{0:T(256)}, u32[]{:S(2)}) copy-start(f32[256]{0:T(256)} %get-tuple-element.189) | copy-start | bytes 3076
  633.2 77.8 %copy-start.207 = (f32[256]{0:T(256)S(1)}, f32[256]{0:T(256)}, u32[]{:S(2)}) copy-start(f32[256]{0:T(256)} %copy-done.206) | copy-start | bytes 3076
  745.2 24.3 %copy-start.48 = (f32[256,1024]{1,0:T(8,128)}, f32[256,1024]{1,0:T(8,128)S(1)}, u32[]{:S(2)}) copy-start(f32[256,1024]{1,0:T(8,128)S(1)} %get-tuple-element.288) | copy-start | bytes 3145732
  882.5 11.6 collective-permute-start.6
  895.4 99.9 %copy-start.7 = (f32[32,64,128]{2,1,0:T(8,128)S(1)}, f32[32,64,128]{2,1,0:T(8,128)}, u32[]{:S(2)}) copy-start(f32[32,64,128]{2,1,0:T(8,128)} %copy-done.6) | copy-start | bytes 3145732
  895.4 100.0 %copy-start.9 = (bf16[16,2,64,64]{3,2,1,0:T(8,128)(2,1)S(1)}, bf16[16,2,64,64]{3,2,1,0:T(8,128)(2,1)}, u32[]{:S(2)}) copy-start(bf16[16,2,64,64]{3,2,1,0:T(8,128)(2,1)} %copy-done.8) | copy-start | bytes 786436
  1066.2 42.5 %all-to-all-start.3 = ((bf16[16,2,128,64]{2,3,1,0:T(8,128)(2,1)}), bf16[16,2,128,64]{2,3,1,0:T(8,128)(2,1)S(1)}, u32[]{:S(2)}, u32[]{:S(2)}) async-start(bf16[16,2,128,64]{2,3,1,0:T(8,128)(2,1)} %copy.231), calls=%async_computation.3 | async-start | bytes 1048576 | tf_op jit(solution)/shard_map/all_to_all | solution.py:908
  1075.9 280.3 %all-gather.4.cloned.1.call-start = ((), (), s32[]{:S(2)}) async-start(), calls=%async_computation.4 | async-start | bytes 1351680 | tf_op jit(solution)/shard_map/all_gather | solution.py:1726
  1109.5 7.7 collective-permute-start.7
  1121.2 260.0 %all-gather.6.cloned.1.call-start = ((), (), s32[]{:S(2)}) async-start(), calls=%async_computation.5 | async-start | bytes 3244032 | tf_op jit(solution)/shard_map/all_gather | solution.py:1745
  1143.3 204.0 %collective-permute-start = (f32[256,512]{1,0:T(8,128)S(1)}, f32[256,512]{1,0:T(8,128)}, u32[]{:S(2)}, u32[]{:S(2)}) collective-permute-start(f32[256,512]{1,0:T(8,128)S(1)} %constant_dynamic-slice_fusion.9), channel_id=1, source_target_pairs={{0,1},{1,0},{2,3},{3,2},{4,5},{5,4},{6,7},{7,6},{8,9},{9,8},{10,11... | collective-permute-start | bytes 1572872 | tf_op jit(solution)/shard_map/ppermute | solution.py:874
  1164.3 182.4 %collective-permute-start.1 = (f32[3,256]{1,0:T(4,128)S(1)}, f32[3,256]{1,0:T(4,128)S(1)}, u32[]{:S(2)}, u32[]{:S(2)}) collective-permute-start(f32[3,256]{1,0:T(4,128)S(1)} %copy-done.229), channel_id=1, source_target_pairs={{0,1},{1,0},{2,3},{3,2},{4,5},{5,4},{6,7},{7,6},{8,9},{9,8},{10,11... | collective-permute-start | bytes 9224 | tf_op jit(solution)/shard_map/ppermute | solution.py:874
  1167.7 180.7 %copy-start.98 = (f32[64,1024]{0,1:T(8,128)S(1)}, f32[64,1024]{0,1:T(8,128)}, u32[]{:S(2)}) copy-start(f32[64,1024]{0,1:T(8,128)} %get-tuple-element.238) | copy-start | bytes 786436
  1348.5 6.7 collective-permute-start.8
  (221 other events, 1204.4 us)
Sparse Core Ops, SparseCore 0:
  1121.3 55.6 all-gather.3
  1180.5 67.1 all-gather.5

commit v3 on v2

--- a/solution.py
+++ b/solution.py
@@ -446,40 +446,8 @@
 product_flip, product_flip_pair = make_products(True)
 
 
-def make_bilinear(left_ids, right_ids, out_ids):
-    @jax.custom_vjp
-    def form(left, right):
-        return einsum_low(f"{left_ids},{right_ids}->{out_ids}", left, right)
-
-    def form_fwd(left, right):
-        return form(left, right), (left, right)
-
-    def form_bwd(kept, cotan):
-        left, right = kept
-        return (
-            einsum_low(f"{out_ids},{right_ids}->{left_ids}", cotan, right),
-            einsum_low(f"{left_ids},{out_ids}->{right_ids}", left, cotan),
-        )
-
-    form.defvjp(form_fwd, form_bwd)
-    return form
-
-
-head_scores = make_bilinear("phd", "qhd", "hpq")
-head_mix = make_bilinear("hpq", "qhd", "phd")
-
-
-def heads_of(rows):
-    return rows.reshape(rows.shape[0], -1, HEAD)
-
-
 def with_tangent(fun, value, tangent):
     return jax.jvp(fun, (value,), (tangent,))
-
-
-def self_scores(q_heads):
-    short = q_heads.astype(jnp.bfloat16).astype(jnp.float32)
-    return jnp.transpose(jnp.sum(short * short, axis=-1))
 
 
 def last_softmax(scores):
@@ -493,77 +461,6 @@
 
 def picture_of(hidden, rgb_scales, rgb_weight):
     return einsum_high("pc,kc->kp", hidden, rgb_scales[None] * rgb_weight)
-
-
-def layer_forward(conv_out, sums, text_rows, small, weights, noise):
-    bias, strength, rgb_scales, rgb_weight = small
-    qk_w, value_w, attn_w, query_w, key_w, cval_w, cout_w, mlp_w, mout_w = weights
-    hidden_one = post_conv(conv_out, sums, bias, strength, noise)
-    normed = rms_norm(hidden_one)
-    queries = heads_of(product(normed, qk_w))
-    values = heads_of(product(normed, value_w))
-    scores = (2.0 * head_scores(queries, queries) - self_scores(queries)[:, None, :]) * HEAD ** (
-        -0.5
-    )
-    mixture = head_mix(last_softmax(scores), values).reshape(normed.shape)
-    hidden_two = hidden_one + product_flip(mixture, attn_w)
-    normed = rms_norm(hidden_two)
-    queries = heads_of(product(normed, query_w))
-    key_rows = heads_of(product(text_rows, key_w))
-    values = heads_of(product(text_rows, cval_w))
-    scores = head_scores(queries, key_rows) * HEAD ** (-0.5)
-    mixture = head_mix(last_softmax(scores), values).reshape(normed.shape)
-    hidden_three = hidden_two + product_flip(mixture, cout_w)
-    normed = rms_norm(hidden_three)
-    inner = jax.nn.gelu(product(normed, mlp_w))
-    hidden_four = hidden_three + product_flip(inner, mout_w)
-    return hidden_four, picture_of(hidden_four, rgb_scales, rgb_weight)
-
-
-def layer_joint(conv_out, conv_tan, sums, text_rows, small, weights, noise):
-    bias, strength, rgb_scales, rgb_weight = small
-    qk_w, value_w, attn_w, query_w, key_w, cval_w, cout_w, mlp_w, mout_w = weights
-    hidden_one, tan_one = with_tangent(
-        lambda value: post_conv(value, sums, bias, strength, noise), conv_out, conv_tan
-    )
-    normed, tan_normed = with_tangent(rms_norm, hidden_one, tan_one)
-    queries, tan_queries = product_pair(normed, tan_normed, qk_w)
-    queries, tan_queries = heads_of(queries), heads_of(tan_queries)
-    values, tan_values = product_pair(normed, tan_normed, value_w)
-    values, tan_values = heads_of(values), heads_of(tan_values)
-    lengths, tan_lengths = with_tangent(self_scores, queries, tan_queries)
-    scores = (2.0 * head_scores(queries, queries) - lengths[:, None, :]) * HEAD ** (-0.5)
-    half = head_scores(tan_queries, queries)
-    tan_scores = (2.0 * (half + jnp.swapaxes(half, 1, 2)) - tan_lengths[:, None, :]) * HEAD ** (
-        -0.5
-    )
-    soft, tan_soft = with_tangent(last_softmax, scores, tan_scores)
-    mixture = head_mix(soft, values).reshape(normed.shape)
-    tan_mixture = (head_mix(tan_soft, values) + head_mix(soft, tan_values)).reshape(normed.shape)
-    added, tan_added = product_flip_pair(mixture, tan_mixture, attn_w)
-    hidden_two, tan_two = hidden_one + added, tan_one + tan_added
-    normed, tan_normed = with_tangent(rms_norm, hidden_two, tan_two)
-    queries, tan_queries = product_pair(normed, tan_normed, query_w)
-    queries, tan_queries = heads_of(queries), heads_of(tan_queries)
-    key_rows = heads_of(product(text_rows, key_w))
-    values = heads_of(product(text_rows, cval_w))
-    scores = head_scores(queries, key_rows) * HEAD ** (-0.5)
-    tan_scores = head_scores(tan_queries, key_rows) * HEAD ** (-0.5)
-    soft, tan_soft = with_tangent(last_softmax, scores, tan_scores)
-    mixture = head_mix(soft, values).reshape(normed.shape)
-    tan_mixture = head_mix(tan_soft, values).reshape(normed.shape)
-    added, tan_added = product_flip_pair(mixture, tan_mixture, cout_w)
-    hidden_three, tan_three = hidden_two + added, tan_two + tan_added
-    normed, tan_normed = with_tangent(rms_norm, hidden_three, tan_three)
-    before, tan_before = product_pair(normed, tan_normed, mlp_w)
-    inner, tan_inner = with_tangent(jax.nn.gelu, before, tan_before)
-    added, tan_added = product_flip_pair(inner, tan_inner, mout_w)
-    hidden_four, tan_four = hidden_three + added, tan_three + tan_added
-    return (
-        hidden_four,
-        picture_of(hidden_four, rgb_scales, rgb_weight),
-        picture_of(tan_four, rgb_scales, rgb_weight),
-    )
 
 
 CHUNK = 16
@@ -867,6 +764,214 @@
     )(mix, bank_rows, grad)
 
 
+@jax.custom_vjp
+def row_products(left, right):
+    return dot_f32(left.astype(jnp.bfloat16), right.astype(jnp.bfloat16), 1, 1)
+
+
+def row_products_fwd(left, right):
+    return row_products(left, right), (left, right)
+
+
+def row_products_bwd(kept, cotan):
+    left, right = (entry.astype(jnp.bfloat16) for entry in kept)
+    short = cotan.astype(jnp.bfloat16)
+    return dot_f32(short, right, 1, 0), dot_f32(short, left, 0, 0)
+
+
+row_products.defvjp(row_products_fwd, row_products_bwd)
+
+
+@jax.custom_vjp
+def mixed_rows(soft, values):
+    return dot_f32(soft.astype(jnp.bfloat16), values.astype(jnp.bfloat16), 1, 0)
+
+
+def mixed_rows_fwd(soft, values):
+    return mixed_rows(soft, values), (soft, values)
+
+
+def mixed_rows_bwd(kept, cotan):
+    soft, values = (entry.astype(jnp.bfloat16) for entry in kept)
+    short = cotan.astype(jnp.bfloat16)
+    return dot_f32(short, values, 1, 1), dot_f32(soft, short, 0, 0)
+
+
+mixed_rows.defvjp(mixed_rows_fwd, mixed_rows_bwd)
+
+
+@jax.custom_vjp
+def as_row(column):
+    count = column.shape[0]
+    lane = lax.broadcasted_iota(jnp.int32, (count, 128), 1)
+    rest, parts = column, jnp.zeros((count, 128), jnp.float32)
+    for place in range(3):
+        short = rest.astype(jnp.bfloat16).astype(jnp.float32)
+        parts = jnp.where(lane == place, short, parts)
+        rest = rest - short
+    ones = jnp.ones((count, 128), jnp.bfloat16)
+    return dot_f32(ones, parts.astype(jnp.bfloat16), 1, 1)
+
+
+def as_row_fwd(column):
+    return as_row(column), None
+
+
+def as_row_bwd(kept, cotan):
+    ones = jnp.ones((cotan.shape[0], 128), jnp.bfloat16)
+    return (dot_f32(cotan.astype(jnp.bfloat16), ones, 0, 0)[:, :1],)
+
+
+as_row.defvjp(as_row_fwd, as_row_bwd)
+
+
+def soft_of(scores):
+    top = lax.stop_gradient(jnp.max(scores, axis=1, keepdims=True))
+    powers = jnp.exp(scores - top)
+    return powers / jnp.sum(powers, axis=1, keepdims=True)
+
+
+def soft_tangent(soft, tangent):
+    return soft * (tangent - jnp.sum(soft * tangent, axis=1, keepdims=True))
+
+
+def squared(left, right):
+    return jnp.sum(left * right, axis=1, keepdims=True)
+
+
+def self_head(queries, values):
+    scores = 2.0 * row_products(queries, queries) - as_row(squared(queries, queries))
+    return (mixed_rows(soft_of(scores * HEAD ** (-0.5)), values),)
+
+
+def self_head_joint(queries, tan_queries, values, tan_values):
+    scores = 2.0 * row_products(queries, queries) - as_row(squared(queries, queries))
+    tan_scores = row_products(tan_queries, queries) + row_products(queries, tan_queries)
+    tan_scores = 2.0 * (tan_scores - as_row(squared(queries, tan_queries)))
+    soft = soft_of(scores * HEAD ** (-0.5))
+    tan_soft = soft_tangent(soft, tan_scores * HEAD ** (-0.5))
+    return (
+        mixed_rows(soft, values),
+        mixed_rows(tan_soft, values) + mixed_rows(soft, tan_values),
+    )
+
+
+def cross_head(queries, keys, values):
+    return (mixed_rows(soft_of(row_products(queries, keys) * HEAD ** (-0.5)), values),)
+
+
+def cross_head_joint(queries, tan_queries, keys, values):
+    soft = soft_of(row_products(queries, keys) * HEAD ** (-0.5))
+    tan_soft = soft_tangent(soft, row_products(tan_queries, keys) * HEAD ** (-0.5))
+    return mixed_rows(soft, values), mixed_rows(tan_soft, values)
+
+
+def per_head(fun, arrays, shapes, name):
+    lanes = 2 * HEAD
+
+    def body(*refs):
+        inputs, outputs = refs[: len(arrays)], refs[len(arrays) :]
+        for head in range(2):
+            span = slice(head * HEAD, (head + 1) * HEAD)
+            results = fun(*[ref[:, span].astype(jnp.float32) for ref in inputs])
+            for ref, result in zip(outputs, results):
+                ref[:, span] = result.astype(jnp.bfloat16)
+
+    return pl.pallas_call(
+        body,
+        grid=(arrays[0].shape[1] // lanes,),
+        in_specs=[pl.BlockSpec((entry.shape[0], lanes), lambda step: (0, step)) for entry in arrays],
+        out_specs=[pl.BlockSpec((shape[0], lanes), lambda step: (0, step)) for shape in shapes],
+        out_shape=[jax.ShapeDtypeStruct(shape, jnp.bfloat16) for shape in shapes],
+        compiler_params=pltpu.CompilerParams(vmem_limit_bytes=32 * 2**20),
+        name=name,
+    )(*arrays)
+
+
+def make_attention(fun, count, name):
+    @jax.custom_vjp
+    def attend(*arrays):
+        return tuple(per_head(fun, arrays, [arrays[0].shape] * count, name))
+
+    def attend_fwd(*arrays):
+        return attend(*arrays), arrays
+
+    def attend_bwd(arrays, cotans):
+        def pull(*given):
+            return jax.vjp(fun, *given[: len(arrays)])[1](tuple(given[len(arrays) :]))
+
+        shapes = [entry.shape for entry in arrays]
+        return tuple(per_head(pull, list(arrays) + list(cotans), shapes, name + "_pull"))
+
+    attend.defvjp(attend_fwd, attend_bwd)
+    return attend
+
+
+self_attend = make_attention(self_head, 1, "self_heads")
+self_attend_joint = make_attention(self_head_joint, 2, "self_heads_joint")
+cross_attend = make_attention(cross_head, 1, "cross_heads")
+cross_attend_joint = make_attention(cross_head_joint, 2, "cross_heads_joint")
+
+
+def short_of(*arrays):
+    return [entry.astype(jnp.bfloat16) for entry in arrays]
+
+
+def layer_forward(conv_out, sums, text_rows, small, weights, noise):
+    bias, strength, rgb_scales, rgb_weight = small
+    qk_w, value_w, attn_w, query_w, key_w, cval_w, cout_w, mlp_w, mout_w = weights
+    hidden_one = post_conv(conv_out, sums, bias, strength, noise)
+    normed = rms_norm(hidden_one)
+    (mixture,) = self_attend(*short_of(product(normed, qk_w), product(normed, value_w)))
+    hidden_two = hidden_one + product_flip(mixture.astype(jnp.float32), attn_w)
+    normed = rms_norm(hidden_two)
+    (mixture,) = cross_attend(
+        *short_of(
+            product(normed, query_w), product(text_rows, key_w), product(text_rows, cval_w)
+        )
+    )
+    hidden_three = hidden_two + product_flip(mixture.astype(jnp.float32), cout_w)
+    normed = rms_norm(hidden_three)
+    inner = jax.nn.gelu(product(normed, mlp_w))
+    hidden_four = hidden_three + product_flip(inner, mout_w)
+    return hidden_four, picture_of(hidden_four, rgb_scales, rgb_weight)
+
+
+def layer_joint(conv_out, conv_tan, sums, text_rows, small, weights, noise):
+    bias, strength, rgb_scales, rgb_weight = small
+    qk_w, value_w, attn_w, query_w, key_w, cval_w, cout_w, mlp_w, mout_w = weights
+    hidden_one, tan_one = with_tangent(
+        lambda value: post_conv(value, sums, bias, strength, noise), conv_out, conv_tan
+    )
+    normed, tan_normed = with_tangent(rms_norm, hidden_one, tan_one)
+    queries, tan_queries = product_pair(normed, tan_normed, qk_w)
+    values, tan_values = product_pair(normed, tan_normed, value_w)
+    mixture, tan_mixture = self_attend_joint(*short_of(queries, tan_queries, values, tan_values))
+    added, tan_added = product_flip_pair(
+        mixture.astype(jnp.float32), tan_mixture.astype(jnp.float32), attn_w
+    )
+    hidden_two, tan_two = hidden_one + added, tan_one + tan_added
+    normed, tan_normed = with_tangent(rms_norm, hidden_two, tan_two)
+    queries, tan_queries = product_pair(normed, tan_normed, query_w)
+    mixture, tan_mixture = cross_attend_joint(
+        *short_of(queries, tan_queries, product(text_rows, key_w), product(text_rows, cval_w))
+    )
+    added, tan_added = product_flip_pair(
+        mixture.astype(jnp.float32), tan_mixture.astype(jnp.float32), cout_w
+    )
+    hidden_three, tan_three = hidden_two + added, tan_two + tan_added
+    normed, tan_normed = with_tangent(rms_norm, hidden_three, tan_three)
+    before, tan_before = product_pair(normed, tan_normed, mlp_w)
+    inner, tan_inner = with_tangent(jax.nn.gelu, before, tan_before)
+    added, tan_added = product_flip_pair(inner, tan_inner, mout_w)
+    hidden_four, tan_four = hidden_three + added, tan_three + tan_added
+    return (
+        hidden_four,
+        picture_of(hidden_four, rgb_scales, rgb_weight),
+        picture_of(tan_four, rgb_scales, rgb_weight),
+    )
+
+
 SWAP = ((0, 1), (1, 0))
 
 
@@ -1085,7 +1190,9 @@
         body,
         in_specs=[pl.BlockSpec(memory_space=pl.ANY)] * count,
         out_specs=[pl.BlockSpec(memory_space=pl.ANY)] * len(shapes),
-        out_shape=[jax.ShapeDtypeStruct(shape, jnp.bfloat16) for shape in shapes],
+        out_shape=[
+            jax.ShapeDtypeStruct(shape, entry.dtype) for shape, entry in zip(shapes, arrays)
+        ],
         scratch_shapes=[
             pltpu.SemaphoreType.DMA((len(pieces), 16, 5)),
             pltpu.SemaphoreType.DMA((len(pieces), 16, 2)),
@@ -1104,26 +1211,27 @@
     return pl.ds(pl.multiple_of(index * lanes, lanes), lanes)
 
 
-def gather_weights(stacks, call_id):
-    def piece(number, first, last, order):
-        rows, lanes = stacks[number].shape[1:]
-        return dict(
-            order=order,
-            of=lambda refs: refs[number].at[first:last],
-            to=lambda refs, dp, mp: refs[number].at[
-                first:last, rows_at(dp, rows), lanes_at(mp, lanes)
-            ],
-        )
-
-    pieces = [
-        piece(0, 0, 2, ("x", "y", "z")),
-        piece(0, 2, 5, ("z", "x", "y")),
-        piece(1, 0, 2, ("z", "y", "x")),
-        piece(2, 0, 1, ("z", "x", "y")),
-        piece(2, 1, 2, ("z", "y", "x")),
-    ]
-    shapes = [(a.shape[0], a.shape[1] * 16, a.shape[2] * 2) for a in stacks]
-    return gather_call(pieces, ("z", "y", "x"), stacks, shapes, call_id, "gather_weights")
+def gather_weights(shards, numbers, call_id):
+    orders = dict(x=("z", "y", "x"), y=("z", "x", "y"), z=("x", "y", "z"))
+    turns = ("x", "y", "x", "y", "x", "y", "z", "y", "z")
+
+    def piece(number, turn):
+        rows, lanes = arrays[number].shape
+        stacked = number == len(shards)
+
+        def to(refs, dp, mp):
+            if stacked:
+                return refs[number].at[rows_at(dp * 2 + mp, rows)]
+            return refs[number].at[rows_at(dp, rows), lanes_at(mp, lanes)]
+
+        return dict(order=orders[turn], of=lambda refs: refs[number], to=to)
+
+    arrays = list(shards) + [numbers]
+    pieces = [piece(len(shards), "x")]
+    pieces += [piece(number, turn) for number, turn in enumerate(turns)]
+    shapes = [(entry.shape[0] * 16, entry.shape[1] * 2) for entry in shards]
+    shapes.append((numbers.shape[0] * 32, numbers.shape[1]))
+    return gather_call(pieces, ("z", "y", "x"), arrays, shapes, call_id, "gather_weights")
 
 
 def gather_dp(values, call_id):
@@ -1580,27 +1688,41 @@
     width_out = kernel_bank.shape[3]
     float32, bfloat16 = jnp.float32, jnp.bfloat16
 
-    stack_attn, stack_text, stack_mlp = gather_weights(
+    input_whole = lax.all_gather(layer_input, "mp", axis=2, tiled=True)
+    raw_slabs = to_slabs(input_whole)
+    numbers = jnp.concatenate([jnp.pad(labels, (0, 126)), text_ids.reshape(-1)]).reshape(2, 128)
+    gathered = gather_weights(
         [
-            jnp.stack([qk_weight, value_weight, attn_out.T, cross_query, cross_out.T]),
-            jnp.stack([cross_key, cross_value]),
-            jnp.stack([mlp_in, mlp_out.T]),
+            mlp_in,
+            mlp_out.T,
+            qk_weight,
+            value_weight,
+            attn_out.T,
+            cross_query,
+            cross_out.T,
+            cross_key,
+            cross_value,
         ],
+        jnp.pad(numbers, ((0, 6), (0, 0))),
         1,
     )
+    mlp_whole, mout_whole, qk_whole, value_whole, attn_whole, query_whole, cout_whole = gathered[:7]
+    key_whole, cval_whole, numbers_all = gathered[7:]
     weights = (
-        stack_attn[0],
-        stack_attn[1],
-        stack_attn[2],
-        stack_attn[3],
-        stack_text[0],
-        stack_text[1],
-        stack_attn[4],
-        stack_mlp[0],
-        stack_mlp[1],
-    )
-
-    labels_all = lax.all_gather(labels, "dp", axis=0, tiled=True)
+        qk_whole,
+        value_whole,
+        attn_whole,
+        query_whole,
+        key_whole,
+        cval_whole,
+        cout_whole,
+        mlp_whole,
+        mout_whole,
+    )
+
+    numbers_all = numbers_all.reshape(16, 2, 8, 128)[:, 0]
+    labels_all = numbers_all[:, 0, :2].reshape(-1)
+    ids_all = numbers_all[:, 1].reshape(-1)
     sample_count = labels_all.shape[0]
     classes = jnp.arange(class_table.shape[0], dtype=jnp.int32)
     onehot_class = (labels_all[:, None] == classes[None, :]).astype(bfloat16)
@@ -1631,10 +1753,8 @@
     kernel, sums_part = mix_kernels(mix, bank_rows, scales_two)
     place = placing(SIDE // 2)
 
-    input_own = own_whole(layer_input, mp).astype(float32)
-    scales_pair = lax.dynamic_slice_in_dim(scales_all, 2 * dp, 2, 0)
-    input_pair = lax.all_gather(layer_input, "mp", axis=2, tiled=True).astype(float32)
-    slabs_x = to_slabs((input_pair * scales_pair[:, None, :]).astype(bfloat16))
+    input_own = pick(input_whole, mp).astype(float32)
+    slabs_x = (raw_slabs.astype(float32) * scales_slab[:, None, :]).astype(bfloat16)
     partial = convolve(slabs_x, place, kernel, sums_part, True)
     summed = sum_samples(partial, 4).astype(float32)
     conv_out, sums = summed[:PIXELS], summed[PIXELS]
@@ -1743,7 +1863,6 @@
     mod_grad = matmul_high(latent.T, scale_terms)
     rgb_mod_grad = matmul_high(latent.T, rgb_terms)
     text_all = lax.all_gather(grad_text.astype(bfloat16), ("dp", "mp"), axis=0, tiled=True)
-    ids_all = lax.all_gather(text_ids, "dp", axis=0, tiled=True).reshape(-1)
     token_grad = dot_wide((ids_all[:, None] == words[None, :]).astype(bfloat16), text_all, 0, 0)
 
     picture_other = swap_mp(picture)

time: 1410 us -> 1290 us (0.915)
  Pallas kernels: 793 us -> 914 us
  matrix products: 244 us -> 158 us
  local copies, waits for them, and re-layouts: 155 us -> 70.3 us
  other arithmetic: 80.6 us -> 26.9 us
  blocking collectives: 32.6 us -> 7.85 us
  waiting for transfers between devices: 29.4 us -> 47.6 us
    pallas_call x0 -> x8, Pallas kernels: none -> 107 us  [the longest x4 41.6 us: per_head(): pl.pallas_call(body, grid=(arrays[0].shape[1] // lanes,), in_specs=[pl.Bl...]
    dot_general x45 -> x13, matrix products: 90.9 us -> 17 us  [the longest x4 7.76 us: layer_joint(): product_flip_pair(mixture.astype(jnp.float32), tan_mixture.astype(jnp.flo...]
    dot_general x10 -> x0, local copies, waits for them, and re-layouts: 40.4 us -> none  [the longest x6 19.3 us: dot_wide(): lax.dot_general(left.astype(jnp.bfloat16), right.astype(jnp.bfloat16), ((...]
    all_gather x2 -> x1, blocking collectives: 23.9 us -> 7.85 us  [sample_parallel(): input_whole = lax.all_gather(layer_input, 'mp', axis=2, tiled=True)]
    ppermute x10 -> x9, waiting for transfers between devices: 29.3 us -> 35.3 us  [swap_mp(): return lax.ppermute(values, 'mp', SWAP)]
    dot_general x22 -> x27, matrix products: 67.6 us -> 62.2 us  [dot_wide(): lax.dot_general(left.astype(jnp.bfloat16), right.astype(jnp.bfloat16), ((...]
    unnamed x568 -> x354, local copies, waits for them, and re-layouts: 55 us -> 50.6 us
  transfers between devices with their start and end apart: 16 -> 15, of which waited for: 6 -> 8; matrix products, arithmetic and copies ran while one was open for 18% -> 9% of each run, Pallas kernels for 37% -> 34%
where the time goes in v3:
time: 1290 us; the launch traced here: 1280 us
  Pallas kernels  914 us (71%)
  matrix products  158 us (12%)
  local copies, waits for them, and re-layouts  70.3 us (5%)
  waiting for transfers between devices  47.6 us (4%)
  starting transfers between devices  37.9 us (3%)
  other arithmetic  26.9 us (2%)
  between operations  18 us (1%)
    pallas_call x3, Pallas kernels, gather_call(): pl.pallas_call(body, in_specs=[pl.BlockSpec(memory_space=pl.ANY)] * count...  294 us
    pallas_call x1, Pallas kernels, sum_weights(): pl.pallas_call(lambda *refs: sum_weights_body(parts, count, refs), in_spe...  178 us
    pallas_call x2, Pallas kernels, sum_samples(): pl.pallas_call(lambda *refs: sum_body(cut, *refs), in_specs=[pl.BlockSpec...  154 us
    pallas_call x1, Pallas kernels, conv_second(): pl.pallas_call(second_body, grid=(samples,), in_specs=[pl.BlockSpec((1, p...  62.7 us
    dot_general x27, matrix products, dot_wide(): lax.dot_general(left.astype(jnp.bfloat16), right.astype(jnp.bfloat16), ((...  62.2 us
    pallas_call x2, Pallas kernels, convolve(): pl.pallas_call(lambda *refs: conv_body(extra, *refs), grid=(samples,), in...  57.1 us
    unnamed x354, local copies, waits for them, and re-layouts  50.6 us
    pallas_call x4, Pallas kernels, per_head(): pl.pallas_call(body, grid=(arrays[0].shape[1] // lanes,), in_specs=[pl.Bl...  41.6 us
  transfers between devices with their start and end apart: 15, of which 8 were waited for; matrix products, arithmetic and copies ran while one was open for 9% of the time, Pallas kernels for 34%

profile of v3, /device:TPU:9, one launch (start us, length us, event | category | flops | bytes accessed | tf_op | source)
XLA Modules:
  0.0 1280.9 jit_solution(8002585614957883682)
XLA Ops:
  8.5 7.9 all_gather.9
  18.2 7.6 all-to-all-start
  27.9 132.5 %gather_weights.1 = (bf16[1024,4096]{1,0:T(8,128)(2,1)}, bf16[1024,4096]{1,0:T(8,128)(2,1)}, bf16[1024,1024]{1,0:T(8,128)(2,1)}, bf16[1024,1024]{1,0:T(8,128)(2,...) custom-call(bf16[64,2048]{1,0:T(8,128)(2,1)} %refs_0_.1, ...), custom_call_target="tpu_custom_call" | custom-call | tf_op jit(solution)/shard_map/gather_weights/pallas_call | solution.py:1189
  168.3 3.2 mul.990.refs_0_
  172.0 1.8 convolution_convert_fusion.21.refs_1_.refs_2_
  174.3 2.3 copy-done.4
  176.6 13.5 %mix_kernels.1 = (bf16[32,576,512]{2,1,0:T(8,128)(2,1)}, f32[32,512]{1,0:T(8,128)S(1)}) custom-call(bf16[512,256]{1,0:T(8,128)(2,1)S(1)} %mul.990.refs_0_, bf16[8,576,512]{2,1,0:T(8,128)(2,1)S(1)} %bitcast.204, f32[32,64,128]{2,1,0:T(8,128)S(1)} %broadcast_in_dim.30.refs_2_.squares_ref), custom_call_target="tpu_custom_call" | custom-call | tf_op jit(solution)/shard_map/mix_kernels/pallas_call | solution.py:528
  192.8 28.6 %conv_forward.2 = bf16[32,272,512]{2,1,0:T(8,128)(2,1)S(1)} custom-call(bf16[32,64,64]{2,1,0:T(8,128)(2,1)S(1)} %fusion.50.refs_0_.slab_ref, bf16[288,192]{1,0:T(8,128)(2,1)S(1)} %copy-done.10, bf16[32,576,512]{2,1,0:T(8,128)(2,1)} %get-tuple-element.63.refs_2_.kernel_ref, f32[32,512]{1,0:T(8,128)S(1)} %get-tuple-element.64.refs_3_), custom_call_target="tpu_custom_call" | custom-call | tf_op jit(solution)/shard_map/conv_forward/pallas_call | solution.py:586
  221.4 76.8 %sum_samples.2 = bf16[272,1024]{1,0:T(8,128)(2,1)S(1)} custom-call(bf16[4,2,2,2,272,512]{5,4,3,2,1,0:T(8,128)(2,1)S(1)} %bitcast.202), custom_call_target="tpu_custom_call" | custom-call | tf_op jit(solution)/shard_map/sum_samples/pallas_call | solution.py:1411
  302.4 11.5 jvp_self_heads_.1
  315.6 7.4 jvp_cross_heads_.1
  323.9 4.3 fusion.54
  328.2 12.1 multiply_reduce_fusion.18
  340.4 2.3 add_add_fusion.11
  343.7 11.0 transpose_jvp_cross_heads_pull__.1
  357.9 14.8 %transpose_jvp_self_heads_pull__.1 = (bf16[256,1024]{1,0:T(8,128)(2,1)S(1)}, bf16[256,1024]{1,0:T(8,128)(2,1)S(1)}) custom-call(bf16[256,1024]{1,0:T(8,128)(2,1)S(1)} %convolution_convert_fusion.19.refs_0_, bf16[256,1024]{1,0:T(8,128)(2,1)S(1)} %convolution_convert_fusion.18.refs_1_.refs_2_, bf16[256,1024]{1,0:T(8,128)(2,1)S(1)} %convolution_convert_fusion.15.refs_2_), custom_call_target="tpu_custom_call" | custom-call | tf_op jit(solution)/shard_map/transpose(jvp(self_heads_pull))/pallas_call | solution.py:925
  378.9 3.9 collective-permute-done.2
  383.8 61.0 %gather_samples.2.cotan_ref = bf16[32,256,512]{2,1,0:T(8,128)(2,1)} custom-call(bf16[2,256,512]{2,1,0:T(8,128)(2,1)} %pad_maximum_fusion.18.refs_0_), custom_call_target="tpu_custom_call" | custom-call | tf_op jit(solution)/shard_map/gather_samples/pallas_call | solution.py:1189
  444.8 3.4 copy-done.3
  448.2 30.6 %conv_back.1 = bf16[32,64,64]{2,1,0:T(8,128)(2,1)S(1)} custom-call(bf16[32,256,512]{2,1,0:T(8,128)(2,1)S(1)} %copy-done.3, bf16[288,192]{1,0:T(8,128)(2,1)S(1)} %copy-done.10, bf16[32,576,512]{2,1,0:T(8,128)(2,1)} %get-tuple-element.63.refs_2_.kernel_ref), custom_call_target="tpu_custom_call" | custom-call | tf_op jit(solution)/shard_map/conv_back/pallas_call | solution.py:626
  479.9 10.5 all-to-all-start.1
  493.6 5.5 all-to-all-done.1
  500.9 7.2 collective-permute-done.3
  510.2 5.7 collective-permute-done.4
  517.5 4.7 all-to-all-start.2
  522.3 11.6 fusion.53
  534.2 28.5 %conv_forward.3 = bf16[32,256,512]{2,1,0:T(8,128)(2,1)S(1)} custom-call(bf16[32,64,64]{2,1,0:T(8,128)(2,1)S(1)} %bitcast.206, bf16[288,192]{1,0:T(8,128)(2,1)S(1)} %copy-done.10, bf16[32,576,512]{2,1,0:T(8,128)(2,1)} %get-tuple-element.63.refs_2_.kernel_ref, f32[32,512]{1,0:T(8,128)S(1)} %get-tuple-element.64.refs_3_), custom_call_target="tpu_custom_call" | custom-call | tf_op jit(solution)/shard_map/conv_forward/pallas_call | solution.py:586
  562.8 76.9 %sum_samples.3 = bf16[256,1024]{1,0:T(8,128)(2,1)S(1)} custom-call(bf16[4,2,2,2,256,512]{5,4,3,2,1,0:T(8,128)(2,1)S(1)} %bitcast.203), custom_call_target="tpu_custom_call" | custom-call | tf_op jit(solution)/shard_map/sum_samples/pallas_call | solution.py:1411
  644.6 13.8 %jvp_self_heads_joint_.1 = (bf16[256,1024]{1,0:T(8,128)(2,1)S(1)}, bf16[256,1024]{1,0:T(8,128)(2,1)S(1)}) custom-call(bf16[256,1024]{1,0:T(8,128)(2,1)S(1)} %convolution_convert_fusion.19.refs_0_, bf16[256,1024]{1,0:T(8,128)(2,1)S(1)} %convolution_convert_fusion.14.refs_1_, bf16[256,1024]{1,0:T(8,128)(2,1)S(1)} %convolution_convert_fusion.18.refs_1_.refs_2_, ...), custom_call_target="tpu_custom_call" | custom-call | tf_op jit(solution)/shard_map/jvp(self_heads_joint)/pallas_call | solution.py:880
  663.8 8.9 jvp_cross_heads_joint_.1
  675.3 2.3 fusion.159
  677.7 15.5 %add_convert_fusion.2 = (bf16[256,4096]{1,0:T(8,128)(2,1)}, bf16[256,4096]{1,0:T(8,128)(2,1)}, bf16[256,4096]{1,0:T(8,128)(2,1)}, bf16[256,4096]{1,0:T(8,128)(2,1)}) fusion(f32[256,4096]{1,0:T(8,128)S(1)} %fusion.159, f32[512,4096]{1,0:T(8,128)} %fusion.53, bf16[256,1024]{1,0:T(8,128)(2,1)S(1)} %get-tuple-element.245, bf16[1024,4096]{1,0:T(8,128)(2,1)} %get-tuple-element.72), kind=kOutput, calls=%fused_computation.27 | convolution fusion | flops 2205155328 | bytes 29884416 | tf_op jit(solution)/shard_map/jvp()/dot_general | solution.py:395
  693.2 10.5 fusion.17
  703.7 2.0 multiply_reduce_fusion.11
  709.5 13.3 %transpose_jvp_cross_heads_joint_pull__.1 = (bf16[256,1024]{1,0:T(8,128)(2,1)S(1)}, bf16[256,1024]{1,0:T(8,128)(2,1)S(1)}, bf16[64,1024]{1,0:T(8,128)(2,1)S(1)}, bf16[64,1024]{1,0:T(8,128)(2,1)S(1)}) custom-call(bf16[256,1024]{1,0:T(8,128)(2,1)S(1)} %convolution_convert_fusion.12.refs_0_, bf16[256,1024]{1,0:T(8,128)(2,1)S(1)} %convolution_convert_fusion.11.refs_1_, ...), custom_call_target="tpu_custom_call" | custom-call | tf_op jit(solution)/shard_map/transpose(jvp(cross_heads_joint_pull))/pallas_call | solution.py:956
  727.6 26.3 %transpose_jvp_self_heads_joint_pull__.1 = (bf16[256,1024]{1,0:T(8,128)(2,1)S(1)}, bf16[256,1024]{1,0:T(8,128)(2,1)S(1)}, bf16[256,1024]{1,0:T(8,128)(2,1)S(1)}, bf16[256,1024]{1,0:T(8,128)(2,1)S(1)}) custom-call(bf16[256,1024]{1,0:T(8,128)(2,1)S(1)} %convolution_convert_fusion.19.refs_0_, bf16[256,1024]{1,0:T(8,128)(2,1)S(1)} %convolution_convert_fusion.14.refs_1_, ...), custom_call_target="tpu_custom_call" | custom-call | tf_op jit(solution)/shard_map/transpose(jvp(self_heads_joint_pull))/pallas_call | solution.py:949
  754.1 2.2 copy-done.72
  759.7 2.6 multiply_convert_fusion.6
  764.9 2.4 convolution_add_fusion.8
  768.3 6.7 collective-permute-done.6
  776.4 100.3 %gather_samples.3.cotan_ref = bf16[32,528,512]{2,1,0:T(8,128)(2,1)} custom-call(bf16[2,528,512]{2,1,0:T(8,128)(2,1)} %pad_maximum_fusion.4.refs_0_), custom_call_target="tpu_custom_call" | custom-call | tf_op jit(solution)/shard_map/gather_samples/pallas_call | solution.py:1189
  876.7 5.9 copy-done.2
  882.6 62.7 %conv_second.1 = (bf16[32,576,512]{2,1,0:T(8,128)(2,1)}, bf16[32,128,64]{2,1,0:T(8,128)(2,1)S(1)}, f32[32,64,128]{2,1,0:T(8,128)S(1)}) custom-call(bf16[32,64,64]{2,1,0:T(8,128)(2,1)S(1)} %copy-done.9, bf16[32,64,64]{2,1,0:T(8,128)(2,1)S(1)} %bitcast.207, bf16[288,192]{1,0:T(8,128)(2,1)S(1)} %copy-done.10, ...), custom_call_target="tpu_custom_call" | custom-call | tf_op jit(solution)/shard_map/conv_second/pallas_call | solution.py:694
  947.5 10.4 all-to-all-start.3
  958.0 6.5 convolution_add_fusion.7
  965.4 6.7 all-to-all-done.3
  974.3 2.3 copy-done.5
  976.6 17.3 %unmix_kernels.1 = (f32[8,576,512]{2,1,0:T(8,128)}, f32[512,128]{1,0:T(8,128)S(1)}) custom-call(bf16[512,256]{1,0:T(8,128)(2,1)S(1)} %copy-done.12, bf16[8,576,512]{2,1,0:T(8,128)(2,1)S(1)} %bitcast.205, bf16[32,576,512]{2,1,0:T(8,128)(2,1)} %get-tuple-element.89.refs_2_), custom_call_target="tpu_custom_call" | custom-call | tf_op jit(solution)/shard_map/unmix_kernels/pallas_call | solution.py:746
  998.5 7.4 fusion.29
  1010.4 10.5 collective-permute-done
  1024.2 2.6 convolution_convert_fusion.4.refs_4_
  1030.4 2.7 convolution_convert_fusion.3.refs_5_
  1033.1 2.6 convolution_convert_fusion.6.refs_2_
  1035.7 2.7 convolution_convert_fusion.5.refs_3_
  1038.8 7.3 convolution_convert_fusion.refs_1_
  1046.2 6.9 convolution_convert_fusion.1.refs_0_
  1053.8 2.6 convolution_convert_fusion.2.refs_6_
  1056.4 178.3 %sum_weights.1 = (f32[64,2048]{1,0:T(8,128)}, f32[64,2048]{1,0:T(8,128)}, f32[64,512]{1,0:T(8,128)}, f32[64,512]{1,0:T(8,128)}, f32[64,512]{1,0:T(8,128)}, /*ind...) custom-call(bf16[1024,4096]{1,0:T(8,128)(2,1)} %convolution_convert_fusion.1.refs_0_, ...), custom_call_target="tpu_custom_call" | custom-call | tf_op jit(solution)/shard_map/sum_weights/pallas_call | solution.py:1634
  1239.6 1.9 reshape.421
  1241.6 1.8 reduce_sum.338
  1251.3 2.4 fusion.66
  1253.6 3.2 fusion.68
  1256.8 3.2 fusion.73
  1260.1 7.6 fusion
  (529 shorter events, 113.4 us)
Async XLA Ops:
  7.2 164.3 %copy-start = (bf16[1000,768]{1,0:T(8,128)(2,1)S(1)}, bf16[1000,768]{1,0:T(8,128)(2,1)}, u32[]{:S(2)}) copy-start(bf16[1000,768]{1,0:T(8,128)(2,1)} %param.33) | copy-start | bytes 4608004
  7.2 18.6 %copy-start.149 = (s32[2,64]{1,0:T(2,128)S(1)}, s32[2,64]{1,0:T(2,128)}, u32[]{:S(2)}) copy-start(s32[2,64]{1,0:T(2,128)} %param.29) | copy-start | bytes 1540
  7.2 18.7 %copy-start.150 = (s32[2]{0:T(128)S(1)}, s32[2]{0:T(128)}, u32[]{:S(2)}) copy-start(s32[2]{0:T(128)} %param.30) | copy-start | bytes 28
  7.2 20.0 %copy-start.144 = (bf16[2,3,256]{2,0,1:T(2,128)(2,1)S(1)}, bf16[2,3,256]{2,0,1:T(2,128)(2,1)}, u32[]{:S(2)}) copy-start(bf16[2,3,256]{2,0,1:T(2,128)(2,1)} %param.52) | copy-start | bytes 9220
  7.2 20.0 %copy-start.148 = (s32[2]{0:T(128)S(1)}, s32[2]{0:T(128)}, u32[]{:S(2)}) copy-start(s32[2]{0:T(128)} %param.28) | copy-start | bytes 28
  7.3 20.6 %copy-start.146 = (bf16[1024]{0:T(1024)(128)(2,1)S(1)}, bf16[1024]{0:T(1024)(128)(2,1)}, u32[]{:S(2)}) copy-start(bf16[1024]{0:T(1024)(128)(2,1)} %param.38) | copy-start | bytes 6148
  7.3 20.6 %copy-start.147 = (bf16[1024]{0:T(1024)(128)(2,1)S(1)}, bf16[1024]{0:T(1024)(128)(2,1)}, u32[]{:S(2)}) copy-start(bf16[1024]{0:T(1024)(128)(2,1)} %param.39) | copy-start | bytes 6148
  16.6 146.9 %copy-start.128 = (bf16[512,8]{0,1:T(8,128)(2,1)S(1)}, bf16[512,8]{0,1:T(8,128)(2,1)}, u32[]{:S(2)}) copy-start(bf16[512,8]{0,1:T(8,128)(2,1)} %param.34) | copy-start | bytes 24580
  18.2 148.2 %copy-start.55 = (bf16[512,1024]{1,0:T(8,128)(2,1)S(1)}, bf16[512,1024]{1,0:T(8,128)(2,1)}, u32[]{:S(2)}) copy-start(bf16[512,1024]{1,0:T(8,128)(2,1)} %param.36) | copy-start | bytes 3145732
  18.2 173.9 %all-to-all-start = ((bf16[16,2,4096]{2,1,0:T(2,128)(2,1)}), bf16[16,2,4096]{2,1,0:T(2,128)(2,1)S(1)}, u32[]{:S(2)}, u32[]{:S(2)}) async-start(bf16[16,2,4096]{2,1,0:T(2,128)(2,1)} %reshape.431), calls=%async_computation | async-start | bytes 524288 | tf_op jit(solution)/shard_map/all_to_all | solution.py:1005
  27.2 162.8 %copy-start.132 = (bf16[1,3,256]{2,0,1:T(2,128)(2,1)}, bf16[1,3,256]{2,0,1:T(2,128)(2,1)S(1)}, u32[]{:S(2)}) copy-start(bf16[1,3,256]{2,0,1:T(2,128)(2,1)S(1)} %constant_dynamic-slice_fusion.5) | copy-start | bytes 4612
  171.9 19.8 %copy-start.63 = (bf16[64,768]{1,0:T(8,128)(2,1)}, bf16[64,768]{1,0:T(8,128)(2,1)S(1)}, u32[]{:S(2)}) copy-start(bf16[64,768]{1,0:T(8,128)(2,1)S(1)} %convolution_convert_fusion.22) | copy-start | bytes 294916
  173.9 18.6 %copy-start.109 = (f32[32,64]{1,0:T(8,128)}, f32[32,64]{1,0:T(8,128)S(1)}, u32[]{:S(2)}) copy-start(f32[32,64]{1,0:T(8,128)S(1)} %get-tuple-element.229) | copy-start | bytes 24580
  173.9 334.5 %copy-start.120 = (f32[1,1024]{1,0:T(1,128)}, f32[1,1024]{1,0:T(1,128)S(1)}, u32[]{:S(2)}) copy-start(f32[1,1024]{1,0:T(1,128)S(1)} %fusion.84) | copy-start | bytes 12292
  176.6 13.5 %copy-start.6 = (f32[32,64,128]{2,1,0:T(8,128)}, f32[32,64,128]{2,1,0:T(8,128)S(1)}, u32[]{:S(2)}) copy-start(f32[32,64,128]{2,1,0:T(8,128)S(1)} %broadcast_in_dim.30.refs_2_.squares_ref) | copy-start | bytes 3145732
  176.6 13.5 %copy-start.113 = (bf16[3,1024]{1,0:T(4,128)(2,1)S(1)}, bf16[3,1024]{1,0:T(4,128)(2,1)}, u32[]{:S(2)}) copy-start(bf16[3,1024]{1,0:T(4,128)(2,1)} %param.37) | copy-start | bytes 18436
  176.6 15.1 %copy-start.52 = (bf16[768,1024]{1,0:T(8,128)(2,1)S(1)}, bf16[768,1024]{1,0:T(8,128)(2,1)}, u32[]{:S(2)}) copy-start(bf16[768,1024]{1,0:T(8,128)(2,1)} %get-tuple-element.70) | copy-start | bytes 4718596
  191.7 136.5 %copy-start.86 = (bf16[256,1024]{1,0:T(8,128)(2,1)}, bf16[256,1024]{1,0:T(8,128)(2,1)S(1)}, u32[]{:S(2)}) copy-start(bf16[256,1024]{1,0:T(8,128)(2,1)S(1)} %get-tuple-element.283) | copy-start | bytes 1572868
  192.7 28.7 %copy-start.8 = (bf16[32,64,64]{2,1,0:T(8,128)(2,1)}, bf16[32,64,64]{2,1,0:T(8,128)(2,1)S(1)}, u32[]{:S(2)}) copy-start(bf16[32,64,64]{2,1,0:T(8,128)(2,1)S(1)} %fusion.50.refs_0_.slab_ref) | copy-start | bytes 786436
  298.9 15.0 %copy-start.27 = (f32[256,1024]{1,0:T(8,128)}, f32[256,1024]{1,0:T(8,128)S(1)}, u32[]{:S(2)}) copy-start(f32[256,1024]{1,0:T(8,128)S(1)} %get-tuple-element.227) | copy-start | bytes 3145732
  299.0 24.9 %slice-start = ((s8[8388608]{0:T(1024)(128)(4,1)}), s8[4194304]{0:T(1024)(128)(4,1)S(1)}, s32[]{:S(2)}) async-start(s8[8388608]{0:T(1024)(128)(4,1)} %bitcast.210), calls=%async_computation.6 | async-start | bytes 8388608
  301.7 12.3 copy-start.33
  302.4 12.4 copy-start.46
  313.9 9.9 slice-start.1
  342.9 11.8 copy-start.40
  342.9 11.8 copy-start.47
  357.1 15.6 %copy-start.70 = (bf16[1024,1024]{1,0:T(8,128)(2,1)S(1)}, bf16[1024,1024]{1,0:T(8,128)(2,1)}, u32[]{:S(2)}) copy-start(bf16[1024,1024]{1,0:T(8,128)(2,1)} %get-tuple-element.66) | copy-start | bytes 6291460
  377.4 5.4 collective-permute-start.2
  377.7 122.2 %collective-permute-start.5 = (bf16[256,512]{1,0:T(8,128)(2,1)S(1)}, bf16[256,512]{1,0:T(8,128)(2,1)S(1)}, u32[]{:S(2)}, u32[]{:S(2)}) collective-permute-start(bf16[256,512]{1,0:T(8,128)(2,1)S(1)} %dynamic-slice_bitcast_fusion.1), channel_id=1, source_target_pairs={{0,1},{1,0},{2,3},{3,2},{4,5},{5,4},{6,7},{7,6},{8,9},{9,8},{10,11... | collective-permute-start | bytes 786440 | tf_op jit(solution)/shard_map/ppermute | solution.py:979
  448.2 42.2 %copy-start.145 = (bf16[2,3,256]{2,0,1:T(2,128)(2,1)S(1)}, bf16[2,3,256]{2,0,1:T(2,128)(2,1)}, u32[]{:S(2)}) copy-start(bf16[2,3,256]{2,0,1:T(2,128)(2,1)} %param.51) | copy-start | bytes 9220
  448.2 43.4 %copy-start.151 = (s32[2]{0:T(128)S(1)}, s32[2]{0:T(128)}, u32[]{:S(2)}) copy-start(s32[2]{0:T(128)} %param.31) | copy-start | bytes 28
  479.9 19.2 %all-to-all-start.1 = ((bf16[16,2,4096]{2,1,0:T(2,128)(2,1)}), bf16[16,2,4096]{2,1,0:T(2,128)(2,1)S(1)}, u32[]{:S(2)}, u32[]{:S(2)}) async-start(bf16[16,2,4096]{2,1,0:T(2,128)(2,1)} %reshape.433), calls=%async_computation.1 | async-start | bytes 524288 | tf_op jit(solution)/shard_map/all_to_all | solution.py:1013
  490.4 18.1 %copy-start.134 = (bf16[1,3,256]{2,0,1:T(2,128)(2,1)}, bf16[1,3,256]{2,0,1:T(2,128)(2,1)S(1)}, u32[]{:S(2)}) copy-start(bf16[1,3,256]{2,0,1:T(2,128)(2,1)S(1)} %constant_dynamic-slice_fusion.2) | copy-start | bytes 4612
  493.6 14.7 %copy-start.126 = (f32[1,1024]{1,0:T(1,128)}, f32[1,1024]{1,0:T(1,128)S(1)}, u32[]{:S(2)}) copy-start(f32[1,1024]{1,0:T(1,128)S(1)} %constant_dynamic-slice_fusion.3) | copy-start | bytes 12292
  499.7 10.5 copy-start.60
  499.7 8.4 collective-permute-start.3
  508.3 7.5 collective-permute-start.4
  517.5 16.4 %all-to-all-start.2 = ((bf16[16,2,4096]{2,1,0:T(2,128)(2,1)}), bf16[16,2,4096]{2,1,0:T(2,128)(2,1)S(1)}, u32[]{:S(2)}, u32[]{:S(2)}) async-start(bf16[16,2,4096]{2,1,0:T(2,128)(2,1)} %reshape.435), calls=%async_computation.2 | async-start | bytes 524288 | tf_op jit(solution)/shard_map/all_to_all | solution.py:1005
  562.7 77.0 %copy-start.29 = (f32[256,1024]{1,0:T(8,128)S(1)}, f32[256,1024]{1,0:T(8,128)}, u32[]{:S(2)}) copy-start(f32[256,1024]{1,0:T(8,128)} %copy-done.27) | copy-start | bytes 3145732
  562.8 77.0 %copy-start.32 = (f32[272,1024]{1,0:T(8,128)S(1)}, f32[272,1024]{1,0:T(8,128)}, u32[]{:S(2)}) copy-start(f32[272,1024]{1,0:T(8,128)} %copy-done.30) | copy-start | bytes 3342340
  643.9 14.5 %copy-start.35 = (bf16[1024,1024]{1,0:T(8,128)(2,1)S(1)}, bf16[1024,1024]{1,0:T(8,128)(2,1)}, u32[]{:S(2)}) copy-start(bf16[1024,1024]{1,0:T(8,128)(2,1)} %get-tuple-element.67) | copy-start | bytes 6291460
  663.1 11.9 slice-start.2
  674.7 31.1 %copy-start.41 = (f32[256,1024]{1,0:T(8,128)}, f32[256,1024]{1,0:T(8,128)S(1)}, u32[]{:S(2)}) copy-start(f32[256,1024]{1,0:T(8,128)S(1)} %get-tuple-element.292) | copy-start | bytes 3145732
  709.5 13.4 %copy-start.49 = (bf16[1024,1024]{1,0:T(8,128)(2,1)S(1)}, bf16[1024,1024]{1,0:T(8,128)(2,1)}, u32[]{:S(2)}) copy-start(bf16[1024,1024]{1,0:T(8,128)(2,1)} %get-tuple-element.68) | copy-start | bytes 6291460
  763.5 11.6 collective-permute-start.6
  776.4 100.3 %copy-start.7 = (f32[32,64,128]{2,1,0:T(8,128)S(1)}, f32[32,64,128]{2,1,0:T(8,128)}, u32[]{:S(2)}) copy-start(f32[32,64,128]{2,1,0:T(8,128)} %copy-done.6) | copy-start | bytes 3145732
  776.4 100.4 %copy-start.9 = (bf16[32,64,64]{2,1,0:T(8,128)(2,1)S(1)}, bf16[32,64,64]{2,1,0:T(8,128)(2,1)}, u32[]{:S(2)}) copy-start(bf16[32,64,64]{2,1,0:T(8,128)(2,1)} %copy-done.8) | copy-start | bytes 786436
  946.4 11.6 copy-start.42
  947.5 24.6 %all-to-all-start.3 = ((bf16[16,2,128,64]{2,3,1,0:T(8,128)(2,1)}), bf16[16,2,128,64]{2,3,1,0:T(8,128)(2,1)S(1)}, u32[]{:S(2)}, u32[]{:S(2)}) async-start(bf16[16,2,128,64]{2,3,1,0:T(8,128)(2,1)} %copy.88), calls=%async_computation.3 | async-start | bytes 1048576 | tf_op jit(solution)/shard_map/all_to_all | solution.py:1013
  957.9 277.9 %all-gather.3.cloned.1.call-start = ((), (), s32[]{:S(2)}) async-start(), calls=%async_computation.4 | async-start | bytes 1351680 | tf_op jit(solution)/shard_map/all_gather | solution.py:1846
  973.6 21.4 %collective-permute-start.7 = (bf16[128,1024]{0,1:T(8,128)(2,1)}, bf16[128,1024]{0,1:T(8,128)(2,1)}, u32[]{:S(2)}, u32[]{:S(2)}) collective-permute-start(bf16[128,1024]{0,1:T(8,128)(2,1)} %dynamic-slice_bitcast_fusion), channel_id=1, source_target_pairs={{0,1},{1,0},{2,3},{3,2},{4,5},{5,4},{6,7},{7,6},{8,9},{9,8},{10,11... | collective-permute-start | bytes 786440 | tf_op jit(solution)/shard_map/ppermute | solution.py:979
  998.5 261.6 %all-gather.5.cloned.1.call-start = ((), (), s32[]{:S(2)}) async-start(), calls=%async_computation.5 | async-start | bytes 3244032 | tf_op jit(solution)/shard_map/all_gather | solution.py:1865
  1006.9 2.9 collective-permute-start.1
  1007.8 13.1 %collective-permute-start = (f32[256,512]{1,0:T(8,128)S(1)}, f32[256,512]{1,0:T(8,128)S(1)}, u32[]{:S(2)}, u32[]{:S(2)}) collective-permute-start(f32[256,512]{1,0:T(8,128)S(1)} %constant_dynamic-slice_fusion.7), channel_id=1, source_target_pairs={{0,1},{1,0},{2,3},{3,2},{4,5},{5,4},{6,7},{7,6},{8,9},{9,8},{10,11... | collective-permute-start | bytes 1572872 | tf_op jit(solution)/shard_map/ppermute | solution.py:979
  1010.4 11.7 copy-start.26
  1010.4 11.7 copy-start.53
  1053.1 181.6 %collective-permute-start.8 = (f32[64,512]{0,1:T(8,128)S(1)}, f32[64,512]{0,1:T(8,128)S(1)}, u32[]{:S(2)}, u32[]{:S(2)}) collective-permute-start(f32[64,512]{0,1:T(8,128)S(1)} %constant_dynamic-slice_fusion), channel_id=1, source_target_pairs={{0,1},{1,0},{2,3},{3,2},{4,5},{5,4},{6,7},{7,6},{8,9},{9,8},{10,11... | collective-permute-start | bytes 393224 | tf_op jit(solution)/shard_map/ppermute | solution.py:979
  1237.5 10.8 copy-start.57
  1239.0 10.3 copy-start.56
  1260.0 10.3 copy-start.123
  1260.0 11.0 copy-start.122
  1260.0 11.6 copy-start.115
  1260.0 12.2 copy-start.89
  1260.1 13.8 %copy-start.1 = (bf16[1000,768]{1,0:T(8,128)(2,1)S(1)}, bf16[1000,768]{1,0:T(8,128)(2,1)}, u32[]{:S(2)}) copy-start(bf16[1000,768]{1,0:T(8,128)(2,1)} %param.33) | copy-start | bytes 4608004
  (114 other events, 419.7 us)
Sparse Core Ops, SparseCore 0:
  998.6 52.7 all-gather.2
  1054.9 65.9 all-gather.4

commit v4 on v3

--- a/solution.py
+++ b/solution.py
@@ -555,13 +555,7 @@
     return dot_f32(place_ref[...], spot_ref[...], 1, 0).astype(jnp.bfloat16)
 
 
-def conv_body(extra, slab_ref, place_ref, kernel_ref, sums_ref, out_ref, spot_ref):
-    sample = pl.program_id(0)
-
-    @pl.when(sample == 0)
-    def _():
-        spot_ref[...] = jnp.zeros_like(spot_ref)
-
+def conv_step(extra, sample, slab_ref, place_ref, kernel_ref, sums_ref, out_ref, spot_ref):
     rows = place_rows(slab_ref[0], place_ref, spot_ref)
     depth = rows.shape[1]
     total = None
@@ -579,27 +573,6 @@
         out_ref[0, PIXELS:, :] = jnp.broadcast_to(line, (CHUNK, line.shape[1])).astype(jnp.bfloat16)
 
 
-def convolve(slabs, place, kernel, sums, extra):
-    samples, pixels, width = slabs.shape
-    depth, width_out = kernel.shape[1:]
-    rows = PIXELS + (CHUNK if extra else 0)
-    return pl.pallas_call(
-        lambda *refs: conv_body(extra, *refs),
-        grid=(samples,),
-        in_specs=[
-            pl.BlockSpec((1, pixels, width), lambda step: (step, 0, 0)),
-            pl.BlockSpec(place.shape, lambda step: (0, 0)),
-            pl.BlockSpec((1, depth, width_out), lambda step: (step, 0, 0)),
-            pl.BlockSpec(sums.shape, lambda step: (0, 0)),
-        ],
-        out_specs=pl.BlockSpec((1, rows, width_out), lambda step: (step, 0, 0)),
-        out_shape=jax.ShapeDtypeStruct((samples, rows, width_out), jnp.bfloat16),
-        scratch_shapes=[pltpu.VMEM((3 * pixels, 3 * width), jnp.bfloat16)],
-        compiler_params=pltpu.CompilerParams(vmem_limit_bytes=32 * 2**20),
-        name="conv_forward",
-    )(slabs, place, kernel, sums)
-
-
 def fold_back(cotan, place_ref, kernel_ref, wide_ref, pixels, width):
     depth = 3 * width
     wide_ref[...] = jnp.zeros_like(wide_ref)
@@ -615,36 +588,13 @@
     return total.astype(jnp.bfloat16)
 
 
-def back_body(cotan_ref, place_ref, kernel_ref, out_ref, wide_ref):
-    pixels, width = out_ref.shape[1:]
-    out_ref[0] = fold_back(cotan_ref[0], place_ref, kernel_ref, wide_ref, pixels, width)
-
-
-def conv_back(cotans, place, kernel, pixels, width):
-    samples, rows, width_out = cotans.shape
-    depth = kernel.shape[1]
-    return pl.pallas_call(
-        back_body,
-        grid=(samples,),
-        in_specs=[
-            pl.BlockSpec((1, rows, width_out), lambda step: (step, 0, 0)),
-            pl.BlockSpec(place.shape, lambda step: (0, 0)),
-            pl.BlockSpec((1, depth, width_out), lambda step: (step, 0, 0)),
-        ],
-        out_specs=pl.BlockSpec((1, pixels, width), lambda step: (step, 0, 0)),
-        out_shape=jax.ShapeDtypeStruct((samples, pixels, width), jnp.bfloat16),
-        scratch_shapes=[pltpu.VMEM((PAD_ROWS, 3 * width), jnp.float32)],
-        compiler_params=pltpu.CompilerParams(vmem_limit_bytes=32 * 2**20),
-        name="conv_back",
-    )(cotans, place, kernel)
-
-
-def second_body(
+def second_step(
     slab_ref,
     tan_ref,
     place_ref,
     kernel_ref,
     cotan_ref,
+    side_ref,
     squares_ref,
     grad_ref,
     back_ref,
@@ -652,21 +602,17 @@
     spot_ref,
     wide_ref,
 ):
-    @pl.when(pl.program_id(0) == 0)
-    def _():
-        spot_ref[...] = jnp.zeros_like(spot_ref)
-
     pixels, width = slab_ref.shape[1:]
     depth = 3 * width
     rows = place_rows(slab_ref[0], place_ref, spot_ref)
     tan_rows = place_rows(tan_ref[0], place_ref, spot_ref)
-    line = cotan_ref[0, 2 * PIXELS : 2 * PIXELS + CHUNK, :][:1].astype(jnp.float32)
+    line = cotan_ref[0, PIXELS : PIXELS + CHUNK, :][:1].astype(jnp.float32)
     factor = 2.0 * lanes_wide(squares_ref[0], line.shape[1]) * line
     totals = None
     for shift in range(3):
         span = slice(shift * SIDE, shift * SIDE + PIXELS)
         grad = dot_f32(rows[span], cotan_ref[0, :PIXELS, :], 0, 0)
-        grad = grad + dot_f32(tan_rows[span], cotan_ref[0, PIXELS : 2 * PIXELS, :], 0, 0)
+        grad = grad + dot_f32(tan_rows[span], side_ref[0], 0, 0)
         for tap in range(3):
             at = shift * depth + tap * width
             own = kernel_ref[0, at : at + width, :].astype(jnp.float32)
@@ -677,48 +623,9 @@
             totals = term if totals is None else totals + term
     summed = jnp.sum(totals * line, axis=1, keepdims=True)
     scale_ref[0] = jnp.broadcast_to(summed, scale_ref.shape[1:])
-    for part in range(2):
-        back_ref[0, part * pixels : (part + 1) * pixels, :] = fold_back(
-            cotan_ref[0, part * PIXELS : (part + 1) * PIXELS, :],
-            place_ref,
-            kernel_ref,
-            wide_ref,
-            pixels,
-            width,
-        )
-
-
-def conv_second(slabs, tans, place, kernel, cotans, squares):
-    samples, pixels, width = slabs.shape
-    depth, width_out = kernel.shape[1:]
-    return pl.pallas_call(
-        second_body,
-        grid=(samples,),
-        in_specs=[
-            pl.BlockSpec((1, pixels, width), lambda step: (step, 0, 0)),
-            pl.BlockSpec((1, pixels, width), lambda step: (step, 0, 0)),
-            pl.BlockSpec(place.shape, lambda step: (0, 0)),
-            pl.BlockSpec((1, depth, width_out), lambda step: (step, 0, 0)),
-            pl.BlockSpec((1,) + cotans.shape[1:], lambda step: (step, 0, 0)),
-            pl.BlockSpec((1,) + squares.shape[1:], lambda step: (step, 0, 0)),
-        ],
-        out_specs=[
-            pl.BlockSpec((1, depth, width_out), lambda step: (step, 0, 0)),
-            pl.BlockSpec((1, 2 * pixels, width), lambda step: (step, 0, 0)),
-            pl.BlockSpec((1,) + squares.shape[1:], lambda step: (step, 0, 0)),
-        ],
-        out_shape=[
-            jax.ShapeDtypeStruct((samples, depth, width_out), jnp.bfloat16),
-            jax.ShapeDtypeStruct((samples, 2 * pixels, width), jnp.bfloat16),
-            jax.ShapeDtypeStruct(squares.shape, jnp.float32),
-        ],
-        scratch_shapes=[
-            pltpu.VMEM((3 * pixels, 3 * width), jnp.bfloat16),
-            pltpu.VMEM((PAD_ROWS, 3 * width), jnp.float32),
-        ],
-        compiler_params=pltpu.CompilerParams(vmem_limit_bytes=32 * 2**20),
-        name="conv_second",
-    )(slabs, tans, place, kernel, cotans, squares)
+    back_ref[0] = fold_back(
+        cotan_ref[0, :PIXELS, :], place_ref, kernel_ref, wide_ref, pixels, width
+    )
 
 
 def unmix_body(pieces, mix_ref, bank_ref, grad_ref, out_ref, select_ref):
@@ -1234,21 +1141,302 @@
     return gather_call(pieces, ("z", "y", "x"), arrays, shapes, call_id, "gather_weights")
 
 
-def gather_dp(values, call_id):
-    samples, rows, lanes = values.shape
-
-    def piece(sample, first, last, order):
-        return dict(
-            order=order,
-            of=lambda refs: refs[0].at[sample, :, first:last],
-            to=lambda refs, dp, mp: refs[0].at[dp * samples + sample, :, first:last],
-        )
-
-    cut = lanes * 3 // 4
-    pieces = [piece(sample, 0, cut, ("z", "y")) for sample in range(samples)]
-    pieces += [piece(sample, cut, lanes, ("y", "z")) for sample in range(samples)]
-    shapes = [(16 * samples, rows, lanes)]
-    return gather_call(pieces, ("z", "y"), [values], shapes, call_id, "gather_samples")[0]
+def plane_of(z, turn):
+    low = jnp.where(turn < 2, 1 - turn, turn)
+    high = jnp.where(turn < 2, 2 + turn, 3 - turn)
+    between = jnp.where(z == 1, low, high)
+    return jnp.where(z == 0, turn, jnp.where(z == PLANES - 1, PLANES - 1 - turn, between))
+
+
+class Stream:
+    def __init__(self, source, slots, sem, where):
+        self.source, self.slots, self.sem, self.where = source, slots, sem, where
+
+    def copy(self, turn):
+        slot = lax.rem(turn, 2)
+        return pltpu.make_async_copy(
+            self.source.at[self.where(turn)], self.slots.at[slot], self.sem.at[slot]
+        )
+
+    def take(self, turn, count):
+        self.copy(turn).wait()
+
+        @pl.when(turn + 1 < count)
+        def _():
+            self.copy(turn + 1).start()
+
+        return lax.rem(turn, 2)
+
+
+def consume_body(cut, samples, value_ref, landing, kernel_ref, slots, sems, work):
+    kernel_sem, send_sem, recv_sem, own_sem = sems
+    place = Place()
+    z, y, core, x = place.z, place.y, place.core, place.x
+    lanes = landing.shape[-1]
+    pieces = [(s, slice(0, cut), "zy") for s in range(samples)]
+    pieces += [(s, slice(cut, lanes), "yz") for s in range(samples)]
+    blocks = 2 * PLANES
+    count = 2 * samples * blocks
+
+    def chip_at(block):
+        return plane_of(z, block // 2), jnp.where(lax.rem(block, 2) == 1, 1 - y, y)
+
+    def first_sample(block, parity):
+        plane, row = chip_at(block)
+        other = jnp.where(parity == 1, 1 - core, core)
+        return ((plane * 2 + row) * 2 + other) * samples
+
+    def sample_at(turn):
+        block = turn // (2 * samples)
+        return first_sample(block, lax.rem(turn // samples, 2)) + lax.rem(turn, samples)
+
+    def sends(block, act):
+        plane, row = chip_at(block)
+        same_row = lax.rem(block, 2) == 0
+        up, down = (plane <= z) & (z < PLANES - 1), (plane >= z) & (z > 0)
+        for number, (s, span, order) in enumerate(pieces):
+            view = landing.at[first_sample(block, 0) + s, :, span]
+            if order == "zy":
+                ways = (up & same_row, down & same_row, same_row)
+            else:
+                ways = (up, down, block == 0)
+            targets = (
+                (z + 1, y, core, 0),
+                (z - 1, y, core, 0),
+                (z, 1 - y, core, 0),
+                (z, y, 1 - core, 1),
+            )
+            for slot, (dz, dy, dcore, parity) in enumerate(targets):
+                copy = pltpu.make_async_remote_copy(
+                    src_ref=view,
+                    dst_ref=view,
+                    send_sem=send_sem.at[block, number, slot],
+                    recv_sem=recv_sem.at[plane * 2 + row, number, parity],
+                    device_id=((dz * 2 + dy) * 2 + dcore, x),
+                    device_id_type=pl.DeviceIdType.MESH,
+                )
+                if slot < 3:
+                    pl.when(ways[slot])(lambda copy=copy: act(copy))
+                else:
+                    act(copy)
+
+    def arrive(block, parity):
+        plane, row = chip_at(block)
+        for number, (s, span, order) in enumerate(pieces):
+            view = landing.at[first_sample(block, parity) + s, :, span]
+            pltpu.make_async_remote_copy(
+                src_ref=view,
+                dst_ref=view,
+                send_sem=send_sem.at[block, number, 3],
+                recv_sem=recv_sem.at[plane * 2 + row, number, parity],
+                device_id=((z * 2 + y) * 2 + 1 - core, x),
+                device_id_type=pl.DeviceIdType.MESH,
+            ).wait_recv()
+
+    stream = Stream(kernel_ref, slots, kernel_sem, sample_at)
+    stream.copy(0).start()
+    own = pltpu.make_async_copy(
+        value_ref, landing.at[pl.ds(first_sample(0, 0), samples)], own_sem
+    )
+    own.start()
+    greet(place, ("z", "y"))
+    own.wait()
+    sends(0, lambda copy: copy.start())
+
+    @pl.loop(0, count)
+    def _(turn):
+        block = turn // (2 * samples)
+        step = lax.rem(turn, 2 * samples)
+
+        @pl.when((step == 0) & (block > 0))
+        def _():
+            arrive(block, 0)
+            sends(block, lambda copy: copy.start())
+
+        @pl.when(step == samples)
+        def _():
+            arrive(block, 1)
+
+        slot = stream.take(turn, count)
+        work(turn, sample_at(turn), slot, sample_at)
+
+    @pl.loop(0, blocks)
+    def _(block):
+        sends(block, lambda copy: copy.wait_send())
+
+
+def consume_scratch(samples, rows, lanes, kernel):
+    dma = pltpu.SemaphoreType.DMA
+    pieces = 2 * samples
+    return [
+        pltpu.VMEM((16 * samples, rows, lanes), jnp.bfloat16),
+        pltpu.VMEM((2,) + kernel.shape[1:], jnp.bfloat16),
+        dma((2,)),
+        dma((2 * PLANES, pieces, 4)),
+        dma((2 * PLANES, pieces, 2)),
+        dma,
+    ]
+
+
+def whole_specs(count):
+    return [pl.BlockSpec(memory_space=pltpu.VMEM)] * count
+
+
+HBM = pl.BlockSpec(memory_space=pl.ANY)
+
+
+def gather_back(cotan, place, kernel, pixels, width, call_id):
+    samples, rows, lanes = cotan.shape
+    total = kernel.shape[0]
+
+    def body(
+        cotan_ref,
+        kernel_ref,
+        place_ref,
+        out_ref,
+        all_ref,
+        landing,
+        slots,
+        s0,
+        s1,
+        s2,
+        s3,
+        wide_ref,
+        all_sem,
+    ):
+        def work(turn, sample, slot, sample_at):
+            out_ref[sample] = fold_back(
+                landing[sample], place_ref, slots.at[pl.ds(slot, 1)], wide_ref, pixels, width
+            )
+
+        consume_body(
+            lanes * 3 // 4,
+            samples,
+            cotan_ref,
+            landing,
+            kernel_ref,
+            slots,
+            (s0, s1, s2, s3),
+            work,
+        )
+        keep = pltpu.make_async_copy(landing, all_ref, all_sem)
+        keep.start()
+        keep.wait()
+
+    return pl.pallas_call(
+        body,
+        in_specs=[HBM, HBM] + whole_specs(1),
+        out_specs=whole_specs(1) + [HBM],
+        out_shape=[
+            jax.ShapeDtypeStruct((total, pixels, width), jnp.bfloat16),
+            jax.ShapeDtypeStruct((total, rows, lanes), jnp.bfloat16),
+        ],
+        scratch_shapes=consume_scratch(samples, rows, lanes, kernel)
+        + [pltpu.VMEM((PAD_ROWS, 3 * width), jnp.float32), pltpu.SemaphoreType.DMA],
+        compiler_params=pltpu.CompilerParams(
+            collective_id=call_id, has_side_effects=True, vmem_limit_bytes=40 * 2**20
+        ),
+        name="gather_back",
+    )(cotan, kernel, place)
+
+
+def gather_second(slabs, tans, place, kernel, cotan, sides, squares, call_id):
+    samples, rows, lanes = cotan.shape
+    total, pixels, width = slabs.shape
+
+    def body(
+        cotan_ref,
+        kernel_ref,
+        sides_ref,
+        slab_ref,
+        tan_ref,
+        place_ref,
+        squares_ref,
+        grad_ref,
+        back_ref,
+        scale_ref,
+        landing,
+        slots,
+        s0,
+        s1,
+        s2,
+        s3,
+        side_slots,
+        side_sem,
+        grad_slots,
+        grad_sem,
+        spot_ref,
+        wide_ref,
+    ):
+        spot_ref[...] = jnp.zeros_like(spot_ref)
+
+        def leave(slot, sample):
+            return pltpu.make_async_copy(
+                grad_slots.at[slot], grad_ref.at[sample], grad_sem.at[slot]
+            )
+
+        def work(turn, sample, slot, sample_at):
+            sides = Stream(sides_ref, side_slots, side_sem, sample_at)
+            pl.when(turn == 0)(lambda: sides.copy(0).start())
+            sides.take(turn, total)
+
+            @pl.when(turn >= 2)
+            def _():
+                leave(slot, sample).wait()
+
+            one = pl.ds(sample, 1)
+            second_step(
+                slab_ref.at[one],
+                tan_ref.at[one],
+                place_ref,
+                slots.at[pl.ds(slot, 1)],
+                landing.at[one],
+                side_slots.at[pl.ds(slot, 1)],
+                squares_ref.at[one],
+                grad_slots.at[pl.ds(slot, 1)],
+                back_ref.at[one],
+                scale_ref.at[one],
+                spot_ref,
+                wide_ref,
+            )
+            leave(slot, sample).start()
+
+        consume_body(
+            lanes * 3 // 4,
+            samples,
+            cotan_ref,
+            landing,
+            kernel_ref,
+            slots,
+            (s0, s1, s2, s3),
+            work,
+        )
+        for slot in range(2):
+            leave(slot, 0).wait()
+
+    return pl.pallas_call(
+        body,
+        in_specs=[HBM, HBM, HBM] + whole_specs(4),
+        out_specs=[HBM] + whole_specs(2),
+        out_shape=[
+            jax.ShapeDtypeStruct(kernel.shape, jnp.bfloat16),
+            jax.ShapeDtypeStruct((total, pixels, width), jnp.bfloat16),
+            jax.ShapeDtypeStruct(squares.shape, jnp.float32),
+        ],
+        scratch_shapes=consume_scratch(samples, rows, lanes, kernel)
+        + [
+            pltpu.VMEM((2,) + sides.shape[1:], jnp.bfloat16),
+            pltpu.SemaphoreType.DMA((2,)),
+            pltpu.VMEM((2,) + kernel.shape[1:], jnp.bfloat16),
+            pltpu.SemaphoreType.DMA((2,)),
+            pltpu.VMEM((3 * pixels, 3 * width), jnp.bfloat16),
+            pltpu.VMEM((PAD_ROWS, 3 * width), jnp.float32),
+        ],
+        compiler_params=pltpu.CompilerParams(
+            collective_id=call_id, has_side_effects=True, vmem_limit_bytes=48 * 2**20
+        ),
+        name="gather_second",
+    )(cotan, kernel, sides, slabs, tans, place, squares)
 
 
 def add_rows(total, part):
@@ -1262,16 +1450,23 @@
 
 def sum_body(
     cut,
-    part_ref,
+    extra,
+    kernel_ref,
+    slab_ref,
+    place_ref,
+    sums_ref,
     out_ref,
+    slots,
+    kernel_sem,
+    spot_ref,
     acc,
+    core_out,
     core_in,
     y_in,
     y_last,
     z_first,
     z_second,
     x_in,
-    load_sem,
     core_send,
     core_recv,
     y_send,
@@ -1282,8 +1477,8 @@
     x_recv,
 ):
     place = Place()
-    greet(place, ("z", "y", "x"))
     z, y, x = place.z, place.y, place.x
+    spot_ref[...] = jnp.zeros_like(spot_ref)
     wide, narrow = slice(0, cut), slice(cut, acc.shape[-1])
     finish = []
 
@@ -1304,40 +1499,66 @@
     other_y = (z, 1 - y, place.core, x)
     other_x = (z, y, place.core, 1 - x)
 
-    chunks = [(dest, 1 - y) for dest in (3, 0, 2, 1)] + [(dest, y) for dest in (3, 0, 2, 1)]
-    first = []
-    for number, (dest, side) in enumerate(chunks):
-        sent = remote(
-            part_ref.at[dest, side, 1 - place.core],
+    def chunk_at(chunk):
+        turn = lax.rem(chunk, PLANES)
+        dest = jnp.where(turn == 0, 3, jnp.where(turn == 1, 0, 4 - turn))
+        return dest, jnp.where(chunk < PLANES, 1 - y, y)
+
+    def sample_at(turn):
+        dest, side = chunk_at(turn // 4)
+        step = lax.rem(turn, 4)
+        owner = jnp.where(step < 2, 1 - place.core, place.core)
+        return ((dest * 2 + side) * 2 + owner) * 2 + lax.rem(step, 2)
+
+    stream = Stream(kernel_ref, slots, kernel_sem, sample_at)
+    stream.copy(0).start()
+    greet(place, ("z", "y", "x"))
+
+    def core_copy(chunk):
+        dest, side = chunk_at(chunk)
+        return remote(
+            core_out.at[dest, side],
             core_in.at[dest, side],
-            core_send.at[number],
-            core_recv.at[number],
+            core_send.at[chunk],
+            core_recv.at[chunk],
             other_core,
         )
-        sent.start()
-        mine = pltpu.make_async_copy(
-            part_ref.at[dest, side, place.core], acc.at[dest, side], load_sem.at[number]
-        )
-        mine.start()
-        first.append((sent, mine))
-
-    y_copies = []
-    for number, (dest, side) in enumerate(chunks):
-        sent, mine = first[number]
-        mine.wait()
-        sent.wait_recv()
-        add_rows(acc.at[dest, side], core_in.at[dest, side])
-        finish.append(sent)
-        if number < 4:
-            copy = remote(
-                acc.at[dest, side, :, :, wide],
-                y_in.at[dest],
-                y_send.at[dest],
-                y_recv.at[dest],
-                other_y,
+
+    def y_copy(dest):
+        return remote(
+            acc.at[dest, 1 - y, :, :, wide], y_in.at[dest], y_send.at[dest], y_recv.at[dest], other_y
+        )
+
+    @pl.loop(0, 16 * 2)
+    def _(turn):
+        chunk, step = turn // 4, lax.rem(turn, 4)
+        dest, side = chunk_at(chunk)
+        sample = sample_at(turn)
+        slot = stream.take(turn, 16 * 2)
+
+        def convolve(target):
+            conv_step(
+                extra,
+                sample,
+                slab_ref.at[pl.ds(sample, 1)],
+                place_ref,
+                slots.at[pl.ds(slot, 1)],
+                sums_ref,
+                target.at[dest, side, pl.ds(lax.rem(step, 2), 1)],
+                spot_ref,
             )
-            copy.start()
-            y_copies.append(copy)
+
+        pl.when(step < 2)(lambda: convolve(core_out))
+        pl.when(step >= 2)(lambda: convolve(acc))
+        pl.when(step == 1)(lambda: core_copy(chunk).start())
+
+        @pl.when(step == 3)
+        def _():
+            core_copy(chunk).wait_recv()
+            add_rows(acc.at[dest, side], core_in.at[dest, side])
+            pl.when(chunk < PLANES)(lambda: y_copy(dest).start())
+
+    y_copies = [y_copy(dest) for dest in (3, 0, 2, 1)]
 
     def along_z(slot, view, landing, dest):
         for way in (0, 1):
@@ -1403,17 +1624,26 @@
         else:
             item.wait_send()
 
-
-def sum_samples(partial, call_id):
-    samples, rows, lanes = partial.shape
+    @pl.loop(0, 2 * PLANES)
+    def _(chunk):
+        core_copy(chunk).wait_send()
+
+
+def conv_sum(slabs, place, kernel, sums, extra, call_id):
+    _, pixels, width = slabs.shape
+    rows, lanes = PIXELS + (CHUNK if extra else 0), kernel.shape[2]
     cut = lanes * 3 // 4
     bf16, dma = jnp.bfloat16, pltpu.SemaphoreType.DMA
     return pl.pallas_call(
-        lambda *refs: sum_body(cut, *refs),
-        in_specs=[pl.BlockSpec(memory_space=pl.ANY)],
+        lambda *refs: sum_body(cut, extra, *refs),
+        in_specs=[HBM] + whole_specs(3),
         out_specs=pl.BlockSpec(memory_space=pltpu.VMEM),
         out_shape=jax.ShapeDtypeStruct((rows, 2 * lanes), bf16),
         scratch_shapes=[
+            pltpu.VMEM((2,) + kernel.shape[1:], bf16),
+            dma((2,)),
+            pltpu.VMEM((3 * pixels, 3 * width), bf16),
+            pltpu.VMEM((PLANES, 2, 2, rows, lanes), bf16),
             pltpu.VMEM((PLANES, 2, 2, rows, lanes), bf16),
             pltpu.VMEM((PLANES, 2, 2, rows, lanes), bf16),
             pltpu.VMEM((PLANES, 2, rows, cut), bf16),
@@ -1421,7 +1651,6 @@
             pltpu.VMEM((2, PLANES, 2, rows, cut), bf16),
             pltpu.VMEM((2, PLANES, 2, 2, rows, lanes - cut), bf16),
             pltpu.VMEM((rows, lanes), bf16),
-            dma((8,)),
             dma((8,)),
             dma((8,)),
             dma((PLANES + 1,)),
@@ -1432,10 +1661,10 @@
             dma,
         ],
         compiler_params=pltpu.CompilerParams(
-            collective_id=call_id, has_side_effects=True, vmem_limit_bytes=40 * 2**20
+            collective_id=call_id, has_side_effects=True, vmem_limit_bytes=48 * 2**20
         ),
-        name="sum_samples",
-    )(partial.reshape(PLANES, 2, 2, 2, rows, lanes))
+        name="conv_sum",
+    )(kernel, slabs, place, sums)
 
 
 def sum_weights_body(parts, count, refs):
@@ -1755,8 +1984,7 @@
 
     input_own = pick(input_whole, mp).astype(float32)
     slabs_x = (raw_slabs.astype(float32) * scales_slab[:, None, :]).astype(bfloat16)
-    partial = convolve(slabs_x, place, kernel, sums_part, True)
-    summed = sum_samples(partial, 4).astype(float32)
+    summed = conv_sum(slabs_x, place, kernel, sums_part, True, 4).astype(float32)
     conv_out, sums = summed[:PIXELS], summed[PIXELS]
 
     (hidden_four, picture), pull = jax.vjp(
@@ -1765,11 +1993,12 @@
 
     dir_own = pick(penalty_dir, mp).astype(float32)
     grad_conv = pull((jnp.zeros_like(hidden_four), dir_own))[0]
-    grads_all = gather_dp(both_half(grad_conv.astype(bfloat16), mp), 2)
-
-    grad_moduled = from_slabs(conv_back(grads_all, place, kernel, half_px, slab), mp)
+    back_slabs, sides_all = gather_back(
+        both_half(grad_conv.astype(bfloat16), mp), place, kernel, half_px, slab, 2
+    )
+    grad_moduled = from_slabs(back_slabs, mp).astype(bfloat16).astype(float32)
     mask_own = pick(penalty_mask, mp).astype(float32)
-    tangent = penalty_weight * mask_own * grad_moduled.astype(bfloat16).astype(float32) * scales
+    tangent = penalty_weight * mask_own * grad_moduled * scales
 
     tan_moduled = (tangent * scales).astype(bfloat16)
     tan_other = swap_mp(tan_moduled)
@@ -1777,7 +2006,7 @@
         [jnp.where(mp == 0, tan_moduled, tan_other), jnp.where(mp == 0, tan_other, tan_moduled)]
     )
     slabs_t = to_slabs(tan_pair)
-    conv_tan = sum_samples(convolve(slabs_t, place, kernel, sums_part, False), 5).astype(float32)
+    conv_tan = conv_sum(slabs_t, place, kernel, sums_part, False, 5).astype(float32)
 
     (ignored_out, ignored_pic, ignored_tan), pull_joint = jax.vjp(
         lambda *given: layer_joint(*given, noise),
@@ -1789,7 +2018,7 @@
         weights,
     )
     cot_own = own_whole(cot_feat, mp).astype(float32)
-    grad_main, grad_side, grad_sums, grad_text, grad_small, grad_weights = pull_joint(
+    grad_main, _, grad_sums, grad_text, grad_small, grad_weights = pull_joint(
         (cot_own, pick(cot_rgb, mp).astype(float32), dir_own)
     )
 
@@ -1813,12 +2042,9 @@
     )
 
     lines = jnp.broadcast_to(grad_sums[None], (CHUNK,) + grad_sums.shape)
-    wide = jnp.concatenate(
-        [grad_main.astype(bfloat16), grad_side.astype(bfloat16), lines.astype(bfloat16)], axis=0
-    )
-    wide_all = gather_dp(both_half(wide, mp), 3)
-    grad_kernel, both_back, scale_sums = conv_second(
-        slabs_x, slabs_t, place, kernel, wide_all, scales_two
+    wide = jnp.concatenate([grad_main.astype(bfloat16), lines.astype(bfloat16)], axis=0)
+    grad_kernel, back_slabs, scale_sums = gather_second(
+        slabs_x, slabs_t, place, kernel, both_half(wide, mp), sides_all, scales_two, 3
     )
     grad_scales_slab = 2.0 * scales_slab * scale_sums[:, :, 0]
     bank_grad, select_products = unmix_kernels(mix, bank_rows, grad_kernel)
@@ -1826,10 +2052,9 @@
     grad_select = jnp.einsum(
         "brkr->bk", select_products.reshape(sample_count, CHUNK, -1, CHUNK)
     )
-    both_back = from_slabs(both_back, mp).astype(bfloat16).astype(float32)
-    back_main, back_side = both_back[:half_px], both_back[half_px:]
+    back_main = from_slabs(back_slabs, mp).astype(bfloat16).astype(float32)
     input_grad = back_main * scales
-    grad_scales = jnp.sum(back_main * input_own + back_side * tangent, axis=0)
+    grad_scales = jnp.sum(back_main * input_own + grad_moduled * tangent, axis=0)
 
     grad_bias, grad_strength, grad_rgb_scales, grad_rgb_weight = grad_small
     row = jnp.concatenate(

time: 1290 us -> 1160 us (0.90)
  Pallas kernels: 914 us -> 786 us
  waiting for transfers between devices: 47.6 us -> 27.9 us
  starting transfers between devices: 37.9 us -> 56.1 us
    pallas_call x3 -> x1, Pallas kernels: 294 us -> 132 us  [gather_call(): pl.pallas_call(body, in_specs=[pl.BlockSpec(memory_space=pl.ANY)] * count...]
    pallas_call x6 -> x4, Pallas kernels: 304 us -> 337 us  [the longest x2 199 us: conv_sum(): pl.pallas_call(lambda *refs: sum_body(cut, extra, *refs), in_specs=[HBM]...]
    all_to_all x2, starting transfers between devices: 20.9 us -> 36.3 us  [from_slabs(): parts = lax.all_to_all(parts, 'dp', 0, 0, tiled=True)]
    unnamed x354 -> x390, local copies, waits for them, and re-layouts: 50.6 us -> 42.2 us
  transfers between devices with their start and end apart: 15 -> 15, of which waited for: 8 -> 7; matrix products, arithmetic and copies ran while one was open for 9% -> 11% of each run, Pallas kernels for 34% -> 36%
where the time goes in v4:
time: 1160 us; the launch traced here: 1150 us
  Pallas kernels  786 us (68%)
  matrix products  164 us (14%)
  local copies, waits for them, and re-layouts  64.7 us (6%)
  starting transfers between devices  56.1 us (5%)
  waiting for transfers between devices  27.9 us (2%)
  other arithmetic  27.3 us (2%)
  between operations  18.2 us (2%)
    pallas_call x2, Pallas kernels, conv_sum(): pl.pallas_call(lambda *refs: sum_body(cut, extra, *refs), in_specs=[HBM]...  199 us
    pallas_call x1, Pallas kernels, sum_weights(): pl.pallas_call(lambda *refs: sum_weights_body(parts, count, refs), in_spe...  180 us
    pallas_call x1, Pallas kernels, gather_call(): pl.pallas_call(body, in_specs=[pl.BlockSpec(memory_space=pl.ANY)] * count...  132 us
    pallas_call x1, Pallas kernels, gather_second(): pl.pallas_call(body, in_specs=[HBM, HBM, HBM] + whole_specs(4), out_specs...  70.2 us
    pallas_call x1, Pallas kernels, gather_back(): pl.pallas_call(body, in_specs=[HBM, HBM] + whole_specs(1), out_specs=whol...  67.5 us
    dot_general x27, matrix products, dot_wide(): lax.dot_general(left.astype(jnp.bfloat16), right.astype(jnp.bfloat16), ((...  65.9 us
    unnamed x390, local copies, waits for them, and re-layouts  42.2 us
    pallas_call x4, Pallas kernels, per_head(): pl.pallas_call(body, grid=(arrays[0].shape[1] // lanes,), in_specs=[pl.Bl...  41.2 us
  transfers between devices with their start and end apart: 15, of which 7 were waited for; matrix products, arithmetic and copies ran while one was open for 11% of the time, Pallas kernels for 36%

profile of v4, /device:TPU:9, one launch (start us, length us, event | category | flops | bytes accessed | tf_op | source)
XLA Modules:
  0.0 1149.2 jit_solution(15398056259451098996)
XLA Ops:
  7.3 5.4 all_gather.9
  15.0 7.6 all-to-all-start
  25.2 132.2 %gather_weights.1 = (bf16[1024,4096]{1,0:T(8,128)(2,1)}, bf16[1024,4096]{1,0:T(8,128)(2,1)}, bf16[1024,1024]{1,0:T(8,128)(2,1)}, bf16[1024,1024]{1,0:T(8,128)(2,...) custom-call(bf16[64,2048]{1,0:T(8,128)(2,1)} %refs_0_.1, ...), custom_call_target="tpu_custom_call" | custom-call | tf_op jit(solution)/shard_map/gather_weights/pallas_call | solution.py:1096
  161.9 2.2 convolution_add_fusion.10
  166.5 3.3 mul.981.refs_0_
  172.7 2.3 copy-done.2
  175.0 13.4 %mix_kernels.1 = (bf16[32,576,512]{2,1,0:T(8,128)(2,1)}, f32[32,512]{1,0:T(8,128)S(1)}) custom-call(bf16[512,256]{1,0:T(8,128)(2,1)S(1)} %mul.981.refs_0_, bf16[8,576,512]{2,1,0:T(8,128)(2,1)S(1)} %bitcast.204, f32[32,64,128]{2,1,0:T(8,128)S(1)} %broadcast_in_dim.30.refs_2_.squares_ref), custom_call_target="tpu_custom_call" | custom-call | tf_op jit(solution)/shard_map/mix_kernels/pallas_call | solution.py:528
  192.0 104.1 %conv_sum.2 = bf16[272,1024]{1,0:T(8,128)(2,1)S(1)} custom-call(bf16[32,576,512]{2,1,0:T(8,128)(2,1)} %get-tuple-element.65.refs_0_.kernel_ref, bf16[32,64,64]{2,1,0:T(8,128)(2,1)S(1)} %fusion.50.refs_1_.slab_ref, bf16[288,192]{1,0:T(8,128)(2,1)S(1)} %copy-done.11, f32[32,512]{1,0:T(8,128)S(1)} %get-tuple-element.66.refs_3_), custom_call_target="tpu_custom_call" | custom-call | tf_op jit(solution)/shard_map/conv_sum/pallas_call | solution.py:1637
  297.1 1.8 copy-done.64
  300.3 11.5 %jvp_self_heads_.1 = bf16[256,1024]{1,0:T(8,128)(2,1)S(1)} custom-call(bf16[256,1024]{1,0:T(8,128)(2,1)S(1)} %convolution_convert_fusion.19.refs_0_, bf16[256,1024]{1,0:T(8,128)(2,1)S(1)} %convolution_convert_fusion.18.refs_1_.refs_2_), custom_call_target="tpu_custom_call" | custom-call | tf_op jit(solution)/shard_map/jvp(self_heads)/pallas_call | solution.py:787
  313.5 7.4 jvp_cross_heads_.1
  321.8 4.4 fusion.54
  326.2 12.1 %multiply_reduce_fusion.18 = (f32[256]{0:T(256)S(1)}, f32[256,1024]{1,0:T(8,128)}) fusion(f32[256,1024]{1,0:T(8,128)} %copy-done.36, bf16[1024,4096]{1,0:T(8,128)(2,1)} %get-tuple-element.74, f32[256,4096]{1,0:T(8,128)} %fusion.54, bf16[256,1024]{1,0:T(8,128)(2,1)S(1)} %get-tuple-element.283, bf16[1024,4096]{1,0:T(8,128)(2,1)} %get-tuple-element.75), kind=kOutput, calls=%fused_computation.156 | convolution fusion | flops 4316463104 | bytes 23593984 | tf_op jit(solution)/shard_map/transpose(jvp())/dot_general | solution.py:842
  338.3 2.3 add_add_fusion.11
  341.6 11.2 transpose_jvp_cross_heads_pull__.1
  356.0 14.6 %transpose_jvp_self_heads_pull__.1 = (bf16[256,1024]{1,0:T(8,128)(2,1)S(1)}, bf16[256,1024]{1,0:T(8,128)(2,1)S(1)}) custom-call(bf16[256,1024]{1,0:T(8,128)(2,1)S(1)} %convolution_convert_fusion.19.refs_0_, bf16[256,1024]{1,0:T(8,128)(2,1)S(1)} %convolution_convert_fusion.18.refs_1_.refs_2_, bf16[256,1024]{1,0:T(8,128)(2,1)S(1)} %convolution_convert_fusion.15.refs_2_), custom_call_target="tpu_custom_call" | custom-call | tf_op jit(solution)/shard_map/transpose(jvp(self_heads_pull))/pallas_call | solution.py:832
  376.9 3.4 collective-permute-done.3
  380.6 67.5 %gather_back.1 = (bf16[32,64,64]{2,1,0:T(8,128)(2,1)S(1)}, bf16[32,256,512]{2,1,0:T(8,128)(2,1)S(1)}) custom-call(bf16[2,256,512]{2,1,0:T(8,128)(2,1)S(1)} %pad_maximum_fusion.18.cotan_ref, bf16[32,576,512]{2,1,0:T(8,128)(2,1)} %get-tuple-element.65.refs_0_.kernel_ref, bf16[288,192]{1,0:T(8,128)(2,1)S(1)} %copy-done.11), custom_call_target="tpu_custom_call" | custom-call | tf_op jit(solution)/shard_map/gather_back/pallas_call | solution.py:1326
  448.1 3.2 copy-done.6
  452.5 17.0 %all-to-all-start.1 = ((bf16[16,2,4096]{2,1,0:T(2,128)(2,1)}), bf16[16,2,4096]{2,1,0:T(2,128)(2,1)S(1)}, u32[]{:S(2)}, u32[]{:S(2)}) async-start(bf16[16,2,4096]{2,1,0:T(2,128)(2,1)} %reshape.425), calls=%async_computation.1 | async-start | bytes 524288 | tf_op jit(solution)/shard_map/all_to_all | solution.py:920
  473.4 4.8 all-to-all-done.1
  480.7 4.1 collective-permute-done.4
  487.0 2.7 collective-permute-done.5
  491.5 5.2 all-to-all-start.2
  496.7 11.5 fusion.53
  508.5 94.8 %conv_sum.3 = bf16[256,1024]{1,0:T(8,128)(2,1)S(1)} custom-call(bf16[32,576,512]{2,1,0:T(8,128)(2,1)} %get-tuple-element.65.refs_0_.kernel_ref, bf16[32,64,64]{2,1,0:T(8,128)(2,1)S(1)} %bitcast.206, bf16[288,192]{1,0:T(8,128)(2,1)S(1)} %copy-done.11, f32[32,512]{1,0:T(8,128)S(1)} %get-tuple-element.66.refs_3_), custom_call_target="tpu_custom_call" | custom-call | tf_op jit(solution)/shard_map/conv_sum/pallas_call | solution.py:1637
  608.3 13.4 %jvp_self_heads_joint_.1 = (bf16[256,1024]{1,0:T(8,128)(2,1)S(1)}, bf16[256,1024]{1,0:T(8,128)(2,1)S(1)}) custom-call(bf16[256,1024]{1,0:T(8,128)(2,1)S(1)} %convolution_convert_fusion.19.refs_0_, bf16[256,1024]{1,0:T(8,128)(2,1)S(1)} %convolution_convert_fusion.14.refs_1_, bf16[256,1024]{1,0:T(8,128)(2,1)S(1)} %convolution_convert_fusion.18.refs_1_.refs_2_, ...), custom_call_target="tpu_custom_call" | custom-call | tf_op jit(solution)/shard_map/jvp(self_heads_joint)/pallas_call | solution.py:787
  627.1 8.9 jvp_cross_heads_joint_.1
  638.4 2.3 fusion.163
  640.8 15.5 %add_convert_fusion.2 = (bf16[256,4096]{1,0:T(8,128)(2,1)}, bf16[256,4096]{1,0:T(8,128)(2,1)}, bf16[256,4096]{1,0:T(8,128)(2,1)}, bf16[256,4096]{1,0:T(8,128)(2,1)}) fusion(f32[256,4096]{1,0:T(8,128)S(1)} %fusion.163, f32[512,4096]{1,0:T(8,128)} %fusion.53, bf16[256,1024]{1,0:T(8,128)(2,1)S(1)} %get-tuple-element.243, bf16[1024,4096]{1,0:T(8,128)(2,1)} %get-tuple-element.74), kind=kOutput, calls=%fused_computation.27 | convolution fusion | flops 2205155328 | bytes 29884416 | tf_op jit(solution)/shard_map/jvp()/dot_general | solution.py:395
  656.3 10.5 fusion.17
  666.8 2.1 multiply_reduce_fusion.13
  669.1 5.9 convolution_add_fusion.8
  677.9 13.3 %transpose_jvp_cross_heads_joint_pull__.1 = (bf16[256,1024]{1,0:T(8,128)(2,1)S(1)}, bf16[256,1024]{1,0:T(8,128)(2,1)S(1)}, bf16[64,1024]{1,0:T(8,128)(2,1)S(1)}, bf16[64,1024]{1,0:T(8,128)(2,1)S(1)}) custom-call(bf16[256,1024]{1,0:T(8,128)(2,1)S(1)} %convolution_convert_fusion.12.refs_0_, bf16[256,1024]{1,0:T(8,128)(2,1)S(1)} %convolution_convert_fusion.11.refs_1_, ...), custom_call_target="tpu_custom_call" | custom-call | tf_op jit(solution)/shard_map/transpose(jvp(cross_heads_joint_pull))/pallas_call | solution.py:863
  696.2 26.3 %transpose_jvp_self_heads_joint_pull__.1 = (bf16[256,1024]{1,0:T(8,128)(2,1)S(1)}, bf16[256,1024]{1,0:T(8,128)(2,1)S(1)}, bf16[256,1024]{1,0:T(8,128)(2,1)S(1)}, bf16[256,1024]{1,0:T(8,128)(2,1)S(1)}) custom-call(bf16[256,1024]{1,0:T(8,128)(2,1)S(1)} %convolution_convert_fusion.19.refs_0_, bf16[256,1024]{1,0:T(8,128)(2,1)S(1)} %convolution_convert_fusion.14.refs_1_, ...), custom_call_target="tpu_custom_call" | custom-call | tf_op jit(solution)/shard_map/transpose(jvp(self_heads_joint_pull))/pallas_call | solution.py:856
  722.7 2.2 copy-done.67
  728.4 3.4 multiply_reduce_fusion.4
  733.5 6.7 convolution_add_fusion.7
  741.5 70.2 %gather_second.1 = (bf16[32,576,512]{2,1,0:T(8,128)(2,1)}, bf16[32,64,64]{2,1,0:T(8,128)(2,1)S(1)}, f32[32,64,128]{2,1,0:T(8,128)S(1)}) custom-call(bf16[2,272,512]{2,1,0:T(8,128)(2,1)S(1)} %pad_maximum_fusion.16.cotan_ref, bf16[32,576,512]{2,1,0:T(8,128)(2,1)} %get-tuple-element.65.refs_0_.kernel_ref, bf16[32,256,512]{2,1,0:T(8,128)(2,1)} %copy-done.6, ...), custom_call_target="tpu_custom_call" | custom-call | tf_op jit(solution)/shard_map/gather_second/pallas_call | solution.py:1417
  812.9 19.3 %all-to-all-start.3 = ((bf16[16,2,4096]{2,1,0:T(2,128)(2,1)}), bf16[16,2,4096]{2,1,0:T(2,128)(2,1)S(1)}, u32[]{:S(2)}, u32[]{:S(2)}) async-start(bf16[16,2,4096]{2,1,0:T(2,128)(2,1)} %reshape.429), calls=%async_computation.3 | async-start | bytes 524288 | tf_op jit(solution)/shard_map/all_to_all | solution.py:920
  832.3 2.3 fusion.83
  835.6 2.3 copy-done.3
  838.0 17.1 %unmix_kernels.1 = (f32[8,576,512]{2,1,0:T(8,128)}, f32[512,128]{1,0:T(8,128)S(1)}) custom-call(bf16[512,256]{1,0:T(8,128)(2,1)S(1)} %copy-done.10, bf16[8,576,512]{2,1,0:T(8,128)(2,1)S(1)} %bitcast.205, bf16[32,576,512]{2,1,0:T(8,128)(2,1)} %get-tuple-element.93.refs_2_), custom_call_target="tpu_custom_call" | custom-call | tf_op jit(solution)/shard_map/unmix_kernels/pallas_call | solution.py:653
  855.1 1.9 reshape.410
  859.3 1.9 select_reduce_fusion
  864.9 7.4 fusion.29
  876.3 10.8 collective-permute-done
  890.4 3.9 convolution_convert_fusion.4.refs_4_
  894.2 1.7 convolution_convert_fusion.7.refs_8_
  896.0 1.7 convolution_convert_fusion.8.refs_7_
  897.7 2.7 convolution_convert_fusion.3.refs_5_
  900.5 2.6 convolution_convert_fusion.6.refs_2_
  903.1 2.7 convolution_convert_fusion.5.refs_3_
  906.2 7.3 convolution_convert_fusion.refs_1_
  913.6 6.9 convolution_convert_fusion.1.refs_0_
  921.0 2.6 convolution_convert_fusion.2.refs_6_
  923.6 179.6 %sum_weights.1 = (f32[64,2048]{1,0:T(8,128)}, f32[64,2048]{1,0:T(8,128)}, f32[64,512]{1,0:T(8,128)}, f32[64,512]{1,0:T(8,128)}, f32[64,512]{1,0:T(8,128)}, /*ind...) custom-call(bf16[1024,4096]{1,0:T(8,128)(2,1)} %convolution_convert_fusion.1.refs_0_, ...), custom_call_target="tpu_custom_call" | custom-call | tf_op jit(solution)/shard_map/sum_weights/pallas_call | solution.py:1863
  1108.0 1.9 reshape.413
  1109.9 1.8 reduce_sum.338
  1111.7 1.8 copy.83
  1119.6 2.4 fusion.70
  1122.0 3.2 fusion.72
  1125.1 3.2 fusion.77
  1128.4 7.6 fusion
  (561 shorter events, 103.6 us)
Async XLA Ops:
  7.2 162.7 %copy-start = (bf16[1000,768]{1,0:T(8,128)(2,1)S(1)}, bf16[1000,768]{1,0:T(8,128)(2,1)}, u32[]{:S(2)}) copy-start(bf16[1000,768]{1,0:T(8,128)(2,1)} %param.33) | copy-start | bytes 4608004
  7.2 15.4 %copy-start.168 = (s32[2,64]{1,0:T(2,128)S(1)}, s32[2,64]{1,0:T(2,128)}, u32[]{:S(2)}) copy-start(s32[2,64]{1,0:T(2,128)} %param.29) | copy-start | bytes 1540
  7.2 16.0 %copy-start.169 = (s32[2]{0:T(128)S(1)}, s32[2]{0:T(128)}, u32[]{:S(2)}) copy-start(s32[2]{0:T(128)} %param.30) | copy-start | bytes 28
  7.2 17.2 %copy-start.161 = (bf16[2,3,256]{2,0,1:T(2,128)(2,1)S(1)}, bf16[2,3,256]{2,0,1:T(2,128)(2,1)}, u32[]{:S(2)}) copy-start(bf16[2,3,256]{2,0,1:T(2,128)(2,1)} %param.52) | copy-start | bytes 9220
  7.2 17.3 %copy-start.167 = (s32[2]{0:T(128)S(1)}, s32[2]{0:T(128)}, u32[]{:S(2)}) copy-start(s32[2]{0:T(128)} %param.28) | copy-start | bytes 28
  7.3 17.9 %copy-start.163 = (bf16[1024]{0:T(1024)(128)(2,1)S(1)}, bf16[1024]{0:T(1024)(128)(2,1)}, u32[]{:S(2)}) copy-start(bf16[1024]{0:T(1024)(128)(2,1)} %param.38) | copy-start | bytes 6148
  7.3 17.9 %copy-start.164 = (bf16[1024]{0:T(1024)(128)(2,1)S(1)}, bf16[1024]{0:T(1024)(128)(2,1)}, u32[]{:S(2)}) copy-start(bf16[1024]{0:T(1024)(128)(2,1)} %param.39) | copy-start | bytes 6148
  13.9 146.6 %copy-start.134 = (bf16[512,8]{0,1:T(8,128)(2,1)S(1)}, bf16[512,8]{0,1:T(8,128)(2,1)}, u32[]{:S(2)}) copy-start(bf16[512,8]{0,1:T(8,128)(2,1)} %param.34) | copy-start | bytes 24580
  15.0 149.1 %copy-start.49 = (bf16[512,1024]{1,0:T(8,128)(2,1)S(1)}, bf16[512,1024]{1,0:T(8,128)(2,1)}, u32[]{:S(2)}) copy-start(bf16[512,1024]{1,0:T(8,128)(2,1)} %param.36) | copy-start | bytes 3145732
  15.0 175.5 %all-to-all-start = ((bf16[16,2,4096]{2,1,0:T(2,128)(2,1)}), bf16[16,2,4096]{2,1,0:T(2,128)(2,1)}, u32[]{:S(2)}, u32[]{:S(2)}) async-start(bf16[16,2,4096]{2,1,0:T(2,128)(2,1)} %reshape.423), calls=%async_computation | async-start | bytes 524288 | tf_op jit(solution)/shard_map/all_to_all | solution.py:912
  24.5 578.9 %copy-start.150 = (f32[256]{0:T(256)}, f32[256]{0:T(256)S(1)}, u32[]{:S(2)}) copy-start(f32[256]{0:T(256)S(1)} %fusion.111) | copy-start | bytes 3076
  24.5 163.9 %copy-start.140 = (bf16[1,3,256]{2,0,1:T(2,128)(2,1)}, bf16[1,3,256]{2,0,1:T(2,128)(2,1)S(1)}, u32[]{:S(2)}) copy-start(bf16[1,3,256]{2,0,1:T(2,128)(2,1)S(1)} %constant_dynamic-slice_fusion.4) | copy-start | bytes 4612
  25.1 578.2 %copy-start.123 = (f32[1024]{0:T(1024)}, f32[1024]{0:T(1024)S(1)}, u32[]{:S(2)}) copy-start(f32[1024]{0:T(1024)S(1)} %convert_element_type.333) | copy-start | bytes 12292
  25.2 578.2 %copy-start.125 = (f32[1024]{0:T(1024)}, f32[1024]{0:T(1024)S(1)}, u32[]{:S(2)}) copy-start(f32[1024]{0:T(1024)S(1)} %convert_element_type.335) | copy-start | bytes 12292
  170.3 19.8 %copy-start.54 = (bf16[64,768]{1,0:T(8,128)(2,1)}, bf16[64,768]{1,0:T(8,128)(2,1)S(1)}, u32[]{:S(2)}) copy-start(bf16[64,768]{1,0:T(8,128)(2,1)S(1)} %convolution_convert_fusion.22) | copy-start | bytes 294916
  171.5 20.3 %copy-start.108 = (f32[32,64]{1,0:T(8,128)}, f32[32,64]{1,0:T(8,128)S(1)}, u32[]{:S(2)}) copy-start(f32[32,64]{1,0:T(8,128)S(1)} %get-tuple-element.231) | copy-start | bytes 24580
  172.3 313.0 %copy-start.120 = (f32[1,1024]{1,0:T(1,128)}, f32[1,1024]{1,0:T(1,128)S(1)}, u32[]{:S(2)}) copy-start(f32[1,1024]{1,0:T(1,128)S(1)} %fusion.88) | copy-start | bytes 12292
  175.0 13.4 %copy-start.4 = (f32[32,64,128]{2,1,0:T(8,128)}, f32[32,64,128]{2,1,0:T(8,128)S(1)}, u32[]{:S(2)}) copy-start(f32[32,64,128]{2,1,0:T(8,128)S(1)} %broadcast_in_dim.30.refs_2_.squares_ref) | copy-start | bytes 3145732
  175.0 13.4 %copy-start.112 = (bf16[3,1024]{1,0:T(4,128)(2,1)S(1)}, bf16[3,1024]{1,0:T(4,128)(2,1)}, u32[]{:S(2)}) copy-start(bf16[3,1024]{1,0:T(4,128)(2,1)} %param.37) | copy-start | bytes 18436
  175.0 15.1 %copy-start.46 = (bf16[768,1024]{1,0:T(8,128)(2,1)S(1)}, bf16[768,1024]{1,0:T(8,128)(2,1)}, u32[]{:S(2)}) copy-start(bf16[768,1024]{1,0:T(8,128)(2,1)} %get-tuple-element.72) | copy-start | bytes 4718596
  190.1 136.1 %copy-start.82 = (bf16[256,1024]{1,0:T(8,128)(2,1)}, bf16[256,1024]{1,0:T(8,128)(2,1)S(1)}, u32[]{:S(2)}) copy-start(bf16[256,1024]{1,0:T(8,128)(2,1)S(1)} %get-tuple-element.283) | copy-start | bytes 1572868
  192.0 104.1 %copy-start.7 = (bf16[32,64,64]{2,1,0:T(8,128)(2,1)}, bf16[32,64,64]{2,1,0:T(8,128)(2,1)S(1)}, u32[]{:S(2)}) copy-start(bf16[32,64,64]{2,1,0:T(8,128)(2,1)S(1)} %fusion.50.refs_1_.slab_ref) | copy-start | bytes 786436
  296.3 307.1 %copy-start.106 = (f32[1,1024]{1,0:T(1,128)}, f32[1,1024]{1,0:T(1,128)S(1)}, u32[]{:S(2)}) copy-start(f32[1,1024]{1,0:T(1,128)S(1)} %fusion.116) | copy-start | bytes 12292
  296.9 15.0 %copy-start.22 = (f32[256,1024]{1,0:T(8,128)}, f32[256,1024]{1,0:T(8,128)S(1)}, u32[]{:S(2)}) copy-start(f32[256,1024]{1,0:T(8,128)S(1)} %get-tuple-element.229) | copy-start | bytes 3145732
  296.9 76.5 %copy-start.146 = (f32[256]{0:T(256)}, f32[256]{0:T(256)S(1)}, u32[]{:S(2)}) copy-start(f32[256]{0:T(256)S(1)} %get-tuple-element.228) | copy-start | bytes 3076
  296.9 307.3 %copy-start.136 = (f32[256]{0:T(256)}, f32[256]{0:T(256)S(1)}, u32[]{:S(2)}) copy-start(f32[256]{0:T(256)S(1)} %fusion.117) | copy-start | bytes 3076
  296.9 24.9 %slice-start = ((s8[8388608]{0:T(1024)(128)(4,1)}), s8[4194304]{0:T(1024)(128)(4,1)S(1)}, s32[]{:S(2)}) async-start(s8[8388608]{0:T(1024)(128)(4,1)} %bitcast.210), calls=%async_computation.6 | async-start | bytes 8388608
  299.6 12.3 %copy-start.25 = (bf16[1024,1024]{1,0:T(8,128)(2,1)S(1)}, bf16[1024,1024]{1,0:T(8,128)(2,1)}, u32[]{:S(2)}) copy-start(bf16[1024,1024]{1,0:T(8,128)(2,1)} %get-tuple-element.69) | copy-start | bytes 6291460
  300.3 12.4 %copy-start.39 = (bf16[1024,1024]{1,0:T(8,128)(2,1)S(1)}, bf16[1024,1024]{1,0:T(8,128)(2,1)}, u32[]{:S(2)}) copy-start(bf16[1024,1024]{1,0:T(8,128)(2,1)} %get-tuple-element.70) | copy-start | bytes 6291460
  340.9 11.9 %copy-start.32 = (f32[256,1024]{1,0:T(8,128)S(1)}, f32[256,1024]{1,0:T(8,128)}, u32[]{:S(2)}) copy-start(f32[256,1024]{1,0:T(8,128)} %copy-done.31) | copy-start | bytes 3145732
  340.9 11.9 %copy-start.40 = (bf16[1024,1024]{1,0:T(8,128)(2,1)S(1)}, bf16[1024,1024]{1,0:T(8,128)(2,1)}, u32[]{:S(2)}) copy-start(bf16[1024,1024]{1,0:T(8,128)(2,1)} %get-tuple-element.70) | copy-start | bytes 6291460
  355.3 15.4 %copy-start.65 = (bf16[1024,1024]{1,0:T(8,128)(2,1)S(1)}, bf16[1024,1024]{1,0:T(8,128)(2,1)}, u32[]{:S(2)}) copy-start(bf16[1024,1024]{1,0:T(8,128)(2,1)} %get-tuple-element.68) | copy-start | bytes 6291460
  373.4 230.8 %copy-start.152 = (f32[256]{0:T(256)}, f32[256]{0:T(256)S(1)}, u32[]{:S(2)}) copy-start(f32[256]{0:T(256)S(1)} %get-tuple-element.227) | copy-start | bytes 3076
  374.7 5.7 collective-permute-start.3
  375.9 103.8 %collective-permute-start.2 = (bf16[256,512]{1,0:T(8,128)(2,1)}, bf16[256,512]{1,0:T(8,128)(2,1)}, u32[]{:S(2)}, u32[]{:S(2)}) collective-permute-start(bf16[256,512]{1,0:T(8,128)(2,1)} %dynamic-slice_bitcast_fusion), channel_id=1, source_target_pairs={{0,1},{1,0},{2,3},{3,2},{4,5},{5,4},{6,7},{7,6},{8,9},{9,8},{10,11... | collective-permute-start | bytes 786440 | tf_op jit(solution)/shard_map/ppermute | solution.py:886
  380.6 88.9 %copy-start.162 = (bf16[2,3,256]{2,0,1:T(2,128)(2,1)S(1)}, bf16[2,3,256]{2,0,1:T(2,128)(2,1)}, u32[]{:S(2)}) copy-start(bf16[2,3,256]{2,0,1:T(2,128)(2,1)} %param.51) | copy-start | bytes 9220
  380.6 90.8 %copy-start.170 = (s32[2]{0:T(128)S(1)}, s32[2]{0:T(128)}, u32[]{:S(2)}) copy-start(s32[2]{0:T(128)} %param.31) | copy-start | bytes 28
  452.5 25.7 %all-to-all-start.1 = ((bf16[16,2,4096]{2,1,0:T(2,128)(2,1)}), bf16[16,2,4096]{2,1,0:T(2,128)(2,1)S(1)}, u32[]{:S(2)}, u32[]{:S(2)}) async-start(bf16[16,2,4096]{2,1,0:T(2,128)(2,1)} %reshape.425), calls=%async_computation.1 | async-start | bytes 524288 | tf_op jit(solution)/shard_map/all_to_all | solution.py:920
  469.5 15.8 %copy-start.142 = (bf16[1,3,256]{2,0,1:T(2,128)(2,1)}, bf16[1,3,256]{2,0,1:T(2,128)(2,1)S(1)}, u32[]{:S(2)}) copy-start(bf16[1,3,256]{2,0,1:T(2,128)(2,1)S(1)} %constant_dynamic-slice_fusion.3) | copy-start | bytes 4612
  479.3 5.6 collective-permute-start.4
  484.9 4.7 collective-permute-start.5
  491.5 16.7 %all-to-all-start.2 = ((bf16[16,2,4096]{2,1,0:T(2,128)(2,1)}), bf16[16,2,4096]{2,1,0:T(2,128)(2,1)S(1)}, u32[]{:S(2)}, u32[]{:S(2)}) async-start(bf16[16,2,4096]{2,1,0:T(2,128)(2,1)} %reshape.427), calls=%async_computation.2 | async-start | bytes 524288 | tf_op jit(solution)/shard_map/all_to_all | solution.py:912
  508.5 94.9 %copy-start.24 = (f32[256,1024]{1,0:T(8,128)S(1)}, f32[256,1024]{1,0:T(8,128)}, u32[]{:S(2)}) copy-start(f32[256,1024]{1,0:T(8,128)} %copy-done.22) | copy-start | bytes 3145732
  508.5 94.9 %copy-start.35 = (f32[272,1024]{1,0:T(8,128)S(1)}, f32[272,1024]{1,0:T(8,128)}, u32[]{:S(2)}) copy-start(f32[272,1024]{1,0:T(8,128)} %copy-done.33) | copy-start | bytes 3342340
  607.6 14.1 %copy-start.27 = (bf16[1024,1024]{1,0:T(8,128)(2,1)S(1)}, bf16[1024,1024]{1,0:T(8,128)(2,1)}, u32[]{:S(2)}) copy-start(bf16[1024,1024]{1,0:T(8,128)(2,1)} %get-tuple-element.69) | copy-start | bytes 6291460
  626.4 11.7 %slice-start.2 = ((s8[8388608]{0:T(1024)(128)(4,1)}), s8[4194304]{0:T(1024)(128)(4,1)S(1)}, s32[]{:S(2)}) async-start(s8[8388608]{0:T(1024)(128)(4,1)} %bitcast.212), calls=%async_computation.8 | async-start | bytes 8388608
  677.9 13.4 %copy-start.42 = (bf16[1024,1024]{1,0:T(8,128)(2,1)S(1)}, bf16[1024,1024]{1,0:T(8,128)(2,1)}, u32[]{:S(2)}) copy-start(bf16[1024,1024]{1,0:T(8,128)(2,1)} %get-tuple-element.70) | copy-start | bytes 6291460
  732.1 8.6 collective-permute-start.6
  741.5 90.7 %copy-start.113 = (bf16[3,1024]{1,0:T(4,128)(2,1)S(1)}, bf16[3,1024]{1,0:T(4,128)(2,1)}, u32[]{:S(2)}) copy-start(bf16[3,1024]{1,0:T(4,128)(2,1)} %param.37) | copy-start | bytes 18436
  741.5 90.7 %copy-start.121 = (f32[1,1024]{1,0:T(1,128)S(1)}, f32[1,1024]{1,0:T(1,128)}, u32[]{:S(2)}) copy-start(f32[1,1024]{1,0:T(1,128)} %copy-done.120) | copy-start | bytes 12292
  741.5 90.7 %copy-start.143 = (bf16[1,3,256]{2,0,1:T(2,128)(2,1)S(1)}, bf16[1,3,256]{2,0,1:T(2,128)(2,1)}, u32[]{:S(2)}) copy-start(bf16[1,3,256]{2,0,1:T(2,128)(2,1)} %copy-done.142) | copy-start | bytes 4612
  811.8 23.7 %copy-start.109 = (f32[32,64]{1,0:T(8,128)S(1)}, f32[32,64]{1,0:T(8,128)}, u32[]{:S(2)}) copy-start(f32[32,64]{1,0:T(8,128)} %copy-done.108) | copy-start | bytes 24580
  811.8 23.8 %copy-start.10 = (bf16[512,256]{1,0:T(8,128)(2,1)S(1)}, bf16[512,256]{1,0:T(8,128)(2,1)}, u32[]{:S(2)}) copy-start(bf16[512,256]{1,0:T(8,128)(2,1)} %copy-done.9) | copy-start | bytes 786436
  812.9 44.1 %all-to-all-start.3 = ((bf16[16,2,4096]{2,1,0:T(2,128)(2,1)}), bf16[16,2,4096]{2,1,0:T(2,128)(2,1)S(1)}, u32[]{:S(2)}, u32[]{:S(2)}) async-start(bf16[16,2,4096]{2,1,0:T(2,128)(2,1)} %reshape.429), calls=%async_computation.3 | async-start | bytes 524288 | tf_op jit(solution)/shard_map/all_to_all | solution.py:920
  832.2 271.9 %all-gather.3.cloned.1.call-start = ((), (), s32[]{:S(2)}) async-start(), calls=%async_computation.4 | async-start | bytes 1351680 | tf_op jit(solution)/shard_map/all_gather | solution.py:2071
  858.2 4.8 collective-permute-start.7
  864.6 263.7 %all-gather.5.cloned.1.call-start = ((), (), s32[]{:S(2)}) async-start(), calls=%async_computation.5 | async-start | bytes 3244032 | tf_op jit(solution)/shard_map/all_gather | solution.py:2090
  873.2 2.5 collective-permute-start.1
  874.3 12.7 %collective-permute-start = (f32[256,512]{1,0:T(8,128)S(1)}, f32[256,512]{1,0:T(8,128)S(1)}, u32[]{:S(2)}, u32[]{:S(2)}) collective-permute-start(f32[256,512]{1,0:T(8,128)S(1)} %constant_dynamic-slice_fusion.6), channel_id=1, source_target_pairs={{0,1},{1,0},{2,3},{3,2},{4,5},{5,4},{6,7},{7,6},{8,9},{9,8},{10,11... | collective-permute-start | bytes 1572872 | tf_op jit(solution)/shard_map/ppermute | solution.py:886
  876.3 12.0 %copy-start.21 = (bf16[64,1024]{1,0:T(8,128)(2,1)S(1)}, bf16[64,1024]{1,0:T(8,128)(2,1)}, u32[]{:S(2)}) copy-start(bf16[64,1024]{1,0:T(8,128)(2,1)} %copy-done.20) | copy-start | bytes 393220
  876.3 12.0 %copy-start.47 = (bf16[768,1024]{1,0:T(8,128)(2,1)S(1)}, bf16[768,1024]{1,0:T(8,128)(2,1)}, u32[]{:S(2)}) copy-start(bf16[768,1024]{1,0:T(8,128)(2,1)} %get-tuple-element.72) | copy-start | bytes 4718596
  920.5 182.8 %collective-permute-start.8 = (f32[64,512]{1,0:T(8,128)S(1)}, f32[64,512]{1,0:T(8,128)S(1)}, u32[]{:S(2)}, u32[]{:S(2)}) collective-permute-start(f32[64,512]{1,0:T(8,128)S(1)} %constant_dynamic-slice_fusion), channel_id=1, source_target_pairs={{0,1},{1,0},{2,3},{3,2},{4,5},{5,4},{6,7},{7,6},{8,9},{9,8},{10,11... | collective-permute-start | bytes 393224 | tf_op jit(solution)/shard_map/ppermute | solution.py:886
  1128.3 12.3 %copy-start.85 = (f32[64,2048]{1,0:T(8,128)S(1)}, f32[64,2048]{1,0:T(8,128)}, u32[]{:S(2)}) copy-start(f32[64,2048]{1,0:T(8,128)} %get-tuple-element.337) | copy-start | bytes 1572868
  1128.4 13.8 %copy-start.1 = (bf16[1000,768]{1,0:T(8,128)(2,1)S(1)}, bf16[1000,768]{1,0:T(8,128)(2,1)}, u32[]{:S(2)}) copy-start(bf16[1000,768]{1,0:T(8,128)(2,1)} %param.33) | copy-start | bytes 4608004
  (132 other events, 571.0 us)
Sparse Core Ops, SparseCore 0:
  864.7 55.2 all-gather.2
  923.5 65.9 all-gather.4

commit v5 on v4

--- a/solution.py
+++ b/solution.py
@@ -824,6 +824,56 @@
     return [entry.astype(jnp.bfloat16) for entry in arrays]
 
 
+def gelu_parts(value):
+    scale, cubic = (2.0 / np.pi) ** 0.5, 0.044715
+    bend = jnp.tanh(scale * (value + cubic * value * value * value))
+    slope = scale * (1.0 + 3.0 * cubic * value * value)
+    steep = 1.0 - bend * bend
+    once = steep * slope
+    twice = steep * (6.0 * cubic * scale) * value - 2.0 * bend * once * slope
+    return (
+        0.5 * value * (1.0 + bend),
+        0.5 * (1.0 + bend) + 0.5 * value * once,
+        once + 0.5 * value * twice,
+    )
+
+
+@jax.custom_vjp
+def gelu_kept(value):
+    return gelu_parts(value)
+
+
+def gelu_kept_fwd(value):
+    result, first, second = lax.optimization_barrier(gelu_parts(value))
+    return (result, first, second), first
+
+
+def gelu_kept_bwd(first, cotans):
+    return (cotans[0] * first,)
+
+
+gelu_kept.defvjp(gelu_kept_fwd, gelu_kept_bwd)
+
+
+@jax.custom_vjp
+def gelu_joint(value, tangent, parts):
+    return parts[0], tangent * parts[1]
+
+
+def gelu_joint_fwd(value, tangent, parts):
+    return gelu_joint(value, tangent, parts), (tangent, parts)
+
+
+def gelu_joint_bwd(kept, cotans):
+    tangent, parts = kept
+    main, side = cotans
+    back = main * parts[1] + side * tangent * parts[2]
+    return back, side * parts[1], tuple(jnp.zeros_like(part) for part in parts)
+
+
+gelu_joint.defvjp(gelu_joint_fwd, gelu_joint_bwd)
+
+
 def layer_forward(conv_out, sums, text_rows, small, weights, noise):
     bias, strength, rgb_scales, rgb_weight = small
     qk_w, value_w, attn_w, query_w, key_w, cval_w, cout_w, mlp_w, mout_w = weights
@@ -839,12 +889,12 @@
     )
     hidden_three = hidden_two + product_flip(mixture.astype(jnp.float32), cout_w)
     normed = rms_norm(hidden_three)
-    inner = jax.nn.gelu(product(normed, mlp_w))
-    hidden_four = hidden_three + product_flip(inner, mout_w)
-    return hidden_four, picture_of(hidden_four, rgb_scales, rgb_weight)
-
-
-def layer_joint(conv_out, conv_tan, sums, text_rows, small, weights, noise):
+    parts = gelu_kept(product(normed, mlp_w))
+    hidden_four = hidden_three + product_flip(parts[0], mout_w)
+    return (hidden_four, picture_of(hidden_four, rgb_scales, rgb_weight)), parts
+
+
+def layer_joint(conv_out, conv_tan, sums, text_rows, small, weights, noise, parts):
     bias, strength, rgb_scales, rgb_weight = small
     qk_w, value_w, attn_w, query_w, key_w, cval_w, cout_w, mlp_w, mout_w = weights
     hidden_one, tan_one = with_tangent(
@@ -869,7 +919,7 @@
     hidden_three, tan_three = hidden_two + added, tan_two + tan_added
     normed, tan_normed = with_tangent(rms_norm, hidden_three, tan_three)
     before, tan_before = product_pair(normed, tan_normed, mlp_w)
-    inner, tan_inner = with_tangent(jax.nn.gelu, before, tan_before)
+    inner, tan_inner = gelu_joint(before, tan_before, parts)
     added, tan_added = product_flip_pair(inner, tan_inner, mout_w)
     hidden_four, tan_four = hidden_three + added, tan_three + tan_added
     return (
@@ -1480,7 +1530,6 @@
     z, y, x = place.z, place.y, place.x
     spot_ref[...] = jnp.zeros_like(spot_ref)
     wide, narrow = slice(0, cut), slice(cut, acc.shape[-1])
-    finish = []
 
     def spot(z, y, core, x):
         return (z * 2 + y) * 2 + core, x
@@ -1499,10 +1548,12 @@
     other_y = (z, 1 - y, place.core, x)
     other_x = (z, y, place.core, 1 - x)
 
+    order = (3, 0, 2, 1)
+
     def chunk_at(chunk):
-        turn = lax.rem(chunk, PLANES)
+        turn = chunk // 2
         dest = jnp.where(turn == 0, 3, jnp.where(turn == 1, 0, 4 - turn))
-        return dest, jnp.where(chunk < PLANES, 1 - y, y)
+        return dest, jnp.where(lax.rem(chunk, 2) == 0, 1 - y, y)
 
     def sample_at(turn):
         dest, side = chunk_at(turn // 4)
@@ -1529,8 +1580,7 @@
             acc.at[dest, 1 - y, :, :, wide], y_in.at[dest], y_send.at[dest], y_recv.at[dest], other_y
         )
 
-    @pl.loop(0, 16 * 2)
-    def _(turn):
+    def one_sample(turn):
         chunk, step = turn // 4, lax.rem(turn, 4)
         dest, side = chunk_at(chunk)
         sample = sample_at(turn)
@@ -1556,59 +1606,76 @@
         def _():
             core_copy(chunk).wait_recv()
             add_rows(acc.at[dest, side], core_in.at[dest, side])
-            pl.when(chunk < PLANES)(lambda: y_copy(dest).start())
-
-    y_copies = [y_copy(dest) for dest in (3, 0, 2, 1)]
-
-    def along_z(slot, view, landing, dest):
+            pl.when(lax.rem(chunk, 2) == 0)(lambda: y_copy(dest).start())
+
+    views = (
+        lambda dest: acc.at[dest, y, :, :, wide],
+        lambda dest: acc.at[dest, :, :, :, narrow],
+    )
+    landings = (z_first, z_second)
+
+    def z_copy(slot, way, dest, device):
+        return remote(
+            views[slot](dest),
+            landings[slot].at[way, dest],
+            z_send.at[slot, way, dest],
+            z_recv.at[slot, way, dest],
+            device,
+        )
+
+    def take_y(dest):
+        y_copy(dest).wait_recv()
+        add_rows(views[0](dest), y_in.at[dest])
+
+    def along_z(slot, dest, act):
         for way in (0, 1):
             near = dest > z if way == 0 else dest < z
             has_before = z > 0 if way == 0 else z < PLANES - 1
-            copy = remote(
-                view,
-                landing.at[way, dest],
-                z_send.at[slot, way, dest],
-                z_recv.at[slot, way, dest],
-                (z + (1 if way == 0 else -1), y, place.core, x),
-            )
-
-            @pl.when(near & has_before)
-            def _():
-                copy.wait_recv()
-                add_rows(view, landing.at[way, dest])
-
-            pl.when(near)(copy.start)
-            finish.append((near, copy))
-
-    def end_z(slot, view, landing):
+            copy = z_copy(slot, way, dest, (z + (1 if way == 0 else -1), y, place.core, x))
+            if act:
+
+                @pl.when(near & has_before)
+                def _():
+                    copy.wait_recv()
+                    add_rows(views[slot](dest), landings[slot].at[way, dest])
+
+                pl.when(near)(copy.start)
+            else:
+                pl.when(near)(copy.wait_send)
+
+    def end_z(slot):
         for way in (0, 1):
-            copy = remote(
-                view,
-                landing.at[way, z],
-                z_send.at[slot, way, z],
-                z_recv.at[slot, way, z],
-                other_core,
-            )
 
             @pl.when(z > 0 if way == 0 else z < PLANES - 1)
             def _():
-                copy.wait_recv()
-                add_rows(view, landing.at[way, z])
-
-    for number, dest in enumerate((3, 0, 2, 1)):
-        along_z(1, acc.at[dest, :, :, :, narrow], z_second, dest)
-        y_copies[number].wait_recv()
-        finish.append(y_copies[number])
-        view = acc.at[dest, y, :, :, wide]
-        add_rows(view, y_in.at[dest])
-        along_z(0, view, z_first, dest)
-    end_z(1, acc.at[z, :, :, :, narrow], z_second)
+                z_copy(slot, way, z, other_core).wait_recv()
+                add_rows(views[slot](z), landings[slot].at[way, z])
+
+    @pl.loop(0, 2 * PLANES)
+    def _(turn):
+        @pl.when(turn < PLANES)
+        def _():
+            pl.loop(0, 8)(lambda step: one_sample(turn * 8 + step))
+
+        for number, dest in enumerate(order):
+            due = number + jnp.where(dest > z, z, PLANES - 1 - z)
+
+            @pl.when((turn == due) & (dest != z))
+            def _():
+                along_z(1, dest, True)
+
+            @pl.when((turn == due + 1) & (dest != z))
+            def _():
+                take_y(dest)
+                along_z(0, dest, True)
+
+    take_y(z)
+    end_z(1)
     last = remote(
         acc.at[z, 1 - y, :, :, narrow], y_last, y_send.at[PLANES], y_recv.at[PLANES], other_y
     )
     last.start()
-    finish.append(last)
-    end_z(0, acc.at[z, y, :, :, wide], z_first)
+    end_z(0)
     last.wait_recv()
     add_rows(acc.at[z, y, :, :, narrow], y_last)
     swap = remote(acc.at[z, y, 1 - x], x_in, x_send, x_recv, other_x)
@@ -1617,12 +1684,12 @@
     out_ref[:, lanes_at(x, lanes)] = acc[z, y, x]
     swap.wait_recv()
     out_ref[:, lanes_at(1 - x, lanes)] = x_in[...]
-    finish.append(swap)
-    for item in finish:
-        if isinstance(item, tuple):
-            pl.when(item[0])(item[1].wait_send)
-        else:
-            item.wait_send()
+    swap.wait_send()
+    last.wait_send()
+    for dest in range(PLANES):
+        y_copy(dest).wait_send()
+        for slot in (0, 1):
+            along_z(slot, dest, False)
 
     @pl.loop(0, 2 * PLANES)
     def _(chunk):
@@ -1740,6 +1807,8 @@
                 sent.wait_recv()
                 finish.append((None, sent))
                 add_rows(acc[w].at[dest, side], core_in[w].at[dest, side])
+                if parts[w] == "z":
+                    continue
                 if parts[w] == "xy":
                     copy = remote(
                         acc[w].at[dest, side, :, half(w, 1 - x)],
@@ -1763,6 +1832,8 @@
 
     def stage_two(dest):
         for w in range(count):
+            if parts[w] == "z":
+                continue
             if parts[w] == "xy":
                 for turn, side in enumerate(sides):
                     copy = ones[w, dest, turn]
@@ -1793,6 +1864,72 @@
                 )
                 twos[w, dest].start()
 
+    def plane_copy(w, dest, way, device):
+        return remote(
+            acc[w].at[dest],
+            z_in[w].at[way, dest],
+            z_send.at[w, way, dest],
+            z_recv.at[w, way, dest],
+            device,
+        )
+
+    def planes_first(turn):
+        for number, dest in enumerate(order):
+            if turn < number + 1 or turn > number + PLANES:
+                continue
+            due = turn == number + 1 + jnp.where(dest > z, z, PLANES - 1 - z)
+            for w in range(count):
+                if parts[w] != "z":
+                    continue
+                for way in (0, 1):
+                    near = dest > z if way == 0 else dest < z
+                    has_before = z > 0 if way == 0 else z < PLANES - 1
+                    device = (z + (1 if way == 0 else -1), y, place.core, x)
+                    copy = plane_copy(w, dest, way, device)
+
+                    @pl.when(due & near & has_before)
+                    def _():
+                        copy.wait_recv()
+                        add_rows(acc[w].at[dest], z_in[w].at[way, dest])
+
+                    pl.when(due & near)(copy.start)
+                    if turn == number + 1:
+                        finish.append((near, copy))
+
+    def planes_last():
+        chosen = [w for w in range(count) if parts[w] == "z"]
+        lasts = []
+        for w in chosen:
+            for way in (0, 1):
+
+                @pl.when(z > 0 if way == 0 else z < PLANES - 1)
+                def _():
+                    plane_copy(w, z, way, other_core).wait_recv()
+                    add_rows(acc[w].at[z], z_in[w].at[way, z])
+
+            copy = remote(
+                acc[w].at[z, 1 - y], one_in[w], one_send.at[w, 0, 0], one_recv.at[w, 0, 0], other_y
+            )
+            copy.start()
+            finish.append((None, copy))
+            lasts.append(copy)
+        for w, copy in zip(chosen, list(lasts)):
+            copy.wait_recv()
+            add_rows(acc[w].at[z, y], one_in[w])
+            more = remote(
+                acc[w].at[z, y, :, half(w, 1 - x)],
+                two_in[w],
+                two_send.at[w, 0],
+                two_recv.at[w, 0],
+                other_x,
+            )
+            more.start()
+            finish.append((None, more))
+            lasts.append(more)
+        for w, copy in zip(chosen, lasts[len(chosen) :]):
+            copy.wait_recv()
+            add_rows(acc[w].at[z, y, :, half(w, x)], two_in[w])
+
     def z_copy(w, dest, way):
         return remote(
             acc[w].at[dest, y, :, half(w, x)],
@@ -1804,6 +1941,8 @@
 
     def stage_z(dest):
         for w in range(count):
+            if parts[w] == "z":
+                continue
             copy = twos[w, dest]
             copy.wait_recv()
             finish.append((None, copy))
@@ -1827,11 +1966,15 @@
             stage_one(order[turn])
         if 0 <= turn - 1 < PLANES:
             stage_two(order[turn - 1])
+        planes_first(turn)
         if turn >= 2:
             stage_z(order[turn - 2])
+    for turn in range(PLANES + 2, 2 * PLANES):
+        planes_first(turn)
+    planes_last()
     for w in range(count):
         view = acc[w].at[z, y, :, half(w, x)]
-        for way in (0, 1):
+        for way in (0, 1) if parts[w] != "z" else ():
 
             @pl.when(z > 0 if way == 0 else z < PLANES - 1)
             def _():
@@ -1856,10 +1999,16 @@
     count = len(grads)
     bf16, dma = jnp.bfloat16, pltpu.SemaphoreType.DMA
     blocks = [(grad.shape[0] // 16, grad.shape[1]) for grad in grads]
-    ones = [
-        (PLANES, 2, rows, lanes // 2) if part == "xy" else (PLANES, rows, lanes)
-        for (rows, lanes), part in zip(blocks, parts)
-    ]
+    ones, twos, planes = [], [], []
+    for (rows, lanes), part in zip(blocks, parts):
+        if part == "z":
+            ones.append((rows, lanes))
+            twos.append((rows, lanes // 2))
+            planes.append((2, PLANES, 2, rows, lanes))
+        else:
+            ones.append((PLANES, 2, rows, lanes // 2) if part == "xy" else (PLANES, rows, lanes))
+            twos.append((PLANES, rows, lanes // 2))
+            planes.append((2, PLANES, rows, lanes // 2))
     return pl.pallas_call(
         lambda *refs: sum_weights_body(parts, count, refs),
         in_specs=[pl.BlockSpec(memory_space=pl.ANY)] * count,
@@ -1870,8 +2019,7 @@
         scratch_shapes=[pltpu.VMEM((PLANES, 2, rows, lanes), bf16) for rows, lanes in blocks]
         + [pltpu.VMEM((PLANES, 2, rows, lanes), bf16) for rows, lanes in blocks]
         + [pltpu.VMEM(shape, bf16) for shape in ones]
-        + [pltpu.VMEM((PLANES, rows, lanes // 2), bf16) for rows, lanes in blocks]
-        + [pltpu.VMEM((2, PLANES, rows, lanes // 2), bf16) for rows, lanes in blocks]
+        + [pltpu.VMEM(shape, bf16) for shape in twos + planes]
         + [dma((count, PLANES, 2))] * 5
         + [dma((count, PLANES))] * 2
         + [dma((count, 2, PLANES))] * 2,
@@ -1987,8 +2135,10 @@
     summed = conv_sum(slabs_x, place, kernel, sums_part, True, 4).astype(float32)
     conv_out, sums = summed[:PIXELS], summed[PIXELS]
 
-    (hidden_four, picture), pull = jax.vjp(
-        lambda value: layer_forward(value, sums, text_rows, small, weights, noise), conv_out
+    (hidden_four, picture), pull, parts = jax.vjp(
+        lambda value: layer_forward(value, sums, text_rows, small, weights, noise),
+        conv_out,
+        has_aux=True,
     )
 
     dir_own = pick(penalty_dir, mp).astype(float32)
@@ -2009,7 +2159,7 @@
     conv_tan = conv_sum(slabs_t, place, kernel, sums_part, False, 5).astype(float32)
 
     (ignored_out, ignored_pic, ignored_tan), pull_joint = jax.vjp(
-        lambda *given: layer_joint(*given, noise),
+        lambda *given: layer_joint(*given, noise, parts),
         conv_out,
         conv_tan,
         sums,
@@ -2022,7 +2172,7 @@
         (cot_own, pick(cot_rgb, mp).astype(float32), dir_own)
     )
 
-    orders = ("xy", "yx", "xy", "yx", "xy", "yx", "yx", "xy", "xy")
+    orders = ("xy", "yx", "xy", "yx", "xy", "yx", "z", "z", "z")
     d_qk, d_value, d_attn, d_query, d_key, d_cval, d_cout, d_mlp, d_mout = grad_weights
     mlp_grad, mout_grad, qk_grad, value_grad, attn_grad, query_grad, cout_grad, key_grad, cval_grad = (
         sum_weights(

time: 1160 us -> 1130 us (0.974)
  Pallas kernels: 786 us -> 748 us
    pallas_call x2, Pallas kernels: 199 us -> 170 us  [conv_sum(): pl.pallas_call(lambda *refs: sum_body(cut, extra, *refs), in_specs=[HBM]...]
    dot_general x27 -> x25, matrix products: 65.9 us -> 52.9 us  [dot_wide(): lax.dot_general(left.astype(jnp.bfloat16), right.astype(jnp.bfloat16), ((...]
    unnamed x390 -> x400, local copies, waits for them, and re-layouts: 42.2 us -> 45.5 us
  transfers between devices with their start and end apart: 15 -> 15, of which waited for: 7 -> 7; matrix products, arithmetic and copies ran while one was open for 11% -> 9% of each run, Pallas kernels for 36% -> 30%
where the time goes in v5:
time: 1130 us; the launch traced here: 1110 us
  Pallas kernels  748 us (66%)
  matrix products  154 us (14%)
  local copies, waits for them, and re-layouts  67.9 us (6%)
  starting transfers between devices  56 us (5%)
  waiting for transfers between devices  30.9 us (3%)
  other arithmetic  29.5 us (3%)
  between operations  18.4 us (2%)
    pallas_call x1, Pallas kernels, sum_weights(): pl.pallas_call(lambda *refs: sum_weights_body(parts, count, refs), in_spe...  173 us
    pallas_call x2, Pallas kernels, conv_sum(): pl.pallas_call(lambda *refs: sum_body(cut, extra, *refs), in_specs=[HBM]...  170 us
    pallas_call x1, Pallas kernels, gather_call(): pl.pallas_call(body, in_specs=[pl.BlockSpec(memory_space=pl.ANY)] * count...  132 us
    pallas_call x1, Pallas kernels, gather_second(): pl.pallas_call(body, in_specs=[HBM, HBM, HBM] + whole_specs(4), out_specs...  71.4 us
    pallas_call x1, Pallas kernels, gather_back(): pl.pallas_call(body, in_specs=[HBM, HBM] + whole_specs(1), out_specs=whol...  64.1 us
    dot_general x25, matrix products, dot_wide(): lax.dot_general(left.astype(jnp.bfloat16), right.astype(jnp.bfloat16), ((...  52.9 us
    unnamed x400, local copies, waits for them, and re-layouts  45.5 us
    pallas_call x4, Pallas kernels, per_head(): pl.pallas_call(body, grid=(arrays[0].shape[1] // lanes,), in_specs=[pl.Bl...  41.2 us
  transfers between devices with their start and end apart: 15, of which 7 were waited for; matrix products, arithmetic and copies ran while one was open for 9% of the time, Pallas kernels for 30%

profile of v5, /device:TPU:9, one launch (start us, length us, event | category | flops | bytes accessed | tf_op | source)
XLA Modules:
  0.0 1110.1 jit_solution(11473516480059549361)
XLA Ops:
  7.3 5.4 all_gather.9
  14.3 7.6 all-to-all-start
  24.0 132.5 %gather_weights.1 = (bf16[1024,4096]{1,0:T(8,128)(2,1)}, bf16[1024,4096]{1,0:T(8,128)(2,1)}, bf16[1024,1024]{1,0:T(8,128)(2,1)}, bf16[1024,1024]{1,0:T(8,128)(2,...) custom-call(bf16[64,2048]{1,0:T(8,128)(2,1)} %refs_0_.1, ...), custom_call_target="tpu_custom_call" | custom-call | tf_op jit(solution)/shard_map/gather_weights/pallas_call | solution.py:1146
  163.2 3.2 mul.913.refs_0_
  166.9 1.8 convolution_convert_fusion.21.refs_1_.refs_2_
  169.2 2.3 copy-done.2
  171.5 13.3 %mix_kernels.1 = (bf16[32,576,512]{2,1,0:T(8,128)(2,1)}, f32[32,512]{1,0:T(8,128)S(1)}) custom-call(bf16[512,256]{1,0:T(8,128)(2,1)S(1)} %mul.913.refs_0_, bf16[8,576,512]{2,1,0:T(8,128)(2,1)S(1)} %bitcast.200, f32[32,64,128]{2,1,0:T(8,128)S(1)} %broadcast_in_dim.30.refs_2_.squares_ref), custom_call_target="tpu_custom_call" | custom-call | tf_op jit(solution)/shard_map/mix_kernels/pallas_call | solution.py:528
  184.8 1.8 fusion.139
  187.6 89.8 %conv_sum.2 = bf16[272,1024]{1,0:T(8,128)(2,1)S(1)} custom-call(bf16[32,576,512]{2,1,0:T(8,128)(2,1)} %get-tuple-element.68.refs_0_.kernel_ref, bf16[32,64,64]{2,1,0:T(8,128)(2,1)S(1)} %fusion.38.refs_1_.slab_ref, bf16[288,192]{1,0:T(8,128)(2,1)S(1)} %copy-done.7, f32[32,512]{1,0:T(8,128)S(1)} %get-tuple-element.69.refs_3_), custom_call_target="tpu_custom_call" | custom-call | tf_op jit(solution)/shard_map/conv_sum/pallas_call | solution.py:1704
  281.5 11.5 %jvp_self_heads_.1 = bf16[256,1024]{1,0:T(8,128)(2,1)S(1)} custom-call(bf16[256,1024]{1,0:T(8,128)(2,1)S(1)} %convolution_convert_fusion.19.refs_0_, bf16[256,1024]{1,0:T(8,128)(2,1)S(1)} %convolution_convert_fusion.18.refs_1_.refs_2_), custom_call_target="tpu_custom_call" | custom-call | tf_op jit(solution)/shard_map/jvp(self_heads)/pallas_call | solution.py:787
  295.4 7.4 jvp_cross_heads_.1
  303.8 4.6 add_multiply_fusion
  308.4 5.6 multiply_add_fusion.1
  314.0 13.4 %multiply_reduce_fusion.18 = (f32[256]{0:T(256)}, f32[256,1024]{1,0:T(8,128)}) fusion(f32[256,1024]{1,0:T(8,128)} %copy-done.80, bf16[1024,4096]{1,0:T(8,128)(2,1)} %get-tuple-element.77, f32[256,4096]{1,0:T(8,128)} %get-tuple-element.80, bf16[256,1024]{1,0:T(8,128)(2,1)} %get-tuple-element.293, bf16[1024,4096]{1,0:T(8,128)(2,1)} %get-tuple-element.79), kind=kOutput, calls=%fused_computation.141 | convolution fusion | flops 4297588736 | bytes 23593984 | tf_op jit(solution)/shard_map/transpose(jvp())/dot_general | solution.py:892
  328.1 8.7 add_add_fusion.11
  337.5 11.0 transpose_jvp_cross_heads_pull__.1
  351.8 15.0 %transpose_jvp_self_heads_pull__.1 = (bf16[256,1024]{1,0:T(8,128)(2,1)S(1)}, bf16[256,1024]{1,0:T(8,128)(2,1)S(1)}) custom-call(bf16[256,1024]{1,0:T(8,128)(2,1)S(1)} %convolution_convert_fusion.19.refs_0_, bf16[256,1024]{1,0:T(8,128)(2,1)S(1)} %convolution_convert_fusion.18.refs_1_.refs_2_, bf16[256,1024]{1,0:T(8,128)(2,1)S(1)} %convolution_convert_fusion.15.refs_2_), custom_call_target="tpu_custom_call" | custom-call | tf_op jit(solution)/shard_map/transpose(jvp(self_heads_pull))/pallas_call | solution.py:882
  372.1 6.3 collective-permute-done.3
  379.5 64.1 %gather_back.1 = (bf16[32,64,64]{2,1,0:T(8,128)(2,1)S(1)}, bf16[32,256,512]{2,1,0:T(8,128)(2,1)S(1)}) custom-call(bf16[2,256,512]{2,1,0:T(8,128)(2,1)S(1)} %pad_maximum_fusion.18.cotan_ref, bf16[32,576,512]{2,1,0:T(8,128)(2,1)} %get-tuple-element.68.refs_0_.kernel_ref, bf16[288,192]{1,0:T(8,128)(2,1)S(1)} %copy-done.7), custom_call_target="tpu_custom_call" | custom-call | tf_op jit(solution)/shard_map/gather_back/pallas_call | solution.py:1376
  443.7 3.3 copy-done.4
  447.8 2.1 reshape.425
  449.9 17.6 %all-to-all-start.1 = ((bf16[16,2,4096]{2,1,0:T(2,128)(2,1)}), bf16[16,2,4096]{2,1,0:T(2,128)(2,1)}, u32[]{:S(2)}, u32[]{:S(2)}) async-start(bf16[16,2,4096]{2,1,0:T(2,128)(2,1)} %reshape.425), calls=%async_computation.1 | async-start | bytes 524288 | tf_op jit(solution)/shard_map/all_to_all | solution.py:970
  473.7 2.7 all-to-all-done.1
  481.8 4.1 collective-permute-done.4
  486.4 1.8 fusion.43
  488.2 2.6 collective-permute-done.5
  494.2 5.5 all-to-all-start.2
  499.7 11.6 %fusion.44 = f32[512,4096]{1,0:T(8,128)} fusion(bf16[1024,4096]{1,0:T(8,128)(2,1)} %get-tuple-element.79, bf16[256,1024]{1,0:T(8,128)(2,1)} %get-tuple-element.293, bf16[256,1024]{1,0:T(8,128)(2,1)} %get-tuple-element.304), kind=kOutput, calls=%fused_computation.156 | convolution fusion | flops 4297064448 | bytes 17825792 | tf_op jit(solution)/shard_map/transpose(jvp())/dot_general | solution.py:923
  513.5 80.4 %conv_sum.3 = bf16[256,1024]{1,0:T(8,128)(2,1)S(1)} custom-call(bf16[32,576,512]{2,1,0:T(8,128)(2,1)} %get-tuple-element.68.refs_0_.kernel_ref, bf16[32,64,64]{2,1,0:T(8,128)(2,1)S(1)} %bitcast.202, bf16[288,192]{1,0:T(8,128)(2,1)S(1)} %copy-done.7, f32[32,512]{1,0:T(8,128)S(1)} %copy-done.25), custom_call_target="tpu_custom_call" | custom-call | tf_op jit(solution)/shard_map/conv_sum/pallas_call | solution.py:1704
  598.9 13.4 %jvp_self_heads_joint_.1 = (bf16[256,1024]{1,0:T(8,128)(2,1)S(1)}, bf16[256,1024]{1,0:T(8,128)(2,1)S(1)}) custom-call(bf16[256,1024]{1,0:T(8,128)(2,1)S(1)} %convolution_convert_fusion.19.refs_0_, bf16[256,1024]{1,0:T(8,128)(2,1)S(1)} %convolution_convert_fusion.14.refs_1_, bf16[256,1024]{1,0:T(8,128)(2,1)S(1)} %convolution_convert_fusion.18.refs_1_.refs_2_, ...), custom_call_target="tpu_custom_call" | custom-call | tf_op jit(solution)/shard_map/jvp(self_heads_joint)/pallas_call | solution.py:787
  617.7 8.9 jvp_cross_heads_joint_.1
  628.8 13.5 %fusion.7 = (bf16[256,4096]{1,0:T(8,128)(2,1)}, bf16[256,4096]{1,0:T(8,128)(2,1)}, bf16[256,4096]{1,0:T(8,128)(2,1)}) fusion(f32[256,4096]{1,0:T(8,128)} %get-tuple-element.80, f32[512,4096]{1,0:T(8,128)} %fusion.44, f32[256,4096]{1,0:T(8,128)} %get-tuple-element.89, bf16[256,1024]{1,0:T(8,128)(2,1)S(1)} %add_convert_fusion, ...), kind=kOutput, calls=%fused_computation.14 | convolution fusion | flops 2156920832 | bytes 31981568 | tf_op jit(solution)/shard_map/jvp()/dot_general | solution.py:395
  642.3 10.5 fusion.13
  652.9 2.1 multiply_reduce_fusion.13
  658.7 13.1 %transpose_jvp_cross_heads_joint_pull__.1 = (bf16[256,1024]{1,0:T(8,128)(2,1)S(1)}, bf16[256,1024]{1,0:T(8,128)(2,1)S(1)}, bf16[64,1024]{1,0:T(8,128)(2,1)S(1)}, bf16[64,1024]{1,0:T(8,128)(2,1)S(1)}) custom-call(bf16[256,1024]{1,0:T(8,128)(2,1)S(1)} %convolution_convert_fusion.12.refs_0_, bf16[256,1024]{1,0:T(8,128)(2,1)S(1)} %convolution_convert_fusion.11.refs_1_, ...), custom_call_target="tpu_custom_call" | custom-call | tf_op jit(solution)/shard_map/transpose(jvp(cross_heads_joint_pull))/pallas_call | solution.py:913
  676.0 26.4 %transpose_jvp_self_heads_joint_pull__.1 = (bf16[256,1024]{1,0:T(8,128)(2,1)S(1)}, bf16[256,1024]{1,0:T(8,128)(2,1)S(1)}, bf16[256,1024]{1,0:T(8,128)(2,1)S(1)}, bf16[256,1024]{1,0:T(8,128)(2,1)S(1)}) custom-call(bf16[256,1024]{1,0:T(8,128)(2,1)S(1)} %convolution_convert_fusion.19.refs_0_, bf16[256,1024]{1,0:T(8,128)(2,1)S(1)} %convolution_convert_fusion.14.refs_1_, ...), custom_call_target="tpu_custom_call" | custom-call | tf_op jit(solution)/shard_map/transpose(jvp(self_heads_joint_pull))/pallas_call | solution.py:906
  702.6 2.2 copy-done.70
  708.9 3.0 multiply_reduce_fusion.4
  713.5 2.4 convolution_add_fusion.7
  717.8 71.4 %gather_second.1 = (bf16[32,576,512]{2,1,0:T(8,128)(2,1)}, bf16[32,64,64]{2,1,0:T(8,128)(2,1)S(1)}, f32[32,64,128]{2,1,0:T(8,128)S(1)}) custom-call(bf16[2,272,512]{2,1,0:T(8,128)(2,1)S(1)} %pad_maximum_fusion.16.cotan_ref, bf16[32,576,512]{2,1,0:T(8,128)(2,1)} %get-tuple-element.68.refs_0_.kernel_ref, bf16[32,256,512]{2,1,0:T(8,128)(2,1)} %copy-done.4, ...), custom_call_target="tpu_custom_call" | custom-call | tf_op jit(solution)/shard_map/gather_second/pallas_call | solution.py:1467
  791.0 2.2 reshape.429
  793.2 19.5 %all-to-all-start.3 = ((bf16[16,2,4096]{2,1,0:T(2,128)(2,1)}), bf16[16,2,4096]{2,1,0:T(2,128)(2,1)S(1)}, u32[]{:S(2)}, u32[]{:S(2)}) async-start(bf16[16,2,4096]{2,1,0:T(2,128)(2,1)} %reshape.429), calls=%async_computation.3 | async-start | bytes 524288 | tf_op jit(solution)/shard_map/all_to_all | solution.py:970
  812.8 2.6 fusion.74
  817.1 2.3 copy-done.3
  819.4 17.1 %unmix_kernels.1 = (f32[8,576,512]{2,1,0:T(8,128)}, f32[512,128]{1,0:T(8,128)S(1)}) custom-call(bf16[512,256]{1,0:T(8,128)(2,1)S(1)} %copy-done.6, bf16[8,576,512]{2,1,0:T(8,128)(2,1)S(1)} %bitcast.201, bf16[32,576,512]{2,1,0:T(8,128)(2,1)} %get-tuple-element.99.refs_2_), custom_call_target="tpu_custom_call" | custom-call | tf_op jit(solution)/shard_map/unmix_kernels/pallas_call | solution.py:653
  840.8 2.3 collective-permute-done.7
  845.8 2.1 fusion.72
  851.2 11.6 %collective-permute-done = f32[256,512]{1,0:T(8,128)S(1)} collective-permute-done((f32[256,512]{1,0:T(8,128)S(1)}, f32[256,512]{1,0:T(8,128)S(1)}, u32[]{:S(2)}, u32[]{:S(2)}) %collective-permute-start) | collective-permute-done | bytes 524320 | tf_op jit(solution)/shard_map/ppermute | solution.py:936
  866.1 3.9 convolution_convert_fusion.4.refs_4_
  870.0 1.7 convolution_convert_fusion.7.refs_8_
  871.7 1.7 convolution_convert_fusion.8.refs_7_
  873.5 2.7 convolution_convert_fusion.3.refs_5_
  876.2 2.6 convolution_convert_fusion.6.refs_2_
  878.8 2.7 convolution_convert_fusion.5.refs_3_
  881.9 7.0 convolution_convert_fusion.refs_1_
  889.0 6.7 convolution_convert_fusion.1.refs_0_
  896.0 2.6 convolution_convert_fusion.2.refs_6_
  898.6 172.7 %sum_weights.1 = (f32[64,2048]{1,0:T(8,128)}, f32[64,2048]{1,0:T(8,128)}, f32[64,512]{1,0:T(8,128)}, f32[64,512]{1,0:T(8,128)}, f32[64,512]{1,0:T(8,128)}, /*ind...) custom-call(bf16[1024,4096]{1,0:T(8,128)(2,1)} %convolution_convert_fusion.1.refs_0_, ...), custom_call_target="tpu_custom_call" | custom-call | tf_op jit(solution)/shard_map/sum_weights/pallas_call | solution.py:2012
  1072.1 1.7 copy.116
  1076.7 2.2 fusion.69
  1080.2 2.4 fusion.61
  1082.6 3.2 fusion.63
  1085.7 3.2 fusion.68
  1089.0 7.6 fusion
  (569 shorter events, 103.3 us)
Async XLA Ops:
  7.2 159.2 %copy-start = (bf16[1000,768]{1,0:T(8,128)(2,1)S(1)}, bf16[1000,768]{1,0:T(8,128)(2,1)}, u32[]{:S(2)}) copy-start(bf16[1000,768]{1,0:T(8,128)(2,1)} %param.33) | copy-start | bytes 4608004
  7.2 14.7 %copy-start.179 = (s32[2,64]{1,0:T(2,128)S(1)}, s32[2,64]{1,0:T(2,128)}, u32[]{:S(2)}) copy-start(s32[2,64]{1,0:T(2,128)} %param.29) | copy-start | bytes 1540
  7.2 14.8 %copy-start.180 = (s32[2]{0:T(128)S(1)}, s32[2]{0:T(128)}, u32[]{:S(2)}) copy-start(s32[2]{0:T(128)} %param.30) | copy-start | bytes 28
  7.2 16.0 %copy-start.174 = (bf16[2,3,256]{2,0,1:T(2,128)(2,1)S(1)}, bf16[2,3,256]{2,0,1:T(2,128)(2,1)}, u32[]{:S(2)}) copy-start(bf16[2,3,256]{2,0,1:T(2,128)(2,1)} %param.52) | copy-start | bytes 9220
  7.2 16.1 %copy-start.178 = (s32[2]{0:T(128)S(1)}, s32[2]{0:T(128)}, u32[]{:S(2)}) copy-start(s32[2]{0:T(128)} %param.28) | copy-start | bytes 28
  7.3 16.7 %copy-start.175 = (bf16[1024]{0:T(1024)(128)(2,1)S(1)}, bf16[1024]{0:T(1024)(128)(2,1)}, u32[]{:S(2)}) copy-start(bf16[1024]{0:T(1024)(128)(2,1)} %param.38) | copy-start | bytes 6148
  7.3 16.7 %copy-start.176 = (bf16[1024]{0:T(1024)(128)(2,1)S(1)}, bf16[1024]{0:T(1024)(128)(2,1)}, u32[]{:S(2)}) copy-start(bf16[1024]{0:T(1024)(128)(2,1)} %param.39) | copy-start | bytes 6148
  12.7 144.7 %copy-start.77 = (bf16[2,64,1024]{2,1,0:T(8,128)(2,1)}, bf16[2,64,1024]{2,1,0:T(8,128)(2,1)S(1)}, u32[]{:S(2)}) copy-start(bf16[2,64,1024]{2,1,0:T(8,128)(2,1)S(1)} %all_gather.9) | copy-start | bytes 786436
  13.2 145.8 %copy-start.144 = (bf16[512,8]{0,1:T(8,128)(2,1)S(1)}, bf16[512,8]{0,1:T(8,128)(2,1)}, u32[]{:S(2)}) copy-start(bf16[512,8]{0,1:T(8,128)(2,1)} %param.34) | copy-start | bytes 24580
  14.3 147.1 %copy-start.51 = (bf16[512,1024]{1,0:T(8,128)(2,1)S(1)}, bf16[512,1024]{1,0:T(8,128)(2,1)}, u32[]{:S(2)}) copy-start(bf16[512,1024]{1,0:T(8,128)(2,1)} %param.36) | copy-start | bytes 3145732
  14.3 172.7 %all-to-all-start = ((bf16[16,2,4096]{2,1,0:T(2,128)(2,1)}), bf16[16,2,4096]{2,1,0:T(2,128)(2,1)S(1)}, u32[]{:S(2)}, u32[]{:S(2)}) async-start(bf16[16,2,4096]{2,1,0:T(2,128)(2,1)} %reshape.423), calls=%async_computation | async-start | bytes 524288 | tf_op jit(solution)/shard_map/all_to_all | solution.py:962
  23.3 254.3 %copy-start.163 = (f32[256]{0:T(256)}, f32[256]{0:T(256)S(1)}, u32[]{:S(2)}) copy-start(f32[256]{0:T(256)S(1)} %fusion.101) | copy-start | bytes 3076
  23.3 161.5 %copy-start.152 = (bf16[1,3,256]{2,0,1:T(2,128)(2,1)}, bf16[1,3,256]{2,0,1:T(2,128)(2,1)S(1)}, u32[]{:S(2)}) copy-start(bf16[1,3,256]{2,0,1:T(2,128)(2,1)S(1)} %constant_dynamic-slice_fusion.4) | copy-start | bytes 4612
  23.9 253.6 %copy-start.129 = (f32[1024]{0:T(1024)}, f32[1024]{0:T(1024)S(1)}, u32[]{:S(2)}) copy-start(f32[1024]{0:T(1024)S(1)} %convert_element_type.330) | copy-start | bytes 12292
  24.0 253.6 %copy-start.132 = (f32[1024]{0:T(1024)}, f32[1024]{0:T(1024)S(1)}, u32[]{:S(2)}) copy-start(f32[1024]{0:T(1024)S(1)} %convert_element_type.332) | copy-start | bytes 12292
  166.9 19.7 %copy-start.57 = (bf16[64,768]{1,0:T(8,128)(2,1)}, bf16[64,768]{1,0:T(8,128)(2,1)S(1)}, u32[]{:S(2)}) copy-start(bf16[64,768]{1,0:T(8,128)(2,1)S(1)} %convolution_convert_fusion.22) | copy-start | bytes 294916
  168.8 18.5 %copy-start.114 = (f32[32,64]{1,0:T(8,128)}, f32[32,64]{1,0:T(8,128)S(1)}, u32[]{:S(2)}) copy-start(f32[32,64]{1,0:T(8,128)S(1)} %get-tuple-element.237) | copy-start | bytes 24580
  168.8 16.0 %copy-start.126 = (f32[1,1024]{1,0:T(1,128)}, f32[1,1024]{1,0:T(1,128)S(1)}, u32[]{:S(2)}) copy-start(f32[1,1024]{1,0:T(1,128)S(1)} %fusion.79) | copy-start | bytes 12292
  171.5 13.3 %copy-start.118 = (bf16[3,1024]{1,0:T(4,128)(2,1)S(1)}, bf16[3,1024]{1,0:T(4,128)(2,1)}, u32[]{:S(2)}) copy-start(bf16[3,1024]{1,0:T(4,128)(2,1)} %param.37) | copy-start | bytes 18436
  171.5 15.1 %copy-start.48 = (bf16[768,1024]{1,0:T(8,128)(2,1)S(1)}, bf16[768,1024]{1,0:T(8,128)(2,1)}, u32[]{:S(2)}) copy-start(bf16[768,1024]{1,0:T(8,128)(2,1)} %get-tuple-element.75) | copy-start | bytes 4718596
  187.6 116.2 %slice-start = ((s8[8388608]{0:T(1024)(128)(4,1)}), s8[4194304]{0:T(1024)(128)(4,1)S(1)}, s32[]{:S(2)}) async-start(s8[8388608]{0:T(1024)(128)(4,1)} %bitcast.206), calls=%async_computation.6 | async-start | bytes 8388608
  278.1 14.9 %copy-start.26 = (f32[256,1024]{1,0:T(8,128)}, f32[256,1024]{1,0:T(8,128)S(1)}, u32[]{:S(2)}) copy-start(f32[256,1024]{1,0:T(8,128)S(1)} %get-tuple-element.235) | copy-start | bytes 3145732
  278.2 25.6 %slice-start.1 = ((s8[8388608]{0:T(1024)(128)(4,1)}), s8[4194304]{0:T(1024)(128)(4,1)S(1)}, s32[]{:S(2)}) async-start(s8[8388608]{0:T(1024)(128)(4,1)} %bitcast.206), calls=%async_computation.7 | async-start | bytes 8388608
  280.8 12.2 %copy-start.29 = (bf16[1024,1024]{1,0:T(8,128)(2,1)S(1)}, bf16[1024,1024]{1,0:T(8,128)(2,1)}, u32[]{:S(2)}) copy-start(bf16[1024,1024]{1,0:T(8,128)(2,1)} %get-tuple-element.72) | copy-start | bytes 6291460
  293.9 14.4 %copy-start.166 = (f32[256]{0:T(256)}, f32[256]{0:T(256)S(1)}, u32[]{:S(2)}) copy-start(f32[256]{0:T(256)S(1)} %get-tuple-element.287) | copy-start | bytes 3076
  351.0 15.8 %copy-start.68 = (bf16[1024,1024]{1,0:T(8,128)(2,1)S(1)}, bf16[1024,1024]{1,0:T(8,128)(2,1)}, u32[]{:S(2)}) copy-start(bf16[1024,1024]{1,0:T(8,128)(2,1)} %get-tuple-element.71) | copy-start | bytes 6291460
  371.8 6.6 collective-permute-start.3
  379.5 88.0 %copy-start.82 = (bf16[2,256,512]{2,1,0:T(8,128)(2,1)S(1)}, bf16[2,256,512]{2,1,0:T(8,128)(2,1)}, u32[]{:S(2)}) copy-start(bf16[2,256,512]{2,1,0:T(8,128)(2,1)} %param.50) | copy-start | bytes 1572868
  449.9 26.4 %all-to-all-start.1 = ((bf16[16,2,4096]{2,1,0:T(2,128)(2,1)}), bf16[16,2,4096]{2,1,0:T(2,128)(2,1)}, u32[]{:S(2)}, u32[]{:S(2)}) async-start(bf16[16,2,4096]{2,1,0:T(2,128)(2,1)} %reshape.425), calls=%async_computation.1 | async-start | bytes 524288 | tf_op jit(solution)/shard_map/all_to_all | solution.py:970
  468.3 12.4 %collective-permute-start.2 = (bf16[256,512]{1,0:T(8,128)(2,1)}, bf16[256,512]{1,0:T(8,128)(2,1)}, u32[]{:S(2)}, u32[]{:S(2)}) collective-permute-start(bf16[256,512]{1,0:T(8,128)(2,1)} %dynamic-slice_bitcast_fusion), channel_id=1, source_target_pairs={{0,1},{1,0},{2,3},{3,2},{4,5},{5,4},{6,7},{7,6},{8,9},{9,8},{10,11... | collective-permute-start | bytes 786440 | tf_op jit(solution)/shard_map/ppermute | solution.py:936
  480.4 5.6 collective-permute-start.4
  486.0 4.7 collective-permute-start.5
  494.2 17.1 %all-to-all-start.2 = ((bf16[16,2,4096]{2,1,0:T(2,128)(2,1)}), bf16[16,2,4096]{2,1,0:T(2,128)(2,1)}, u32[]{:S(2)}, u32[]{:S(2)}) async-start(bf16[16,2,4096]{2,1,0:T(2,128)(2,1)} %reshape.427), calls=%async_computation.2 | async-start | bytes 524288 | tf_op jit(solution)/shard_map/all_to_all | solution.py:962
  513.5 80.4 %copy-start.28 = (f32[256,1024]{1,0:T(8,128)S(1)}, f32[256,1024]{1,0:T(8,128)}, u32[]{:S(2)}) copy-start(f32[256,1024]{1,0:T(8,128)} %copy-done.26) | copy-start | bytes 3145732
  513.5 80.5 %copy-start.40 = (f32[272,1024]{1,0:T(8,128)S(1)}, f32[272,1024]{1,0:T(8,128)}, u32[]{:S(2)}) copy-start(f32[272,1024]{1,0:T(8,128)} %copy-done.38) | copy-start | bytes 3342340
  513.5 80.5 %copy-start.113 = (f32[1,1024]{1,0:T(1,128)S(1)}, f32[1,1024]{1,0:T(1,128)}, u32[]{:S(2)}) copy-start(f32[1,1024]{1,0:T(1,128)} %copy-done.111) | copy-start | bytes 12292
  513.5 80.5 %copy-start.131 = (f32[1024]{0:T(1024)S(1)}, f32[1024]{0:T(1024)}, u32[]{:S(2)}) copy-start(f32[1024]{0:T(1024)} %copy-done.129) | copy-start | bytes 12292
  513.5 80.5 %copy-start.134 = (f32[1024]{0:T(1024)S(1)}, f32[1024]{0:T(1024)}, u32[]{:S(2)}) copy-start(f32[1024]{0:T(1024)} %copy-done.132) | copy-start | bytes 12292
  513.5 80.5 %copy-start.165 = (f32[256]{0:T(256)S(1)}, f32[256]{0:T(256)}, u32[]{:S(2)}) copy-start(f32[256]{0:T(256)} %copy-done.163) | copy-start | bytes 3076
  598.2 14.1 %copy-start.31 = (bf16[1024,1024]{1,0:T(8,128)(2,1)S(1)}, bf16[1024,1024]{1,0:T(8,128)(2,1)}, u32[]{:S(2)}) copy-start(bf16[1024,1024]{1,0:T(8,128)(2,1)} %get-tuple-element.72) | copy-start | bytes 6291460
  628.6 26.4 %copy-start.35 = (f32[256,1024]{1,0:T(8,128)}, f32[256,1024]{1,0:T(8,128)S(1)}, u32[]{:S(2)}) copy-start(f32[256,1024]{1,0:T(8,128)S(1)} %get-tuple-element.303) | copy-start | bytes 3145732
  628.8 13.5 %copy-start.71 = (bf16[256,1024]{1,0:T(8,128)(2,1)}, bf16[256,1024]{1,0:T(8,128)(2,1)S(1)}, u32[]{:S(2)}) copy-start(bf16[256,1024]{1,0:T(8,128)(2,1)S(1)} %add_convert_fusion) | copy-start | bytes 1572868
  642.3 12.7 %copy-start.60 = (bf16[256,512]{1,0:T(8,128)(2,1)S(1)}, bf16[256,512]{1,0:T(8,128)(2,1)}, u32[]{:S(2)}) copy-start(bf16[256,512]{1,0:T(8,128)(2,1)} %copy-done.59) | copy-start | bytes 786436
  642.3 12.7 %copy-start.62 = (bf16[256,512]{1,0:T(8,128)(2,1)S(1)}, bf16[256,512]{1,0:T(8,128)(2,1)}, u32[]{:S(2)}) copy-start(bf16[256,512]{1,0:T(8,128)(2,1)} %copy-done.61) | copy-start | bytes 786436
  658.7 13.2 %copy-start.46 = (bf16[1024,1024]{1,0:T(8,128)(2,1)S(1)}, bf16[1024,1024]{1,0:T(8,128)(2,1)}, u32[]{:S(2)}) copy-start(bf16[1024,1024]{1,0:T(8,128)(2,1)} %get-tuple-element.73) | copy-start | bytes 6291460
  712.1 5.5 collective-permute-start.6
  717.8 95.0 %copy-start.120 = (bf16[3,1024]{1,0:T(4,128)(2,1)S(1)}, bf16[3,1024]{1,0:T(4,128)(2,1)}, u32[]{:S(2)}) copy-start(bf16[3,1024]{1,0:T(4,128)(2,1)} %param.37) | copy-start | bytes 18436
  717.8 95.0 %copy-start.128 = (f32[1,1024]{1,0:T(1,128)S(1)}, f32[1,1024]{1,0:T(1,128)}, u32[]{:S(2)}) copy-start(f32[1,1024]{1,0:T(1,128)} %copy-done.126) | copy-start | bytes 12292
  717.8 95.0 %copy-start.155 = (bf16[1,3,256]{2,0,1:T(2,128)(2,1)S(1)}, bf16[1,3,256]{2,0,1:T(2,128)(2,1)}, u32[]{:S(2)}) copy-start(bf16[1,3,256]{2,0,1:T(2,128)(2,1)} %constant_dynamic-slice_fusion.3) | copy-start | bytes 4612
  791.0 25.1 %copy-start.9 = (f32[32,64,128]{2,1,0:T(8,128)S(1)}, f32[32,64,128]{2,1,0:T(8,128)}, u32[]{:S(2)}) copy-start(f32[32,64,128]{2,1,0:T(8,128)} %copy-done.8) | copy-start | bytes 3145732
  791.0 25.4 %copy-start.115 = (f32[32,64]{1,0:T(8,128)S(1)}, f32[32,64]{1,0:T(8,128)}, u32[]{:S(2)}) copy-start(f32[32,64]{1,0:T(8,128)} %copy-done.114) | copy-start | bytes 24580
  793.2 23.9 %copy-start.6 = (bf16[512,256]{1,0:T(8,128)(2,1)S(1)}, bf16[512,256]{1,0:T(8,128)(2,1)}, u32[]{:S(2)}) copy-start(bf16[512,256]{1,0:T(8,128)(2,1)} %copy-done.5) | copy-start | bytes 786436
  793.2 43.9 %all-to-all-start.3 = ((bf16[16,2,4096]{2,1,0:T(2,128)(2,1)}), bf16[16,2,4096]{2,1,0:T(2,128)(2,1)S(1)}, u32[]{:S(2)}, u32[]{:S(2)}) async-start(bf16[16,2,4096]{2,1,0:T(2,128)(2,1)} %reshape.429), calls=%async_computation.3 | async-start | bytes 524288 | tf_op jit(solution)/shard_map/all_to_all | solution.py:970
  812.7 259.3 %all-gather.3.cloned.1.call-start = ((), (), s32[]{:S(2)}) async-start(), calls=%async_computation.4 | async-start | bytes 1351680 | tf_op jit(solution)/shard_map/all_gather | solution.py:2221
  838.4 4.8 collective-permute-start.7
  840.7 22.1 %copy-start.54 = (f32[256,1024]{1,0:T(8,128)S(1)}, f32[256,1024]{1,0:T(8,128)}, u32[]{:S(2)}) copy-start(f32[256,1024]{1,0:T(8,128)} %get-tuple-element.257) | copy-start | bytes 3145732
  845.0 243.9 %all-gather.5.cloned.1.call-start = ((), (), s32[]{:S(2)}) async-start(), calls=%async_computation.5 | async-start | bytes 3244032 | tf_op jit(solution)/shard_map/all_gather | solution.py:2240
  847.9 2.6 collective-permute-start.1
  850.4 12.4 %collective-permute-start = (f32[256,512]{1,0:T(8,128)S(1)}, f32[256,512]{1,0:T(8,128)S(1)}, u32[]{:S(2)}, u32[]{:S(2)}) collective-permute-start(f32[256,512]{1,0:T(8,128)S(1)} %constant_dynamic-slice_fusion.6), channel_id=1, source_target_pairs={{0,1},{1,0},{2,3},{3,2},{4,5},{5,4},{6,7},{7,6},{8,9},{9,8},{10,11... | collective-permute-start | bytes 1572872 | tf_op jit(solution)/shard_map/ppermute | solution.py:936
  851.2 12.8 %copy-start.23 = (bf16[64,1024]{1,0:T(8,128)(2,1)S(1)}, bf16[64,1024]{1,0:T(8,128)(2,1)}, u32[]{:S(2)}) copy-start(bf16[64,1024]{1,0:T(8,128)(2,1)} %copy-done.22) | copy-start | bytes 393220
  851.2 12.8 %copy-start.49 = (bf16[768,1024]{1,0:T(8,128)(2,1)S(1)}, bf16[768,1024]{1,0:T(8,128)(2,1)}, u32[]{:S(2)}) copy-start(bf16[768,1024]{1,0:T(8,128)(2,1)} %get-tuple-element.75) | copy-start | bytes 4718596
  895.7 175.6 %collective-permute-start.8 = (f32[64,512]{1,0:T(8,128)S(1)}, f32[64,512]{1,0:T(8,128)S(1)}, u32[]{:S(2)}, u32[]{:S(2)}) collective-permute-start(f32[64,512]{1,0:T(8,128)S(1)} %constant_dynamic-slice_fusion), channel_id=1, source_target_pairs={{0,1},{1,0},{2,3},{3,2},{4,5},{5,4},{6,7},{7,6},{8,9},{9,8},{10,11... | collective-permute-start | bytes 393224 | tf_op jit(solution)/shard_map/ppermute | solution.py:936
  1088.9 12.2 %copy-start.93 = (f32[64,2048]{1,0:T(8,128)S(1)}, f32[64,2048]{1,0:T(8,128)}, u32[]{:S(2)}) copy-start(f32[64,2048]{1,0:T(8,128)} %get-tuple-element.348) | copy-start | bytes 1572868
  1089.0 13.8 %copy-start.1 = (bf16[1000,768]{1,0:T(8,128)(2,1)S(1)}, bf16[1000,768]{1,0:T(8,128)(2,1)}, u32[]{:S(2)}) copy-start(bf16[1000,768]{1,0:T(8,128)(2,1)} %param.33) | copy-start | bytes 4608004
  (137 other events, 523.6 us)
Sparse Core Ops, SparseCore 0:
  845.2 55.6 all-gather.2
  904.4 67.2 all-gather.4

commit v6 on v5

--- a/solution.py
+++ b/solution.py
@@ -1170,7 +1170,7 @@
 
 def gather_weights(shards, numbers, call_id):
     orders = dict(x=("z", "y", "x"), y=("z", "x", "y"), z=("x", "y", "z"))
-    turns = ("x", "y", "x", "y", "x", "y", "z", "y", "z")
+    turns = ("x", "y", "x", "y", "x", "z", "z", "y", "z")
 
     def piece(number, turn):
         rows, lanes = arrays[number].shape

time: 1130 us -> 1120 us (level)
  no operation moved by 1% of the time
where the time goes in v6:
time: 1120 us; the launch traced here: 1100 us
  Pallas kernels  741 us (66%)
  matrix products  154 us (14%)
  local copies, waits for them, and re-layouts  68 us (6%)
  starting transfers between devices  56.1 us (5%)
  waiting for transfers between devices  30.8 us (3%)
  other arithmetic  29.5 us (3%)
  between operations  18.4 us (2%)
    pallas_call x1, Pallas kernels, sum_weights(): pl.pallas_call(lambda *refs: sum_weights_body(parts, count, refs), in_spe...  173 us
    pallas_call x2, Pallas kernels, conv_sum(): pl.pallas_call(lambda *refs: sum_body(cut, extra, *refs), in_specs=[HBM]...  171 us
    pallas_call x1, Pallas kernels, gather_call(): pl.pallas_call(body, in_specs=[pl.BlockSpec(memory_space=pl.ANY)] * count...  124 us
    pallas_call x1, Pallas kernels, gather_second(): pl.pallas_call(body, in_specs=[HBM, HBM, HBM] + whole_specs(4), out_specs...  71.4 us
    pallas_call x1, Pallas kernels, gather_back(): pl.pallas_call(body, in_specs=[HBM, HBM] + whole_specs(1), out_specs=whol...  64.1 us
    dot_general x25, matrix products, dot_wide(): lax.dot_general(left.astype(jnp.bfloat16), right.astype(jnp.bfloat16), ((...  52.9 us
    unnamed x400, local copies, waits for them, and re-layouts  45.6 us
    pallas_call x4, Pallas kernels, per_head(): pl.pallas_call(body, grid=(arrays[0].shape[1] // lanes,), in_specs=[pl.Bl...  41.2 us
  transfers between devices with their start and end apart: 15, of which 7 were waited for; matrix products, arithmetic and copies ran while one was open for 9% of the time, Pallas kernels for 30%

profile of v6, /device:TPU:9, one launch (start us, length us, event | category | flops | bytes accessed | tf_op | source)
XLA Modules:
  0.0 1102.7 jit_solution(4591317181311266726)
XLA Ops:
  7.3 5.4 all_gather.9
  14.3 7.6 all-to-all-start
  24.0 124.1 %gather_weights.1 = (bf16[1024,4096]{1,0:T(8,128)(2,1)}, bf16[1024,4096]{1,0:T(8,128)(2,1)}, bf16[1024,1024]{1,0:T(8,128)(2,1)}, bf16[1024,1024]{1,0:T(8,128)(2,...) custom-call(bf16[64,2048]{1,0:T(8,128)(2,1)} %refs_0_.1, ...), custom_call_target="tpu_custom_call" | custom-call | tf_op jit(solution)/shard_map/gather_weights/pallas_call | solution.py:1146
  154.8 3.2 mul.913.refs_0_
  158.5 1.8 convolution_convert_fusion.21.refs_1_.refs_2_
  160.8 2.3 copy-done.2
  163.1 13.3 %mix_kernels.1 = (bf16[32,576,512]{2,1,0:T(8,128)(2,1)}, f32[32,512]{1,0:T(8,128)S(1)}) custom-call(bf16[512,256]{1,0:T(8,128)(2,1)S(1)} %mul.913.refs_0_, bf16[8,576,512]{2,1,0:T(8,128)(2,1)S(1)} %bitcast.200, f32[32,64,128]{2,1,0:T(8,128)S(1)} %broadcast_in_dim.30.refs_2_.squares_ref), custom_call_target="tpu_custom_call" | custom-call | tf_op jit(solution)/shard_map/mix_kernels/pallas_call | solution.py:528
  176.4 1.8 fusion.139
  179.2 90.8 %conv_sum.2 = bf16[272,1024]{1,0:T(8,128)(2,1)S(1)} custom-call(bf16[32,576,512]{2,1,0:T(8,128)(2,1)} %get-tuple-element.68.refs_0_.kernel_ref, bf16[32,64,64]{2,1,0:T(8,128)(2,1)S(1)} %fusion.38.refs_1_.slab_ref, bf16[288,192]{1,0:T(8,128)(2,1)S(1)} %copy-done.7, f32[32,512]{1,0:T(8,128)S(1)} %get-tuple-element.69.refs_3_), custom_call_target="tpu_custom_call" | custom-call | tf_op jit(solution)/shard_map/conv_sum/pallas_call | solution.py:1704
  274.1 11.5 %jvp_self_heads_.1 = bf16[256,1024]{1,0:T(8,128)(2,1)S(1)} custom-call(bf16[256,1024]{1,0:T(8,128)(2,1)S(1)} %convolution_convert_fusion.19.refs_0_, bf16[256,1024]{1,0:T(8,128)(2,1)S(1)} %convolution_convert_fusion.18.refs_1_.refs_2_), custom_call_target="tpu_custom_call" | custom-call | tf_op jit(solution)/shard_map/jvp(self_heads)/pallas_call | solution.py:787
  288.1 7.4 jvp_cross_heads_.1
  296.4 4.6 add_multiply_fusion
  301.0 5.6 multiply_add_fusion.1
  306.6 13.4 %multiply_reduce_fusion.18 = (f32[256]{0:T(256)}, f32[256,1024]{1,0:T(8,128)}) fusion(f32[256,1024]{1,0:T(8,128)} %copy-done.80, bf16[1024,4096]{1,0:T(8,128)(2,1)} %get-tuple-element.77, f32[256,4096]{1,0:T(8,128)} %get-tuple-element.80, bf16[256,1024]{1,0:T(8,128)(2,1)} %get-tuple-element.293, bf16[1024,4096]{1,0:T(8,128)(2,1)} %get-tuple-element.79), kind=kOutput, calls=%fused_computation.141 | convolution fusion | flops 4297588736 | bytes 23593984 | tf_op jit(solution)/shard_map/transpose(jvp())/dot_general | solution.py:892
  320.8 8.7 add_add_fusion.11
  330.2 11.0 transpose_jvp_cross_heads_pull__.1
  344.4 15.0 %transpose_jvp_self_heads_pull__.1 = (bf16[256,1024]{1,0:T(8,128)(2,1)S(1)}, bf16[256,1024]{1,0:T(8,128)(2,1)S(1)}) custom-call(bf16[256,1024]{1,0:T(8,128)(2,1)S(1)} %convolution_convert_fusion.19.refs_0_, bf16[256,1024]{1,0:T(8,128)(2,1)S(1)} %convolution_convert_fusion.18.refs_1_.refs_2_, bf16[256,1024]{1,0:T(8,128)(2,1)S(1)} %convolution_convert_fusion.15.refs_2_), custom_call_target="tpu_custom_call" | custom-call | tf_op jit(solution)/shard_map/transpose(jvp(self_heads_pull))/pallas_call | solution.py:882
  364.7 6.3 collective-permute-done.3
  372.2 64.1 %gather_back.1 = (bf16[32,64,64]{2,1,0:T(8,128)(2,1)S(1)}, bf16[32,256,512]{2,1,0:T(8,128)(2,1)S(1)}) custom-call(bf16[2,256,512]{2,1,0:T(8,128)(2,1)S(1)} %pad_maximum_fusion.18.cotan_ref, bf16[32,576,512]{2,1,0:T(8,128)(2,1)} %get-tuple-element.68.refs_0_.kernel_ref, bf16[288,192]{1,0:T(8,128)(2,1)S(1)} %copy-done.7), custom_call_target="tpu_custom_call" | custom-call | tf_op jit(solution)/shard_map/gather_back/pallas_call | solution.py:1376
  436.3 3.3 copy-done.4
  440.4 2.1 reshape.425
  442.5 17.6 %all-to-all-start.1 = ((bf16[16,2,4096]{2,1,0:T(2,128)(2,1)}), bf16[16,2,4096]{2,1,0:T(2,128)(2,1)}, u32[]{:S(2)}, u32[]{:S(2)}) async-start(bf16[16,2,4096]{2,1,0:T(2,128)(2,1)} %reshape.425), calls=%async_computation.1 | async-start | bytes 524288 | tf_op jit(solution)/shard_map/all_to_all | solution.py:970
  466.3 2.6 all-to-all-done.1
  474.5 4.1 collective-permute-done.4
  479.0 1.8 fusion.43
  480.8 2.5 collective-permute-done.5
  486.8 5.5 all-to-all-start.2
  492.3 11.6 %fusion.44 = f32[512,4096]{1,0:T(8,128)} fusion(bf16[1024,4096]{1,0:T(8,128)(2,1)} %get-tuple-element.79, bf16[256,1024]{1,0:T(8,128)(2,1)} %get-tuple-element.293, bf16[256,1024]{1,0:T(8,128)(2,1)} %get-tuple-element.304), kind=kOutput, calls=%fused_computation.156 | convolution fusion | flops 4297064448 | bytes 17825792 | tf_op jit(solution)/shard_map/transpose(jvp())/dot_general | solution.py:923
  506.1 80.4 %conv_sum.3 = bf16[256,1024]{1,0:T(8,128)(2,1)S(1)} custom-call(bf16[32,576,512]{2,1,0:T(8,128)(2,1)} %get-tuple-element.68.refs_0_.kernel_ref, bf16[32,64,64]{2,1,0:T(8,128)(2,1)S(1)} %bitcast.202, bf16[288,192]{1,0:T(8,128)(2,1)S(1)} %copy-done.7, f32[32,512]{1,0:T(8,128)S(1)} %copy-done.25), custom_call_target="tpu_custom_call" | custom-call | tf_op jit(solution)/shard_map/conv_sum/pallas_call | solution.py:1704
  591.6 13.4 %jvp_self_heads_joint_.1 = (bf16[256,1024]{1,0:T(8,128)(2,1)S(1)}, bf16[256,1024]{1,0:T(8,128)(2,1)S(1)}) custom-call(bf16[256,1024]{1,0:T(8,128)(2,1)S(1)} %convolution_convert_fusion.19.refs_0_, bf16[256,1024]{1,0:T(8,128)(2,1)S(1)} %convolution_convert_fusion.14.refs_1_, bf16[256,1024]{1,0:T(8,128)(2,1)S(1)} %convolution_convert_fusion.18.refs_1_.refs_2_, ...), custom_call_target="tpu_custom_call" | custom-call | tf_op jit(solution)/shard_map/jvp(self_heads_joint)/pallas_call | solution.py:787
  610.4 8.9 jvp_cross_heads_joint_.1
  621.5 13.5 %fusion.7 = (bf16[256,4096]{1,0:T(8,128)(2,1)}, bf16[256,4096]{1,0:T(8,128)(2,1)}, bf16[256,4096]{1,0:T(8,128)(2,1)}) fusion(f32[256,4096]{1,0:T(8,128)} %get-tuple-element.80, f32[512,4096]{1,0:T(8,128)} %fusion.44, f32[256,4096]{1,0:T(8,128)} %get-tuple-element.89, bf16[256,1024]{1,0:T(8,128)(2,1)S(1)} %add_convert_fusion, ...), kind=kOutput, calls=%fused_computation.14 | convolution fusion | flops 2156920832 | bytes 31981568 | tf_op jit(solution)/shard_map/jvp()/dot_general | solution.py:395
  635.0 10.5 fusion.13
  645.5 2.1 multiply_reduce_fusion.13
  651.4 13.1 %transpose_jvp_cross_heads_joint_pull__.1 = (bf16[256,1024]{1,0:T(8,128)(2,1)S(1)}, bf16[256,1024]{1,0:T(8,128)(2,1)S(1)}, bf16[64,1024]{1,0:T(8,128)(2,1)S(1)}, bf16[64,1024]{1,0:T(8,128)(2,1)S(1)}) custom-call(bf16[256,1024]{1,0:T(8,128)(2,1)S(1)} %convolution_convert_fusion.12.refs_0_, bf16[256,1024]{1,0:T(8,128)(2,1)S(1)} %convolution_convert_fusion.11.refs_1_, ...), custom_call_target="tpu_custom_call" | custom-call | tf_op jit(solution)/shard_map/transpose(jvp(cross_heads_joint_pull))/pallas_call | solution.py:913
  668.7 26.4 %transpose_jvp_self_heads_joint_pull__.1 = (bf16[256,1024]{1,0:T(8,128)(2,1)S(1)}, bf16[256,1024]{1,0:T(8,128)(2,1)S(1)}, bf16[256,1024]{1,0:T(8,128)(2,1)S(1)}, bf16[256,1024]{1,0:T(8,128)(2,1)S(1)}) custom-call(bf16[256,1024]{1,0:T(8,128)(2,1)S(1)} %convolution_convert_fusion.19.refs_0_, bf16[256,1024]{1,0:T(8,128)(2,1)S(1)} %convolution_convert_fusion.14.refs_1_, ...), custom_call_target="tpu_custom_call" | custom-call | tf_op jit(solution)/shard_map/transpose(jvp(self_heads_joint_pull))/pallas_call | solution.py:906
  695.3 2.2 copy-done.70
  701.6 3.0 multiply_reduce_fusion.4
  706.2 2.4 convolution_add_fusion.7
  710.5 71.4 %gather_second.1 = (bf16[32,576,512]{2,1,0:T(8,128)(2,1)}, bf16[32,64,64]{2,1,0:T(8,128)(2,1)S(1)}, f32[32,64,128]{2,1,0:T(8,128)S(1)}) custom-call(bf16[2,272,512]{2,1,0:T(8,128)(2,1)S(1)} %pad_maximum_fusion.16.cotan_ref, bf16[32,576,512]{2,1,0:T(8,128)(2,1)} %get-tuple-element.68.refs_0_.kernel_ref, bf16[32,256,512]{2,1,0:T(8,128)(2,1)} %copy-done.4, ...), custom_call_target="tpu_custom_call" | custom-call | tf_op jit(solution)/shard_map/gather_second/pallas_call | solution.py:1467
  783.6 2.2 reshape.429
  785.9 19.5 %all-to-all-start.3 = ((bf16[16,2,4096]{2,1,0:T(2,128)(2,1)}), bf16[16,2,4096]{2,1,0:T(2,128)(2,1)S(1)}, u32[]{:S(2)}, u32[]{:S(2)}) async-start(bf16[16,2,4096]{2,1,0:T(2,128)(2,1)} %reshape.429), calls=%async_computation.3 | async-start | bytes 524288 | tf_op jit(solution)/shard_map/all_to_all | solution.py:970
  805.5 2.6 fusion.74
  809.8 2.3 copy-done.3
  812.1 17.1 %unmix_kernels.1 = (f32[8,576,512]{2,1,0:T(8,128)}, f32[512,128]{1,0:T(8,128)S(1)}) custom-call(bf16[512,256]{1,0:T(8,128)(2,1)S(1)} %copy-done.6, bf16[8,576,512]{2,1,0:T(8,128)(2,1)S(1)} %bitcast.201, bf16[32,576,512]{2,1,0:T(8,128)(2,1)} %get-tuple-element.99.refs_2_), custom_call_target="tpu_custom_call" | custom-call | tf_op jit(solution)/shard_map/unmix_kernels/pallas_call | solution.py:653
  833.5 2.4 collective-permute-done.7
  838.5 2.1 fusion.72
  843.9 11.5 %collective-permute-done = f32[256,512]{1,0:T(8,128)S(1)} collective-permute-done((f32[256,512]{1,0:T(8,128)S(1)}, f32[256,512]{1,0:T(8,128)S(1)}, u32[]{:S(2)}, u32[]{:S(2)}) %collective-permute-start) | collective-permute-done | bytes 524320 | tf_op jit(solution)/shard_map/ppermute | solution.py:936
  858.7 3.9 convolution_convert_fusion.4.refs_4_
  862.6 1.7 convolution_convert_fusion.7.refs_8_
  864.3 1.7 convolution_convert_fusion.8.refs_7_
  866.1 2.7 convolution_convert_fusion.3.refs_5_
  868.8 2.6 convolution_convert_fusion.6.refs_2_
  871.5 2.7 convolution_convert_fusion.5.refs_3_
  874.6 7.0 convolution_convert_fusion.refs_1_
  881.6 6.7 convolution_convert_fusion.1.refs_0_
  888.6 2.6 convolution_convert_fusion.2.refs_6_
  891.2 172.6 %sum_weights.1 = (f32[64,2048]{1,0:T(8,128)}, f32[64,2048]{1,0:T(8,128)}, f32[64,512]{1,0:T(8,128)}, f32[64,512]{1,0:T(8,128)}, f32[64,512]{1,0:T(8,128)}, /*ind...) custom-call(bf16[1024,4096]{1,0:T(8,128)(2,1)} %convolution_convert_fusion.1.refs_0_, ...), custom_call_target="tpu_custom_call" | custom-call | tf_op jit(solution)/shard_map/sum_weights/pallas_call | solution.py:2012
  1064.7 1.7 copy.116
  1069.3 2.2 fusion.69
  1072.8 2.4 fusion.61
  1075.2 3.2 fusion.63
  1078.3 3.2 fusion.68
  1081.6 7.6 fusion
  (569 shorter events, 103.4 us)
Async XLA Ops:
  7.2 150.8 %copy-start = (bf16[1000,768]{1,0:T(8,128)(2,1)S(1)}, bf16[1000,768]{1,0:T(8,128)(2,1)}, u32[]{:S(2)}) copy-start(bf16[1000,768]{1,0:T(8,128)(2,1)} %param.33) | copy-start | bytes 4608004
  7.2 14.7 %copy-start.179 = (s32[2,64]{1,0:T(2,128)S(1)}, s32[2,64]{1,0:T(2,128)}, u32[]{:S(2)}) copy-start(s32[2,64]{1,0:T(2,128)} %param.29) | copy-start | bytes 1540
  7.2 14.8 %copy-start.180 = (s32[2]{0:T(128)S(1)}, s32[2]{0:T(128)}, u32[]{:S(2)}) copy-start(s32[2]{0:T(128)} %param.30) | copy-start | bytes 28
  7.2 16.0 %copy-start.174 = (bf16[2,3,256]{2,0,1:T(2,128)(2,1)S(1)}, bf16[2,3,256]{2,0,1:T(2,128)(2,1)}, u32[]{:S(2)}) copy-start(bf16[2,3,256]{2,0,1:T(2,128)(2,1)} %param.52) | copy-start | bytes 9220
  7.2 16.1 %copy-start.178 = (s32[2]{0:T(128)S(1)}, s32[2]{0:T(128)}, u32[]{:S(2)}) copy-start(s32[2]{0:T(128)} %param.28) | copy-start | bytes 28
  7.3 16.7 %copy-start.175 = (bf16[1024]{0:T(1024)(128)(2,1)S(1)}, bf16[1024]{0:T(1024)(128)(2,1)}, u32[]{:S(2)}) copy-start(bf16[1024]{0:T(1024)(128)(2,1)} %param.38) | copy-start | bytes 6148
  7.3 16.7 %copy-start.176 = (bf16[1024]{0:T(1024)(128)(2,1)S(1)}, bf16[1024]{0:T(1024)(128)(2,1)}, u32[]{:S(2)}) copy-start(bf16[1024]{0:T(1024)(128)(2,1)} %param.39) | copy-start | bytes 6148
  12.7 136.2 %copy-start.77 = (bf16[2,64,1024]{2,1,0:T(8,128)(2,1)}, bf16[2,64,1024]{2,1,0:T(8,128)(2,1)S(1)}, u32[]{:S(2)}) copy-start(bf16[2,64,1024]{2,1,0:T(8,128)(2,1)S(1)} %all_gather.9) | copy-start | bytes 786436
  13.2 137.4 %copy-start.144 = (bf16[512,8]{0,1:T(8,128)(2,1)S(1)}, bf16[512,8]{0,1:T(8,128)(2,1)}, u32[]{:S(2)}) copy-start(bf16[512,8]{0,1:T(8,128)(2,1)} %param.34) | copy-start | bytes 24580
  14.3 138.7 %copy-start.51 = (bf16[512,1024]{1,0:T(8,128)(2,1)S(1)}, bf16[512,1024]{1,0:T(8,128)(2,1)}, u32[]{:S(2)}) copy-start(bf16[512,1024]{1,0:T(8,128)(2,1)} %param.36) | copy-start | bytes 3145732
  14.3 164.3 %all-to-all-start = ((bf16[16,2,4096]{2,1,0:T(2,128)(2,1)}), bf16[16,2,4096]{2,1,0:T(2,128)(2,1)S(1)}, u32[]{:S(2)}, u32[]{:S(2)}) async-start(bf16[16,2,4096]{2,1,0:T(2,128)(2,1)} %reshape.423), calls=%async_computation | async-start | bytes 524288 | tf_op jit(solution)/shard_map/all_to_all | solution.py:962
  23.3 246.9 %copy-start.163 = (f32[256]{0:T(256)}, f32[256]{0:T(256)S(1)}, u32[]{:S(2)}) copy-start(f32[256]{0:T(256)S(1)} %fusion.101) | copy-start | bytes 3076
  23.3 153.1 %copy-start.152 = (bf16[1,3,256]{2,0,1:T(2,128)(2,1)}, bf16[1,3,256]{2,0,1:T(2,128)(2,1)S(1)}, u32[]{:S(2)}) copy-start(bf16[1,3,256]{2,0,1:T(2,128)(2,1)S(1)} %constant_dynamic-slice_fusion.4) | copy-start | bytes 4612
  23.9 246.2 %copy-start.129 = (f32[1024]{0:T(1024)}, f32[1024]{0:T(1024)S(1)}, u32[]{:S(2)}) copy-start(f32[1024]{0:T(1024)S(1)} %convert_element_type.330) | copy-start | bytes 12292
  24.0 246.2 %copy-start.132 = (f32[1024]{0:T(1024)}, f32[1024]{0:T(1024)S(1)}, u32[]{:S(2)}) copy-start(f32[1024]{0:T(1024)S(1)} %convert_element_type.332) | copy-start | bytes 12292
  158.4 19.7 %copy-start.57 = (bf16[64,768]{1,0:T(8,128)(2,1)}, bf16[64,768]{1,0:T(8,128)(2,1)S(1)}, u32[]{:S(2)}) copy-start(bf16[64,768]{1,0:T(8,128)(2,1)S(1)} %convolution_convert_fusion.22) | copy-start | bytes 294916
  160.4 18.5 %copy-start.114 = (f32[32,64]{1,0:T(8,128)}, f32[32,64]{1,0:T(8,128)S(1)}, u32[]{:S(2)}) copy-start(f32[32,64]{1,0:T(8,128)S(1)} %get-tuple-element.237) | copy-start | bytes 24580
  160.4 16.0 %copy-start.126 = (f32[1,1024]{1,0:T(1,128)}, f32[1,1024]{1,0:T(1,128)S(1)}, u32[]{:S(2)}) copy-start(f32[1,1024]{1,0:T(1,128)S(1)} %fusion.79) | copy-start | bytes 12292
  163.1 13.3 %copy-start.118 = (bf16[3,1024]{1,0:T(4,128)(2,1)S(1)}, bf16[3,1024]{1,0:T(4,128)(2,1)}, u32[]{:S(2)}) copy-start(bf16[3,1024]{1,0:T(4,128)(2,1)} %param.37) | copy-start | bytes 18436
  163.1 15.1 %copy-start.48 = (bf16[768,1024]{1,0:T(8,128)(2,1)S(1)}, bf16[768,1024]{1,0:T(8,128)(2,1)}, u32[]{:S(2)}) copy-start(bf16[768,1024]{1,0:T(8,128)(2,1)} %get-tuple-element.75) | copy-start | bytes 4718596
  179.1 117.2 %slice-start = ((s8[8388608]{0:T(1024)(128)(4,1)}), s8[4194304]{0:T(1024)(128)(4,1)S(1)}, s32[]{:S(2)}) async-start(s8[8388608]{0:T(1024)(128)(4,1)} %bitcast.206), calls=%async_computation.6 | async-start | bytes 8388608
  270.8 14.9 %copy-start.26 = (f32[256,1024]{1,0:T(8,128)}, f32[256,1024]{1,0:T(8,128)S(1)}, u32[]{:S(2)}) copy-start(f32[256,1024]{1,0:T(8,128)S(1)} %get-tuple-element.235) | copy-start | bytes 3145732
  270.8 25.6 %slice-start.1 = ((s8[8388608]{0:T(1024)(128)(4,1)}), s8[4194304]{0:T(1024)(128)(4,1)S(1)}, s32[]{:S(2)}) async-start(s8[8388608]{0:T(1024)(128)(4,1)} %bitcast.206), calls=%async_computation.7 | async-start | bytes 8388608
  273.4 12.2 %copy-start.29 = (bf16[1024,1024]{1,0:T(8,128)(2,1)S(1)}, bf16[1024,1024]{1,0:T(8,128)(2,1)}, u32[]{:S(2)}) copy-start(bf16[1024,1024]{1,0:T(8,128)(2,1)} %get-tuple-element.72) | copy-start | bytes 6291460
  286.5 14.4 %copy-start.166 = (f32[256]{0:T(256)}, f32[256]{0:T(256)S(1)}, u32[]{:S(2)}) copy-start(f32[256]{0:T(256)S(1)} %get-tuple-element.287) | copy-start | bytes 3076
  343.7 15.8 %copy-start.68 = (bf16[1024,1024]{1,0:T(8,128)(2,1)S(1)}, bf16[1024,1024]{1,0:T(8,128)(2,1)}, u32[]{:S(2)}) copy-start(bf16[1024,1024]{1,0:T(8,128)(2,1)} %get-tuple-element.71) | copy-start | bytes 6291460
  364.4 6.6 collective-permute-start.3
  372.1 88.0 %copy-start.82 = (bf16[2,256,512]{2,1,0:T(8,128)(2,1)S(1)}, bf16[2,256,512]{2,1,0:T(8,128)(2,1)}, u32[]{:S(2)}) copy-start(bf16[2,256,512]{2,1,0:T(8,128)(2,1)} %param.50) | copy-start | bytes 1572868
  442.5 26.4 %all-to-all-start.1 = ((bf16[16,2,4096]{2,1,0:T(2,128)(2,1)}), bf16[16,2,4096]{2,1,0:T(2,128)(2,1)}, u32[]{:S(2)}, u32[]{:S(2)}) async-start(bf16[16,2,4096]{2,1,0:T(2,128)(2,1)} %reshape.425), calls=%async_computation.1 | async-start | bytes 524288 | tf_op jit(solution)/shard_map/all_to_all | solution.py:970
  460.9 12.5 %collective-permute-start.2 = (bf16[256,512]{1,0:T(8,128)(2,1)}, bf16[256,512]{1,0:T(8,128)(2,1)}, u32[]{:S(2)}, u32[]{:S(2)}) collective-permute-start(bf16[256,512]{1,0:T(8,128)(2,1)} %dynamic-slice_bitcast_fusion), channel_id=1, source_target_pairs={{0,1},{1,0},{2,3},{3,2},{4,5},{5,4},{6,7},{7,6},{8,9},{9,8},{10,11... | collective-permute-start | bytes 786440 | tf_op jit(solution)/shard_map/ppermute | solution.py:936
  473.0 5.6 collective-permute-start.4
  478.6 4.7 collective-permute-start.5
  486.8 17.1 %all-to-all-start.2 = ((bf16[16,2,4096]{2,1,0:T(2,128)(2,1)}), bf16[16,2,4096]{2,1,0:T(2,128)(2,1)}, u32[]{:S(2)}, u32[]{:S(2)}) async-start(bf16[16,2,4096]{2,1,0:T(2,128)(2,1)} %reshape.427), calls=%async_computation.2 | async-start | bytes 524288 | tf_op jit(solution)/shard_map/all_to_all | solution.py:962
  506.1 80.5 %copy-start.28 = (f32[256,1024]{1,0:T(8,128)S(1)}, f32[256,1024]{1,0:T(8,128)}, u32[]{:S(2)}) copy-start(f32[256,1024]{1,0:T(8,128)} %copy-done.26) | copy-start | bytes 3145732
  506.1 80.5 %copy-start.40 = (f32[272,1024]{1,0:T(8,128)S(1)}, f32[272,1024]{1,0:T(8,128)}, u32[]{:S(2)}) copy-start(f32[272,1024]{1,0:T(8,128)} %copy-done.38) | copy-start | bytes 3342340
  506.1 80.5 %copy-start.113 = (f32[1,1024]{1,0:T(1,128)S(1)}, f32[1,1024]{1,0:T(1,128)}, u32[]{:S(2)}) copy-start(f32[1,1024]{1,0:T(1,128)} %copy-done.111) | copy-start | bytes 12292
  506.1 80.5 %copy-start.131 = (f32[1024]{0:T(1024)S(1)}, f32[1024]{0:T(1024)}, u32[]{:S(2)}) copy-start(f32[1024]{0:T(1024)} %copy-done.129) | copy-start | bytes 12292
  506.1 80.5 %copy-start.134 = (f32[1024]{0:T(1024)S(1)}, f32[1024]{0:T(1024)}, u32[]{:S(2)}) copy-start(f32[1024]{0:T(1024)} %copy-done.132) | copy-start | bytes 12292
  506.1 80.5 %copy-start.165 = (f32[256]{0:T(256)S(1)}, f32[256]{0:T(256)}, u32[]{:S(2)}) copy-start(f32[256]{0:T(256)} %copy-done.163) | copy-start | bytes 3076
  590.8 14.1 %copy-start.31 = (bf16[1024,1024]{1,0:T(8,128)(2,1)S(1)}, bf16[1024,1024]{1,0:T(8,128)(2,1)}, u32[]{:S(2)}) copy-start(bf16[1024,1024]{1,0:T(8,128)(2,1)} %get-tuple-element.72) | copy-start | bytes 6291460
  621.2 26.4 %copy-start.35 = (f32[256,1024]{1,0:T(8,128)}, f32[256,1024]{1,0:T(8,128)S(1)}, u32[]{:S(2)}) copy-start(f32[256,1024]{1,0:T(8,128)S(1)} %get-tuple-element.303) | copy-start | bytes 3145732
  621.5 13.5 %copy-start.71 = (bf16[256,1024]{1,0:T(8,128)(2,1)}, bf16[256,1024]{1,0:T(8,128)(2,1)S(1)}, u32[]{:S(2)}) copy-start(bf16[256,1024]{1,0:T(8,128)(2,1)S(1)} %add_convert_fusion) | copy-start | bytes 1572868
  635.0 12.7 %copy-start.60 = (bf16[256,512]{1,0:T(8,128)(2,1)S(1)}, bf16[256,512]{1,0:T(8,128)(2,1)}, u32[]{:S(2)}) copy-start(bf16[256,512]{1,0:T(8,128)(2,1)} %copy-done.59) | copy-start | bytes 786436
  635.0 12.7 %copy-start.62 = (bf16[256,512]{1,0:T(8,128)(2,1)S(1)}, bf16[256,512]{1,0:T(8,128)(2,1)}, u32[]{:S(2)}) copy-start(bf16[256,512]{1,0:T(8,128)(2,1)} %copy-done.61) | copy-start | bytes 786436
  651.4 13.2 %copy-start.46 = (bf16[1024,1024]{1,0:T(8,128)(2,1)S(1)}, bf16[1024,1024]{1,0:T(8,128)(2,1)}, u32[]{:S(2)}) copy-start(bf16[1024,1024]{1,0:T(8,128)(2,1)} %get-tuple-element.73) | copy-start | bytes 6291460
  704.8 5.5 collective-permute-start.6
  710.5 95.0 %copy-start.120 = (bf16[3,1024]{1,0:T(4,128)(2,1)S(1)}, bf16[3,1024]{1,0:T(4,128)(2,1)}, u32[]{:S(2)}) copy-start(bf16[3,1024]{1,0:T(4,128)(2,1)} %param.37) | copy-start | bytes 18436
  710.5 95.0 %copy-start.128 = (f32[1,1024]{1,0:T(1,128)S(1)}, f32[1,1024]{1,0:T(1,128)}, u32[]{:S(2)}) copy-start(f32[1,1024]{1,0:T(1,128)} %copy-done.126) | copy-start | bytes 12292
  710.5 95.0 %copy-start.155 = (bf16[1,3,256]{2,0,1:T(2,128)(2,1)S(1)}, bf16[1,3,256]{2,0,1:T(2,128)(2,1)}, u32[]{:S(2)}) copy-start(bf16[1,3,256]{2,0,1:T(2,128)(2,1)} %constant_dynamic-slice_fusion.3) | copy-start | bytes 4612
  783.6 25.1 %copy-start.9 = (f32[32,64,128]{2,1,0:T(8,128)S(1)}, f32[32,64,128]{2,1,0:T(8,128)}, u32[]{:S(2)}) copy-start(f32[32,64,128]{2,1,0:T(8,128)} %copy-done.8) | copy-start | bytes 3145732
  783.6 25.4 %copy-start.115 = (f32[32,64]{1,0:T(8,128)S(1)}, f32[32,64]{1,0:T(8,128)}, u32[]{:S(2)}) copy-start(f32[32,64]{1,0:T(8,128)} %copy-done.114) | copy-start | bytes 24580
  785.9 23.9 %copy-start.6 = (bf16[512,256]{1,0:T(8,128)(2,1)S(1)}, bf16[512,256]{1,0:T(8,128)(2,1)}, u32[]{:S(2)}) copy-start(bf16[512,256]{1,0:T(8,128)(2,1)} %copy-done.5) | copy-start | bytes 786436
  785.9 44.0 %all-to-all-start.3 = ((bf16[16,2,4096]{2,1,0:T(2,128)(2,1)}), bf16[16,2,4096]{2,1,0:T(2,128)(2,1)S(1)}, u32[]{:S(2)}, u32[]{:S(2)}) async-start(bf16[16,2,4096]{2,1,0:T(2,128)(2,1)} %reshape.429), calls=%async_computation.3 | async-start | bytes 524288 | tf_op jit(solution)/shard_map/all_to_all | solution.py:970
  805.4 259.3 %all-gather.3.cloned.1.call-start = ((), (), s32[]{:S(2)}) async-start(), calls=%async_computation.4 | async-start | bytes 1351680 | tf_op jit(solution)/shard_map/all_gather | solution.py:2221
  831.0 4.8 collective-permute-start.7
  833.4 22.1 %copy-start.54 = (f32[256,1024]{1,0:T(8,128)S(1)}, f32[256,1024]{1,0:T(8,128)}, u32[]{:S(2)}) copy-start(f32[256,1024]{1,0:T(8,128)} %get-tuple-element.257) | copy-start | bytes 3145732
  837.7 243.9 %all-gather.5.cloned.1.call-start = ((), (), s32[]{:S(2)}) async-start(), calls=%async_computation.5 | async-start | bytes 3244032 | tf_op jit(solution)/shard_map/all_gather | solution.py:2240
  840.6 2.6 collective-permute-start.1
  843.0 12.4 %collective-permute-start = (f32[256,512]{1,0:T(8,128)S(1)}, f32[256,512]{1,0:T(8,128)S(1)}, u32[]{:S(2)}, u32[]{:S(2)}) collective-permute-start(f32[256,512]{1,0:T(8,128)S(1)} %constant_dynamic-slice_fusion.6), channel_id=1, source_target_pairs={{0,1},{1,0},{2,3},{3,2},{4,5},{5,4},{6,7},{7,6},{8,9},{9,8},{10,11... | collective-permute-start | bytes 1572872 | tf_op jit(solution)/shard_map/ppermute | solution.py:936
  843.9 12.8 %copy-start.23 = (bf16[64,1024]{1,0:T(8,128)(2,1)S(1)}, bf16[64,1024]{1,0:T(8,128)(2,1)}, u32[]{:S(2)}) copy-start(bf16[64,1024]{1,0:T(8,128)(2,1)} %copy-done.22) | copy-start | bytes 393220
  843.9 12.8 %copy-start.49 = (bf16[768,1024]{1,0:T(8,128)(2,1)S(1)}, bf16[768,1024]{1,0:T(8,128)(2,1)}, u32[]{:S(2)}) copy-start(bf16[768,1024]{1,0:T(8,128)(2,1)} %get-tuple-element.75) | copy-start | bytes 4718596
  888.3 175.5 %collective-permute-start.8 = (f32[64,512]{1,0:T(8,128)S(1)}, f32[64,512]{1,0:T(8,128)S(1)}, u32[]{:S(2)}, u32[]{:S(2)}) collective-permute-start(f32[64,512]{1,0:T(8,128)S(1)} %constant_dynamic-slice_fusion), channel_id=1, source_target_pairs={{0,1},{1,0},{2,3},{3,2},{4,5},{5,4},{6,7},{7,6},{8,9},{9,8},{10,11... | collective-permute-start | bytes 393224 | tf_op jit(solution)/shard_map/ppermute | solution.py:936
  1081.6 12.2 %copy-start.93 = (f32[64,2048]{1,0:T(8,128)S(1)}, f32[64,2048]{1,0:T(8,128)}, u32[]{:S(2)}) copy-start(f32[64,2048]{1,0:T(8,128)} %get-tuple-element.348) | copy-start | bytes 1572868
  1081.6 13.8 %copy-start.1 = (bf16[1000,768]{1,0:T(8,128)(2,1)S(1)}, bf16[1000,768]{1,0:T(8,128)(2,1)}, u32[]{:S(2)}) copy-start(bf16[1000,768]{1,0:T(8,128)(2,1)} %param.33) | copy-start | bytes 4608004
  (137 other events, 523.9 us)
Sparse Core Ops, SparseCore 0:
  837.8 55.5 all-gather.2
  896.9 67.2 all-gather.4
